TPU v7x, 32 devices: a whole 2x2x4 slice. The times are simulated.
32 devices in a mesh: section: 4 (over z), dp: 2 (over x), tensor: 4 (over y, core).
Axes of the slice: x: 2, y: 2, z: 4, core: 2. Of those that a mesh axis runs over, the one named last changes fastest.
Arguments:
- inputs: bfloat16 [4, 2, 256, 3584], P('section', 'dp', None, 'tensor'), may hold values from -8 to 8
- qkv_weight: bfloat16 [4, 3, 3584, 3584], P('section', None, 'dp', 'tensor')
- norm_gain: bfloat16 [4, 3584], P('section'), may hold values from 0.25 to 1.75
- preempted: int32 [4], P('section'), may hold values 0 or 1
Outputs:
- outputs: bfloat16 [4, 2, 256, 3584], P('section', 'dp', None, 'tensor')
All inputs are finite; a program needn't handle non-finite values. No bound on the sum of `preempted` on one device may be relied on, other than what follows from the above.
Results may differ from a plain program's by a relative error of at most 0.008.
Values may be sent and summed in bfloat16 or wider, within the bound.
No kernel may reach another device: no remote copies, remote signals or barrier semaphores. Data moves between devices by JAX's collectives and lax.ppermute only.
A program may use at most 64 MiB of HBM per device.

v0:
```python
import jax
import jax.numpy as jnp
from jax import lax
from jax.sharding import PartitionSpec as P

HD = 128


def from_behind(array, axis, by):
    size = lax.axis_size(axis)
    pairs = [(i, i + by) for i in range(size) if 0 <= i + by < size]
    return lax.ppermute(array, axis, pairs)


def project(normed, weight):
    all_rows = lax.all_to_all(normed, "dp", split_axis=1, concat_axis=0, tiled=True)
    return lax.psum_scatter(
        jnp.einsum("rd,kde->rke", all_rows, weight, preferred_element_type=jnp.float32),
        "dp",
        scatter_dimension=0,
        tiled=True,
    )


def gather_rows(hidden_in):
    return lax.all_gather(hidden_in, "tensor", axis=2, tiled=True)


def attend(hidden_in, gathered, weight, gain_row):
    seq_count, length, local_width = hidden_in.shape
    float_acts = gathered.astype(jnp.float32)
    inverse_rms = lax.rsqrt(jnp.mean(float_acts * float_acts, axis=-1, keepdims=True) + 1e-05)
    normed = (float_acts * inverse_rms * gain_row).astype(jnp.bfloat16)
    flat_rows = normed.reshape(seq_count * length, gathered.shape[2])
    projected = project(flat_rows, weight).astype(jnp.bfloat16)
    head_size = HD
    local_heads = local_width // head_size
    head_shape = (seq_count, length, local_heads, head_size)
    queries = projected[:, 0].reshape(head_shape)
    key_rows = projected[:, 1].reshape(head_shape)
    values = projected[:, 2].reshape(head_shape)
    scores = jnp.einsum(
        "sqhd,skhd->shqk", queries, key_rows, preferred_element_type=jnp.float32
    ) / jnp.sqrt(jnp.float32(head_size))
    causal = jnp.arange(length)[:, None] >= jnp.arange(length)[None, :]
    scores = jnp.where(causal, scores, jnp.float32(-1e30))
    probability = jax.nn.softmax(scores, axis=-1).astype(jnp.bfloat16)
    mixture = jnp.einsum("shqk,skhd->sqhd", probability, values, preferred_element_type=jnp.float32)
    return (hidden_in.astype(jnp.float32) + mixture.reshape(seq_count, length, local_width)).astype(
        jnp.bfloat16
    )


def local(inputs, qkv_weight, norm_gain, preempted):
    hidden_in = inputs[0]
    weight = qkv_weight[0]
    gain_row = norm_gain[0]
    own_out = attend(hidden_in, gather_rows(hidden_in), weight, gain_row)
    before = from_behind(own_out, "section", 1)
    recovered = attend(before, gather_rows(before), weight, gain_row)
    result = jnp.where(preempted[0] == 1, recovered, own_out)
    return result[None]


def solution(mesh):
    placed = (
        P("section", "dp", None, "tensor"),
        P("section", None, "dp", "tensor"),
        P("section", None),
        P("section"),
    )
    return jax.shard_map(
        local,
        mesh=mesh,
        in_specs=placed,
        out_specs=P("section", "dp", None, "tensor"),
        check_vma=False,
    )
```

profile of v0, /device:TPU:0, one launch (start us, length us, event | category | flops | bytes accessed | tf_op | source)
XLA Modules:
  0.0 315.9 jit_solution(13094964915256303967)
XLA Ops:
  8.1 24.7 %all-gather.6.cloned.1.call-done = bf16[1,1,256,3584]{3,2,1,0:T(8,128)(2,1)} async-done(((bf16[1,1,256,896]{3,2,1,0:T(8,128)(2,1)}), bf16[1,1,256,3584]{3,2,1,0:T(8,128)(2,1)}) %all-gather.6.cloned.1.call-update) | async-done | bytes 1835024 | tf_op jit(solution)/shard_map/all_gather | solution.py:26
  32.8 2.1 fusion.9
  34.9 1.8 fusion.11
  36.6 4.0 %all_to_all.28 = bf16[256,2,1792]{2,1,0:T(2,128)(2,1)S(1)} reshape(bf16[1,256,3584]{2,1,0:T(8,128)(2,1)} %fusion.11) | data formatting | bytes 3670016 | tf_op jit(solution)/shard_map/all_to_all | solution.py:16
  40.9 25.2 %all_to_all.38 = bf16[256,2,1792]{2,0,1:T(8,128)(2,1)S(1)} all-to-all(bf16[256,2,1792]{2,0,1:T(8,128)(2,1)S(1)} %copy.17), channel_id=1, replica_groups=mesh['section'=4,'dp'=2,'tensor'=4] {'dp'}, dimensions={1} | all-to-all | bytes 3670016 | tf_op jit(solution)/shard_map/all_to_all | solution.py:16
  66.1 11.0 %fusion.4 = f32[512,3,896]{2,0,1:T(8,128)} fusion(bf16[512,1792,1]{1,0,2:T(8,128)(2,1)S(1)} %bitcast.49, bf16[1,3,1792,896]{3,2,1,0:T(8,128)(2,1)} %param.5), kind=kOutput, calls=%fused_computation.4 | convolution fusion | flops 4932501504 | bytes 16973824 | tf_op jit(solution)/shard_map/rd,kde->rke/dot_general | solution.py:18
  77.2 67.7 %reduce-scatter.3.cloned.1.call-done = f32[256,3,896]{2,0,1:T(8,128)} async-done(((f32[512,3,896]{2,0,1:T(8,128)}), f32[256,3,896]{2,0,1:T(8,128)}) %reduce-scatter.3.cloned.1.call-update) | async-done | bytes 2752528 | tf_op jit(solution)/shard_map/reduce_scatter | solution.py:17
  144.9 1.9 convert_element_type.70
  147.6 2.0 fusion.35
  149.6 1.8 fusion.19
  152.5 3.4 %collective-permute-start = (bf16[1,256,896]{2,1,0:T(8,128)(2,1)S(1)}, bf16[1,256,896]{2,1,0:T(8,128)(2,1)S(1)}, u32[]{:S(2)}, u32[]{:S(2)}) collective-permute-start(bf16[1,256,896]{2,1,0:T(8,128)(2,1)S(1)} %fusion.14), channel_id=1, source_target_pairs={{0,8},{8,16},{16,24},{1,9},{9,17},{17,25},{2,10},{10,18},{18,26},{... | collective-permute-start | bytes 1376264 | tf_op jit(solution)/shard_map/ppermute | solution.py:12
  155.9 9.8 %collective-permute-done = bf16[1,256,896]{2,1,0:T(8,128)(2,1)S(1)} collective-permute-done((bf16[1,256,896]{2,1,0:T(8,128)(2,1)S(1)}, bf16[1,256,896]{2,1,0:T(8,128)(2,1)S(1)}, u32[]{:S(2)}, u32[]{:S(2)}) %collective-permute-start) | collective-permute-done | bytes 458784 | tf_op jit(solution)/shard_map/ppermute | solution.py:12
  165.7 0.8 copy-done.3
  166.5 22.2 %all-gather.4.cloned.1.call-done = bf16[1,256,3584]{2,1,0:T(8,128)(2,1)} async-done(((bf16[1,256,896]{2,1,0:T(8,128)(2,1)}), bf16[1,256,3584]{2,1,0:T(8,128)(2,1)}) %all-gather.4.cloned.1.call-update) | async-done | bytes 1835024 | tf_op jit(solution)/shard_map/all_gather | solution.py:26
  188.8 2.1 fusion.6
  190.9 1.8 fusion.8
  192.6 4.0 %all_to_all.32 = bf16[256,2,1792]{2,1,0:T(2,128)(2,1)S(1)} reshape(bf16[1,256,3584]{2,1,0:T(8,128)(2,1)} %fusion.8) | data formatting | bytes 3670016 | tf_op jit(solution)/shard_map/all_to_all | solution.py:16
  196.9 25.2 %all_to_all.39 = bf16[256,2,1792]{2,0,1:T(8,128)(2,1)S(1)} all-to-all(bf16[256,2,1792]{2,0,1:T(8,128)(2,1)S(1)} %copy.25), channel_id=1, replica_groups=mesh['section'=4,'dp'=2,'tensor'=4] {'dp'}, dimensions={1} | all-to-all | bytes 3670016 | tf_op jit(solution)/shard_map/all_to_all | solution.py:16
  222.1 11.0 %fusion.2 = f32[512,3,896]{2,0,1:T(8,128)} fusion(bf16[512,1792,1]{1,0,2:T(8,128)(2,1)S(1)} %bitcast.50, bf16[1,3,1792,896]{3,2,1,0:T(8,128)(2,1)} %param.5), kind=kOutput, calls=%fused_computation.2 | convolution fusion | flops 4932501504 | bytes 16973824 | tf_op jit(solution)/shard_map/rd,kde->rke/dot_general | solution.py:18
  233.8 67.1 %reduce-scatter.5.cloned.1.call-done = f32[256,3,896]{2,0,1:T(8,128)} async-done(((f32[512,3,896]{2,0,1:T(8,128)}), f32[256,3,896]{2,0,1:T(8,128)}) %reduce-scatter.5.cloned.1.call-update) | async-done | bytes 2752528 | tf_op jit(solution)/shard_map/reduce_scatter | solution.py:17
  300.9 1.9 convert_element_type.76
  303.6 2.0 fusion.36
  305.6 1.8 fusion.20
  308.4 0.9 fusion.24
  (34 shorter events, 5.6 us)
Async XLA Ops:
  6.5 26.2 %all-gather.6.cloned.1.call-start = ((), (), s32[]{:S(2)}) async-start(), calls=%async_computation.7 | async-start | bytes 2293760 | tf_op jit(solution)/shard_map/all_gather | solution.py:26
  7.3 137.6 %reduce-scatter.3.cloned.1.call-start = ((), (), s32[]{:S(2)}) async-start(), calls=%async_computation.4 | async-start | bytes 8257536 | tf_op jit(solution)/shard_map/reduce_scatter | solution.py:17
  32.8 2.1 copy-start
  77.1 111.6 %all-gather.4.cloned.1.call-start = ((), (), s32[]{:S(2)}) async-start(), calls=%async_computation.5 | async-start | bytes 2293760 | tf_op jit(solution)/shard_map/all_gather | solution.py:26
  151.4 1.0 copy-start.2
  152.5 13.2 %collective-permute-start = (bf16[1,256,896]{2,1,0:T(8,128)(2,1)S(1)}, bf16[1,256,896]{2,1,0:T(8,128)(2,1)S(1)}, u32[]{:S(2)}, u32[]{:S(2)}) collective-permute-start(bf16[1,256,896]{2,1,0:T(8,128)(2,1)S(1)} %fusion.14), channel_id=1, source_target_pairs={{0,8},{8,16},{16,24},{1,9},{9,17},{17,25},{2,10},{10,18},{18,26},{... | collective-permute-start | bytes 1376264 | tf_op jit(solution)/shard_map/ppermute | solution.py:12
  165.7 0.8 copy-start.3
  166.5 134.4 %reduce-scatter.5.cloned.1.call-start = ((), (), s32[]{:S(2)}) async-start(), calls=%async_computation.6 | async-start | bytes 8257536 | tf_op jit(solution)/shard_map/reduce_scatter | solution.py:17
  188.8 2.1 copy-start.1
  307.4 1.0 copy-start.4
Sparse Core Ops, SparseCore 0:
  8.9 23.8 all-gather.5
  77.2 67.5 reduce-scatter.2
  166.6 22.1 all-gather.3
  233.2 67.6 reduce-scatter.4
where the time goes:
time: 317 us; the launch traced here: 316 us
  waiting for transfers between devices  192 us (61%)
  blocking collectives  50.5 us (16%)
  matrix products  29.6 us (9%)
  between operations  13.9 us (4%)
  other arithmetic  13.3 us (4%)
  local copies, waits for them, and re-layouts  12.7 us (4%)
  starting transfers between devices  3.54 us (1%)
    reduce_scatter x2, waiting for transfers between devices, project(): lax.psum_scatter(jnp.einsum('rd,kde->rke', all_rows, weight, preferred_el...  135 us
    all_to_all x2, blocking collectives, project(): lax.all_to_all(normed, 'dp', split_axis=1, concat_axis=0, tiled=True)  50.5 us
    all_gather x2, waiting for transfers between devices, gather_rows(): return lax.all_gather(hidden_in, 'tensor', axis=2, tiled=True)  46.9 us
    dot_general x2, matrix products, project(): jnp.einsum('rd,kde->rke', all_rows, weight, preferred_element_type=jnp.fl...  22 us
    ppermute x1, waiting for transfers between devices, from_behind(): return lax.ppermute(array, axis, pairs)  9.75 us
    all_to_all x4, local copies, waits for them, and re-layouts, project(): lax.all_to_all(normed, 'dp', split_axis=1, concat_axis=0, tiled=True)  8.45 us
  transfers between devices with their start and end apart: 5, of which 5 were waited for; matrix products, arithmetic and copies ran while one was open for 0% of the time, Pallas kernels for 0%

commit v1 on v0

v1 whole, which is shorter than its diff:
```python
import jax
import jax.numpy as jnp
from jax import lax
from jax.sharding import PartitionSpec as P

HD = 128
EPS = 1e-05
AXES = ("section", "dp", "tensor")
F32 = jnp.float32
BF16 = jnp.bfloat16


def permute(array, sections, hop):
    pairs = []
    for s in range(sections):
        for d in range(2):
            for y in range(2):
                for c in range(2):
                    to = hop(s, d, y, c)
                    if to is None or not 0 <= to[0] < sections:
                        continue
                    ts, td, ty, tc = to
                    pairs.append((s * 8 + d * 4 + y * 2 + c, ts * 8 + td * 4 + ty * 2 + tc))
    return lax.ppermute(array, AXES, pairs)


def ring(s, d, y, c):
    return (s, 1 - d, y, c) if d != y else (s, d, 1 - y, c)


def across(s, d, y, c):
    return (s, 1 - d, 1 - y, c) if d != y else None


def sibling(s, d, y, c):
    return (s, d, y, 1 - c)


def peer(s, d, y, c):
    return (s, 1 - d, y, c)


def onward(s, d, y, c):
    return (s + 1, d, y, c)


def chunks_of(heads):
    sizes = []
    while heads > 0:
        sizes.append(min(2, heads))
        heads -= sizes[-1]
    return sizes


def collect(block, sections, d, y, c):
    on_diagonal = d == y
    from_ring = permute(block, sections, ring)
    from_across = permute(block, sections, across)
    mine = jnp.where(on_diagonal, block, from_ring)
    other = jnp.where(on_diagonal, from_ring, from_across)
    both = jnp.stack([other, mine])
    theirs = permute(both, sections, sibling)
    return jnp.where(
        c == 0,
        jnp.concatenate([both, theirs], axis=-1),
        jnp.concatenate([theirs, both], axis=-1),
    )


def layer(block, weight, gain_half, sections, d, y, c):
    length, width = block.shape
    half = weight.shape[1]
    rows = collect(block, sections, d, y, c).astype(F32)
    squares = jnp.sum(rows * rows, axis=-1, keepdims=True)
    mean_half = squares / half
    normed = (rows * lax.rsqrt(mean_half + EPS) * gain_half).astype(BF16)
    peer_mean = permute(mean_half[0], sections, peer)
    inverse = lax.rsqrt((mean_half[1] + peer_mean) * 0.5 + EPS)
    scale_own = inverse * jnp.sqrt(mean_half[1] + EPS)
    scale_peer = inverse * jnp.sqrt(peer_mean + EPS)
    causal = jnp.arange(length)[:, None] >= jnp.arange(length)[None, :]
    outs = []
    start = 0
    for heads in chunks_of(width // HD):
        columns = slice(start * HD, (start + heads) * HD)
        start += heads
        part = weight[:, :, columns]
        sent = jnp.einsum("rd,kde->kre", normed[0], part, preferred_element_type=F32).astype(BF16)
        received = permute(sent, sections, peer)
        kept = jnp.einsum("rd,kde->kre", normed[1], part, preferred_element_type=F32)
        total = (kept * scale_own + received.astype(F32) * scale_peer).astype(BF16)
        queries, keys, values = total.reshape(3, length, heads, HD)
        scores = jnp.einsum("qhd,khd->hqk", queries, keys, preferred_element_type=F32) / jnp.sqrt(F32(HD))
        scores = jnp.where(causal, scores, F32(-1e30))
        probability = jax.nn.softmax(scores, axis=-1).astype(BF16)
        mixture = jnp.einsum("hqk,khd->qhd", probability, values, preferred_element_type=F32)
        outs.append((block[:, columns].astype(F32) + mixture.reshape(length, heads * HD)).astype(BF16))
    return jnp.concatenate(outs, axis=-1)


def solution(mesh):
    sections = mesh.shape["section"]

    def local(inputs, qkv_weight, norm_gain, preempted):
        d = lax.axis_index("dp")
        t = lax.axis_index("tensor")
        y, c = t // 2, t % 2
        weight = qkv_weight[0]
        half = weight.shape[1]
        gain_half = lax.dynamic_slice_in_dim(norm_gain[0], d * half, half)
        own = layer(inputs[0, 0], weight, gain_half, sections, d, y, c)
        before = permute(own, sections, onward)
        shadow = layer(before, weight, gain_half, sections, d, y, c)
        return jnp.where(preempted[0] == 1, shadow, own)[None, None]

    placed = (
        P("section", "dp", None, "tensor"),
        P("section", None, "dp", "tensor"),
        P("section", None),
        P("section"),
    )
    return jax.shard_map(
        local,
        mesh=mesh,
        in_specs=placed,
        out_specs=P("section", "dp", None, "tensor"),
        check_vma=False,
    )
```

time: 317 us -> 194 us (0.61)
  waiting for transfers between devices: 192 us -> 104 us
  blocking collectives: 50.5 us -> 0 us
  starting transfers between devices: 3.54 us -> 25.2 us
  between operations: 13.9 us -> 1.35 us
  matrix products: 29.6 us -> 38.3 us
  other arithmetic: 13.3 us -> 5.69 us
  local copies, waits for them, and re-layouts: 12.7 us -> 18.3 us
    reduce_scatter x2 -> x0, waiting for transfers between devices: 135 us -> none  [project(): lax.psum_scatter(jnp.einsum('rd,kde->rke', all_rows, weight, preferred_el...]
    ppermute x1 -> x17, waiting for transfers between devices: 9.75 us -> 104 us  [permute(): return lax.ppermute(array, AXES, pairs)]
    all_to_all x2 -> x0, blocking collectives: 50.5 us -> none  [project(): lax.all_to_all(normed, 'dp', split_axis=1, concat_axis=0, tiled=True)]
    all_gather x2 -> x0, waiting for transfers between devices: 46.9 us -> none  [gather_rows(): return lax.all_gather(hidden_in, 'tensor', axis=2, tiled=True)]
    ppermute x1 -> x17, starting transfers between devices: 3.42 us -> 25.2 us  [permute(): return lax.ppermute(array, AXES, pairs)]
    unnamed x10 -> x41, local copies, waits for them, and re-layouts: 2.19 us -> 14.8 us
    dot_general x4 -> x32, matrix products: 25.6 us -> 34.8 us  [the longest x8 13.8 us: layer(): jnp.einsum('rd,kde->kre', normed[0], part, preferred_element_type=F32)]
    all_to_all x4 -> x0, local copies, waits for them, and re-layouts: 8.45 us -> none  [project(): lax.all_to_all(normed, 'dp', split_axis=1, concat_axis=0, tiled=True)]
  transfers between devices with their start and end apart: 5 -> 17, of which waited for: 5 -> 6; matrix products, arithmetic and copies ran while one was open for 0% -> 16% of each run, Pallas kernels for 0% -> 0%
where the time goes in v1:
time: 194 us; the launch traced here: 193 us
  waiting for transfers between devices  104 us (54%)
  matrix products  38.3 us (20%)
  starting transfers between devices  25.2 us (13%)
  local copies, waits for them, and re-layouts  18.3 us (9%)
  other arithmetic  5.69 us (3%)
    ppermute x17, waiting for transfers between devices, permute(): return lax.ppermute(array, AXES, pairs)  104 us
    ppermute x17, starting transfers between devices, permute(): return lax.ppermute(array, AXES, pairs)  25.2 us
    unnamed x41, local copies, waits for them, and re-layouts  14.8 us
    dot_general x8, matrix products, layer(): jnp.einsum('rd,kde->kre', normed[0], part, preferred_element_type=F32)  13.8 us
    dot_general x8, matrix products, layer(): jnp.einsum('rd,kde->kre', normed[1], part, preferred_element_type=F32)  10.5 us
    dot_general x8, matrix products, layer(): jnp.einsum('hqk,khd->qhd', probability, values, preferred_element_type=F32)  5.9 us
    dot_general x8, matrix products, layer(): jnp.einsum('qhd,khd->hqk', queries, keys, preferred_element_type=F32)  4.56 us
  transfers between devices with their start and end apart: 17, of which 6 were waited for; matrix products, arithmetic and copies ran while one was open for 16% of the time, Pallas kernels for 0%

profile of v1, /device:TPU:0, one launch (start us, length us, event | category | flops | bytes accessed | tf_op | source)
XLA Modules:
  0.0 193.1 jit_solution(2496849425457611307)
XLA Ops:
  0.0 3.0 %collective-permute-start = (bf16[256,896]{1,0:T(8,128)(2,1)}, bf16[256,896]{1,0:T(8,128)(2,1)S(1)}, u32[]{:S(2)}, u32[]{:S(2)}) collective-permute-start(bf16[256,896]{1,0:T(8,128)(2,1)} %bitcast.280), channel_id=1, source_target_pairs={{0,2},{1,3},{2,6},{3,7},{4,0},{5,1},{6,4},{7,5},{8,10},{9,11},{10,... | collective-permute-start | bytes 1376264 | tf_op jit(solution)/shard_map/ppermute | solution.py:24
  3.7 19.3 %collective-permute-done = bf16[256,896]{1,0:T(8,128)(2,1)S(1)} collective-permute-done((bf16[256,896]{1,0:T(8,128)(2,1)}, bf16[256,896]{1,0:T(8,128)(2,1)S(1)}, u32[]{:S(2)}, u32[]{:S(2)}) %collective-permute-start) | collective-permute-done | bytes 458784 | tf_op jit(solution)/shard_map/ppermute | solution.py:24
  24.3 13.5 %copy.48 = bf16[1,3,1792,896]{2,3,1,0:T(8,128)(2,1)} copy(bf16[1,3,1792,896]{3,2,1,0:T(8,128)(2,1)} %param.5) | data formatting | bytes 19267584 | tf_op args[1]
  39.4 3.7 %fusion.153 = bf16[3,256,256]{1,2,0:T(8,128)(2,1)S(1)} fusion(bf16[3,1792,896]{1,2,0:T(8,128)(2,1)} %bitcast.262, bf16[2,256,1792]{2,1,0:T(8,128)(2,1)S(1)} %fusion.8), kind=kOutput, calls=%fused_computation.99 | convolution fusion | flops 704839680 | bytes 4063232 | tf_op jit(solution)/shard_map/rd,kde->kre/dot_general | solution.py:88
  44.8 1.7 fusion.159
  46.4 3.3 %collective-permute-start.3 = (f32[256,1]{0,1:T(1,128)S(1)}, f32[256,1]{0,1:T(1,128)S(1)}, u32[]{:S(2)}, u32[]{:S(2)}) collective-permute-start(f32[256,1]{0,1:T(1,128)S(1)} %slice_bitcast_fusion.34), channel_id=1, source_target_pairs={{0,4},{1,5},{2,6},{3,7},{4,0},{5,1},{6,2},{7,3},{8,12},{9,13},{10,... | collective-permute-start | bytes 3080 | tf_op jit(solution)/shard_map/ppermute | solution.py:24
  50.4 2.0 %collective-permute-start.6 = (bf16[3,256,256]{1,2,0:T(8,128)(2,1)S(1)}, bf16[3,256,256]{1,2,0:T(8,128)(2,1)S(1)}, u32[]{:S(2)}, u32[]{:S(2)}) collective-permute-start(bf16[3,256,256]{1,2,0:T(8,128)(2,1)S(1)} %fusion.147), channel_id=1, source_target_pairs={{0,4},{1,5},{2,6},{3,7},{4,0},{5,1},{6,2},{7,3},{8,12},{9,13},{10,... | collective-permute-start | bytes 1179656 | tf_op jit(solution)/shard_map/ppermute | solution.py:24
  52.5 1.9 %collective-permute-start.7 = (bf16[3,256,128]{2,1,0:T(8,128)(2,1)S(1)}, bf16[3,256,128]{2,1,0:T(8,128)(2,1)S(1)}, u32[]{:S(2)}, u32[]{:S(2)}) collective-permute-start(bf16[3,256,128]{2,1,0:T(8,128)(2,1)S(1)} %fusion.170), channel_id=1, source_target_pairs={{0,4},{1,5},{2,6},{3,7},{4,0},{5,1},{6,2},{7,3},{8,12},{9,13},{10,... | collective-permute-start | bytes 589832 | tf_op jit(solution)/shard_map/ppermute | solution.py:24
  54.5 28.2 %collective-permute-done.7 = bf16[3,256,128]{2,1,0:T(8,128)(2,1)S(1)} collective-permute-done((bf16[3,256,128]{2,1,0:T(8,128)(2,1)S(1)}, bf16[3,256,128]{2,1,0:T(8,128)(2,1)S(1)}, u32[]{:S(2)}, u32[]{:S(2)}) %collective-permute-start.7) | collective-permute-done | bytes 196640 | tf_op jit(solution)/shard_map/ppermute | solution.py:24
  91.2 2.7 %fusion.96 = bf16[3,256,256]{1,2,0:T(8,128)(2,1)S(1)} fusion(bf16[3,1792,896]{1,2,0:T(8,128)(2,1)} %bitcast.263, bf16[3,256,256]{1,2,0:T(8,128)(2,1)} %collective-permute-done.4, bf16[2,256,1792]{2,1,0:T(8,128)(2,1)S(1)} %copy-done.4, f32[256]{0:T(256)S(1)} %bitcast.339, f32[256]{0:T(256)S(1)} %bitcast.335), kind=kOutput, calls=%fused_computation.66 | convolution fusion | flops 705626112 | bytes 4458496 | tf_op jit(solution)/shard_map/rd,kde->kre/dot_general | solution.py:90
  96.4 1.6 fusion.178
  98.3 3.8 %collective-permute-start.8 = (bf16[256,896]{1,0:T(8,128)(2,1)S(1)}, bf16[256,896]{1,0:T(8,128)(2,1)S(1)}, u32[]{:S(2)}, u32[]{:S(2)}) collective-permute-start(bf16[256,896]{1,0:T(8,128)(2,1)S(1)} %pad_maximum_fusion.2), channel_id=1, source_target_pairs={{0,8},{1,9},{2,10},{3,11},{4,12},{5,13},{6,14},{7,15},{8,16},{9,17... | collective-permute-start | bytes 1376264 | tf_op jit(solution)/shard_map/ppermute | solution.py:24
  102.0 9.3 %collective-permute-done.8 = bf16[256,896]{1,0:T(8,128)(2,1)S(1)} collective-permute-done((bf16[256,896]{1,0:T(8,128)(2,1)S(1)}, bf16[256,896]{1,0:T(8,128)(2,1)S(1)}, u32[]{:S(2)}, u32[]{:S(2)}) %collective-permute-start.8) | collective-permute-done | bytes 458784 | tf_op jit(solution)/shard_map/ppermute | solution.py:24
  112.0 3.5 %collective-permute-start.9 = (bf16[256,896]{1,0:T(8,128)(2,1)S(1)}, bf16[256,896]{1,0:T(8,128)(2,1)S(1)}, u32[]{:S(2)}, u32[]{:S(2)}) collective-permute-start(bf16[256,896]{1,0:T(8,128)(2,1)S(1)} %collective-permute-done.8), channel_id=1, source_target_pairs={{0,2},{1,3},{2,6},{3,7},{4,0},{5,1},{6,4},{7,5},{8,10},{9,11},{10,... | collective-permute-start | bytes 1376264 | tf_op jit(solution)/shard_map/ppermute | solution.py:24
  115.5 17.9 %collective-permute-done.9 = bf16[256,896]{1,0:T(8,128)(2,1)S(1)} collective-permute-done((bf16[256,896]{1,0:T(8,128)(2,1)S(1)}, bf16[256,896]{1,0:T(8,128)(2,1)S(1)}, u32[]{:S(2)}, u32[]{:S(2)}) %collective-permute-start.9) | collective-permute-done | bytes 458784 | tf_op jit(solution)/shard_map/ppermute | solution.py:24
  134.3 1.8 collective-permute-done.11
  137.6 3.7 %fusion.150 = bf16[3,256,256]{1,2,0:T(8,128)(2,1)S(1)} fusion(bf16[3,1792,896]{1,2,0:T(8,128)(2,1)} %bitcast.264, bf16[2,256,1792]{2,1,0:T(8,128)(2,1)S(1)} %fusion.11), kind=kOutput, calls=%fused_computation.98 | convolution fusion | flops 704839680 | bytes 4063232 | tf_op jit(solution)/shard_map/rd,kde->kre/dot_general | solution.py:88
  142.3 1.7 fusion.156
  144.0 2.0 %collective-permute-start.12 = (f32[256,1]{0,1:T(1,128)S(1)}, f32[256,1]{0,1:T(1,128)S(1)}, u32[]{:S(2)}, u32[]{:S(2)}) collective-permute-start(f32[256,1]{0,1:T(1,128)S(1)} %slice_bitcast_fusion.32), channel_id=1, source_target_pairs={{0,4},{1,5},{2,6},{3,7},{4,0},{5,1},{6,2},{7,3},{8,12},{9,13},{10,... | collective-permute-start | bytes 3080 | tf_op jit(solution)/shard_map/ppermute | solution.py:24
  146.7 2.0 %collective-permute-start.15 = (bf16[3,256,256]{1,2,0:T(8,128)(2,1)S(1)}, bf16[3,256,256]{1,2,0:T(8,128)(2,1)S(1)}, u32[]{:S(2)}, u32[]{:S(2)}) collective-permute-start(bf16[3,256,256]{1,2,0:T(8,128)(2,1)S(1)} %fusion.144), channel_id=1, source_target_pairs={{0,4},{1,5},{2,6},{3,7},{4,0},{5,1},{6,2},{7,3},{8,12},{9,13},{10,... | collective-permute-start | bytes 1179656 | tf_op jit(solution)/shard_map/ppermute | solution.py:24
  148.8 1.9 %collective-permute-start.16 = (bf16[3,256,128]{2,1,0:T(8,128)(2,1)S(1)}, bf16[3,256,128]{2,1,0:T(8,128)(2,1)S(1)}, u32[]{:S(2)}, u32[]{:S(2)}) collective-permute-start(bf16[3,256,128]{2,1,0:T(8,128)(2,1)S(1)} %fusion.171), channel_id=1, source_target_pairs={{0,4},{1,5},{2,6},{3,7},{4,0},{5,1},{6,2},{7,3},{8,12},{9,13},{10,... | collective-permute-start | bytes 589832 | tf_op jit(solution)/shard_map/ppermute | solution.py:24
  150.7 27.9 %collective-permute-done.16 = bf16[3,256,128]{2,1,0:T(8,128)(2,1)S(1)} collective-permute-done((bf16[3,256,128]{2,1,0:T(8,128)(2,1)S(1)}, bf16[3,256,128]{2,1,0:T(8,128)(2,1)S(1)}, u32[]{:S(2)}, u32[]{:S(2)}) %collective-permute-start.16) | collective-permute-done | bytes 196640 | tf_op jit(solution)/shard_map/ppermute | solution.py:24
  185.8 2.7 %fusion.99 = bf16[3,256,256]{1,2,0:T(8,128)(2,1)S(1)} fusion(bf16[3,1792,896]{1,2,0:T(8,128)(2,1)} %bitcast.265, bf16[3,256,256]{1,2,0:T(8,128)(2,1)} %collective-permute-done.13, bf16[2,256,1792]{2,1,0:T(8,128)(2,1)S(1)} %copy-done.2, f32[256]{0:T(256)S(1)} %bitcast.331, f32[256]{0:T(256)S(1)} %bitcast.327), kind=kOutput, calls=%fused_computation.67 | convolution fusion | flops 705626112 | bytes 4458496 | tf_op jit(solution)/shard_map/rd,kde->kre/dot_general | solution.py:90
  189.4 1.5 fusion.182
  (124 shorter events, 31.4 us)
Async XLA Ops:
  0.0 22.9 %collective-permute-start = (bf16[256,896]{1,0:T(8,128)(2,1)}, bf16[256,896]{1,0:T(8,128)(2,1)S(1)}, u32[]{:S(2)}, u32[]{:S(2)}) collective-permute-start(bf16[256,896]{1,0:T(8,128)(2,1)} %bitcast.280), channel_id=1, source_target_pairs={{0,2},{1,3},{2,6},{3,7},{4,0},{5,1},{6,4},{7,5},{8,10},{9,11},{10,... | collective-permute-start | bytes 1376264 | tf_op jit(solution)/shard_map/ppermute | solution.py:24
  3.0 20.0 %collective-permute-start.1 = (bf16[256,896]{1,0:T(8,128)(2,1)}, bf16[256,896]{1,0:T(8,128)(2,1)S(1)}, u32[]{:S(2)}, u32[]{:S(2)}) collective-permute-start(bf16[256,896]{1,0:T(8,128)(2,1)} %bitcast.281), channel_id=1, source_target_pairs={{2,4},{3,5},{4,2},{5,3},{10,12},{11,13},{12,10},{13,11},{18,20},{1... | collective-permute-start | bytes 1376264 | tf_op jit(solution)/shard_map/ppermute | solution.py:24
  24.1 13.7 %collective-permute-start.2 = (bf16[2,256,896]{2,1,0:T(8,128)(2,1)S(1)}, bf16[2,256,896]{2,1,0:T(8,128)(2,1)S(1)}, u32[]{:S(2)}, u32[]{:S(2)}) collective-permute-start(bf16[2,256,896]{2,1,0:T(8,128)(2,1)S(1)} %pad_maximum_fusion), channel_id=1, source_target_pairs={{0,1},{1,0},{2,3},{3,2},{4,5},{5,4},{6,7},{7,6},{8,9},{9,8},{10,11... | collective-permute-start | bytes 2752520 | tf_op jit(solution)/shard_map/ppermute | solution.py:24
  24.2 13.5 %copy-start.14 = (bf16[1,3584]{1,0:T(2,128)(2,1)S(1)}, bf16[1,3584]{1,0:T(2,128)(2,1)}, u32[]{:S(2)}) copy-start(bf16[1,3584]{1,0:T(2,128)(2,1)} %param.6) | copy-start | bytes 21508
  38.6 5.2 %copy-start = (bf16[1,3,1792,896]{2,3,1,0:T(8,128)(2,1)S(1)}, bf16[1,3,1792,896]{2,3,1,0:T(8,128)(2,1)}, u32[]{:S(2)}) copy-start(bf16[1,3,1792,896]{2,3,1,0:T(8,128)(2,1)} %copy.48) | copy-start | bytes 28901380
  39.4 46.8 %copy-start.3 = (bf16[2,256,1792]{2,1,0:T(8,128)(2,1)}, bf16[2,256,1792]{2,1,0:T(8,128)(2,1)S(1)}, u32[]{:S(2)}) copy-start(bf16[2,256,1792]{2,1,0:T(8,128)(2,1)S(1)} %fusion.8) | copy-start | bytes 5505028
  46.4 8.1 %collective-permute-start.3 = (f32[256,1]{0,1:T(1,128)S(1)}, f32[256,1]{0,1:T(1,128)S(1)}, u32[]{:S(2)}, u32[]{:S(2)}) collective-permute-start(f32[256,1]{0,1:T(1,128)S(1)} %slice_bitcast_fusion.34), channel_id=1, source_target_pairs={{0,4},{1,5},{2,6},{3,7},{4,0},{5,1},{6,2},{7,3},{8,12},{9,13},{10,... | collective-permute-start | bytes 3080 | tf_op jit(solution)/shard_map/ppermute | solution.py:24
  50.3 33.3 %copy-start.5 = (bf16[1,1,256,896]{3,2,1,0:T(8,128)(2,1)S(1)}, bf16[1,1,256,896]{3,2,1,0:T(8,128)(2,1)}, u32[]{:S(2)}) copy-start(bf16[1,1,256,896]{3,2,1,0:T(8,128)(2,1)} %param.4) | copy-start | bytes 1376260
  50.4 34.2 %collective-permute-start.5 = (bf16[3,256,256]{1,2,0:T(8,128)(2,1)S(1)}, bf16[3,256,256]{1,2,0:T(8,128)(2,1)S(1)}, u32[]{:S(2)}, u32[]{:S(2)}) collective-permute-start(bf16[3,256,256]{1,2,0:T(8,128)(2,1)S(1)} %fusion.153), channel_id=1, source_target_pairs={{0,4},{1,5},{2,6},{3,7},{4,0},{5,1},{6,2},{7,3},{8,12},{9,13},{10,... | collective-permute-start | bytes 1179656 | tf_op jit(solution)/shard_map/ppermute | solution.py:24
  50.4 35.7 %collective-permute-start.6 = (bf16[3,256,256]{1,2,0:T(8,128)(2,1)S(1)}, bf16[3,256,256]{1,2,0:T(8,128)(2,1)S(1)}, u32[]{:S(2)}, u32[]{:S(2)}) collective-permute-start(bf16[3,256,256]{1,2,0:T(8,128)(2,1)S(1)} %fusion.147), channel_id=1, source_target_pairs={{0,4},{1,5},{2,6},{3,7},{4,0},{5,1},{6,2},{7,3},{8,12},{9,13},{10,... | collective-permute-start | bytes 1179656 | tf_op jit(solution)/shard_map/ppermute | solution.py:24
  52.5 38.7 %collective-permute-start.4 = (bf16[3,256,256]{1,2,0:T(8,128)(2,1)}, bf16[3,256,256]{1,2,0:T(8,128)(2,1)}, u32[]{:S(2)}, u32[]{:S(2)}) collective-permute-start(bf16[3,256,256]{1,2,0:T(8,128)(2,1)} %fusion.159), channel_id=1, source_target_pairs={{0,4},{1,5},{2,6},{3,7},{4,0},{5,1},{6,2},{7,3},{8,12},{9,13},{10,... | collective-permute-start | bytes 1179656 | tf_op jit(solution)/shard_map/ppermute | solution.py:24
  52.5 30.2 %collective-permute-start.7 = (bf16[3,256,128]{2,1,0:T(8,128)(2,1)S(1)}, bf16[3,256,128]{2,1,0:T(8,128)(2,1)S(1)}, u32[]{:S(2)}, u32[]{:S(2)}) collective-permute-start(bf16[3,256,128]{2,1,0:T(8,128)(2,1)S(1)} %fusion.170), channel_id=1, source_target_pairs={{0,4},{1,5},{2,6},{3,7},{4,0},{5,1},{6,2},{7,3},{8,12},{9,13},{10,... | collective-permute-start | bytes 589832 | tf_op jit(solution)/shard_map/ppermute | solution.py:24
  96.4 45.0 %slice-start = ((s8[9633792]{0:T(1024)(128)(4,1)}), s8[1245184]{0:T(1024)(128)(4,1)S(1)}, s32[]{:S(2)}) async-start(s8[9633792]{0:T(1024)(128)(4,1)} %bitcast.272), calls=%async_computation | async-start | bytes 2490368
  98.3 43.1 %slice-start.1 = ((s8[9633792]{0:T(1024)(128)(4,1)}), s8[4194304]{0:T(1024)(128)(4,1)S(1)}, s32[]{:S(2)}) async-start(s8[9633792]{0:T(1024)(128)(4,1)} %bitcast.272), calls=%async_computation.1 | async-start | bytes 8388608
  98.3 13.0 %collective-permute-start.8 = (bf16[256,896]{1,0:T(8,128)(2,1)S(1)}, bf16[256,896]{1,0:T(8,128)(2,1)S(1)}, u32[]{:S(2)}, u32[]{:S(2)}) collective-permute-start(bf16[256,896]{1,0:T(8,128)(2,1)S(1)} %pad_maximum_fusion.2), channel_id=1, source_target_pairs={{0,8},{1,9},{2,10},{3,11},{4,12},{5,13},{6,14},{7,15},{8,16},{9,17... | collective-permute-start | bytes 1376264 | tf_op jit(solution)/shard_map/ppermute | solution.py:24
  111.3 4.2 %collective-permute-start.10 = (bf16[256,896]{1,0:T(8,128)(2,1)S(1)}, bf16[256,896]{1,0:T(8,128)(2,1)S(1)}, u32[]{:S(2)}, u32[]{:S(2)}) collective-permute-start(bf16[256,896]{1,0:T(8,128)(2,1)S(1)} %collective-permute-done.8), channel_id=1, source_target_pairs={{2,4},{3,5},{4,2},{5,3},{10,12},{11,13},{12,10},{13,11},{18,20},{1... | collective-permute-start | bytes 1376264 | tf_op jit(solution)/shard_map/ppermute | solution.py:24
  112.0 21.4 %collective-permute-start.9 = (bf16[256,896]{1,0:T(8,128)(2,1)S(1)}, bf16[256,896]{1,0:T(8,128)(2,1)S(1)}, u32[]{:S(2)}, u32[]{:S(2)}) collective-permute-start(bf16[256,896]{1,0:T(8,128)(2,1)S(1)} %collective-permute-done.8), channel_id=1, source_target_pairs={{0,2},{1,3},{2,6},{3,7},{4,0},{5,1},{6,4},{7,5},{8,10},{9,11},{10,... | collective-permute-start | bytes 1376264 | tf_op jit(solution)/shard_map/ppermute | solution.py:24
  133.6 2.5 %collective-permute-start.11 = (bf16[2,256,896]{2,1,0:T(8,128)(2,1)S(1)}, bf16[2,256,896]{2,1,0:T(8,128)(2,1)S(1)}, u32[]{:S(2)}, u32[]{:S(2)}) collective-permute-start(bf16[2,256,896]{2,1,0:T(8,128)(2,1)S(1)} %pad_maximum_fusion.1), channel_id=1, source_target_pairs={{0,1},{1,0},{2,3},{3,2},{4,5},{5,4},{6,7},{7,6},{8,9},{9,8},{10,11... | collective-permute-start | bytes 2752520 | tf_op jit(solution)/shard_map/ppermute | solution.py:24
  137.6 44.4 %copy-start.1 = (bf16[2,256,1792]{2,1,0:T(8,128)(2,1)}, bf16[2,256,1792]{2,1,0:T(8,128)(2,1)S(1)}, u32[]{:S(2)}) copy-start(bf16[2,256,1792]{2,1,0:T(8,128)(2,1)S(1)} %fusion.11) | copy-start | bytes 5505028
  144.0 6.7 %collective-permute-start.12 = (f32[256,1]{0,1:T(1,128)S(1)}, f32[256,1]{0,1:T(1,128)S(1)}, u32[]{:S(2)}, u32[]{:S(2)}) collective-permute-start(f32[256,1]{0,1:T(1,128)S(1)} %slice_bitcast_fusion.32), channel_id=1, source_target_pairs={{0,4},{1,5},{2,6},{3,7},{4,0},{5,1},{6,2},{7,3},{8,12},{9,13},{10,... | collective-permute-start | bytes 3080 | tf_op jit(solution)/shard_map/ppermute | solution.py:24
  146.6 33.8 %collective-permute-start.14 = (bf16[3,256,256]{1,2,0:T(8,128)(2,1)S(1)}, bf16[3,256,256]{1,2,0:T(8,128)(2,1)S(1)}, u32[]{:S(2)}, u32[]{:S(2)}) collective-permute-start(bf16[3,256,256]{1,2,0:T(8,128)(2,1)S(1)} %fusion.150), channel_id=1, source_target_pairs={{0,4},{1,5},{2,6},{3,7},{4,0},{5,1},{6,2},{7,3},{8,12},{9,13},{10,... | collective-permute-start | bytes 1179656 | tf_op jit(solution)/shard_map/ppermute | solution.py:24
  146.7 35.3 %collective-permute-start.15 = (bf16[3,256,256]{1,2,0:T(8,128)(2,1)S(1)}, bf16[3,256,256]{1,2,0:T(8,128)(2,1)S(1)}, u32[]{:S(2)}, u32[]{:S(2)}) collective-permute-start(bf16[3,256,256]{1,2,0:T(8,128)(2,1)S(1)} %fusion.144), channel_id=1, source_target_pairs={{0,4},{1,5},{2,6},{3,7},{4,0},{5,1},{6,2},{7,3},{8,12},{9,13},{10,... | collective-permute-start | bytes 1179656 | tf_op jit(solution)/shard_map/ppermute | solution.py:24
  148.7 37.1 %collective-permute-start.13 = (bf16[3,256,256]{1,2,0:T(8,128)(2,1)}, bf16[3,256,256]{1,2,0:T(8,128)(2,1)}, u32[]{:S(2)}, u32[]{:S(2)}) collective-permute-start(bf16[3,256,256]{1,2,0:T(8,128)(2,1)} %fusion.156), channel_id=1, source_target_pairs={{0,4},{1,5},{2,6},{3,7},{4,0},{5,1},{6,2},{7,3},{8,12},{9,13},{10,... | collective-permute-start | bytes 1179656 | tf_op jit(solution)/shard_map/ppermute | solution.py:24
  148.8 29.8 %collective-permute-start.16 = (bf16[3,256,128]{2,1,0:T(8,128)(2,1)S(1)}, bf16[3,256,128]{2,1,0:T(8,128)(2,1)S(1)}, u32[]{:S(2)}, u32[]{:S(2)}) collective-permute-start(bf16[3,256,128]{2,1,0:T(8,128)(2,1)S(1)} %fusion.171), channel_id=1, source_target_pairs={{0,4},{1,5},{2,6},{3,7},{4,0},{5,1},{6,2},{7,3},{8,12},{9,13},{10,... | collective-permute-start | bytes 589832 | tf_op jit(solution)/shard_map/ppermute | solution.py:24
  (13 other events, 26.8 us)

commit v2 on v1

v2 whole, which is shorter than its diff:
```python
import functools
import math

import jax
import jax.numpy as jnp
from jax import lax
from jax.experimental import pallas as pl
from jax.experimental.pallas import tpu as pltpu
from jax.sharding import PartitionSpec as P

HD = 128
EPS = 1e-05
AXES = ("section", "dp", "tensor")
F32 = jnp.float32
BF16 = jnp.bfloat16
PARTS = 2
WIDE = 2 * HD
VMEM_BYTES = 40 * 1024 * 1024


def permute(array, sections, hop):
    pairs = []
    for s in range(sections):
        for d in range(2):
            for y in range(2):
                for c in range(2):
                    to = hop(s, d, y, c)
                    if to is None or not 0 <= to[0] < sections:
                        continue
                    ts, td, ty, tc = to
                    pairs.append((s * 8 + d * 4 + y * 2 + c, ts * 8 + td * 4 + ty * 2 + tc))
    return lax.ppermute(array, AXES, pairs)


def direct(s, d, y, c):
    return (s, d, y, c)


def ring(s, d, y, c):
    return (s, 1 - d, y, c) if d != y else (s, d, 1 - y, c)


def across(s, d, y, c):
    return (s, 1 - d, 1 - y, c) if d != y else None


def sibling(s, d, y, c):
    return (s, d, y, 1 - c)


def peer(s, d, y, c):
    return (s, 1 - d, y, c)


def onward(hop):
    def moved(s, d, y, c):
        to = hop(s, d, y, c)
        return None if to is None else (to[0] + 1, *to[1:])

    return moved


def cost(microseconds):
    return pl.CostEstimate(flops=0, bytes_accessed=int(microseconds * 3.69e4), transcendentals=0)


def any_spec():
    return pl.BlockSpec(memory_space=pl.ANY)


def pick_kernel(place, block, from_ring, from_across, *refs):
    both = refs[-1]

    @pl.when(place[2] == 1)
    def _():
        both[0] = from_ring[...]
        both[1] = block[...]

    @pl.when(place[2] == 0)
    def _():
        both[0] = from_across[...]
        both[1] = from_ring[...]


def pick(place, block, from_ring, from_across, after):
    in_smem = pl.BlockSpec(memory_space=pltpu.SMEM)
    in_vmem = pl.BlockSpec(memory_space=pltpu.VMEM)
    return pl.pallas_call(
        pick_kernel,
        in_specs=[in_smem, in_vmem, in_vmem, in_vmem] + [any_spec() for _ in after],
        out_shape=jax.ShapeDtypeStruct((2, *block.shape), BF16),
        cost_estimate=cost(0.8),
        name="pick",
    )(place, block, from_ring, from_across, *after)


def project_kernel(place, both, theirs, gain, weight, sent, kept, sent_mean, kept_mean, normed):
    rows, width = both.shape[1:]
    half = 2 * width

    @pl.when(pl.program_id(0) == 0)
    def _():
        core = place[0]
        first = pl.ds(pl.multiple_of(core * width, HD), width)
        second = pl.ds(pl.multiple_of((1 - core) * width, HD), width)
        for seq, mean_ref in ((0, sent_mean), (1, kept_mean)):
            mine = both[seq].astype(F32)
            their = theirs[seq].astype(F32)
            squares = jnp.sum(mine * mine, axis=-1, keepdims=True)
            squares += jnp.sum(their * their, axis=-1, keepdims=True)
            mean = squares * (1.0 / half)
            inverse = lax.rsqrt(mean + EPS)
            at = pl.ds(seq * rows, rows)
            normed[at, first] = (mine * inverse * gain[:, first].astype(F32)).astype(BF16)
            normed[at, second] = (their * inverse * gain[:, second].astype(F32)).astype(BF16)
            mean_ref[...] = jnp.transpose(jnp.broadcast_to(mean, (rows, HD)))[:8]

    for k in range(3):
        product = jnp.dot(normed[...], weight[0, k], preferred_element_type=F32)
        sent[k] = product[:rows].astype(BF16)
        kept[k] = product[rows:]


def project(place, both, theirs, gain, weight):
    rows, width = both.shape[1:]
    half = weight.shape[2]
    steps = pl.cdiv(width, WIDE)
    whole = lambda *shape: pl.BlockSpec(shape, lambda i, place: (0,) * len(shape))
    tall = pl.BlockSpec((3, rows, WIDE), lambda i, place: (0, 0, i))
    return pl.pallas_call(
        project_kernel,
        grid_spec=pltpu.PrefetchScalarGridSpec(
            num_scalar_prefetch=1,
            grid=(steps,),
            in_specs=[
                whole(2, rows, width),
                whole(2, rows, width),
                pl.BlockSpec((1, half), lambda i, place: (0, place[1])),
                pl.BlockSpec((1, 3, half, WIDE), lambda i, place: (0, 0, 0, i)),
            ],
            out_specs=[tall, tall, whole(8, rows), whole(8, rows)],
            scratch_shapes=[pltpu.VMEM((2 * rows, half), BF16)],
        ),
        out_shape=[
            jax.ShapeDtypeStruct((3, rows, width), BF16),
            jax.ShapeDtypeStruct((3, rows, width), F32),
            jax.ShapeDtypeStruct((8, rows), F32),
            jax.ShapeDtypeStruct((8, rows), F32),
        ],
        compiler_params=pltpu.CompilerParams(vmem_limit_bytes=VMEM_BYTES),
        cost_estimate=cost(3.5),
        name="project",
    )(place, both, theirs, gain, weight)


def column(row):
    return jnp.transpose(jnp.broadcast_to(row[:1], (HD, row.shape[1])))[:, :1]


def attend_kernel(chunk, last, flag, kept, received, kept_mean, peer_mean, block, own, *refs):
    earlier = refs[:chunk]
    out, pairs = refs[-2:]
    rows, width = block.shape
    mean_kept = column(kept_mean[...])
    mean_peer = column(peer_mean[...])
    inverse = lax.rsqrt((mean_kept + mean_peer) * 0.5 + EPS)
    scale_kept = inverse * jnp.sqrt(mean_kept + EPS)
    scale_peer = inverse * jnp.sqrt(mean_peer + EPS)
    causal = lax.broadcasted_iota(jnp.int32, (rows, rows), 0) >= lax.broadcasted_iota(
        jnp.int32, (rows, rows), 1
    )
    for head in range(width // HD):
        at = slice(head * HD, (head + 1) * HD)
        queries, keys, values = (
            (kept[k, :, at] * scale_kept + received[k, :, at].astype(F32) * scale_peer).astype(BF16)
            for k in range(3)
        )
        pairs[0, :, at] = keys
        pairs[1, :, at] = values
        held = [(ref[0, :, at], ref[1, :, at]) for ref in earlier] + [(keys, values)]
        scores = [
            lax.dot_general(queries, key, (((1,), (1,)), ((), ())), preferred_element_type=F32)
            * (1.0 / math.sqrt(HD))
            for key, _ in held
        ]
        scores[-1] = jnp.where(causal, scores[-1], F32(-1e30))
        top = functools.reduce(
            jnp.maximum, [jnp.max(score, axis=-1, keepdims=True) for score in scores]
        )
        raised = [jnp.exp(score - top) for score in scores]
        total = sum(jnp.sum(item, axis=-1, keepdims=True) for item in raised)
        over = 1.0 / total
        mixture = sum(
            jnp.dot((item * over).astype(BF16), value, preferred_element_type=F32)
            for item, (_, value) in zip(raised, held)
        )
        result = block[:, at].astype(F32) + mixture
        if last:
            result = jnp.where(flag[0] == 1, result, own[:, at].astype(F32))
        out[:, at] = result.astype(BF16)


def attend(last, flag, sums, block, own, earlier, after):
    rows, width = block.shape
    chunk = len(earlier)
    in_vmem = pl.BlockSpec(memory_space=pltpu.VMEM)
    return pl.pallas_call(
        functools.partial(attend_kernel, chunk, last),
        in_specs=[pl.BlockSpec(memory_space=pltpu.SMEM)]
        + [in_vmem] * (6 + chunk)
        + [any_spec() for _ in after],
        out_shape=[
            jax.ShapeDtypeStruct((rows, width), BF16),
            jax.ShapeDtypeStruct((2, rows, width), BF16),
        ],
        compiler_params=pltpu.CompilerParams(vmem_limit_bytes=VMEM_BYTES),
        cost_estimate=cost(2.5),
        name="attend",
    )(flag, *sums, block, own, *earlier, *after)


def solution(mesh):
    sections = mesh.shape["section"]

    def local(inputs, qkv_weight, norm_gain, preempted):
        d = lax.axis_index("dp")
        t = lax.axis_index("tensor")
        y, c = t // 2, t % 2
        place = jnp.stack([c, d, (d == y).astype(c.dtype)]).astype(jnp.int32)

        def partial(block, from_ring, from_across, after):
            both = pick(place, block, from_ring, from_across, after)
            theirs = permute(both, sections, sibling)
            sent, kept, sent_mean, kept_mean = project(place, both, theirs, norm_gain, qkv_weight)
            peer_mean = permute(sent_mean, sections, peer)
            received = permute(sent, sections, peer)
            return kept, received, kept_mean, peer_mean

        block = inputs[0, 0]
        rows = block.shape[0] // PARTS
        blocks = [block[i * rows : (i + 1) * rows] for i in range(PARTS)]
        moved = [(permute(part, sections, ring), permute(part, sections, across)) for part in blocks]
        sums = []
        after = []
        for part, pair in zip(blocks, moved):
            sums.append(partial(part, *pair, after))
            after = [sums[-1][2]]
        owns, befores, held = [], [], []
        for part, item in zip(blocks, sums):
            own, pairs = attend(False, preempted, item, part, part, held, after)
            held.append(pairs)
            owns.append(own)
            before = permute(own, sections, onward(direct))
            befores.append(
                (before, permute(own, sections, onward(ring)), permute(own, sections, onward(across)))
            )
            after = [before]
        sums, after = [], [owns[-1]]
        for three in befores:
            sums.append(partial(*three, after))
            after = [sums[-1][2]]
        outs, held = [], []
        for own, three, item in zip(owns, befores, sums):
            out, pairs = attend(True, preempted, item, three[0], own, held, after)
            held.append(pairs)
            outs.append(out)
        return jnp.concatenate(outs)[None, None]

    placed = (
        P("section", "dp", None, "tensor"),
        P("section", None, "dp", "tensor"),
        P("section", None),
        P("section"),
    )
    return jax.shard_map(
        local,
        mesh=mesh,
        in_specs=placed,
        out_specs=P("section", "dp", None, "tensor"),
        check_vma=False,
    )
```

time: 194 us -> 162 us (0.84)
  waiting for transfers between devices: 104 us -> 52 us
  Pallas kernels: 0 us -> 43.1 us
  matrix products: 38.3 us -> 0 us
  starting transfers between devices: 25.2 us -> 38.2 us
  local copies, waits for them, and re-layouts: 18.3 us -> 25.8 us
  other arithmetic: 5.69 us -> 1.46 us
    ppermute x17 -> x22, waiting for transfers between devices: 104 us -> 52 us  [permute(): return lax.ppermute(array, AXES, pairs)]
    pallas_call x0 -> x12, Pallas kernels: none -> 43.1 us  [the longest x4 23.4 us: project(): pl.pallas_call(project_kernel, grid_spec=pltpu.PrefetchScalarGridSpec(num...]
    dot_general x32 -> x0, matrix products: 34.8 us -> none  [the longest x8 13.8 us: layer(): jnp.einsum('rd,kde->kre', normed[0], part, preferred_element_type=F32)]
    ppermute x17 -> x22, starting transfers between devices: 25.2 us -> 38.2 us  [permute(): return lax.ppermute(array, AXES, pairs)]
    unnamed x41 -> x70, local copies, waits for them, and re-layouts: 14.8 us -> 24.7 us
    sub x6 -> x0, matrix products: 3.51 us -> none  [layer(): probability = jax.nn.softmax(scores, axis=-1).astype(BF16)]
    another operation x6 -> x0, local copies, waits for them, and re-layouts: 2.75 us -> none  [layer(): queries, keys, values = total.reshape(3, length, heads, HD)]
  transfers between devices with their start and end apart: 17 -> 22, of which waited for: 6 -> 6; matrix products, arithmetic and copies ran while one was open for 16% -> 0% of each run, Pallas kernels for 0% -> 20%
where the time goes in v2:
time: 162 us
  waiting for transfers between devices  52 us (32%)
  Pallas kernels  43.1 us (27%)
  starting transfers between devices  38.2 us (24%)
  local copies, waits for them, and re-layouts  25.8 us (16%)
    ppermute x22, waiting for transfers between devices, permute(): return lax.ppermute(array, AXES, pairs)  52 us
    ppermute x22, starting transfers between devices, permute(): return lax.ppermute(array, AXES, pairs)  38.2 us
    unnamed x70, local copies, waits for them, and re-layouts  24.7 us
    pallas_call x4, Pallas kernels, project(): pl.pallas_call(project_kernel, grid_spec=pltpu.PrefetchScalarGridSpec(num...  23.4 us
    pallas_call x4, Pallas kernels, attend(): pl.pallas_call(functools.partial(attend_kernel, chunk, last), in_specs=[p...  11.8 us
    pallas_call x4, Pallas kernels, pick(): pl.pallas_call(pick_kernel, in_specs=[in_smem, in_vmem, in_vmem, in_vmem]...  7.92 us
  transfers between devices with their start and end apart: 22, of which 6 were waited for; matrix products, arithmetic and copies ran while one was open for 0% of the time, Pallas kernels for 20%

profile of v2, /device:TPU:0, one launch (start us, length us, event | category | flops | bytes accessed | tf_op | source)
XLA Modules:
  0.0 161.5 jit_solution(8008042064310305296)
XLA Ops:
  1.8 5.7 %collective-permute-start = (bf16[128,896]{1,0:T(8,128)(2,1)S(1)}, bf16[128,896]{1,0:T(8,128)(2,1)S(1)}, u32[]{:S(2)}, u32[]{:S(2)}) collective-permute-start(bf16[128,896]{1,0:T(8,128)(2,1)S(1)} %get-tuple-element.49.block.own), channel_id=1, source_target_pairs={{0,2},{1,3},{2,6},{3,7},{4,0},{5,1},{6,4},{7,5},{8,10},{9,11},{10,... | collective-permute-start | bytes 688136 | tf_op jit(solution)/shard_map/ppermute | solution.py:32
  8.2 9.6 %collective-permute-done.from_ring = bf16[128,896]{1,0:T(8,128)(2,1)S(1)} collective-permute-done((bf16[128,896]{1,0:T(8,128)(2,1)S(1)}, bf16[128,896]{1,0:T(8,128)(2,1)S(1)}, u32[]{:S(2)}, u32[]{:S(2)}) %collective-permute-start) | collective-permute-done | bytes 229408 | tf_op jit(solution)/shard_map/ppermute | solution.py:32
  18.4 2.0 %pick.4.both = bf16[2,128,896]{2,1,0:T(8,128)(2,1)} custom-call(s32[3]{0:T(128)} %pad_add_fusion.place, bf16[128,896]{1,0:T(8,128)(2,1)} %copy-done.6, bf16[128,896]{1,0:T(8,128)(2,1)} %copy-done.30, bf16[128,896]{1,0:T(8,128)(2,1)} %copy-done.29), custom_call_target="tpu_custom_call" | custom-call | bytes 29520 | tf_op jit(solution)/shard_map/pick/pallas_call | solution.py:88
  21.2 4.2 %collective-permute-start.5 = (bf16[128,896]{1,0:T(8,128)(2,1)S(1)}, bf16[128,896]{1,0:T(8,128)(2,1)S(1)}, u32[]{:S(2)}, u32[]{:S(2)}) collective-permute-start(bf16[128,896]{1,0:T(8,128)(2,1)S(1)} %get-tuple-element.50.block.own), channel_id=1, source_target_pairs={{0,2},{1,3},{2,6},{3,7},{4,0},{5,1},{6,4},{7,5},{8,10},{9,11},{10,... | collective-permute-start | bytes 688136 | tf_op jit(solution)/shard_map/ppermute | solution.py:32
  25.4 3.8 %copy-done = bf16[1,3,1792,896]{3,2,1,0:T(8,128)(2,1)S(1)} copy-done((bf16[1,3,1792,896]{3,2,1,0:T(8,128)(2,1)S(1)}, bf16[1,3,1792,896]{3,2,1,0:T(8,128)(2,1)}, u32[]{:S(2)}) %copy-start) | copy-done | bytes 9633816
  30.8 5.8 %project.4 = (bf16[3,128,896]{2,1,0:T(8,128)(2,1)S(1)}, f32[3,128,896]{2,1,0:T(8,128)S(1)}, f32[8,128]{1,0:T(8,128)S(1)}, f32[8,128]{1,0:T(8,128)S(1)}) custom-call(s32[3]{0:T(128)S(1)} %copy-done.19, bf16[2,128,896]{2,1,0:T(8,128)(2,1)S(1)} %copy-done.11, bf16[2,128,896]{2,1,0:T(8,128)(2,1)S(1)} %collective-permute-done.2.theirs, ...), custom_call_target="tpu_custom_call" | custom-call | bytes 129150 | tf_op jit(solution)/shard_map/project/pallas_call | solution.py:130
  38.0 2.0 %pick.5.both = bf16[2,128,896]{2,1,0:T(8,128)(2,1)} custom-call(s32[3]{0:T(128)} %pad_add_fusion.place, bf16[128,896]{1,0:T(8,128)(2,1)} %copy-done.4, bf16[128,896]{1,0:T(8,128)(2,1)} %copy-done.34, bf16[128,896]{1,0:T(8,128)(2,1)} %copy-done.33, f32[8,128]{1,0:T(8,128)} %copy-done.25), custom_call_target="tpu_custom_call" | custom-call | bytes 29520 | tf_op jit(solution)/shard_map/pick/pallas_call | solution.py:88
  42.1 3.8 %copy-done.1 = bf16[1,3,1792,896]{3,2,1,0:T(8,128)(2,1)S(1)} copy-done((bf16[1,3,1792,896]{3,2,1,0:T(8,128)(2,1)S(1)}, bf16[1,3,1792,896]{3,2,1,0:T(8,128)(2,1)}, u32[]{:S(2)}) %copy-start.1) | copy-done | bytes 9633816
  46.8 5.8 %project.5 = (bf16[3,128,896]{2,1,0:T(8,128)(2,1)S(1)}, f32[3,128,896]{2,1,0:T(8,128)S(1)}, f32[8,128]{1,0:T(8,128)S(1)}, f32[8,128]{1,0:T(8,128)S(1)}) custom-call(s32[3]{0:T(128)S(1)} %copy-done.20, bf16[2,128,896]{2,1,0:T(8,128)(2,1)S(1)} %copy-done.13, bf16[2,128,896]{2,1,0:T(8,128)(2,1)S(1)} %collective-permute-done.7.theirs, ...), custom_call_target="tpu_custom_call" | custom-call | bytes 129150 | tf_op jit(solution)/shard_map/project/pallas_call | solution.py:130
  55.4 17.3 %collective-permute-done.4.peer_mean = f32[8,128]{1,0:T(8,128)S(1)} collective-permute-done((f32[8,128]{1,0:T(8,128)S(1)}, f32[8,128]{1,0:T(8,128)S(1)}, u32[]{:S(2)}, u32[]{:S(2)}) %collective-permute-start.4) | collective-permute-done | bytes 4128 | tf_op jit(solution)/shard_map/ppermute | solution.py:32
  72.7 2.5 %attend.4 = (bf16[128,896]{1,0:T(8,128)(2,1)S(1)}, bf16[2,128,896]{2,1,0:T(8,128)(2,1)S(1)}) custom-call(s32[1]{0:T(128)S(6)} %copy.5.flag, f32[3,128,896]{2,1,0:T(8,128)S(1)} %get-tuple-element.27.kept, bf16[3,128,896]{2,1,0:T(8,128)(2,1)S(1)} %collective-permute-done.3.received, f32[8,128]{1,0:T(8,128)S(1)} %copy-done.26, ...), custom_call_target="tpu_custom_call" | custom-call | bytes 92250 | tf_op jit(solution)/shard_map/attend/pallas_call | solution.py:207
  75.3 3.5 %collective-permute-start.8 = (bf16[128,896]{1,0:T(8,128)(2,1)S(1)}, bf16[128,896]{1,0:T(8,128)(2,1)S(1)}, u32[]{:S(2)}, u32[]{:S(2)}) collective-permute-start(bf16[128,896]{1,0:T(8,128)(2,1)S(1)} %get-tuple-element.32.own), channel_id=1, source_target_pairs={{0,8},{1,9},{2,10},{3,11},{4,12},{5,13},{6,14},{7,15},{8,16},{9,17... | collective-permute-start | bytes 688136 | tf_op jit(solution)/shard_map/ppermute | solution.py:32
  79.4 6.9 %collective-permute-start.9 = (bf16[128,896]{1,0:T(8,128)(2,1)S(1)}, bf16[128,896]{1,0:T(8,128)(2,1)S(1)}, u32[]{:S(2)}, u32[]{:S(2)}) collective-permute-start(bf16[128,896]{1,0:T(8,128)(2,1)S(1)} %get-tuple-element.32.own), channel_id=1, source_target_pairs={{0,10},{1,11},{2,14},{3,15},{4,8},{5,9},{6,12},{7,13},{8,18},{9,19... | collective-permute-start | bytes 688136 | tf_op jit(solution)/shard_map/ppermute | solution.py:32
  86.4 3.6 %collective-permute-done.12.peer_mean = f32[8,128]{1,0:T(8,128)S(1)} collective-permute-done((f32[8,128]{1,0:T(8,128)S(1)}, f32[8,128]{1,0:T(8,128)S(1)}, u32[]{:S(2)}, u32[]{:S(2)}) %collective-permute-start.12) | collective-permute-done | bytes 4128 | tf_op jit(solution)/shard_map/ppermute | solution.py:32
  90.1 3.4 %attend.5 = (bf16[128,896]{1,0:T(8,128)(2,1)S(1)}, bf16[2,128,896]{2,1,0:T(8,128)(2,1)}) custom-call(s32[1]{0:T(128)S(6)} %copy.5.flag, f32[3,128,896]{2,1,0:T(8,128)S(1)} %get-tuple-element.33.kept, bf16[3,128,896]{2,1,0:T(8,128)(2,1)S(1)} %collective-permute-done.11.received, f32[8,128]{1,0:T(8,128)S(1)} %get-tuple-element.31.refs_0_.kept_mean, ...), custom_call_target="tpu_custom_call" | custom-call | bytes 92250 | tf_op jit(solution)/shard_map/attend/pallas_call | solution.py:207
  97.6 7.7 %collective-permute-start.17 = (bf16[128,896]{1,0:T(8,128)(2,1)S(1)}, bf16[128,896]{1,0:T(8,128)(2,1)S(1)}, u32[]{:S(2)}, u32[]{:S(2)}) collective-permute-start(bf16[128,896]{1,0:T(8,128)(2,1)S(1)} %copy-done.15), channel_id=1, source_target_pairs={{0,10},{1,11},{2,14},{3,15},{4,8},{5,9},{6,12},{7,13},{8,18},{9,19... | collective-permute-start | bytes 688136 | tf_op jit(solution)/shard_map/ppermute | solution.py:32
  105.2 2.7 %collective-permute-start.16 = (bf16[128,896]{1,0:T(8,128)(2,1)S(1)}, bf16[128,896]{1,0:T(8,128)(2,1)S(1)}, u32[]{:S(2)}, u32[]{:S(2)}) collective-permute-start(bf16[128,896]{1,0:T(8,128)(2,1)S(1)} %copy-done.15), channel_id=1, source_target_pairs={{0,8},{1,9},{2,10},{3,11},{4,12},{5,13},{6,14},{7,15},{8,16},{9,17... | collective-permute-start | bytes 688136 | tf_op jit(solution)/shard_map/ppermute | solution.py:32
  108.0 3.8 %copy-done.2 = bf16[1,3,1792,896]{3,2,1,0:T(8,128)(2,1)S(1)} copy-done((bf16[1,3,1792,896]{3,2,1,0:T(8,128)(2,1)S(1)}, bf16[1,3,1792,896]{3,2,1,0:T(8,128)(2,1)}, u32[]{:S(2)}) %copy-start.2) | copy-done | bytes 9633816
  112.7 5.9 %project.6 = (bf16[3,128,896]{2,1,0:T(8,128)(2,1)S(1)}, f32[3,128,896]{2,1,0:T(8,128)S(1)}, f32[8,128]{1,0:T(8,128)S(1)}, f32[8,128]{1,0:T(8,128)S(1)}) custom-call(s32[3]{0:T(128)S(1)} %copy-done.21, bf16[2,128,896]{2,1,0:T(8,128)(2,1)S(1)} %copy-done.10, bf16[2,128,896]{2,1,0:T(8,128)(2,1)S(1)} %collective-permute-done.13.theirs, ...), custom_call_target="tpu_custom_call" | custom-call | bytes 129150 | tf_op jit(solution)/shard_map/project/pallas_call | solution.py:130
  124.0 3.8 %copy-done.3 = bf16[1,3,1792,896]{3,2,1,0:T(8,128)(2,1)S(1)} copy-done((bf16[1,3,1792,896]{3,2,1,0:T(8,128)(2,1)S(1)}, bf16[1,3,1792,896]{3,2,1,0:T(8,128)(2,1)}, u32[]{:S(2)}) %copy-start.3) | copy-done | bytes 9633816
  128.8 5.9 %project.7 = (bf16[3,128,896]{2,1,0:T(8,128)(2,1)S(1)}, f32[3,128,896]{2,1,0:T(8,128)S(1)}, f32[8,128]{1,0:T(8,128)S(1)}, f32[8,128]{1,0:T(8,128)S(1)}) custom-call(s32[3]{0:T(128)S(1)} %copy-done.22, bf16[2,128,896]{2,1,0:T(8,128)(2,1)S(1)} %copy-done.12, bf16[2,128,896]{2,1,0:T(8,128)(2,1)S(1)} %collective-permute-done.19.theirs, ...), custom_call_target="tpu_custom_call" | custom-call | bytes 129150 | tf_op jit(solution)/shard_map/project/pallas_call | solution.py:130
  136.9 17.9 %collective-permute-done.15.peer_mean = f32[8,128]{1,0:T(8,128)S(1)} collective-permute-done((f32[8,128]{1,0:T(8,128)S(1)}, f32[8,128]{1,0:T(8,128)S(1)}, u32[]{:S(2)}, u32[]{:S(2)}) %collective-permute-start.15) | collective-permute-done | bytes 4128 | tf_op jit(solution)/shard_map/ppermute | solution.py:32
  154.8 2.5 %attend.6 = (bf16[128,896]{1,0:T(8,128)(2,1)S(1)}, bf16[2,128,896]{2,1,0:T(8,128)(2,1)S(1)}) custom-call(s32[1]{0:T(128)S(6)} %copy.5.flag, f32[3,128,896]{2,1,0:T(8,128)S(1)} %get-tuple-element.38.kept, bf16[3,128,896]{2,1,0:T(8,128)(2,1)S(1)} %collective-permute-done.14.received, f32[8,128]{1,0:T(8,128)S(1)} %copy-done.24, ...), custom_call_target="tpu_custom_call" | custom-call | bytes 92250 | tf_op jit(solution)/shard_map/attend/pallas_call | solution.py:207
  157.3 3.4 %attend.7 = (bf16[128,896]{1,0:T(8,128)(2,1)S(1)}, bf16[2,128,896]{2,1,0:T(8,128)(2,1)}) custom-call(s32[1]{0:T(128)S(6)} %copy.5.flag, f32[3,128,896]{2,1,0:T(8,128)S(1)} %get-tuple-element.44.kept, bf16[3,128,896]{2,1,0:T(8,128)(2,1)S(1)} %collective-permute-done.20.received, f32[8,128]{1,0:T(8,128)S(1)} %get-tuple-element.42.refs_0_.kept_mean.refs_1_, ...), custom_call_target="tpu_custom_call" | custom-call | bytes 92250 | tf_op jit(solution)/shard_map/attend/pallas_call | solution.py:207
  (105 shorter events, 27.4 us)
Async XLA Ops:
  1.1 35.5 %copy-start.4 = (bf16[128,896]{1,0:T(8,128)(2,1)}, bf16[128,896]{1,0:T(8,128)(2,1)S(1)}, u32[]{:S(2)}) copy-start(bf16[128,896]{1,0:T(8,128)(2,1)S(1)} %get-tuple-element.50.block.own) | copy-start | bytes 688132
  1.1 7.0 %collective-permute-start.1 = (bf16[128,896]{1,0:T(8,128)(2,1)S(1)}, bf16[128,896]{1,0:T(8,128)(2,1)S(1)}, u32[]{:S(2)}, u32[]{:S(2)}) collective-permute-start(bf16[128,896]{1,0:T(8,128)(2,1)S(1)} %get-tuple-element.49.block.own), channel_id=1, source_target_pairs={{2,4},{3,5},{4,2},{5,3},{10,12},{11,13},{12,10},{13,11},{18,20},{1... | collective-permute-start | bytes 688136 | tf_op jit(solution)/shard_map/ppermute | solution.py:32
  1.8 15.9 %collective-permute-start = (bf16[128,896]{1,0:T(8,128)(2,1)S(1)}, bf16[128,896]{1,0:T(8,128)(2,1)S(1)}, u32[]{:S(2)}, u32[]{:S(2)}) collective-permute-start(bf16[128,896]{1,0:T(8,128)(2,1)S(1)} %get-tuple-element.49.block.own), channel_id=1, source_target_pairs={{0,2},{1,3},{2,6},{3,7},{4,0},{5,1},{6,4},{7,5},{8,10},{9,11},{10,... | collective-permute-start | bytes 688136 | tf_op jit(solution)/shard_map/ppermute | solution.py:32
  20.4 5.0 %collective-permute-start.2 = (bf16[2,128,896]{2,1,0:T(8,128)(2,1)}, bf16[2,128,896]{2,1,0:T(8,128)(2,1)S(1)}, u32[]{:S(2)}, u32[]{:S(2)}) collective-permute-start(bf16[2,128,896]{2,1,0:T(8,128)(2,1)} %pick.4.both), channel_id=1, source_target_pairs={{0,1},{1,0},{2,3},{3,2},{4,5},{5,4},{6,7},{7,6},{8,9},{9,8},{10,11... | collective-permute-start | bytes 1376264 | tf_op jit(solution)/shard_map/ppermute | solution.py:32
  20.4 16.9 %collective-permute-start.6 = (bf16[128,896]{1,0:T(8,128)(2,1)S(1)}, bf16[128,896]{1,0:T(8,128)(2,1)S(1)}, u32[]{:S(2)}, u32[]{:S(2)}) collective-permute-start(bf16[128,896]{1,0:T(8,128)(2,1)S(1)} %get-tuple-element.50.block.own), channel_id=1, source_target_pairs={{2,4},{3,5},{4,2},{5,3},{10,12},{11,13},{12,10},{13,11},{18,20},{1... | collective-permute-start | bytes 688136 | tf_op jit(solution)/shard_map/ppermute | solution.py:32
  21.2 16.1 %collective-permute-start.5 = (bf16[128,896]{1,0:T(8,128)(2,1)S(1)}, bf16[128,896]{1,0:T(8,128)(2,1)S(1)}, u32[]{:S(2)}, u32[]{:S(2)}) collective-permute-start(bf16[128,896]{1,0:T(8,128)(2,1)S(1)} %get-tuple-element.50.block.own), channel_id=1, source_target_pairs={{0,2},{1,3},{2,6},{3,7},{4,0},{5,1},{6,4},{7,5},{8,10},{9,11},{10,... | collective-permute-start | bytes 688136 | tf_op jit(solution)/shard_map/ppermute | solution.py:32
  40.0 2.0 %collective-permute-start.7 = (bf16[2,128,896]{2,1,0:T(8,128)(2,1)}, bf16[2,128,896]{2,1,0:T(8,128)(2,1)S(1)}, u32[]{:S(2)}, u32[]{:S(2)}) collective-permute-start(bf16[2,128,896]{2,1,0:T(8,128)(2,1)} %pick.5.both), channel_id=1, source_target_pairs={{0,1},{1,0},{2,3},{3,2},{4,5},{5,4},{6,7},{7,6},{8,9},{9,8},{10,11... | collective-permute-start | bytes 1376264 | tf_op jit(solution)/shard_map/ppermute | solution.py:32
  40.0 32.7 %collective-permute-start.3 = (bf16[3,128,896]{2,1,0:T(8,128)(2,1)S(1)}, bf16[3,128,896]{2,1,0:T(8,128)(2,1)S(1)}, u32[]{:S(2)}, u32[]{:S(2)}) collective-permute-start(bf16[3,128,896]{2,1,0:T(8,128)(2,1)S(1)} %get-tuple-element.28), channel_id=1, source_target_pairs={{0,4},{1,5},{2,6},{3,7},{4,0},{5,1},{6,2},{7,3},{8,12},{9,13},{10,... | collective-permute-start | bytes 2064392 | tf_op jit(solution)/shard_map/ppermute | solution.py:32
  52.7 37.4 %copy-start.5 = (bf16[128,896]{1,0:T(8,128)(2,1)S(1)}, bf16[128,896]{1,0:T(8,128)(2,1)}, u32[]{:S(2)}) copy-start(bf16[128,896]{1,0:T(8,128)(2,1)} %copy-done.4) | copy-start | bytes 688132
  52.7 37.3 %collective-permute-start.11 = (bf16[3,128,896]{2,1,0:T(8,128)(2,1)S(1)}, bf16[3,128,896]{2,1,0:T(8,128)(2,1)S(1)}, u32[]{:S(2)}, u32[]{:S(2)}) collective-permute-start(bf16[3,128,896]{2,1,0:T(8,128)(2,1)S(1)} %get-tuple-element.34), channel_id=1, source_target_pairs={{0,4},{1,5},{2,6},{3,7},{4,0},{5,1},{6,2},{7,3},{8,12},{9,13},{10,... | collective-permute-start | bytes 2064392 | tf_op jit(solution)/shard_map/ppermute | solution.py:32
  53.0 19.7 %collective-permute-start.4 = (f32[8,128]{1,0:T(8,128)S(1)}, f32[8,128]{1,0:T(8,128)S(1)}, u32[]{:S(2)}, u32[]{:S(2)}) collective-permute-start(f32[8,128]{1,0:T(8,128)S(1)} %get-tuple-element.30), channel_id=1, source_target_pairs={{0,4},{1,5},{2,6},{3,7},{4,0},{5,1},{6,2},{7,3},{8,12},{9,13},{10,... | collective-permute-start | bytes 12296 | tf_op jit(solution)/shard_map/ppermute | solution.py:32
  75.3 14.8 %collective-permute-start.8 = (bf16[128,896]{1,0:T(8,128)(2,1)S(1)}, bf16[128,896]{1,0:T(8,128)(2,1)S(1)}, u32[]{:S(2)}, u32[]{:S(2)}) collective-permute-start(bf16[128,896]{1,0:T(8,128)(2,1)S(1)} %get-tuple-element.32.own), channel_id=1, source_target_pairs={{0,8},{1,9},{2,10},{3,11},{4,12},{5,13},{6,14},{7,15},{8,16},{9,17... | collective-permute-start | bytes 688136 | tf_op jit(solution)/shard_map/ppermute | solution.py:32
  78.8 15.4 %collective-permute-start.10 = (bf16[128,896]{1,0:T(8,128)(2,1)S(1)}, bf16[128,896]{1,0:T(8,128)(2,1)S(1)}, u32[]{:S(2)}, u32[]{:S(2)}) collective-permute-start(bf16[128,896]{1,0:T(8,128)(2,1)S(1)} %get-tuple-element.32.own), channel_id=1, source_target_pairs={{2,12},{3,13},{4,10},{5,11},{10,20},{11,21},{12,18},{13,19},{18,28... | collective-permute-start | bytes 688136 | tf_op jit(solution)/shard_map/ppermute | solution.py:32
  79.4 14.7 %collective-permute-start.9 = (bf16[128,896]{1,0:T(8,128)(2,1)S(1)}, bf16[128,896]{1,0:T(8,128)(2,1)S(1)}, u32[]{:S(2)}, u32[]{:S(2)}) collective-permute-start(bf16[128,896]{1,0:T(8,128)(2,1)S(1)} %get-tuple-element.32.own), channel_id=1, source_target_pairs={{0,10},{1,11},{2,14},{3,15},{4,8},{5,9},{6,12},{7,13},{8,18},{9,19... | collective-permute-start | bytes 688136 | tf_op jit(solution)/shard_map/ppermute | solution.py:32
  86.4 3.7 %collective-permute-start.12 = (f32[8,128]{1,0:T(8,128)S(1)}, f32[8,128]{1,0:T(8,128)S(1)}, u32[]{:S(2)}, u32[]{:S(2)}) collective-permute-start(f32[8,128]{1,0:T(8,128)S(1)} %get-tuple-element.35), channel_id=1, source_target_pairs={{0,4},{1,5},{2,6},{3,7},{4,0},{5,1},{6,2},{7,3},{8,12},{9,13},{10,... | collective-permute-start | bytes 12296 | tf_op jit(solution)/shard_map/ppermute | solution.py:32
  96.9 11.0 %collective-permute-start.13 = (bf16[2,128,896]{2,1,0:T(8,128)(2,1)}, bf16[2,128,896]{2,1,0:T(8,128)(2,1)S(1)}, u32[]{:S(2)}, u32[]{:S(2)}) collective-permute-start(bf16[2,128,896]{2,1,0:T(8,128)(2,1)} %pick.6.both), channel_id=1, source_target_pairs={{0,1},{1,0},{2,3},{3,2},{4,5},{5,4},{6,7},{7,6},{8,9},{9,8},{10,11... | collective-permute-start | bytes 1376264 | tf_op jit(solution)/shard_map/ppermute | solution.py:32
  96.9 22.3 %collective-permute-start.18 = (bf16[128,896]{1,0:T(8,128)(2,1)S(1)}, bf16[128,896]{1,0:T(8,128)(2,1)S(1)}, u32[]{:S(2)}, u32[]{:S(2)}) collective-permute-start(bf16[128,896]{1,0:T(8,128)(2,1)S(1)} %copy-done.15), channel_id=1, source_target_pairs={{2,12},{3,13},{4,10},{5,11},{10,20},{11,21},{12,18},{13,19},{18,28... | collective-permute-start | bytes 688136 | tf_op jit(solution)/shard_map/ppermute | solution.py:32
  97.6 21.6 %collective-permute-start.17 = (bf16[128,896]{1,0:T(8,128)(2,1)S(1)}, bf16[128,896]{1,0:T(8,128)(2,1)S(1)}, u32[]{:S(2)}, u32[]{:S(2)}) collective-permute-start(bf16[128,896]{1,0:T(8,128)(2,1)S(1)} %copy-done.15), channel_id=1, source_target_pairs={{0,10},{1,11},{2,14},{3,15},{4,8},{5,9},{6,12},{7,13},{8,18},{9,19... | collective-permute-start | bytes 688136 | tf_op jit(solution)/shard_map/ppermute | solution.py:32
  105.2 14.0 %collective-permute-start.16 = (bf16[128,896]{1,0:T(8,128)(2,1)S(1)}, bf16[128,896]{1,0:T(8,128)(2,1)S(1)}, u32[]{:S(2)}, u32[]{:S(2)}) collective-permute-start(bf16[128,896]{1,0:T(8,128)(2,1)S(1)} %copy-done.15), channel_id=1, source_target_pairs={{0,8},{1,9},{2,10},{3,11},{4,12},{5,13},{6,14},{7,15},{8,16},{9,17... | collective-permute-start | bytes 688136 | tf_op jit(solution)/shard_map/ppermute | solution.py:32
  122.0 2.0 %collective-permute-start.19 = (bf16[2,128,896]{2,1,0:T(8,128)(2,1)}, bf16[2,128,896]{2,1,0:T(8,128)(2,1)S(1)}, u32[]{:S(2)}, u32[]{:S(2)}) collective-permute-start(bf16[2,128,896]{2,1,0:T(8,128)(2,1)} %pick.7.both), channel_id=1, source_target_pairs={{0,1},{1,0},{2,3},{3,2},{4,5},{5,4},{6,7},{7,6},{8,9},{9,8},{10,11... | collective-permute-start | bytes 1376264 | tf_op jit(solution)/shard_map/ppermute | solution.py:32
  122.0 32.7 %collective-permute-start.14 = (bf16[3,128,896]{2,1,0:T(8,128)(2,1)S(1)}, bf16[3,128,896]{2,1,0:T(8,128)(2,1)S(1)}, u32[]{:S(2)}, u32[]{:S(2)}) collective-permute-start(bf16[3,128,896]{2,1,0:T(8,128)(2,1)S(1)} %get-tuple-element.39), channel_id=1, source_target_pairs={{0,4},{1,5},{2,6},{3,7},{4,0},{5,1},{6,2},{7,3},{8,12},{9,13},{10,... | collective-permute-start | bytes 2064392 | tf_op jit(solution)/shard_map/ppermute | solution.py:32
  134.7 22.6 %collective-permute-start.20 = (bf16[3,128,896]{2,1,0:T(8,128)(2,1)S(1)}, bf16[3,128,896]{2,1,0:T(8,128)(2,1)S(1)}, u32[]{:S(2)}, u32[]{:S(2)}) collective-permute-start(bf16[3,128,896]{2,1,0:T(8,128)(2,1)S(1)} %get-tuple-element.45), channel_id=1, source_target_pairs={{0,4},{1,5},{2,6},{3,7},{4,0},{5,1},{6,2},{7,3},{8,12},{9,13},{10,... | collective-permute-start | bytes 2064392 | tf_op jit(solution)/shard_map/ppermute | solution.py:32
  134.9 19.9 %collective-permute-start.15 = (f32[8,128]{1,0:T(8,128)S(1)}, f32[8,128]{1,0:T(8,128)S(1)}, u32[]{:S(2)}, u32[]{:S(2)}) collective-permute-start(f32[8,128]{1,0:T(8,128)S(1)} %get-tuple-element.41), channel_id=1, source_target_pairs={{0,4},{1,5},{2,6},{3,7},{4,0},{5,1},{6,2},{7,3},{8,12},{9,13},{10,... | collective-permute-start | bytes 12296 | tf_op jit(solution)/shard_map/ppermute | solution.py:32
  136.8 20.5 %collective-permute-start.21 = (f32[8,128]{1,0:T(8,128)S(1)}, f32[8,128]{1,0:T(8,128)S(1)}, u32[]{:S(2)}, u32[]{:S(2)}) collective-permute-start(f32[8,128]{1,0:T(8,128)S(1)} %get-tuple-element.46), channel_id=1, source_target_pairs={{0,4},{1,5},{2,6},{3,7},{4,0},{5,1},{6,2},{7,3},{8,12},{9,13},{10,... | collective-permute-start | bytes 12296 | tf_op jit(solution)/shard_map/ppermute | solution.py:32
  (33 other events, 276.0 us)

commit v3 on v2

v3 whole, which is shorter than its diff:
```python
import functools
import math

import jax
import jax.numpy as jnp
from jax import lax
from jax.experimental import pallas as pl
from jax.experimental.pallas import tpu as pltpu
from jax.sharding import PartitionSpec as P

HD = 128
EPS = 1e-05
AXES = ("section", "dp", "tensor")
F32 = jnp.float32
BF16 = jnp.bfloat16
PARTS = 2
WIDE = 2 * HD
VMEM_BYTES = 16 * 1024 * 1024
STAT_ROWS = 16


def permute(array, sections, hop):
    pairs = []
    for s in range(sections):
        for d in range(2):
            for y in range(2):
                for c in range(2):
                    to = hop(s, d, y, c)
                    if to is None or not 0 <= to[0] < sections:
                        continue
                    ts, td, ty, tc = to
                    pairs.append((s * 8 + d * 4 + y * 2 + c, ts * 8 + td * 4 + ty * 2 + tc))
    return lax.ppermute(array, AXES, pairs)


def ring(s, d, y, c):
    return (s, 1 - d, y, c) if d != y else (s, d, 1 - y, c)


def cross(s, d, y, c):
    return (s, 1 - d, 1 - y, c) if d != y else (s, d, y, c)


def direct(s, d, y, c):
    return (s, d, y, c) if d != y else None


def sibling(s, d, y, c):
    return (s, d, y, 1 - c)


def peer(s, d, y, c):
    return (s, 1 - d, y, c)


def onward(hop):
    def moved(s, d, y, c):
        to = hop(s, d, y, c)
        return None if to is None else (to[0] + 1, *to[1:])

    return moved


def cost(microseconds):
    return pl.CostEstimate(flops=int(microseconds * 1.15e9), bytes_accessed=1000, transcendentals=0)


def any_spec():
    return pl.BlockSpec(memory_space=pl.ANY)


def vmem_spec():
    return pl.BlockSpec(memory_space=pltpu.VMEM)


def smem_spec():
    return pl.BlockSpec(memory_space=pltpu.SMEM)


def stage_kernel(weight, staged, semaphore):
    copy = pltpu.make_async_copy(weight, staged, semaphore)
    copy.start()
    copy.wait()


def stage(weight):
    return pl.pallas_call(
        stage_kernel,
        in_specs=[any_spec()],
        out_specs=vmem_spec(),
        out_shape=pltpu.VMEM(weight.shape, weight.dtype),
        scratch_shapes=[pltpu.SemaphoreType.DMA(())],
        compiler_params=pltpu.CompilerParams(vmem_limit_bytes=VMEM_BYTES),
        cost_estimate=cost(4),
        name="stage",
    )(weight)


def project_kernel(start, place, crossed, ringed, sib_crossed, sib_ringed, gain, weight, *refs):
    sent, kept, kept_mean, normed = refs[-4:]
    rows = normed.shape[0] // 2
    width = crossed.shape[1]
    half = 2 * width
    core, dp, diagonal = place[0], place[1], place[2]
    means = []
    for mine, theirs, offset in (
        (crossed, sib_crossed, diagonal),
        (ringed, sib_ringed, 1 - diagonal),
    ):
        at = pl.ds(pl.multiple_of(offset * rows, rows), rows)
        pieces = [ref[start : start + rows].astype(F32) for ref in (mine, theirs)]
        squares = sum(jnp.sum(piece * piece, axis=-1, keepdims=True) for piece in pieces)
        mean = squares * (1.0 / half)
        means.append(mean)
        inverse = lax.rsqrt(mean + EPS)
        for piece, order in zip(pieces, (core, 1 - core)):
            gains = gain[:, pl.ds(pl.multiple_of(dp * half + order * width, HD), width)]
            normed[at, pl.ds(pl.multiple_of(order * width, HD), width)] = (
                piece * inverse * gains.astype(F32)
            ).astype(BF16)
    on_diagonal = diagonal == 1
    sent_mean = jnp.where(on_diagonal, means[1], means[0])
    kept_mean[...] = jnp.where(on_diagonal, means[0], means[1])
    row = jnp.transpose(jnp.broadcast_to(sent_mean, (rows, HD)))[:STAT_ROWS]
    high = row.astype(BF16).astype(F32)
    mid = (row - high).astype(BF16).astype(F32)
    low = row - high - mid
    which = lax.broadcasted_iota(jnp.int32, row.shape, 0)
    stat = jnp.where(which == 0, high, jnp.where(which == 1, mid, low))
    for begin in range(0, width, rows):
        sent[3 * rows :, begin : begin + rows] = stat.astype(BF16)
    for begin in range(0, width, WIDE):
        at = slice(begin, min(begin + WIDE, width))
        for k in range(3):
            product = jnp.dot(normed[...], weight[0, k, :, at], preferred_element_type=F32)
            sent[k * rows : (k + 1) * rows, at] = product[:rows].astype(BF16)
            kept[k, :, at] = product[rows:]


def project(start, rows, place, four, gain, weight, after):
    width = four[0].shape[1]
    return pl.pallas_call(
        functools.partial(project_kernel, start),
        in_specs=[smem_spec()] + [vmem_spec()] * 6 + [any_spec() for _ in after],
        out_shape=[
            jax.ShapeDtypeStruct((3 * rows + STAT_ROWS, width), BF16),
            jax.ShapeDtypeStruct((3, rows, width), F32),
            jax.ShapeDtypeStruct((rows, 1), F32),
        ],
        scratch_shapes=[pltpu.VMEM((2 * rows, 2 * width), BF16)],
        compiler_params=pltpu.CompilerParams(vmem_limit_bytes=VMEM_BYTES),
        cost_estimate=cost(3.0),
        name="project",
    )(place, *four, gain, weight, *after)


def attend_kernel(
    chunk, last, place, flag, kept, received, kept_mean, crossed, block, own, *refs
):
    earlier = refs[:chunk]
    earlier_outs = refs[chunk : 2 * chunk] if last else ()
    out, pairs = refs[-2:]
    rows, width = own.shape
    out_start = rows * len(earlier_outs)
    for i, ref in enumerate(earlier_outs):
        out[i * rows : (i + 1) * rows] = ref[...]
    stat = received[3 * rows :, :rows].astype(F32)
    row = stat[0:1] + stat[1:2] + stat[2:3]
    mean_peer = jnp.transpose(jnp.broadcast_to(row, (HD, rows)))[:, :1]
    mean_kept = kept_mean[...]
    inverse = lax.rsqrt((mean_kept + mean_peer) * 0.5 + EPS)
    scale_kept = inverse * jnp.sqrt(mean_kept + EPS)
    scale_peer = inverse * jnp.sqrt(mean_peer + EPS)
    causal = lax.broadcasted_iota(jnp.int32, (rows, rows), 0) >= lax.broadcasted_iota(
        jnp.int32, (rows, rows), 1
    )
    for head in range(width // HD):
        at = slice(head * HD, (head + 1) * HD)
        queries, keys, values = (
            (
                kept[k, :, at] * scale_kept
                + received[k * rows : (k + 1) * rows, at].astype(F32) * scale_peer
            ).astype(BF16)
            for k in range(3)
        )
        pairs[0, :, at] = keys
        pairs[1, :, at] = values
        held = [(ref[0, :, at], ref[1, :, at]) for ref in earlier] + [(keys, values)]
        scores = [
            lax.dot_general(queries, key, (((1,), (1,)), ((), ())), preferred_element_type=F32)
            * (1.0 / math.sqrt(HD))
            for key, _ in held
        ]
        scores[-1] = jnp.where(causal, scores[-1], F32(-1e30))
        top = functools.reduce(
            jnp.maximum, [jnp.max(score, axis=-1, keepdims=True) for score in scores]
        )
        raised = [jnp.exp(score - top) for score in scores]
        total = sum(jnp.sum(item, axis=-1, keepdims=True) for item in raised)
        over = 1.0 / total
        mixture = sum(
            jnp.dot((item * over).astype(BF16), value, preferred_element_type=F32)
            for item, (_, value) in zip(raised, held)
        )
        residual = block[:, at].astype(F32)
        if last:
            residual = jnp.where(place[2] == 1, crossed[:, at].astype(F32), residual)
        result = residual + mixture
        if last:
            result = jnp.where(flag[0] == 1, result, own[:, at].astype(F32))
        out[out_start : out_start + rows, at] = result.astype(BF16)


def attend(last, place, flag, sums, crossed, block, own, earlier, outs, after):
    rows, width = own.shape
    chunk = len(earlier)
    return pl.pallas_call(
        functools.partial(attend_kernel, chunk, last),
        in_specs=[smem_spec()] * 2
        + [vmem_spec()] * (6 + chunk + len(outs))
        + [any_spec() for _ in after],
        out_shape=[
            jax.ShapeDtypeStruct(((len(outs) + 1) * rows, width), BF16),
            jax.ShapeDtypeStruct((2, rows, width), BF16),
        ],
        compiler_params=pltpu.CompilerParams(vmem_limit_bytes=VMEM_BYTES),
        cost_estimate=cost(250),
        name="attend",
    )(place, flag, *sums, crossed, block, own, *earlier, *outs, *after)


def solution(mesh):
    sections = mesh.shape["section"]

    def local(inputs, qkv_weight, norm_gain, preempted):
        d = lax.axis_index("dp")
        t = lax.axis_index("tensor")
        y, c = t // 2, t % 2
        place = jnp.stack([c, d, (d == y).astype(c.dtype)]).astype(jnp.int32)
        weight = stage(qkv_weight)

        def spread(crossed, ringed):
            return (
                crossed,
                ringed,
                permute(crossed, sections, sibling),
                permute(ringed, sections, sibling),
            )

        def partial(start, four, after):
            sent, kept, kept_mean = project(start, rows, place, four, norm_gain, weight, after)
            return kept, permute(sent, sections, peer), kept_mean

        block = inputs[0, 0]
        rows = block.shape[0] // PARTS
        starts = range(0, block.shape[0], rows)
        pair = permute(block, sections, cross), permute(block, sections, ring)
        *pair, weight = lax.optimization_barrier((*pair, weight))
        weight = pltpu.with_memory_space_constraint(weight, pltpu.VMEM)
        four = spread(*pair)
        sums, after = [], []
        for start in starts:
            sums.append(partial(start, four, after))
            after = [sums[-1][2]]
        owns, moved, held = [], [], []
        for start, item in zip(starts, sums):
            part = block[start : start + rows]
            own, pairs = attend(False, place, preempted, item, part, part, part, held, [], after)
            held.append(pairs)
            owns.append(own)
            crossed = permute(own, sections, onward(cross))
            ringed = permute(own, sections, onward(ring))
            moved.append(((crossed, ringed), permute(own, sections, onward(direct))))
            after = [crossed]
        sums, after = [], owns[-1]
        for i, (pair, _) in enumerate(moved):
            if i:
                pair = lax.optimization_barrier((*pair, after))[:2]
            four = spread(*pair)
            sums.append(partial(0, four, [after]))
            after = sums[-1][2]
        outs, held = [], []
        for own, (pair, before), item in zip(owns, moved, sums):
            out, pairs = attend(
                True, place, preempted, item, pair[0], before, own, held, outs, [after]
            )
            held.append(pairs)
            outs.append(out)
        return outs[-1][None, None]

    placed = (
        P("section", "dp", None, "tensor"),
        P("section", None, "dp", "tensor"),
        P("section", None),
        P("section"),
    )
    return jax.shard_map(
        local,
        mesh=mesh,
        in_specs=placed,
        out_specs=P("section", "dp", None, "tensor"),
        check_vma=False,
    )
```

time: 162 us -> 135 us (0.83)
  local copies, waits for them, and re-layouts: 25.8 us -> 11.2 us
  waiting for transfers between devices: 52 us -> 42.1 us
  Pallas kernels: 43.1 us -> 35.6 us
  starting transfers between devices: 38.2 us -> 44.4 us
    unnamed x70 -> x20, local copies, waits for them, and re-layouts: 24.7 us -> 11.2 us
    ppermute x22 -> x18, waiting for transfers between devices: 52 us -> 42.1 us  [permute(): return lax.ppermute(array, AXES, pairs)]
    pallas_call x12 -> x9, Pallas kernels: 43.1 us -> 35.6 us  [the longest x4 18.5 us: project(): pl.pallas_call(functools.partial(project_kernel, start), in_specs=[smem_s...]
    ppermute x22 -> x18, starting transfers between devices: 38.2 us -> 44.4 us  [permute(): return lax.ppermute(array, AXES, pairs)]
  transfers between devices with their start and end apart: 22 -> 18, of which waited for: 6 -> 7; matrix products, arithmetic and copies ran while one was open for 0% -> 0% of each run, Pallas kernels for 20% -> 20%
where the time goes in v3:
time: 135 us; the launch traced here: 134 us
  starting transfers between devices  44.4 us (33%)
  waiting for transfers between devices  42.1 us (31%)
  Pallas kernels  35.6 us (26%)
  local copies, waits for them, and re-layouts  11.2 us (8%)
    ppermute x18, starting transfers between devices, permute(): return lax.ppermute(array, AXES, pairs)  44.4 us
    ppermute x18, waiting for transfers between devices, permute(): return lax.ppermute(array, AXES, pairs)  42.1 us
    pallas_call x4, Pallas kernels, project(): pl.pallas_call(functools.partial(project_kernel, start), in_specs=[smem_s...  18.5 us
    pallas_call x4, Pallas kernels, attend(): pl.pallas_call(functools.partial(attend_kernel, chunk, last), in_specs=[s...  16.2 us
    unnamed x20, local copies, waits for them, and re-layouts  11.2 us
  transfers between devices with their start and end apart: 18, of which 7 were waited for; matrix products, arithmetic and copies ran while one was open for 0% of the time, Pallas kernels for 20%

profile of v3, /device:TPU:0, one launch (start us, length us, event | category | flops | bytes accessed | tf_op | source)
XLA Modules:
  0.0 134.3 jit_solution(17694106154132107450)
XLA Ops:
  0.0 1.7 %collective-permute-start = (bf16[256,896]{1,0:T(8,128)(2,1)}, bf16[256,896]{1,0:T(8,128)(2,1)S(1)}, u32[]{:S(2)}, u32[]{:S(2)}) collective-permute-start(bf16[256,896]{1,0:T(8,128)(2,1)} %bitcast.9), channel_id=1, source_target_pairs={{0,0},{1,1},{2,4},{3,5},{4,2},{5,3},{6,6},{7,7},{8,8},{9,9},{10,12... | collective-permute-start | bytes 1376264 | tf_op jit(solution)/shard_map/ppermute | solution.py:33
  1.7 4.7 %collective-permute-start.1 = (bf16[256,896]{1,0:T(8,128)(2,1)}, bf16[256,896]{1,0:T(8,128)(2,1)S(1)}, u32[]{:S(2)}, u32[]{:S(2)}) collective-permute-start(bf16[256,896]{1,0:T(8,128)(2,1)} %bitcast.10), channel_id=1, source_target_pairs={{0,2},{1,3},{2,6},{3,7},{4,0},{5,1},{6,4},{7,5},{8,10},{9,11},{10,... | collective-permute-start | bytes 1376264 | tf_op jit(solution)/shard_map/ppermute | solution.py:33
  6.4 3.7 %copy-done = bf16[1,3,1792,896]{3,2,1,0:T(8,128)(2,1)S(1)} copy-done((bf16[1,3,1792,896]{3,2,1,0:T(8,128)(2,1)S(1)}, bf16[1,3,1792,896]{3,2,1,0:T(8,128)(2,1)}, u32[]{:S(2)}) %copy-start) | copy-done | bytes 9633816
  11.0 3.7 %copy-done.1 = bf16[1,3,1792,896]{3,2,1,0:T(8,128)(2,1)} copy-done((bf16[1,3,1792,896]{3,2,1,0:T(8,128)(2,1)}, bf16[1,3,1792,896]{3,2,1,0:T(8,128)(2,1)S(1)}, u32[]{:S(2)}) %copy-start.1) | copy-done | bytes 9633816
  14.7 11.9 %collective-permute-done.1.ringed = bf16[256,896]{1,0:T(8,128)(2,1)S(1)} collective-permute-done((bf16[256,896]{1,0:T(8,128)(2,1)}, bf16[256,896]{1,0:T(8,128)(2,1)S(1)}, u32[]{:S(2)}, u32[]{:S(2)}) %collective-permute-start.1) | collective-permute-done | bytes 458784 | tf_op jit(solution)/shard_map/ppermute | solution.py:33
  29.1 3.7 %copy-done.2 = bf16[1,3,1792,896]{3,2,1,0:T(8,128)(2,1)S(1)} copy-done((bf16[1,3,1792,896]{3,2,1,0:T(8,128)(2,1)S(1)}, bf16[1,3,1792,896]{3,2,1,0:T(8,128)(2,1)}, u32[]{:S(2)}) %copy-start.2) | copy-done | bytes 9633816
  32.8 4.0 %project.4 = (bf16[400,896]{1,0:T(8,128)(2,1)S(1)}, f32[3,128,896]{2,1,0:T(8,128)S(1)}, f32[128,1]{1,0:T(8,128)S(1)}) custom-call(s32[3]{0:T(128)S(1)} %pad_add_fusion.place, bf16[256,896]{1,0:T(8,128)(2,1)S(1)} %collective-permute-done.crossed, bf16[256,896]{1,0:T(8,128)(2,1)S(1)} %collective-permute-done.1.ringed, ...), custom_call_target="tpu_custom_call" | custom-call | flops 3449999872 | bytes 1000 | tf_op jit(solution)/shard_map/project/pallas_call | solution.py:142
  36.9 1.5 %collective-permute-start.5 = (bf16[400,896]{1,0:T(8,128)(2,1)S(1)}, bf16[400,896]{1,0:T(8,128)(2,1)S(1)}, u32[]{:S(2)}, u32[]{:S(2)}) collective-permute-start(bf16[400,896]{1,0:T(8,128)(2,1)S(1)} %get-tuple-element.36), channel_id=1, source_target_pairs={{0,4},{1,5},{2,6},{3,7},{4,0},{5,1},{6,2},{7,3},{8,12},{9,13},{10,... | collective-permute-start | bytes 2150408 | tf_op jit(solution)/shard_map/ppermute | solution.py:33
  39.0 4.9 %project.5 = (bf16[400,896]{1,0:T(8,128)(2,1)}, f32[3,128,896]{2,1,0:T(8,128)S(1)}, f32[128,1]{1,0:T(8,128)S(1)}) custom-call(s32[3]{0:T(128)S(1)} %pad_add_fusion.place, bf16[256,896]{1,0:T(8,128)(2,1)S(1)} %collective-permute-done.crossed, bf16[256,896]{1,0:T(8,128)(2,1)S(1)} %collective-permute-done.1.ringed, ...), custom_call_target="tpu_custom_call" | custom-call | flops 3449999872 | bytes 1000 | tf_op jit(solution)/shard_map/project/pallas_call | solution.py:142
  44.5 11.3 %collective-permute-done.5.received = bf16[400,896]{1,0:T(8,128)(2,1)S(1)} collective-permute-done((bf16[400,896]{1,0:T(8,128)(2,1)S(1)}, bf16[400,896]{1,0:T(8,128)(2,1)S(1)}, u32[]{:S(2)}, u32[]{:S(2)}) %collective-permute-start.5) | collective-permute-done | bytes 716832 | tf_op jit(solution)/shard_map/ppermute | solution.py:33
  55.8 3.1 %attend.4 = (bf16[128,896]{1,0:T(8,128)(2,1)S(1)}, bf16[2,128,896]{2,1,0:T(8,128)(2,1)S(1)}) custom-call(s32[3]{0:T(128)S(1)} %pad_add_fusion.place, s32[1]{0:T(128)S(6)} %copy.5.flag, f32[3,128,896]{2,1,0:T(8,128)S(1)} %get-tuple-element.35.kept, bf16[400,896]{1,0:T(8,128)(2,1)S(1)} %collective-permute-done.5.received, ...), custom_call_target="tpu_custom_call" | custom-call | flops 287500009472 | bytes 1000 | tf_op jit(solution)/shard_map/attend/pallas_call | solution.py:217
  58.9 4.2 %collective-permute-start.6 = (bf16[128,896]{1,0:T(8,128)(2,1)S(1)}, bf16[128,896]{1,0:T(8,128)(2,1)}, u32[]{:S(2)}, u32[]{:S(2)}) collective-permute-start(bf16[128,896]{1,0:T(8,128)(2,1)S(1)} %get-tuple-element.38.own), channel_id=1, source_target_pairs={{0,8},{1,9},{2,12},{3,13},{4,10},{5,11},{6,14},{7,15},{8,16},{9,17... | collective-permute-start | bytes 688136 | tf_op jit(solution)/shard_map/ppermute | solution.py:33
  63.1 5.2 %collective-permute-start.9 = (bf16[128,896]{1,0:T(8,128)(2,1)S(1)}, bf16[128,896]{1,0:T(8,128)(2,1)}, u32[]{:S(2)}, u32[]{:S(2)}) collective-permute-start(bf16[128,896]{1,0:T(8,128)(2,1)S(1)} %get-tuple-element.38.own), channel_id=1, source_target_pairs={{0,10},{1,11},{2,14},{3,15},{4,8},{5,9},{6,12},{7,13},{8,18},{9,19... | collective-permute-start | bytes 688136 | tf_op jit(solution)/shard_map/ppermute | solution.py:33
  68.3 4.6 %collective-permute-done.9.ringed = bf16[128,896]{1,0:T(8,128)(2,1)} collective-permute-done((bf16[128,896]{1,0:T(8,128)(2,1)S(1)}, bf16[128,896]{1,0:T(8,128)(2,1)}, u32[]{:S(2)}, u32[]{:S(2)}) %collective-permute-start.9) | collective-permute-done | bytes 229408 | tf_op jit(solution)/shard_map/ppermute | solution.py:33
  73.0 4.7 %attend.5 = (bf16[128,896]{1,0:T(8,128)(2,1)}, bf16[2,128,896]{2,1,0:T(8,128)(2,1)}) custom-call(s32[3]{0:T(128)S(1)} %pad_add_fusion.place, s32[1]{0:T(128)S(6)} %copy.5.flag, f32[3,128,896]{2,1,0:T(8,128)S(1)} %get-tuple-element.32.kept, bf16[400,896]{1,0:T(8,128)(2,1)} %collective-permute-done.4.received, ...), custom_call_target="tpu_custom_call" | custom-call | flops 287500009472 | bytes 1000 | tf_op jit(solution)/shard_map/attend/pallas_call | solution.py:217
  77.7 10.9 %collective-permute-start.7 = (bf16[128,896]{1,0:T(8,128)(2,1)}, bf16[128,896]{1,0:T(8,128)(2,1)S(1)}, u32[]{:S(2)}, u32[]{:S(2)}) collective-permute-start(bf16[128,896]{1,0:T(8,128)(2,1)} %get-tuple-element.39.refs_0_.own), channel_id=1, source_target_pairs={{0,8},{1,9},{2,12},{3,13},{4,10},{5,11},{6,14},{7,15},{8,16},{9,17... | collective-permute-start | bytes 688136 | tf_op jit(solution)/shard_map/ppermute | solution.py:33
  88.7 3.5 %collective-permute-start.8 = (bf16[128,896]{1,0:T(8,128)(2,1)}, bf16[128,896]{1,0:T(8,128)(2,1)S(1)}, u32[]{:S(2)}, u32[]{:S(2)}) collective-permute-start(bf16[128,896]{1,0:T(8,128)(2,1)} %get-tuple-element.39.refs_0_.own), channel_id=1, source_target_pairs={{0,10},{1,11},{2,14},{3,15},{4,8},{5,9},{6,12},{7,13},{8,18},{9,19... | collective-permute-start | bytes 688136 | tf_op jit(solution)/shard_map/ppermute | solution.py:33
  92.3 4.8 %project.6 = (bf16[400,896]{1,0:T(8,128)(2,1)S(1)}, f32[3,128,896]{2,1,0:T(8,128)S(1)}, f32[128,1]{1,0:T(8,128)S(1)}) custom-call(s32[3]{0:T(128)S(1)} %pad_add_fusion.place, bf16[128,896]{1,0:T(8,128)(2,1)} %collective-permute-done.6.refs_1_.crossed, bf16[128,896]{1,0:T(8,128)(2,1)} %collective-permute-done.9.ringed, ...), custom_call_target="tpu_custom_call" | custom-call | flops 3449999872 | bytes 1000 | tf_op jit(solution)/shard_map/project/pallas_call | solution.py:142
  97.0 1.6 %collective-permute-start.16 = (bf16[400,896]{1,0:T(8,128)(2,1)S(1)}, bf16[400,896]{1,0:T(8,128)(2,1)S(1)}, u32[]{:S(2)}, u32[]{:S(2)}) collective-permute-start(bf16[400,896]{1,0:T(8,128)(2,1)S(1)} %get-tuple-element.47), channel_id=1, source_target_pairs={{0,4},{1,5},{2,6},{3,7},{4,0},{5,1},{6,2},{7,3},{8,12},{9,13},{10,... | collective-permute-start | bytes 2150408 | tf_op jit(solution)/shard_map/ppermute | solution.py:33
  101.3 4.9 %project.7 = (bf16[400,896]{1,0:T(8,128)(2,1)}, f32[3,128,896]{2,1,0:T(8,128)S(1)}, f32[128,1]{1,0:T(8,128)S(1)}) custom-call(s32[3]{0:T(128)S(1)} %pad_add_fusion.place, bf16[128,896]{1,0:T(8,128)(2,1)S(1)} %collective-permute-done.7.crossed, bf16[128,896]{1,0:T(8,128)(2,1)S(1)} %collective-permute-done.8.ringed, ...), custom_call_target="tpu_custom_call" | custom-call | flops 3449999872 | bytes 1000 | tf_op jit(solution)/shard_map/project/pallas_call | solution.py:142
  106.2 7.3 %collective-permute-start.14 = (bf16[400,896]{1,0:T(8,128)(2,1)}, bf16[400,896]{1,0:T(8,128)(2,1)}, u32[]{:S(2)}, u32[]{:S(2)}) collective-permute-start(bf16[400,896]{1,0:T(8,128)(2,1)} %get-tuple-element.44), channel_id=1, source_target_pairs={{0,4},{1,5},{2,6},{3,7},{4,0},{5,1},{6,2},{7,3},{8,12},{9,13},{10,... | collective-permute-start | bytes 2150408 | tf_op jit(solution)/shard_map/ppermute | solution.py:33
  113.8 3.5 %attend.6 = (bf16[128,896]{1,0:T(8,128)(2,1)S(1)}, bf16[2,128,896]{2,1,0:T(8,128)(2,1)S(1)}) custom-call(s32[3]{0:T(128)S(1)} %pad_add_fusion.place, s32[1]{0:T(128)S(6)} %copy.5.flag, f32[3,128,896]{2,1,0:T(8,128)S(1)} %get-tuple-element.46.kept, bf16[400,896]{1,0:T(8,128)(2,1)S(1)} %collective-permute-done.16.received, ...), custom_call_target="tpu_custom_call" | custom-call | flops 287500009472 | bytes 1000 | tf_op jit(solution)/shard_map/attend/pallas_call | solution.py:217
  117.3 12.1 %collective-permute-done.14.received = bf16[400,896]{1,0:T(8,128)(2,1)} collective-permute-done((bf16[400,896]{1,0:T(8,128)(2,1)}, bf16[400,896]{1,0:T(8,128)(2,1)}, u32[]{:S(2)}, u32[]{:S(2)}) %collective-permute-start.14) | collective-permute-done | bytes 716832 | tf_op jit(solution)/shard_map/ppermute | solution.py:33
  129.5 4.8 %attend.7 = (bf16[256,896]{1,0:T(8,128)(2,1)}, bf16[2,128,896]{2,1,0:T(8,128)(2,1)}) custom-call(s32[3]{0:T(128)S(1)} %pad_add_fusion.place, s32[1]{0:T(128)S(6)} %copy.5.flag, f32[3,128,896]{2,1,0:T(8,128)S(1)} %get-tuple-element.43.kept, bf16[400,896]{1,0:T(8,128)(2,1)} %collective-permute-done.14.received, ...), custom_call_target="tpu_custom_call" | custom-call | flops 287500009472 | bytes 1000 | tf_op jit(solution)/shard_map/attend/pallas_call | solution.py:217
  (43 shorter events, 7.0 us)
Async XLA Ops:
  0.0 14.7 %collective-permute-start = (bf16[256,896]{1,0:T(8,128)(2,1)}, bf16[256,896]{1,0:T(8,128)(2,1)S(1)}, u32[]{:S(2)}, u32[]{:S(2)}) collective-permute-start(bf16[256,896]{1,0:T(8,128)(2,1)} %bitcast.9), channel_id=1, source_target_pairs={{0,0},{1,1},{2,4},{3,5},{4,2},{5,3},{6,6},{7,7},{8,8},{9,9},{10,12... | collective-permute-start | bytes 1376264 | tf_op jit(solution)/shard_map/ppermute | solution.py:33
  1.7 25.0 %collective-permute-start.1 = (bf16[256,896]{1,0:T(8,128)(2,1)}, bf16[256,896]{1,0:T(8,128)(2,1)S(1)}, u32[]{:S(2)}, u32[]{:S(2)}) collective-permute-start(bf16[256,896]{1,0:T(8,128)(2,1)} %bitcast.10), channel_id=1, source_target_pairs={{0,2},{1,3},{2,6},{3,7},{4,0},{5,1},{6,4},{7,5},{8,10},{9,11},{10,... | collective-permute-start | bytes 1376264 | tf_op jit(solution)/shard_map/ppermute | solution.py:33
  10.1 19.0 %copy-start.8 = (bf16[1,3584]{1,0:T(2,128)(2,1)S(1)}, bf16[1,3584]{1,0:T(2,128)(2,1)}, u32[]{:S(2)}) copy-start(bf16[1,3584]{1,0:T(2,128)(2,1)} %gain.7) | copy-start | bytes 21508
  26.6 1.8 %collective-permute-start.2 = (bf16[256,896]{1,0:T(8,128)(2,1)S(1)}, bf16[256,896]{1,0:T(8,128)(2,1)S(1)}, u32[]{:S(2)}, u32[]{:S(2)}) collective-permute-start(bf16[256,896]{1,0:T(8,128)(2,1)S(1)} %collective-permute-done.crossed), channel_id=1, source_target_pairs={{0,1},{1,0},{2,3},{3,2},{4,5},{5,4},{6,7},{7,6},{8,9},{9,8},{10,11... | collective-permute-start | bytes 1376264 | tf_op jit(solution)/shard_map/ppermute | solution.py:33
  26.6 2.5 %collective-permute-start.3 = (bf16[256,896]{1,0:T(8,128)(2,1)S(1)}, bf16[256,896]{1,0:T(8,128)(2,1)S(1)}, u32[]{:S(2)}, u32[]{:S(2)}) collective-permute-start(bf16[256,896]{1,0:T(8,128)(2,1)S(1)} %collective-permute-done.1.ringed), channel_id=1, source_target_pairs={{0,1},{1,0},{2,3},{3,2},{4,5},{5,4},{6,7},{7,6},{8,9},{9,8},{10,11... | collective-permute-start | bytes 1376264 | tf_op jit(solution)/shard_map/ppermute | solution.py:33
  36.9 19.0 %collective-permute-start.5 = (bf16[400,896]{1,0:T(8,128)(2,1)S(1)}, bf16[400,896]{1,0:T(8,128)(2,1)S(1)}, u32[]{:S(2)}, u32[]{:S(2)}) collective-permute-start(bf16[400,896]{1,0:T(8,128)(2,1)S(1)} %get-tuple-element.36), channel_id=1, source_target_pairs={{0,4},{1,5},{2,6},{3,7},{4,0},{5,1},{6,2},{7,3},{8,12},{9,13},{10,... | collective-permute-start | bytes 2150408 | tf_op jit(solution)/shard_map/ppermute | solution.py:33
  43.9 29.1 %collective-permute-start.4 = (bf16[400,896]{1,0:T(8,128)(2,1)}, bf16[400,896]{1,0:T(8,128)(2,1)}, u32[]{:S(2)}, u32[]{:S(2)}) collective-permute-start(bf16[400,896]{1,0:T(8,128)(2,1)} %get-tuple-element.33), channel_id=1, source_target_pairs={{0,4},{1,5},{2,6},{3,7},{4,0},{5,1},{6,2},{7,3},{8,12},{9,13},{10,... | collective-permute-start | bytes 2150408 | tf_op jit(solution)/shard_map/ppermute | solution.py:33
  58.9 14.1 %copy-start.4 = (bf16[128,896]{1,0:T(8,128)(2,1)}, bf16[128,896]{1,0:T(8,128)(2,1)S(1)}, u32[]{:S(2)}) copy-start(bf16[128,896]{1,0:T(8,128)(2,1)S(1)} %get-tuple-element.38.own) | copy-start | bytes 688132
  58.9 9.4 %collective-permute-start.6 = (bf16[128,896]{1,0:T(8,128)(2,1)S(1)}, bf16[128,896]{1,0:T(8,128)(2,1)}, u32[]{:S(2)}, u32[]{:S(2)}) collective-permute-start(bf16[128,896]{1,0:T(8,128)(2,1)S(1)} %get-tuple-element.38.own), channel_id=1, source_target_pairs={{0,8},{1,9},{2,12},{3,13},{4,10},{5,11},{6,14},{7,15},{8,16},{9,17... | collective-permute-start | bytes 688136 | tf_op jit(solution)/shard_map/ppermute | solution.py:33
  63.1 9.9 %collective-permute-start.9 = (bf16[128,896]{1,0:T(8,128)(2,1)S(1)}, bf16[128,896]{1,0:T(8,128)(2,1)}, u32[]{:S(2)}, u32[]{:S(2)}) collective-permute-start(bf16[128,896]{1,0:T(8,128)(2,1)S(1)} %get-tuple-element.38.own), channel_id=1, source_target_pairs={{0,10},{1,11},{2,14},{3,15},{4,8},{5,9},{6,12},{7,13},{8,18},{9,19... | collective-permute-start | bytes 688136 | tf_op jit(solution)/shard_map/ppermute | solution.py:33
  68.3 23.9 %collective-permute-start.10 = (bf16[128,896]{1,0:T(8,128)(2,1)}, bf16[128,896]{1,0:T(8,128)(2,1)}, u32[]{:S(2)}, u32[]{:S(2)}) collective-permute-start(bf16[128,896]{1,0:T(8,128)(2,1)} %collective-permute-done.6.refs_1_.crossed), channel_id=1, source_target_pairs={{0,1},{1,0},{2,3},{3,2},{4,5},{5,4},{6,7},{7,6},{8,9},{9,8},{10,11... | collective-permute-start | bytes 688136 | tf_op jit(solution)/shard_map/ppermute | solution.py:33
  73.0 19.3 %collective-permute-start.11 = (bf16[128,896]{1,0:T(8,128)(2,1)}, bf16[128,896]{1,0:T(8,128)(2,1)}, u32[]{:S(2)}, u32[]{:S(2)}) collective-permute-start(bf16[128,896]{1,0:T(8,128)(2,1)} %collective-permute-done.9.ringed), channel_id=1, source_target_pairs={{0,1},{1,0},{2,3},{3,2},{4,5},{5,4},{6,7},{7,6},{8,9},{9,8},{10,11... | collective-permute-start | bytes 688136 | tf_op jit(solution)/shard_map/ppermute | solution.py:33
  73.0 19.3 %copy-start.3 = (bf16[1,3,1792,896]{3,2,1,0:T(8,128)(2,1)S(1)}, bf16[1,3,1792,896]{3,2,1,0:T(8,128)(2,1)}, u32[]{:S(2)}) copy-start(bf16[1,3,1792,896]{3,2,1,0:T(8,128)(2,1)} %copy-done.1) | copy-start | bytes 28901380
  77.7 21.5 %copy-start.5 = (bf16[128,896]{1,0:T(8,128)(2,1)S(1)}, bf16[128,896]{1,0:T(8,128)(2,1)}, u32[]{:S(2)}) copy-start(bf16[128,896]{1,0:T(8,128)(2,1)} %copy-done.4) | copy-start | bytes 688132
  77.7 20.9 %collective-permute-start.7 = (bf16[128,896]{1,0:T(8,128)(2,1)}, bf16[128,896]{1,0:T(8,128)(2,1)S(1)}, u32[]{:S(2)}, u32[]{:S(2)}) collective-permute-start(bf16[128,896]{1,0:T(8,128)(2,1)} %get-tuple-element.39.refs_0_.own), channel_id=1, source_target_pairs={{0,8},{1,9},{2,12},{3,13},{4,10},{5,11},{6,14},{7,15},{8,16},{9,17... | collective-permute-start | bytes 688136 | tf_op jit(solution)/shard_map/ppermute | solution.py:33
  88.7 10.0 %collective-permute-start.8 = (bf16[128,896]{1,0:T(8,128)(2,1)}, bf16[128,896]{1,0:T(8,128)(2,1)S(1)}, u32[]{:S(2)}, u32[]{:S(2)}) collective-permute-start(bf16[128,896]{1,0:T(8,128)(2,1)} %get-tuple-element.39.refs_0_.own), channel_id=1, source_target_pairs={{0,10},{1,11},{2,14},{3,15},{4,8},{5,9},{6,12},{7,13},{8,18},{9,19... | collective-permute-start | bytes 688136 | tf_op jit(solution)/shard_map/ppermute | solution.py:33
  97.0 16.8 %collective-permute-start.16 = (bf16[400,896]{1,0:T(8,128)(2,1)S(1)}, bf16[400,896]{1,0:T(8,128)(2,1)S(1)}, u32[]{:S(2)}, u32[]{:S(2)}) collective-permute-start(bf16[400,896]{1,0:T(8,128)(2,1)S(1)} %get-tuple-element.47), channel_id=1, source_target_pairs={{0,4},{1,5},{2,6},{3,7},{4,0},{5,1},{6,2},{7,3},{8,12},{9,13},{10,... | collective-permute-start | bytes 2150408 | tf_op jit(solution)/shard_map/ppermute | solution.py:33
  98.7 7.5 %copy-start.6 = (bf16[128,896]{1,0:T(8,128)(2,1)}, bf16[128,896]{1,0:T(8,128)(2,1)S(1)}, u32[]{:S(2)}) copy-start(bf16[128,896]{1,0:T(8,128)(2,1)S(1)} %collective-permute-done.7.crossed) | copy-start | bytes 688132
  98.7 2.6 %collective-permute-start.12 = (bf16[128,896]{1,0:T(8,128)(2,1)S(1)}, bf16[128,896]{1,0:T(8,128)(2,1)S(1)}, u32[]{:S(2)}, u32[]{:S(2)}) collective-permute-start(bf16[128,896]{1,0:T(8,128)(2,1)S(1)} %collective-permute-done.7.crossed), channel_id=1, source_target_pairs={{0,1},{1,0},{2,3},{3,2},{4,5},{5,4},{6,7},{7,6},{8,9},{9,8},{10,11... | collective-permute-start | bytes 688136 | tf_op jit(solution)/shard_map/ppermute | solution.py:33
  98.8 2.5 %collective-permute-start.13 = (bf16[128,896]{1,0:T(8,128)(2,1)S(1)}, bf16[128,896]{1,0:T(8,128)(2,1)S(1)}, u32[]{:S(2)}, u32[]{:S(2)}) collective-permute-start(bf16[128,896]{1,0:T(8,128)(2,1)S(1)} %collective-permute-done.8.ringed), channel_id=1, source_target_pairs={{0,1},{1,0},{2,3},{3,2},{4,5},{5,4},{6,7},{7,6},{8,9},{9,8},{10,11... | collective-permute-start | bytes 688136 | tf_op jit(solution)/shard_map/ppermute | solution.py:33
  99.3 14.2 %collective-permute-start.17 = (bf16[128,896]{1,0:T(8,128)(2,1)S(1)}, bf16[128,896]{1,0:T(8,128)(2,1)S(1)}, u32[]{:S(2)}, u32[]{:S(2)}) collective-permute-start(bf16[128,896]{1,0:T(8,128)(2,1)S(1)} %copy-done.5), channel_id=1, source_target_pairs={{2,10},{3,11},{4,12},{5,13},{10,18},{11,19},{12,20},{13,21},{18,26... | collective-permute-start | bytes 688136 | tf_op jit(solution)/shard_map/ppermute | solution.py:33
  99.9 17.4 %collective-permute-start.15 = (bf16[128,896]{1,0:T(8,128)(2,1)}, bf16[128,896]{1,0:T(8,128)(2,1)}, u32[]{:S(2)}, u32[]{:S(2)}) collective-permute-start(bf16[128,896]{1,0:T(8,128)(2,1)} %get-tuple-element.39.refs_0_.own), channel_id=1, source_target_pairs={{2,10},{3,11},{4,12},{5,13},{10,18},{11,19},{12,20},{13,21},{18,26... | collective-permute-start | bytes 688136 | tf_op jit(solution)/shard_map/ppermute | solution.py:33
  106.2 23.3 %collective-permute-start.14 = (bf16[400,896]{1,0:T(8,128)(2,1)}, bf16[400,896]{1,0:T(8,128)(2,1)}, u32[]{:S(2)}, u32[]{:S(2)}) collective-permute-start(bf16[400,896]{1,0:T(8,128)(2,1)} %get-tuple-element.44), channel_id=1, source_target_pairs={{0,4},{1,5},{2,6},{3,7},{4,0},{5,1},{6,2},{7,3},{8,12},{9,13},{10,... | collective-permute-start | bytes 2150408 | tf_op jit(solution)/shard_map/ppermute | solution.py:33
  113.8 15.7 %copy-start.7 = (bf16[128,896]{1,0:T(8,128)(2,1)S(1)}, bf16[128,896]{1,0:T(8,128)(2,1)}, u32[]{:S(2)}) copy-start(bf16[128,896]{1,0:T(8,128)(2,1)} %copy-done.6) | copy-start | bytes 688132
  (4 other events, 17.3 us)

commit v4 on v3

--- a/solution.py
+++ b/solution.py
@@ -45,6 +45,14 @@
     return (s, d, y, c) if d != y else None
 
 
+def across_y(s, d, y, c):
+    return (s, d, 1 - y, c) if d != y else None
+
+
+def across_x(s, d, y, c):
+    return (s, 1 - d, y, c) if d == y else None
+
+
 def sibling(s, d, y, c):
     return (s, d, y, 1 - c)
 
@@ -77,27 +85,27 @@
     return pl.BlockSpec(memory_space=pltpu.SMEM)
 
 
-def stage_kernel(weight, staged, semaphore):
+def stage_kernel(place, weight, staged, semaphore):
     copy = pltpu.make_async_copy(weight, staged, semaphore)
     copy.start()
     copy.wait()
 
 
-def stage(weight):
+def stage(place, weight):
     return pl.pallas_call(
         stage_kernel,
-        in_specs=[any_spec()],
+        in_specs=[smem_spec(), any_spec()],
         out_specs=vmem_spec(),
         out_shape=pltpu.VMEM(weight.shape, weight.dtype),
         scratch_shapes=[pltpu.SemaphoreType.DMA(())],
         compiler_params=pltpu.CompilerParams(vmem_limit_bytes=VMEM_BYTES),
         cost_estimate=cost(4),
         name="stage",
-    )(weight)
-
-
-def project_kernel(start, place, crossed, ringed, sib_crossed, sib_ringed, gain, weight, *refs):
-    sent, kept, kept_mean, normed = refs[-4:]
+    )(place, weight)
+
+
+def project_kernel(place, crossed, ringed, sib_crossed, sib_ringed, gain, weight, *refs):
+    sent, kept, kept_mean, normed = refs
     rows = normed.shape[0] // 2
     width = crossed.shape[1]
     half = 2 * width
@@ -108,7 +116,7 @@
         (ringed, sib_ringed, 1 - diagonal),
     ):
         at = pl.ds(pl.multiple_of(offset * rows, rows), rows)
-        pieces = [ref[start : start + rows].astype(F32) for ref in (mine, theirs)]
+        pieces = [ref[...].astype(F32) for ref in (mine, theirs)]
         squares = sum(jnp.sum(piece * piece, axis=-1, keepdims=True) for piece in pieces)
         mean = squares * (1.0 / half)
         means.append(mean)
@@ -137,11 +145,11 @@
             kept[k, :, at] = product[rows:]
 
 
-def project(start, rows, place, four, gain, weight, after):
+def project(rows, place, four, gain, weight, estimate):
     width = four[0].shape[1]
     return pl.pallas_call(
-        functools.partial(project_kernel, start),
-        in_specs=[smem_spec()] + [vmem_spec()] * 6 + [any_spec() for _ in after],
+        project_kernel,
+        in_specs=[smem_spec()] + [vmem_spec()] * 6,
         out_shape=[
             jax.ShapeDtypeStruct((3 * rows + STAT_ROWS, width), BF16),
             jax.ShapeDtypeStruct((3, rows, width), F32),
@@ -149,9 +157,9 @@
         ],
         scratch_shapes=[pltpu.VMEM((2 * rows, 2 * width), BF16)],
         compiler_params=pltpu.CompilerParams(vmem_limit_bytes=VMEM_BYTES),
-        cost_estimate=cost(3.0),
+        cost_estimate=cost(estimate),
         name="project",
-    )(place, *four, gain, weight, *after)
+    )(place, *four, gain, weight)
 
 
 def attend_kernel(
@@ -237,7 +245,8 @@
         t = lax.axis_index("tensor")
         y, c = t // 2, t % 2
         place = jnp.stack([c, d, (d == y).astype(c.dtype)]).astype(jnp.int32)
-        weight = stage(qkv_weight)
+        place, diagonal, weight = lax.optimization_barrier((place, d == y, qkv_weight))
+        weight = stage(place, weight)
 
         def spread(crossed, ringed):
             return (
@@ -247,42 +256,40 @@
                 permute(ringed, sections, sibling),
             )
 
-        def partial(start, four, after):
-            sent, kept, kept_mean = project(start, rows, place, four, norm_gain, weight, after)
+        def partial(four, estimate):
+            sent, kept, kept_mean = project(rows, place, four, norm_gain, weight, estimate)
             return kept, permute(sent, sections, peer), kept_mean
 
         block = inputs[0, 0]
         rows = block.shape[0] // PARTS
-        starts = range(0, block.shape[0], rows)
-        pair = permute(block, sections, cross), permute(block, sections, ring)
+        parts = [block[i * rows : (i + 1) * rows] for i in range(PARTS)]
+        pair = permute(parts[0], sections, cross), permute(parts[0], sections, ring)
+        relayed = permute(parts[1], sections, across_y)
+        ringed = permute(parts[1], sections, ring)
         *pair, weight = lax.optimization_barrier((*pair, weight))
         weight = pltpu.with_memory_space_constraint(weight, pltpu.VMEM)
-        four = spread(*pair)
-        sums, after = [], []
-        for start in starts:
-            sums.append(partial(start, four, after))
-            after = [sums[-1][2]]
-        owns, moved, held = [], [], []
-        for start, item in zip(starts, sums):
-            part = block[start : start + rows]
+        sums = [partial(spread(*pair), 3)]
+        crossed = jnp.where(diagonal, parts[1], permute(relayed, sections, across_x))
+        crossed, ringed, _ = lax.optimization_barrier((crossed, ringed, sums[0][2]))
+        sums.append(partial(spread(crossed, ringed), 3))
+        owns, held, moved = [], [], []
+        after = [sums[1][2]]
+        seconds = []
+        for part, item in zip(parts, sums):
             own, pairs = attend(False, place, preempted, item, part, part, part, held, [], after)
             held.append(pairs)
             owns.append(own)
-            crossed = permute(own, sections, onward(cross))
-            ringed = permute(own, sections, onward(ring))
-            moved.append(((crossed, ringed), permute(own, sections, onward(direct))))
-            after = [crossed]
-        sums, after = [], owns[-1]
-        for i, (pair, _) in enumerate(moved):
-            if i:
-                pair = lax.optimization_barrier((*pair, after))[:2]
-            four = spread(*pair)
-            sums.append(partial(0, four, [after]))
-            after = sums[-1][2]
+            pair = permute(own, sections, onward(cross)), permute(own, sections, onward(ring))
+            moved.append((pair[0], permute(own, sections, onward(direct))))
+            if seconds:
+                pair = lax.optimization_barrier((*pair, seconds[0][2]))[:2]
+            seconds.append(partial(spread(*pair), 0.001))
+            after = [seconds[0][2]]
+        sums, after = seconds, seconds[1][2]
         outs, held = [], []
-        for own, (pair, before), item in zip(owns, moved, sums):
+        for own, (crossed, before), item in zip(owns, moved, sums):
             out, pairs = attend(
-                True, place, preempted, item, pair[0], before, own, held, outs, [after]
+                True, place, preempted, item, crossed, before, own, held, outs, [after]
             )
             held.append(pairs)
             outs.append(out)

time: 135 us -> 126 us (0.933)
  local copies, waits for them, and re-layouts: 11.2 us -> 4.88 us
  waiting for transfers between devices: 42.1 us -> 39.6 us
    unnamed x20 -> x18, local copies, waits for them, and re-layouts: 11.2 us -> 3.8 us
    ppermute x18 -> x23, waiting for transfers between devices: 42.1 us -> 39.6 us  [permute(): return lax.ppermute(array, AXES, pairs)]
    ppermute x18 -> x23, starting transfers between devices: 44.4 us -> 43.7 us  [permute(): return lax.ppermute(array, AXES, pairs)]
  transfers between devices with their start and end apart: 18 -> 23, of which waited for: 7 -> 11; matrix products, arithmetic and copies ran while one was open for 0% -> 0% of each run, Pallas kernels for 20% -> 25%
where the time goes in v4:
time: 126 us; the launch traced here: 125 us
  starting transfers between devices  43.7 us (35%)
  waiting for transfers between devices  39.6 us (31%)
  Pallas kernels  36.2 us (29%)
  local copies, waits for them, and re-layouts  4.88 us (4%)
    ppermute x23, starting transfers between devices, permute(): return lax.ppermute(array, AXES, pairs)  43.7 us
    ppermute x23, waiting for transfers between devices, permute(): return lax.ppermute(array, AXES, pairs)  39.6 us
    pallas_call x4, Pallas kernels, project(): pl.pallas_call(project_kernel, in_specs=[smem_spec()] + [vmem_spec()] * 6...  18.5 us
    pallas_call x4, Pallas kernels, attend(): pl.pallas_call(functools.partial(attend_kernel, chunk, last), in_specs=[s...  16.3 us
    unnamed x18, local copies, waits for them, and re-layouts  3.8 us
  transfers between devices with their start and end apart: 23, of which 11 were waited for; matrix products, arithmetic and copies ran while one was open for 0% of the time, Pallas kernels for 25%

profile of v4, /device:TPU:0, one launch (start us, length us, event | category | flops | bytes accessed | tf_op | source)
XLA Modules:
  0.0 125.4 jit_solution(16677323427864883350)
XLA Ops:
  1.8 5.7 %collective-permute-start.4 = (bf16[128,896]{1,0:T(8,128)(2,1)S(1)}, bf16[128,896]{1,0:T(8,128)(2,1)S(1)}, u32[]{:S(2)}, u32[]{:S(2)}) collective-permute-start(bf16[128,896]{1,0:T(8,128)(2,1)S(1)} %get-tuple-element.61.crossed.block.own), channel_id=1, source_target_pairs={{0,2},{1,3},{2,6},{3,7},{4,0},{5,1},{6,4},{7,5},{8,10},{9,11},{10,... | collective-permute-start | bytes 688136 | tf_op jit(solution)/shard_map/ppermute | solution.py:33
  8.8 3.8 %copy-done = bf16[1,3,1792,896]{3,2,1,0:T(8,128)(2,1)S(1)} copy-done((bf16[1,3,1792,896]{3,2,1,0:T(8,128)(2,1)S(1)}, bf16[1,3,1792,896]{3,2,1,0:T(8,128)(2,1)}, u32[]{:S(2)}) %copy-start) | copy-done | bytes 9633816
  14.1 3.6 %collective-permute-done.4.ringed = bf16[128,896]{1,0:T(8,128)(2,1)S(1)} collective-permute-done((bf16[128,896]{1,0:T(8,128)(2,1)S(1)}, bf16[128,896]{1,0:T(8,128)(2,1)S(1)}, u32[]{:S(2)}, u32[]{:S(2)}) %collective-permute-start.4) | collective-permute-done | bytes 229408 | tf_op jit(solution)/shard_map/ppermute | solution.py:33
  19.6 2.5 %collective-permute-start.1 = (bf16[128,896]{1,0:T(8,128)(2,1)S(1)}, bf16[128,896]{1,0:T(8,128)(2,1)S(1)}, u32[]{:S(2)}, u32[]{:S(2)}) collective-permute-start(bf16[128,896]{1,0:T(8,128)(2,1)S(1)} %collective-permute-done), channel_id=1, source_target_pairs={{0,4},{1,5},{6,2},{7,3},{8,12},{9,13},{14,10},{15,11},{16,20},{17,... | collective-permute-start | bytes 688136 | tf_op jit(solution)/shard_map/ppermute | solution.py:33
  22.2 4.0 %project.4 = (bf16[400,896]{1,0:T(8,128)(2,1)S(1)}, f32[3,128,896]{2,1,0:T(8,128)S(1)}, f32[128,1]{1,0:T(8,128)S(1)}) custom-call(s32[3]{0:T(128)S(1)} %pad_add_fusion.place, bf16[128,896]{1,0:T(8,128)(2,1)S(1)} %collective-permute-done.3.crossed, bf16[128,896]{1,0:T(8,128)(2,1)S(1)} %collective-permute-done.4.ringed, ...), custom_call_target="tpu_custom_call" | custom-call | flops 3449999872 | bytes 1000 | tf_op jit(solution)/shard_map/project/pallas_call | solution.py:150
  29.5 4.8 %project.5 = (bf16[400,896]{1,0:T(8,128)(2,1)}, f32[3,128,896]{2,1,0:T(8,128)S(1)}, f32[128,1]{1,0:T(8,128)S(1)}) custom-call(s32[3]{0:T(128)S(1)} %pad_add_fusion.place, bf16[128,896]{1,0:T(8,128)(2,1)S(1)} %broadcast_select_fusion.crossed, bf16[128,896]{1,0:T(8,128)(2,1)S(1)} %collective-permute-done.2.ringed, ...), custom_call_target="tpu_custom_call" | custom-call | flops 3449999872 | bytes 1000 | tf_op jit(solution)/shard_map/project/pallas_call | solution.py:150
  34.3 2.5 %collective-permute-start.9 = (bf16[400,896]{1,0:T(8,128)(2,1)}, bf16[400,896]{1,0:T(8,128)(2,1)}, u32[]{:S(2)}, u32[]{:S(2)}) collective-permute-start(bf16[400,896]{1,0:T(8,128)(2,1)} %get-tuple-element.43), channel_id=1, source_target_pairs={{0,4},{1,5},{2,6},{3,7},{4,0},{5,1},{6,2},{7,3},{8,12},{9,13},{10,... | collective-permute-start | bytes 2150408 | tf_op jit(solution)/shard_map/ppermute | solution.py:33
  36.8 8.4 %collective-permute-done.10.received = bf16[400,896]{1,0:T(8,128)(2,1)S(1)} collective-permute-done((bf16[400,896]{1,0:T(8,128)(2,1)S(1)}, bf16[400,896]{1,0:T(8,128)(2,1)S(1)}, u32[]{:S(2)}, u32[]{:S(2)}) %collective-permute-start.10) | collective-permute-done | bytes 716832 | tf_op jit(solution)/shard_map/ppermute | solution.py:33
  45.2 3.1 %attend.4 = (bf16[128,896]{1,0:T(8,128)(2,1)S(1)}, bf16[2,128,896]{2,1,0:T(8,128)(2,1)S(1)}) custom-call(s32[3]{0:T(128)S(1)} %pad_add_fusion.place, s32[1]{0:T(128)S(6)} %copy.5.flag, f32[3,128,896]{2,1,0:T(8,128)S(1)} %get-tuple-element.45.kept, bf16[400,896]{1,0:T(8,128)(2,1)S(1)} %collective-permute-done.10.received, ...), custom_call_target="tpu_custom_call" | custom-call | flops 287500009472 | bytes 1000 | tf_op jit(solution)/shard_map/attend/pallas_call | solution.py:225
  48.4 3.5 %collective-permute-start.11 = (bf16[128,896]{1,0:T(8,128)(2,1)S(1)}, bf16[128,896]{1,0:T(8,128)(2,1)S(1)}, u32[]{:S(2)}, u32[]{:S(2)}) collective-permute-start(bf16[128,896]{1,0:T(8,128)(2,1)S(1)} %get-tuple-element.48.own), channel_id=1, source_target_pairs={{0,8},{1,9},{2,12},{3,13},{4,10},{5,11},{6,14},{7,15},{8,16},{9,17... | collective-permute-start | bytes 688136 | tf_op jit(solution)/shard_map/ppermute | solution.py:33
  51.9 4.2 %collective-permute-start.12 = (bf16[128,896]{1,0:T(8,128)(2,1)S(1)}, bf16[128,896]{1,0:T(8,128)(2,1)S(1)}, u32[]{:S(2)}, u32[]{:S(2)}) collective-permute-start(bf16[128,896]{1,0:T(8,128)(2,1)S(1)} %get-tuple-element.48.own), channel_id=1, source_target_pairs={{0,10},{1,11},{2,14},{3,15},{4,8},{5,9},{6,12},{7,13},{8,18},{9,19... | collective-permute-start | bytes 688136 | tf_op jit(solution)/shard_map/ppermute | solution.py:33
  56.3 5.0 %collective-permute-done.12.ringed = bf16[128,896]{1,0:T(8,128)(2,1)S(1)} collective-permute-done((bf16[128,896]{1,0:T(8,128)(2,1)S(1)}, bf16[128,896]{1,0:T(8,128)(2,1)S(1)}, u32[]{:S(2)}, u32[]{:S(2)}) %collective-permute-start.12) | collective-permute-done | bytes 229408 | tf_op jit(solution)/shard_map/ppermute | solution.py:33
  61.3 1.5 %collective-permute-done.14.sib_ringed = bf16[128,896]{1,0:T(8,128)(2,1)S(1)} collective-permute-done((bf16[128,896]{1,0:T(8,128)(2,1)S(1)}, bf16[128,896]{1,0:T(8,128)(2,1)S(1)}, u32[]{:S(2)}, u32[]{:S(2)}) %collective-permute-start.14) | collective-permute-done | bytes 229408 | tf_op jit(solution)/shard_map/ppermute | solution.py:33
  62.8 4.8 %project.6 = (bf16[400,896]{1,0:T(8,128)(2,1)}, f32[3,128,896]{2,1,0:T(8,128)S(1)}, f32[128,1]{1,0:T(8,128)S(1)}) custom-call(s32[3]{0:T(128)S(1)} %pad_add_fusion.place, bf16[128,896]{1,0:T(8,128)(2,1)S(1)} %collective-permute-done.11.crossed, bf16[128,896]{1,0:T(8,128)(2,1)S(1)} %collective-permute-done.12.ringed, ...), custom_call_target="tpu_custom_call" | custom-call | flops 1150000 | bytes 1000 | tf_op jit(solution)/shard_map/project/pallas_call | solution.py:150
  67.9 4.6 %attend.5 = (bf16[128,896]{1,0:T(8,128)(2,1)}, bf16[2,128,896]{2,1,0:T(8,128)(2,1)}) custom-call(s32[3]{0:T(128)S(1)} %pad_add_fusion.place, s32[1]{0:T(128)S(6)} %copy.5.flag, f32[3,128,896]{2,1,0:T(8,128)S(1)} %get-tuple-element.42.kept, bf16[400,896]{1,0:T(8,128)(2,1)} %collective-permute-done.9.received, ...), custom_call_target="tpu_custom_call" | custom-call | flops 287500009472 | bytes 1000 | tf_op jit(solution)/shard_map/attend/pallas_call | solution.py:225
  72.5 5.8 %collective-permute-start.15 = (bf16[128,896]{1,0:T(8,128)(2,1)}, bf16[128,896]{1,0:T(8,128)(2,1)S(1)}, u32[]{:S(2)}, u32[]{:S(2)}) collective-permute-start(bf16[128,896]{1,0:T(8,128)(2,1)} %get-tuple-element.50.own), channel_id=1, source_target_pairs={{0,8},{1,9},{2,12},{3,13},{4,10},{5,11},{6,14},{7,15},{8,16},{9,17... | collective-permute-start | bytes 688136 | tf_op jit(solution)/shard_map/ppermute | solution.py:33
  78.3 4.1 %collective-permute-start.16 = (bf16[128,896]{1,0:T(8,128)(2,1)}, bf16[128,896]{1,0:T(8,128)(2,1)S(1)}, u32[]{:S(2)}, u32[]{:S(2)}) collective-permute-start(bf16[128,896]{1,0:T(8,128)(2,1)} %get-tuple-element.50.own), channel_id=1, source_target_pairs={{0,10},{1,11},{2,14},{3,15},{4,8},{5,9},{6,12},{7,13},{8,18},{9,19... | collective-permute-start | bytes 688136 | tf_op jit(solution)/shard_map/ppermute | solution.py:33
  82.4 2.1 %collective-permute-done.15.crossed = bf16[128,896]{1,0:T(8,128)(2,1)S(1)} collective-permute-done((bf16[128,896]{1,0:T(8,128)(2,1)}, bf16[128,896]{1,0:T(8,128)(2,1)S(1)}, u32[]{:S(2)}, u32[]{:S(2)}) %collective-permute-start.15) | collective-permute-done | bytes 229408 | tf_op jit(solution)/shard_map/ppermute | solution.py:33
  84.5 4.6 %collective-permute-done.16.ringed = bf16[128,896]{1,0:T(8,128)(2,1)S(1)} collective-permute-done((bf16[128,896]{1,0:T(8,128)(2,1)}, bf16[128,896]{1,0:T(8,128)(2,1)S(1)}, u32[]{:S(2)}, u32[]{:S(2)}) %collective-permute-start.16) | collective-permute-done | bytes 229408 | tf_op jit(solution)/shard_map/ppermute | solution.py:33
  91.6 4.8 %project.7 = (bf16[400,896]{1,0:T(8,128)(2,1)}, f32[3,128,896]{2,1,0:T(8,128)S(1)}, f32[128,1]{1,0:T(8,128)S(1)}) custom-call(s32[3]{0:T(128)S(1)} %pad_add_fusion.place, bf16[128,896]{1,0:T(8,128)(2,1)S(1)} %collective-permute-done.15.crossed, bf16[128,896]{1,0:T(8,128)(2,1)S(1)} %collective-permute-done.16.ringed, ...), custom_call_target="tpu_custom_call" | custom-call | flops 1150000 | bytes 1000 | tf_op jit(solution)/shard_map/project/pallas_call | solution.py:150
  96.5 8.2 %collective-permute-start.19 = (bf16[400,896]{1,0:T(8,128)(2,1)}, bf16[400,896]{1,0:T(8,128)(2,1)}, u32[]{:S(2)}, u32[]{:S(2)}) collective-permute-start(bf16[400,896]{1,0:T(8,128)(2,1)} %get-tuple-element.54), channel_id=1, source_target_pairs={{0,4},{1,5},{2,6},{3,7},{4,0},{5,1},{6,2},{7,3},{8,12},{9,13},{10,... | collective-permute-start | bytes 2150408 | tf_op jit(solution)/shard_map/ppermute | solution.py:33
  104.6 3.7 %attend.6 = (bf16[128,896]{1,0:T(8,128)(2,1)S(1)}, bf16[2,128,896]{2,1,0:T(8,128)(2,1)S(1)}) custom-call(s32[3]{0:T(128)S(1)} %pad_add_fusion.place, s32[1]{0:T(128)S(6)} %copy.5.flag, f32[3,128,896]{2,1,0:T(8,128)S(1)} %get-tuple-element.56.kept, bf16[400,896]{1,0:T(8,128)(2,1)} %collective-permute-done.21.received, ...), custom_call_target="tpu_custom_call" | custom-call | flops 287500009472 | bytes 1000 | tf_op jit(solution)/shard_map/attend/pallas_call | solution.py:225
  108.4 12.2 %collective-permute-done.19.received = bf16[400,896]{1,0:T(8,128)(2,1)} collective-permute-done((bf16[400,896]{1,0:T(8,128)(2,1)}, bf16[400,896]{1,0:T(8,128)(2,1)}, u32[]{:S(2)}, u32[]{:S(2)}) %collective-permute-start.19) | collective-permute-done | bytes 716832 | tf_op jit(solution)/shard_map/ppermute | solution.py:33
  120.6 4.8 %attend.7 = (bf16[256,896]{1,0:T(8,128)(2,1)}, bf16[2,128,896]{2,1,0:T(8,128)(2,1)}) custom-call(s32[3]{0:T(128)S(1)} %pad_add_fusion.place, s32[1]{0:T(128)S(6)} %copy.5.flag, f32[3,128,896]{2,1,0:T(8,128)S(1)} %get-tuple-element.53.kept, bf16[400,896]{1,0:T(8,128)(2,1)} %collective-permute-done.19.received, ...), custom_call_target="tpu_custom_call" | custom-call | flops 287500009472 | bytes 1000 | tf_op jit(solution)/shard_map/attend/pallas_call | solution.py:225
  (52 shorter events, 12.3 us)
Async XLA Ops:
  1.1 13.0 %collective-permute-start.3 = (bf16[128,896]{1,0:T(8,128)(2,1)S(1)}, bf16[128,896]{1,0:T(8,128)(2,1)S(1)}, u32[]{:S(2)}, u32[]{:S(2)}) collective-permute-start(bf16[128,896]{1,0:T(8,128)(2,1)S(1)} %get-tuple-element.61.crossed.block.own), channel_id=1, source_target_pairs={{0,0},{1,1},{2,4},{3,5},{4,2},{5,3},{6,6},{7,7},{8,8},{9,9},{10,12... | collective-permute-start | bytes 688136 | tf_op jit(solution)/shard_map/ppermute | solution.py:33
  1.8 15.9 %collective-permute-start.4 = (bf16[128,896]{1,0:T(8,128)(2,1)S(1)}, bf16[128,896]{1,0:T(8,128)(2,1)S(1)}, u32[]{:S(2)}, u32[]{:S(2)}) collective-permute-start(bf16[128,896]{1,0:T(8,128)(2,1)S(1)} %get-tuple-element.61.crossed.block.own), channel_id=1, source_target_pairs={{0,2},{1,3},{2,6},{3,7},{4,0},{5,1},{6,4},{7,5},{8,10},{9,11},{10,... | collective-permute-start | bytes 688136 | tf_op jit(solution)/shard_map/ppermute | solution.py:33
  7.5 12.2 %collective-permute-start = (bf16[128,896]{1,0:T(8,128)(2,1)S(1)}, bf16[128,896]{1,0:T(8,128)(2,1)S(1)}, u32[]{:S(2)}, u32[]{:S(2)}) collective-permute-start(bf16[128,896]{1,0:T(8,128)(2,1)S(1)} %get-tuple-element.62.crossed.block.own), channel_id=1, source_target_pairs={{2,0},{3,1},{4,6},{5,7},{10,8},{11,9},{12,14},{13,15},{18,16},{19,... | collective-permute-start | bytes 688136 | tf_op jit(solution)/shard_map/ppermute | solution.py:33
  17.7 4.5 %collective-permute-start.5 = (bf16[128,896]{1,0:T(8,128)(2,1)S(1)}, bf16[128,896]{1,0:T(8,128)(2,1)S(1)}, u32[]{:S(2)}, u32[]{:S(2)}) collective-permute-start(bf16[128,896]{1,0:T(8,128)(2,1)S(1)} %collective-permute-done.3.crossed), channel_id=1, source_target_pairs={{0,1},{1,0},{2,3},{3,2},{4,5},{5,4},{6,7},{7,6},{8,9},{9,8},{10,11... | collective-permute-start | bytes 688136 | tf_op jit(solution)/shard_map/ppermute | solution.py:33
  17.7 4.5 %collective-permute-start.6 = (bf16[128,896]{1,0:T(8,128)(2,1)S(1)}, bf16[128,896]{1,0:T(8,128)(2,1)S(1)}, u32[]{:S(2)}, u32[]{:S(2)}) collective-permute-start(bf16[128,896]{1,0:T(8,128)(2,1)S(1)} %collective-permute-done.4.ringed), channel_id=1, source_target_pairs={{0,1},{1,0},{2,3},{3,2},{4,5},{5,4},{6,7},{7,6},{8,9},{9,8},{10,11... | collective-permute-start | bytes 688136 | tf_op jit(solution)/shard_map/ppermute | solution.py:33
  18.2 9.4 %collective-permute-start.2 = (bf16[128,896]{1,0:T(8,128)(2,1)S(1)}, bf16[128,896]{1,0:T(8,128)(2,1)S(1)}, u32[]{:S(2)}, u32[]{:S(2)}) collective-permute-start(bf16[128,896]{1,0:T(8,128)(2,1)S(1)} %get-tuple-element.62.crossed.block.own), channel_id=1, source_target_pairs={{0,2},{1,3},{2,6},{3,7},{4,0},{5,1},{6,4},{7,5},{8,10},{9,11},{10,... | collective-permute-start | bytes 688136 | tf_op jit(solution)/shard_map/ppermute | solution.py:33
  19.6 7.9 %collective-permute-start.1 = (bf16[128,896]{1,0:T(8,128)(2,1)S(1)}, bf16[128,896]{1,0:T(8,128)(2,1)S(1)}, u32[]{:S(2)}, u32[]{:S(2)}) collective-permute-start(bf16[128,896]{1,0:T(8,128)(2,1)S(1)} %collective-permute-done), channel_id=1, source_target_pairs={{0,4},{1,5},{6,2},{7,3},{8,12},{9,13},{14,10},{15,11},{16,20},{17,... | collective-permute-start | bytes 688136 | tf_op jit(solution)/shard_map/ppermute | solution.py:33
  26.2 19.1 %collective-permute-start.10 = (bf16[400,896]{1,0:T(8,128)(2,1)S(1)}, bf16[400,896]{1,0:T(8,128)(2,1)S(1)}, u32[]{:S(2)}, u32[]{:S(2)}) collective-permute-start(bf16[400,896]{1,0:T(8,128)(2,1)S(1)} %get-tuple-element.46), channel_id=1, source_target_pairs={{0,4},{1,5},{2,6},{3,7},{4,0},{5,1},{6,2},{7,3},{8,12},{9,13},{10,... | collective-permute-start | bytes 2150408 | tf_op jit(solution)/shard_map/ppermute | solution.py:33
  27.6 1.6 %collective-permute-start.7 = (bf16[128,896]{1,0:T(8,128)(2,1)S(1)}, bf16[128,896]{1,0:T(8,128)(2,1)S(1)}, u32[]{:S(2)}, u32[]{:S(2)}) collective-permute-start(bf16[128,896]{1,0:T(8,128)(2,1)S(1)} %broadcast_select_fusion.crossed), channel_id=1, source_target_pairs={{0,1},{1,0},{2,3},{3,2},{4,5},{5,4},{6,7},{7,6},{8,9},{9,8},{10,11... | collective-permute-start | bytes 688136 | tf_op jit(solution)/shard_map/ppermute | solution.py:33
  27.7 1.8 %collective-permute-start.8 = (bf16[128,896]{1,0:T(8,128)(2,1)S(1)}, bf16[128,896]{1,0:T(8,128)(2,1)S(1)}, u32[]{:S(2)}, u32[]{:S(2)}) collective-permute-start(bf16[128,896]{1,0:T(8,128)(2,1)S(1)} %collective-permute-done.2.ringed), channel_id=1, source_target_pairs={{0,1},{1,0},{2,3},{3,2},{4,5},{5,4},{6,7},{7,6},{8,9},{9,8},{10,11... | collective-permute-start | bytes 688136 | tf_op jit(solution)/shard_map/ppermute | solution.py:33
  34.3 33.6 %collective-permute-start.9 = (bf16[400,896]{1,0:T(8,128)(2,1)}, bf16[400,896]{1,0:T(8,128)(2,1)}, u32[]{:S(2)}, u32[]{:S(2)}) collective-permute-start(bf16[400,896]{1,0:T(8,128)(2,1)} %get-tuple-element.43), channel_id=1, source_target_pairs={{0,4},{1,5},{2,6},{3,7},{4,0},{5,1},{6,2},{7,3},{8,12},{9,13},{10,... | collective-permute-start | bytes 2150408 | tf_op jit(solution)/shard_map/ppermute | solution.py:33
  48.4 8.0 %collective-permute-start.11 = (bf16[128,896]{1,0:T(8,128)(2,1)S(1)}, bf16[128,896]{1,0:T(8,128)(2,1)S(1)}, u32[]{:S(2)}, u32[]{:S(2)}) collective-permute-start(bf16[128,896]{1,0:T(8,128)(2,1)S(1)} %get-tuple-element.48.own), channel_id=1, source_target_pairs={{0,8},{1,9},{2,12},{3,13},{4,10},{5,11},{6,14},{7,15},{8,16},{9,17... | collective-permute-start | bytes 688136 | tf_op jit(solution)/shard_map/ppermute | solution.py:33
  51.9 9.4 %collective-permute-start.12 = (bf16[128,896]{1,0:T(8,128)(2,1)S(1)}, bf16[128,896]{1,0:T(8,128)(2,1)S(1)}, u32[]{:S(2)}, u32[]{:S(2)}) collective-permute-start(bf16[128,896]{1,0:T(8,128)(2,1)S(1)} %get-tuple-element.48.own), channel_id=1, source_target_pairs={{0,10},{1,11},{2,14},{3,15},{4,8},{5,9},{6,12},{7,13},{8,18},{9,19... | collective-permute-start | bytes 688136 | tf_op jit(solution)/shard_map/ppermute | solution.py:33
  56.3 5.0 %collective-permute-start.13 = (bf16[128,896]{1,0:T(8,128)(2,1)S(1)}, bf16[128,896]{1,0:T(8,128)(2,1)S(1)}, u32[]{:S(2)}, u32[]{:S(2)}) collective-permute-start(bf16[128,896]{1,0:T(8,128)(2,1)S(1)} %collective-permute-done.11.crossed), channel_id=1, source_target_pairs={{0,1},{1,0},{2,3},{3,2},{4,5},{5,4},{6,7},{7,6},{8,9},{9,8},{10,11... | collective-permute-start | bytes 688136 | tf_op jit(solution)/shard_map/ppermute | solution.py:33
  61.3 1.5 %collective-permute-start.14 = (bf16[128,896]{1,0:T(8,128)(2,1)S(1)}, bf16[128,896]{1,0:T(8,128)(2,1)S(1)}, u32[]{:S(2)}, u32[]{:S(2)}) collective-permute-start(bf16[128,896]{1,0:T(8,128)(2,1)S(1)} %collective-permute-done.12.ringed), channel_id=1, source_target_pairs={{0,1},{1,0},{2,3},{3,2},{4,5},{5,4},{6,7},{7,6},{8,9},{9,8},{10,11... | collective-permute-start | bytes 688136 | tf_op jit(solution)/shard_map/ppermute | solution.py:33
  67.6 37.0 %collective-permute-start.21 = (bf16[400,896]{1,0:T(8,128)(2,1)}, bf16[400,896]{1,0:T(8,128)(2,1)}, u32[]{:S(2)}, u32[]{:S(2)}) collective-permute-start(bf16[400,896]{1,0:T(8,128)(2,1)} %get-tuple-element.57), channel_id=1, source_target_pairs={{0,4},{1,5},{2,6},{3,7},{4,0},{5,1},{6,2},{7,3},{8,12},{9,13},{10,... | collective-permute-start | bytes 2150408 | tf_op jit(solution)/shard_map/ppermute | solution.py:33
  72.5 32.1 %copy-start.2 = (bf16[128,896]{1,0:T(8,128)(2,1)S(1)}, bf16[128,896]{1,0:T(8,128)(2,1)}, u32[]{:S(2)}) copy-start(bf16[128,896]{1,0:T(8,128)(2,1)} %copy-done.1) | copy-start | bytes 688132
  72.5 11.9 %collective-permute-start.15 = (bf16[128,896]{1,0:T(8,128)(2,1)}, bf16[128,896]{1,0:T(8,128)(2,1)S(1)}, u32[]{:S(2)}, u32[]{:S(2)}) collective-permute-start(bf16[128,896]{1,0:T(8,128)(2,1)} %get-tuple-element.50.own), channel_id=1, source_target_pairs={{0,8},{1,9},{2,12},{3,13},{4,10},{5,11},{6,14},{7,15},{8,16},{9,17... | collective-permute-start | bytes 688136 | tf_op jit(solution)/shard_map/ppermute | solution.py:33
  78.3 10.8 %collective-permute-start.16 = (bf16[128,896]{1,0:T(8,128)(2,1)}, bf16[128,896]{1,0:T(8,128)(2,1)S(1)}, u32[]{:S(2)}, u32[]{:S(2)}) collective-permute-start(bf16[128,896]{1,0:T(8,128)(2,1)} %get-tuple-element.50.own), channel_id=1, source_target_pairs={{0,10},{1,11},{2,14},{3,15},{4,8},{5,9},{6,12},{7,13},{8,18},{9,19... | collective-permute-start | bytes 688136 | tf_op jit(solution)/shard_map/ppermute | solution.py:33
  89.1 2.5 %collective-permute-start.17 = (bf16[128,896]{1,0:T(8,128)(2,1)S(1)}, bf16[128,896]{1,0:T(8,128)(2,1)S(1)}, u32[]{:S(2)}, u32[]{:S(2)}) collective-permute-start(bf16[128,896]{1,0:T(8,128)(2,1)S(1)} %collective-permute-done.15.crossed), channel_id=1, source_target_pairs={{0,1},{1,0},{2,3},{3,2},{4,5},{5,4},{6,7},{7,6},{8,9},{9,8},{10,11... | collective-permute-start | bytes 688136 | tf_op jit(solution)/shard_map/ppermute | solution.py:33
  89.1 2.5 %collective-permute-start.18 = (bf16[128,896]{1,0:T(8,128)(2,1)S(1)}, bf16[128,896]{1,0:T(8,128)(2,1)S(1)}, u32[]{:S(2)}, u32[]{:S(2)}) collective-permute-start(bf16[128,896]{1,0:T(8,128)(2,1)S(1)} %collective-permute-done.16.ringed), channel_id=1, source_target_pairs={{0,1},{1,0},{2,3},{3,2},{4,5},{5,4},{6,7},{7,6},{8,9},{9,8},{10,11... | collective-permute-start | bytes 688136 | tf_op jit(solution)/shard_map/ppermute | solution.py:33
  89.6 15.0 %collective-permute-start.22 = (bf16[128,896]{1,0:T(8,128)(2,1)S(1)}, bf16[128,896]{1,0:T(8,128)(2,1)S(1)}, u32[]{:S(2)}, u32[]{:S(2)}) collective-permute-start(bf16[128,896]{1,0:T(8,128)(2,1)S(1)} %copy-done.7), channel_id=1, source_target_pairs={{2,10},{3,11},{4,12},{5,13},{10,18},{11,19},{12,20},{13,21},{18,26... | collective-permute-start | bytes 688136 | tf_op jit(solution)/shard_map/ppermute | solution.py:33
  90.3 18.1 %collective-permute-start.20 = (bf16[128,896]{1,0:T(8,128)(2,1)}, bf16[128,896]{1,0:T(8,128)(2,1)}, u32[]{:S(2)}, u32[]{:S(2)}) collective-permute-start(bf16[128,896]{1,0:T(8,128)(2,1)} %get-tuple-element.50.own), channel_id=1, source_target_pairs={{2,10},{3,11},{4,12},{5,13},{10,18},{11,19},{12,20},{13,21},{18,26... | collective-permute-start | bytes 688136 | tf_op jit(solution)/shard_map/ppermute | solution.py:33
  96.5 24.1 %collective-permute-start.19 = (bf16[400,896]{1,0:T(8,128)(2,1)}, bf16[400,896]{1,0:T(8,128)(2,1)}, u32[]{:S(2)}, u32[]{:S(2)}) collective-permute-start(bf16[400,896]{1,0:T(8,128)(2,1)} %get-tuple-element.54), channel_id=1, source_target_pairs={{0,4},{1,5},{2,6},{3,7},{4,0},{5,1},{6,2},{7,3},{8,12},{9,13},{10,... | collective-permute-start | bytes 2150408 | tf_op jit(solution)/shard_map/ppermute | solution.py:33
  (8 other events, 107.0 us)

commit v5 on v4

--- a/solution.py
+++ b/solution.py
@@ -14,7 +14,6 @@
 F32 = jnp.float32
 BF16 = jnp.bfloat16
 PARTS = 2
-WIDE = 2 * HD
 VMEM_BYTES = 16 * 1024 * 1024
 STAT_ROWS = 16
 
@@ -137,12 +136,10 @@
     stat = jnp.where(which == 0, high, jnp.where(which == 1, mid, low))
     for begin in range(0, width, rows):
         sent[3 * rows :, begin : begin + rows] = stat.astype(BF16)
-    for begin in range(0, width, WIDE):
-        at = slice(begin, min(begin + WIDE, width))
-        for k in range(3):
-            product = jnp.dot(normed[...], weight[0, k, :, at], preferred_element_type=F32)
-            sent[k * rows : (k + 1) * rows, at] = product[:rows].astype(BF16)
-            kept[k, :, at] = product[rows:]
+    for k in range(3):
+        product = jnp.dot(normed[...], weight[0, k], preferred_element_type=F32)
+        sent[k * rows : (k + 1) * rows] = product[:rows].astype(BF16)
+        kept[k] = product[rows:]
 
 
 def project(rows, place, four, gain, weight, estimate):
@@ -151,9 +148,9 @@
         project_kernel,
         in_specs=[smem_spec()] + [vmem_spec()] * 6,
         out_shape=[
-            jax.ShapeDtypeStruct((3 * rows + STAT_ROWS, width), BF16),
-            jax.ShapeDtypeStruct((3, rows, width), F32),
-            jax.ShapeDtypeStruct((rows, 1), F32),
+            pltpu.VMEM((3 * rows + STAT_ROWS, width), BF16),
+            pltpu.VMEM((3, rows, width), F32),
+            pltpu.VMEM((rows, 1), F32),
         ],
         scratch_shapes=[pltpu.VMEM((2 * rows, 2 * width), BF16)],
         compiler_params=pltpu.CompilerParams(vmem_limit_bytes=VMEM_BYTES),
@@ -162,16 +159,8 @@
     )(place, *four, gain, weight)
 
 
-def attend_kernel(
-    chunk, last, place, flag, kept, received, kept_mean, crossed, block, own, *refs
-):
-    earlier = refs[:chunk]
-    earlier_outs = refs[chunk : 2 * chunk] if last else ()
-    out, pairs = refs[-2:]
-    rows, width = own.shape
-    out_start = rows * len(earlier_outs)
-    for i, ref in enumerate(earlier_outs):
-        out[i * rows : (i + 1) * rows] = ref[...]
+def mix(kept, received, kept_mean, earlier, pairs, put):
+    rows, width = kept.shape[1:]
     stat = received[3 * rows :, :rows].astype(F32)
     row = stat[0:1] + stat[1:2] + stat[2:3]
     mean_peer = jnp.transpose(jnp.broadcast_to(row, (HD, rows)))[:, :1]
@@ -182,8 +171,9 @@
     causal = lax.broadcasted_iota(jnp.int32, (rows, rows), 0) >= lax.broadcasted_iota(
         jnp.int32, (rows, rows), 1
     )
-    for head in range(width // HD):
-        at = slice(head * HD, (head + 1) * HD)
+    heads = [slice(begin, begin + HD) for begin in range(0, width, HD)]
+    held, scores = [], []
+    for at in heads:
         queries, keys, values = (
             (
                 kept[k, :, at] * scale_kept
@@ -193,48 +183,78 @@
         )
         pairs[0, :, at] = keys
         pairs[1, :, at] = values
-        held = [(ref[0, :, at], ref[1, :, at]) for ref in earlier] + [(keys, values)]
-        scores = [
-            lax.dot_general(queries, key, (((1,), (1,)), ((), ())), preferred_element_type=F32)
-            * (1.0 / math.sqrt(HD))
-            for key, _ in held
-        ]
-        scores[-1] = jnp.where(causal, scores[-1], F32(-1e30))
-        top = functools.reduce(
-            jnp.maximum, [jnp.max(score, axis=-1, keepdims=True) for score in scores]
-        )
-        raised = [jnp.exp(score - top) for score in scores]
-        total = sum(jnp.sum(item, axis=-1, keepdims=True) for item in raised)
-        over = 1.0 / total
+        held.append([(ref[0, :, at], ref[1, :, at]) for ref in earlier] + [(keys, values)])
+        scores.append(
+            [
+                lax.dot_general(queries, key, (((1,), (1,)), ((), ())), preferred_element_type=F32)
+                * (1.0 / math.sqrt(HD))
+                for key, _ in held[-1]
+            ]
+        )
+        scores[-1][-1] = jnp.where(causal, scores[-1][-1], F32(-1e30))
+    tops = [
+        functools.reduce(jnp.maximum, [jnp.max(item, axis=-1, keepdims=True) for item in score])
+        for score in scores
+    ]
+    raised = [[jnp.exp(item - top) for item in score] for score, top in zip(scores, tops)]
+    overs = [1.0 / sum(jnp.sum(item, axis=-1, keepdims=True) for item in items) for items in raised]
+    for at, items, over, pair in zip(heads, raised, overs, held):
         mixture = sum(
             jnp.dot((item * over).astype(BF16), value, preferred_element_type=F32)
-            for item, (_, value) in zip(raised, held)
-        )
-        residual = block[:, at].astype(F32)
-        if last:
-            residual = jnp.where(place[2] == 1, crossed[:, at].astype(F32), residual)
-        result = residual + mixture
-        if last:
-            result = jnp.where(flag[0] == 1, result, own[:, at].astype(F32))
-        out[out_start : out_start + rows, at] = result.astype(BF16)
-
-
-def attend(last, place, flag, sums, crossed, block, own, earlier, outs, after):
-    rows, width = own.shape
-    chunk = len(earlier)
+            for item, (_, value) in zip(items, pair)
+        )
+        put(at, mixture)
+
+
+def attend_kernel(kept, received, kept_mean, block, *refs):
+    earlier, (out, pairs) = refs[:-2], refs[-2:]
+
+    def put(at, mixture):
+        out[:, at] = (block[:, at].astype(F32) + mixture).astype(BF16)
+
+    mix(kept, received, kept_mean, earlier, pairs, put)
+
+
+def hold_kernel(kept, received, kept_mean, *refs):
+    owns, (held, pairs, whole) = refs[:-3], refs[-3:]
+    rows = kept.shape[1]
+
+    def put(at, mixture):
+        held[:, at] = mixture
+
+    mix(kept, received, kept_mean, (), pairs, put)
+    for i, own in enumerate(owns):
+        whole[i * rows : (i + 1) * rows] = own[...]
+
+
+def final_kernel(
+    place, flag, kept, received, kept_mean, earlier, held, first, second, before, own, out, pairs
+):
+    rows = kept.shape[1]
+    diagonal, shadow = place[2] == 1, flag[0] == 1
+
+    def settle(start, crossed, at, mixture):
+        here = slice(start, start + rows)
+        residual = jnp.where(diagonal, crossed[:, at].astype(F32), before[here, at].astype(F32))
+        result = jnp.where(shadow, residual + mixture, own[here, at].astype(F32))
+        out[here, at] = result.astype(BF16)
+
+    def put(at, mixture):
+        settle(rows, second, at, mixture)
+
+    settle(0, first, slice(None), held[...])
+    mix(kept, received, kept_mean, (earlier,), pairs, put)
+
+
+def call_attend(kernel, name, scalars, arrays, out_shape):
     return pl.pallas_call(
-        functools.partial(attend_kernel, chunk, last),
-        in_specs=[smem_spec()] * 2
-        + [vmem_spec()] * (6 + chunk + len(outs))
-        + [any_spec() for _ in after],
-        out_shape=[
-            jax.ShapeDtypeStruct(((len(outs) + 1) * rows, width), BF16),
-            jax.ShapeDtypeStruct((2, rows, width), BF16),
-        ],
+        kernel,
+        in_specs=[smem_spec() for _ in scalars] + [vmem_spec() for _ in arrays],
+        out_shape=out_shape,
         compiler_params=pltpu.CompilerParams(vmem_limit_bytes=VMEM_BYTES),
         cost_estimate=cost(250),
-        name="attend",
-    )(place, flag, *sums, crossed, block, own, *earlier, *outs, *after)
+        name=name,
+    )(*scalars, *arrays)
 
 
 def solution(mesh):
@@ -272,28 +292,39 @@
         crossed = jnp.where(diagonal, parts[1], permute(relayed, sections, across_x))
         crossed, ringed, _ = lax.optimization_barrier((crossed, ringed, sums[0][2]))
         sums.append(partial(spread(crossed, ringed), 3))
-        owns, held, moved = [], [], []
-        after = [sums[1][2]]
-        seconds = []
+        width = block.shape[1]
+        rows_of = pltpu.VMEM((rows, width), BF16)
+        pairs_of = pltpu.VMEM((2, rows, width), BF16)
+        owns, held, moved, seconds = [], [], [], []
         for part, item in zip(parts, sums):
-            own, pairs = attend(False, place, preempted, item, part, part, part, held, [], after)
+            if seconds:
+                part = lax.optimization_barrier((part, seconds[0][2]))[0]
+            own, pairs = call_attend(
+                attend_kernel, "attend", [], [*item, part, *held], [rows_of, pairs_of]
+            )
             held.append(pairs)
             owns.append(own)
             pair = permute(own, sections, onward(cross)), permute(own, sections, onward(ring))
-            moved.append((pair[0], permute(own, sections, onward(direct))))
+            moved.append(pair[0])
             if seconds:
                 pair = lax.optimization_barrier((*pair, seconds[0][2]))[:2]
             seconds.append(partial(spread(*pair), 0.001))
-            after = [seconds[0][2]]
-        sums, after = seconds, seconds[1][2]
-        outs, held = [], []
-        for own, (crossed, before), item in zip(owns, moved, sums):
-            out, pairs = attend(
-                True, place, preempted, item, crossed, before, own, held, outs, [after]
-            )
-            held.append(pairs)
-            outs.append(out)
-        return outs[-1][None, None]
+        mixture, pairs, own = call_attend(
+            hold_kernel,
+            "hold",
+            [],
+            [*seconds[0], *owns],
+            [pltpu.VMEM((rows, width), F32), pairs_of, pltpu.VMEM(block.shape, BF16)],
+        )
+        before = permute(own, sections, onward(direct))
+        out, _ = call_attend(
+            final_kernel,
+            "final",
+            [place, preempted],
+            [*seconds[1], pairs, mixture, *moved, before, own],
+            [jax.ShapeDtypeStruct(block.shape, BF16), pairs_of],
+        )
+        return out[None, None]
 
     placed = (
         P("section", "dp", None, "tensor"),

time: 126 us -> 111 us (0.88)
  starting transfers between devices: 43.7 us -> 35.6 us
  Pallas kernels: 36.2 us -> 28.4 us
    ppermute x23 -> x22, starting transfers between devices: 43.7 us -> 35.6 us  [permute(): return lax.ppermute(array, AXES, pairs)]
    pallas_call x4, Pallas kernels: 16.3 us -> 8.4 us  [call_attend(): pl.pallas_call(kernel, in_specs=[smem_spec() for _ in scalars] + [vmem_sp...]
    ppermute x23 -> x22, waiting for transfers between devices: 39.6 us -> 40 us  [permute(): return lax.ppermute(array, AXES, pairs)]
  transfers between devices with their start and end apart: 23 -> 22, of which waited for: 11 -> 13; matrix products, arithmetic and copies ran while one was open for 0% -> 0% of each run, Pallas kernels for 25% -> 23%
where the time goes in v5:
time: 111 us; the launch traced here: 110 us
  waiting for transfers between devices  40 us (36%)
  starting transfers between devices  35.6 us (32%)
  Pallas kernels  28.4 us (26%)
  local copies, waits for them, and re-layouts  4.88 us (4%)
    ppermute x22, waiting for transfers between devices, permute(): return lax.ppermute(array, AXES, pairs)  40 us
    ppermute x22, starting transfers between devices, permute(): return lax.ppermute(array, AXES, pairs)  35.6 us
    pallas_call x4, Pallas kernels, project(): pl.pallas_call(project_kernel, in_specs=[smem_spec()] + [vmem_spec()] * 6...  18.6 us
    pallas_call x4, Pallas kernels, call_attend(): pl.pallas_call(kernel, in_specs=[smem_spec() for _ in scalars] + [vmem_sp...  8.4 us
    unnamed x18, local copies, waits for them, and re-layouts  3.8 us
  transfers between devices with their start and end apart: 22, of which 13 were waited for; matrix products, arithmetic and copies ran while one was open for 0% of the time, Pallas kernels for 23%

profile of v5, /device:TPU:0, one launch (start us, length us, event | category | flops | bytes accessed | tf_op | source)
XLA Modules:
  0.0 109.9 jit_solution(7541296536001089663)
XLA Ops:
  1.1 3.0 %collective-permute-start.4 = (bf16[128,896]{1,0:T(8,128)(2,1)S(1)}, bf16[128,896]{1,0:T(8,128)(2,1)S(1)}, u32[]{:S(2)}, u32[]{:S(2)}) collective-permute-start(bf16[128,896]{1,0:T(8,128)(2,1)S(1)} %get-tuple-element.65.block), channel_id=1, source_target_pairs={{0,2},{1,3},{2,6},{3,7},{4,0},{5,1},{6,4},{7,5},{8,10},{9,11},{10,... | collective-permute-start | bytes 688136 | tf_op jit(solution)/shard_map/ppermute | solution.py:32
  6.2 3.8 %copy-done = bf16[1,3,1792,896]{3,2,1,0:T(8,128)(2,1)S(1)} copy-done((bf16[1,3,1792,896]{3,2,1,0:T(8,128)(2,1)S(1)}, bf16[1,3,1792,896]{3,2,1,0:T(8,128)(2,1)}, u32[]{:S(2)}) %copy-start) | copy-done | bytes 9633816
  11.4 2.5 %collective-permute-done.4.ringed = bf16[128,896]{1,0:T(8,128)(2,1)S(1)} collective-permute-done((bf16[128,896]{1,0:T(8,128)(2,1)S(1)}, bf16[128,896]{1,0:T(8,128)(2,1)S(1)}, u32[]{:S(2)}, u32[]{:S(2)}) %collective-permute-start.4) | collective-permute-done | bytes 229408 | tf_op jit(solution)/shard_map/ppermute | solution.py:32
  14.4 2.4 %collective-permute-start.2 = (bf16[128,896]{1,0:T(8,128)(2,1)S(1)}, bf16[128,896]{1,0:T(8,128)(2,1)S(1)}, u32[]{:S(2)}, u32[]{:S(2)}) collective-permute-start(bf16[128,896]{1,0:T(8,128)(2,1)S(1)} %get-tuple-element.51.block), channel_id=1, source_target_pairs={{0,2},{1,3},{2,6},{3,7},{4,0},{5,1},{6,4},{7,5},{8,10},{9,11},{10,... | collective-permute-start | bytes 688136 | tf_op jit(solution)/shard_map/ppermute | solution.py:32
  16.9 2.8 %collective-permute-start.1 = (bf16[128,896]{1,0:T(8,128)(2,1)S(1)}, bf16[128,896]{1,0:T(8,128)(2,1)S(1)}, u32[]{:S(2)}, u32[]{:S(2)}) collective-permute-start(bf16[128,896]{1,0:T(8,128)(2,1)S(1)} %collective-permute-done), channel_id=1, source_target_pairs={{0,4},{1,5},{6,2},{7,3},{8,12},{9,13},{14,10},{15,11},{16,20},{17,... | collective-permute-start | bytes 688136 | tf_op jit(solution)/shard_map/ppermute | solution.py:32
  19.8 4.0 %project.4 = (bf16[400,896]{1,0:T(8,128)(2,1)S(1)}, f32[3,128,896]{2,1,0:T(8,128)S(1)}, f32[128,1]{1,0:T(8,128)S(1)}) custom-call(s32[3]{0:T(128)S(1)} %pad_add_fusion.place, bf16[128,896]{1,0:T(8,128)(2,1)S(1)} %collective-permute-done.3.crossed, bf16[128,896]{1,0:T(8,128)(2,1)S(1)} %collective-permute-done.4.ringed, ...), custom_call_target="tpu_custom_call" | custom-call | flops 3449999872 | bytes 1000 | tf_op jit(solution)/shard_map/project/pallas_call | solution.py:147
  27.4 4.9 %project.5 = (bf16[400,896]{1,0:T(8,128)(2,1)}, f32[3,128,896]{2,1,0:T(8,128)S(1)}, f32[128,1]{1,0:T(8,128)S(1)}) custom-call(s32[3]{0:T(128)S(1)} %pad_add_fusion.place, bf16[128,896]{1,0:T(8,128)(2,1)S(1)} %broadcast_select_fusion.crossed, bf16[128,896]{1,0:T(8,128)(2,1)S(1)} %collective-permute-done.2.ringed, ...), custom_call_target="tpu_custom_call" | custom-call | flops 3449999872 | bytes 1000 | tf_op jit(solution)/shard_map/project/pallas_call | solution.py:147
  32.2 2.5 %collective-permute-start.9 = (bf16[400,896]{1,0:T(8,128)(2,1)}, bf16[400,896]{1,0:T(8,128)(2,1)}, u32[]{:S(2)}, u32[]{:S(2)}) collective-permute-start(bf16[400,896]{1,0:T(8,128)(2,1)} %get-tuple-element.45), channel_id=1, source_target_pairs={{0,4},{1,5},{2,6},{3,7},{4,0},{5,1},{6,2},{7,3},{8,12},{9,13},{10,... | collective-permute-start | bytes 2150408 | tf_op jit(solution)/shard_map/ppermute | solution.py:32
  34.7 8.1 %collective-permute-done.10.received = bf16[400,896]{1,0:T(8,128)(2,1)S(1)} collective-permute-done((bf16[400,896]{1,0:T(8,128)(2,1)S(1)}, bf16[400,896]{1,0:T(8,128)(2,1)S(1)}, u32[]{:S(2)}, u32[]{:S(2)}) %collective-permute-start.10) | collective-permute-done | bytes 716832 | tf_op jit(solution)/shard_map/ppermute | solution.py:32
  43.7 2.8 %collective-permute-start.12 = (bf16[128,896]{1,0:T(8,128)(2,1)S(1)}, bf16[128,896]{1,0:T(8,128)(2,1)S(1)}, u32[]{:S(2)}, u32[]{:S(2)}) collective-permute-start(bf16[128,896]{1,0:T(8,128)(2,1)S(1)} %get-tuple-element.49.refs_0_), channel_id=1, source_target_pairs={{0,10},{1,11},{2,14},{3,15},{4,8},{5,9},{6,12},{7,13},{8,18},{9,19... | collective-permute-start | bytes 688136 | tf_op jit(solution)/shard_map/ppermute | solution.py:32
  46.5 3.7 %collective-permute-start.11 = (bf16[128,896]{1,0:T(8,128)(2,1)S(1)}, bf16[128,896]{1,0:T(8,128)(2,1)S(1)}, u32[]{:S(2)}, u32[]{:S(2)}) collective-permute-start(bf16[128,896]{1,0:T(8,128)(2,1)S(1)} %get-tuple-element.49.refs_0_), channel_id=1, source_target_pairs={{0,8},{1,9},{2,12},{3,13},{4,10},{5,11},{6,14},{7,15},{8,16},{9,17... | collective-permute-start | bytes 688136 | tf_op jit(solution)/shard_map/ppermute | solution.py:32
  51.9 3.2 %collective-permute-done.11.crossed.first = bf16[128,896]{1,0:T(8,128)(2,1)S(1)} collective-permute-done((bf16[128,896]{1,0:T(8,128)(2,1)S(1)}, bf16[128,896]{1,0:T(8,128)(2,1)S(1)}, u32[]{:S(2)}, u32[]{:S(2)}) %collective-permute-start.11) | collective-permute-done | bytes 229408 | tf_op jit(solution)/shard_map/ppermute | solution.py:32
  56.6 4.8 %project.6 = (bf16[400,896]{1,0:T(8,128)(2,1)}, f32[3,128,896]{2,1,0:T(8,128)S(1)}, f32[128,1]{1,0:T(8,128)S(1)}) custom-call(s32[3]{0:T(128)S(1)} %pad_add_fusion.place, bf16[128,896]{1,0:T(8,128)(2,1)S(1)} %collective-permute-done.11.crossed.first, bf16[128,896]{1,0:T(8,128)(2,1)S(1)} %collective-permute-done.12.ringed, ...), custom_call_target="tpu_custom_call" | custom-call | flops 1150000 | bytes 1000 | tf_op jit(solution)/shard_map/project/pallas_call | solution.py:147
  61.4 2.0 %collective-permute-start.20 = (bf16[400,896]{1,0:T(8,128)(2,1)}, bf16[400,896]{1,0:T(8,128)(2,1)}, u32[]{:S(2)}, u32[]{:S(2)}) collective-permute-start(bf16[400,896]{1,0:T(8,128)(2,1)} %get-tuple-element.60), channel_id=1, source_target_pairs={{0,4},{1,5},{2,6},{3,7},{4,0},{5,1},{6,2},{7,3},{8,12},{9,13},{10,... | collective-permute-start | bytes 2150408 | tf_op jit(solution)/shard_map/ppermute | solution.py:32
  63.4 2.4 %attend.3 = (bf16[128,896]{1,0:T(8,128)(2,1)S(1)}, bf16[2,128,896]{2,1,0:T(8,128)(2,1)}) custom-call(f32[3,128,896]{2,1,0:T(8,128)S(1)} %get-tuple-element.44.kept, bf16[400,896]{1,0:T(8,128)(2,1)} %collective-permute-done.9.received, f32[128,1]{1,0:T(8,128)S(1)} %get-tuple-element.46.kept_mean, bf16[128,896]{1,0:T(8,128)(2,1)S(1)} %get-tuple-element.51.block, ...), custom_call_target="tpu_custom_call" | custom-call | flops 287500009472 | bytes 1000 | tf_op jit(solution)/shard_map/attend/pallas_call | solution.py:250
  65.8 5.4 %collective-permute-start.16 = (bf16[128,896]{1,0:T(8,128)(2,1)S(1)}, bf16[128,896]{1,0:T(8,128)(2,1)S(1)}, u32[]{:S(2)}, u32[]{:S(2)}) collective-permute-start(bf16[128,896]{1,0:T(8,128)(2,1)S(1)} %get-tuple-element.53.refs_1_), channel_id=1, source_target_pairs={{0,10},{1,11},{2,14},{3,15},{4,8},{5,9},{6,12},{7,13},{8,18},{9,19... | collective-permute-start | bytes 688136 | tf_op jit(solution)/shard_map/ppermute | solution.py:32
  71.2 4.2 %collective-permute-start.15 = (bf16[128,896]{1,0:T(8,128)(2,1)S(1)}, bf16[128,896]{1,0:T(8,128)(2,1)S(1)}, u32[]{:S(2)}, u32[]{:S(2)}) collective-permute-start(bf16[128,896]{1,0:T(8,128)(2,1)S(1)} %get-tuple-element.53.refs_1_), channel_id=1, source_target_pairs={{0,8},{1,9},{2,12},{3,13},{4,10},{5,11},{6,14},{7,15},{8,16},{9,17... | collective-permute-start | bytes 688136 | tf_op jit(solution)/shard_map/ppermute | solution.py:32
  75.3 1.8 %collective-permute-done.16.ringed = bf16[128,896]{1,0:T(8,128)(2,1)S(1)} collective-permute-done((bf16[128,896]{1,0:T(8,128)(2,1)S(1)}, bf16[128,896]{1,0:T(8,128)(2,1)S(1)}, u32[]{:S(2)}, u32[]{:S(2)}) %collective-permute-start.16) | collective-permute-done | bytes 229408 | tf_op jit(solution)/shard_map/ppermute | solution.py:32
  77.2 3.6 %collective-permute-done.15.crossed.second = bf16[128,896]{1,0:T(8,128)(2,1)S(1)} collective-permute-done((bf16[128,896]{1,0:T(8,128)(2,1)S(1)}, bf16[128,896]{1,0:T(8,128)(2,1)S(1)}, u32[]{:S(2)}, u32[]{:S(2)}) %collective-permute-start.15) | collective-permute-done | bytes 229408 | tf_op jit(solution)/shard_map/ppermute | solution.py:32
  82.6 4.8 %project.7 = (bf16[400,896]{1,0:T(8,128)(2,1)}, f32[3,128,896]{2,1,0:T(8,128)S(1)}, f32[128,1]{1,0:T(8,128)S(1)}) custom-call(s32[3]{0:T(128)S(1)} %pad_add_fusion.place, bf16[128,896]{1,0:T(8,128)(2,1)S(1)} %collective-permute-done.15.crossed.second, bf16[128,896]{1,0:T(8,128)(2,1)S(1)} %collective-permute-done.16.ringed, ...), custom_call_target="tpu_custom_call" | custom-call | flops 1150000 | bytes 1000 | tf_op jit(solution)/shard_map/project/pallas_call | solution.py:147
  87.4 2.5 %collective-permute-start.19 = (bf16[400,896]{1,0:T(8,128)(2,1)}, bf16[400,896]{1,0:T(8,128)(2,1)}, u32[]{:S(2)}, u32[]{:S(2)}) collective-permute-start(bf16[400,896]{1,0:T(8,128)(2,1)} %get-tuple-element.57), channel_id=1, source_target_pairs={{0,4},{1,5},{2,6},{3,7},{4,0},{5,1},{6,2},{7,3},{8,12},{9,13},{10,... | collective-permute-start | bytes 2150408 | tf_op jit(solution)/shard_map/ppermute | solution.py:32
  90.0 2.0 %hold.1 = (f32[128,896]{1,0:T(8,128)S(1)}, bf16[2,128,896]{2,1,0:T(8,128)(2,1)S(1)}, bf16[256,896]{1,0:T(8,128)(2,1)S(1)}) custom-call(f32[3,128,896]{2,1,0:T(8,128)S(1)} %get-tuple-element.59.kept, bf16[400,896]{1,0:T(8,128)(2,1)} %collective-permute-done.20.received, f32[128,1]{1,0:T(8,128)S(1)} %get-tuple-element.50.kept_mean, ...), custom_call_target="tpu_custom_call" | custom-call | flops 287500009472 | bytes 1000 | tf_op jit(solution)/shard_map/hold/pallas_call | solution.py:250
  93.3 13.3 %collective-permute-done.19.received = bf16[400,896]{1,0:T(8,128)(2,1)} collective-permute-done((bf16[400,896]{1,0:T(8,128)(2,1)}, bf16[400,896]{1,0:T(8,128)(2,1)}, u32[]{:S(2)}, u32[]{:S(2)}) %collective-permute-start.19) | collective-permute-done | bytes 716832 | tf_op jit(solution)/shard_map/ppermute | solution.py:32
  106.7 3.2 %final.1 = (bf16[256,896]{1,0:T(8,128)(2,1)}, bf16[2,128,896]{2,1,0:T(8,128)(2,1)}) custom-call(s32[3]{0:T(128)S(1)} %pad_add_fusion.place, s32[1]{0:T(128)S(6)} %copy.5.flag, f32[3,128,896]{2,1,0:T(8,128)S(1)} %get-tuple-element.56.kept, bf16[400,896]{1,0:T(8,128)(2,1)} %collective-permute-done.19.received, f32[128,1]{1,0:T(8,128)S(1)} %get-tuple-element.58.kept_mean, ...), custom_call_target="tpu_custom_call" | custom-call | flops 287500009472 | bytes 1000 | tf_op jit(solution)/shard_map/final/pallas_call | solution.py:250
  (50 shorter events, 15.3 us)
Async XLA Ops:
  1.1 12.8 %collective-permute-start.4 = (bf16[128,896]{1,0:T(8,128)(2,1)S(1)}, bf16[128,896]{1,0:T(8,128)(2,1)S(1)}, u32[]{:S(2)}, u32[]{:S(2)}) collective-permute-start(bf16[128,896]{1,0:T(8,128)(2,1)S(1)} %get-tuple-element.65.block), channel_id=1, source_target_pairs={{0,2},{1,3},{2,6},{3,7},{4,0},{5,1},{6,4},{7,5},{8,10},{9,11},{10,... | collective-permute-start | bytes 688136 | tf_op jit(solution)/shard_map/ppermute | solution.py:32
  4.1 9.8 %collective-permute-start.3 = (bf16[128,896]{1,0:T(8,128)(2,1)S(1)}, bf16[128,896]{1,0:T(8,128)(2,1)S(1)}, u32[]{:S(2)}, u32[]{:S(2)}) collective-permute-start(bf16[128,896]{1,0:T(8,128)(2,1)S(1)} %get-tuple-element.65.block), channel_id=1, source_target_pairs={{0,0},{1,1},{2,4},{3,5},{4,2},{5,3},{6,6},{7,7},{8,8},{9,9},{10,12... | collective-permute-start | bytes 688136 | tf_op jit(solution)/shard_map/ppermute | solution.py:32
  4.8 12.1 %collective-permute-start = (bf16[128,896]{1,0:T(8,128)(2,1)S(1)}, bf16[128,896]{1,0:T(8,128)(2,1)S(1)}, u32[]{:S(2)}, u32[]{:S(2)}) collective-permute-start(bf16[128,896]{1,0:T(8,128)(2,1)S(1)} %get-tuple-element.51.block), channel_id=1, source_target_pairs={{2,0},{3,1},{4,6},{5,7},{10,8},{11,9},{12,14},{13,15},{18,16},{19,... | collective-permute-start | bytes 688136 | tf_op jit(solution)/shard_map/ppermute | solution.py:32
  13.9 5.8 %collective-permute-start.5 = (bf16[128,896]{1,0:T(8,128)(2,1)S(1)}, bf16[128,896]{1,0:T(8,128)(2,1)S(1)}, u32[]{:S(2)}, u32[]{:S(2)}) collective-permute-start(bf16[128,896]{1,0:T(8,128)(2,1)S(1)} %collective-permute-done.3.crossed), channel_id=1, source_target_pairs={{0,1},{1,0},{2,3},{3,2},{4,5},{5,4},{6,7},{7,6},{8,9},{9,8},{10,11... | collective-permute-start | bytes 688136 | tf_op jit(solution)/shard_map/ppermute | solution.py:32
  13.9 5.8 %collective-permute-start.6 = (bf16[128,896]{1,0:T(8,128)(2,1)S(1)}, bf16[128,896]{1,0:T(8,128)(2,1)S(1)}, u32[]{:S(2)}, u32[]{:S(2)}) collective-permute-start(bf16[128,896]{1,0:T(8,128)(2,1)S(1)} %collective-permute-done.4.ringed), channel_id=1, source_target_pairs={{0,1},{1,0},{2,3},{3,2},{4,5},{5,4},{6,7},{7,6},{8,9},{9,8},{10,11... | collective-permute-start | bytes 688136 | tf_op jit(solution)/shard_map/ppermute | solution.py:32
  14.4 11.0 %collective-permute-start.2 = (bf16[128,896]{1,0:T(8,128)(2,1)S(1)}, bf16[128,896]{1,0:T(8,128)(2,1)S(1)}, u32[]{:S(2)}, u32[]{:S(2)}) collective-permute-start(bf16[128,896]{1,0:T(8,128)(2,1)S(1)} %get-tuple-element.51.block), channel_id=1, source_target_pairs={{0,2},{1,3},{2,6},{3,7},{4,0},{5,1},{6,4},{7,5},{8,10},{9,11},{10,... | collective-permute-start | bytes 688136 | tf_op jit(solution)/shard_map/ppermute | solution.py:32
  16.9 8.6 %collective-permute-start.1 = (bf16[128,896]{1,0:T(8,128)(2,1)S(1)}, bf16[128,896]{1,0:T(8,128)(2,1)S(1)}, u32[]{:S(2)}, u32[]{:S(2)}) collective-permute-start(bf16[128,896]{1,0:T(8,128)(2,1)S(1)} %collective-permute-done), channel_id=1, source_target_pairs={{0,4},{1,5},{6,2},{7,3},{8,12},{9,13},{14,10},{15,11},{16,20},{17,... | collective-permute-start | bytes 688136 | tf_op jit(solution)/shard_map/ppermute | solution.py:32
  23.8 19.0 %collective-permute-start.10 = (bf16[400,896]{1,0:T(8,128)(2,1)S(1)}, bf16[400,896]{1,0:T(8,128)(2,1)S(1)}, u32[]{:S(2)}, u32[]{:S(2)}) collective-permute-start(bf16[400,896]{1,0:T(8,128)(2,1)S(1)} %get-tuple-element.48), channel_id=1, source_target_pairs={{0,4},{1,5},{2,6},{3,7},{4,0},{5,1},{6,2},{7,3},{8,12},{9,13},{10,... | collective-permute-start | bytes 2150408 | tf_op jit(solution)/shard_map/ppermute | solution.py:32
  25.5 1.6 %collective-permute-start.7 = (bf16[128,896]{1,0:T(8,128)(2,1)S(1)}, bf16[128,896]{1,0:T(8,128)(2,1)S(1)}, u32[]{:S(2)}, u32[]{:S(2)}) collective-permute-start(bf16[128,896]{1,0:T(8,128)(2,1)S(1)} %broadcast_select_fusion.crossed), channel_id=1, source_target_pairs={{0,1},{1,0},{2,3},{3,2},{4,5},{5,4},{6,7},{7,6},{8,9},{9,8},{10,11... | collective-permute-start | bytes 688136 | tf_op jit(solution)/shard_map/ppermute | solution.py:32
  25.6 1.8 %collective-permute-start.8 = (bf16[128,896]{1,0:T(8,128)(2,1)S(1)}, bf16[128,896]{1,0:T(8,128)(2,1)S(1)}, u32[]{:S(2)}, u32[]{:S(2)}) collective-permute-start(bf16[128,896]{1,0:T(8,128)(2,1)S(1)} %collective-permute-done.2.ringed), channel_id=1, source_target_pairs={{0,1},{1,0},{2,3},{3,2},{4,5},{5,4},{6,7},{7,6},{8,9},{9,8},{10,11... | collective-permute-start | bytes 688136 | tf_op jit(solution)/shard_map/ppermute | solution.py:32
  32.2 31.2 %collective-permute-start.9 = (bf16[400,896]{1,0:T(8,128)(2,1)}, bf16[400,896]{1,0:T(8,128)(2,1)}, u32[]{:S(2)}, u32[]{:S(2)}) collective-permute-start(bf16[400,896]{1,0:T(8,128)(2,1)} %get-tuple-element.45), channel_id=1, source_target_pairs={{0,4},{1,5},{2,6},{3,7},{4,0},{5,1},{6,2},{7,3},{8,12},{9,13},{10,... | collective-permute-start | bytes 2150408 | tf_op jit(solution)/shard_map/ppermute | solution.py:32
  43.6 17.8 %copy-start.6 = (bf16[128,896]{1,0:T(8,128)(2,1)}, bf16[128,896]{1,0:T(8,128)(2,1)S(1)}, u32[]{:S(2)}) copy-start(bf16[128,896]{1,0:T(8,128)(2,1)S(1)} %get-tuple-element.49.refs_0_) | copy-start | bytes 688132
  43.7 8.2 %collective-permute-start.12 = (bf16[128,896]{1,0:T(8,128)(2,1)S(1)}, bf16[128,896]{1,0:T(8,128)(2,1)S(1)}, u32[]{:S(2)}, u32[]{:S(2)}) collective-permute-start(bf16[128,896]{1,0:T(8,128)(2,1)S(1)} %get-tuple-element.49.refs_0_), channel_id=1, source_target_pairs={{0,10},{1,11},{2,14},{3,15},{4,8},{5,9},{6,12},{7,13},{8,18},{9,19... | collective-permute-start | bytes 688136 | tf_op jit(solution)/shard_map/ppermute | solution.py:32
  46.5 8.6 %collective-permute-start.11 = (bf16[128,896]{1,0:T(8,128)(2,1)S(1)}, bf16[128,896]{1,0:T(8,128)(2,1)S(1)}, u32[]{:S(2)}, u32[]{:S(2)}) collective-permute-start(bf16[128,896]{1,0:T(8,128)(2,1)S(1)} %get-tuple-element.49.refs_0_), channel_id=1, source_target_pairs={{0,8},{1,9},{2,12},{3,13},{4,10},{5,11},{6,14},{7,15},{8,16},{9,17... | collective-permute-start | bytes 688136 | tf_op jit(solution)/shard_map/ppermute | solution.py:32
  51.9 3.2 %collective-permute-start.14 = (bf16[128,896]{1,0:T(8,128)(2,1)S(1)}, bf16[128,896]{1,0:T(8,128)(2,1)S(1)}, u32[]{:S(2)}, u32[]{:S(2)}) collective-permute-start(bf16[128,896]{1,0:T(8,128)(2,1)S(1)} %collective-permute-done.12.ringed), channel_id=1, source_target_pairs={{0,1},{1,0},{2,3},{3,2},{4,5},{5,4},{6,7},{7,6},{8,9},{9,8},{10,11... | collective-permute-start | bytes 688136 | tf_op jit(solution)/shard_map/ppermute | solution.py:32
  55.1 1.5 %collective-permute-start.13 = (bf16[128,896]{1,0:T(8,128)(2,1)S(1)}, bf16[128,896]{1,0:T(8,128)(2,1)S(1)}, u32[]{:S(2)}, u32[]{:S(2)}) collective-permute-start(bf16[128,896]{1,0:T(8,128)(2,1)S(1)} %collective-permute-done.11.crossed.first), channel_id=1, source_target_pairs={{0,1},{1,0},{2,3},{3,2},{4,5},{5,4},{6,7},{7,6},{8,9},{9,8},{10,11... | collective-permute-start | bytes 688136 | tf_op jit(solution)/shard_map/ppermute | solution.py:32
  61.4 28.6 %collective-permute-start.20 = (bf16[400,896]{1,0:T(8,128)(2,1)}, bf16[400,896]{1,0:T(8,128)(2,1)}, u32[]{:S(2)}, u32[]{:S(2)}) collective-permute-start(bf16[400,896]{1,0:T(8,128)(2,1)} %get-tuple-element.60), channel_id=1, source_target_pairs={{0,4},{1,5},{2,6},{3,7},{4,0},{5,1},{6,2},{7,3},{8,12},{9,13},{10,... | collective-permute-start | bytes 2150408 | tf_op jit(solution)/shard_map/ppermute | solution.py:32
  65.8 24.2 %copy-start.7 = (bf16[128,896]{1,0:T(8,128)(2,1)S(1)}, bf16[128,896]{1,0:T(8,128)(2,1)}, u32[]{:S(2)}) copy-start(bf16[128,896]{1,0:T(8,128)(2,1)} %copy-done.6) | copy-start | bytes 688132
  65.8 11.4 %collective-permute-start.16 = (bf16[128,896]{1,0:T(8,128)(2,1)S(1)}, bf16[128,896]{1,0:T(8,128)(2,1)S(1)}, u32[]{:S(2)}, u32[]{:S(2)}) collective-permute-start(bf16[128,896]{1,0:T(8,128)(2,1)S(1)} %get-tuple-element.53.refs_1_), channel_id=1, source_target_pairs={{0,10},{1,11},{2,14},{3,15},{4,8},{5,9},{6,12},{7,13},{8,18},{9,19... | collective-permute-start | bytes 688136 | tf_op jit(solution)/shard_map/ppermute | solution.py:32
  71.2 9.6 %collective-permute-start.15 = (bf16[128,896]{1,0:T(8,128)(2,1)S(1)}, bf16[128,896]{1,0:T(8,128)(2,1)S(1)}, u32[]{:S(2)}, u32[]{:S(2)}) collective-permute-start(bf16[128,896]{1,0:T(8,128)(2,1)S(1)} %get-tuple-element.53.refs_1_), channel_id=1, source_target_pairs={{0,8},{1,9},{2,12},{3,13},{4,10},{5,11},{6,14},{7,15},{8,16},{9,17... | collective-permute-start | bytes 688136 | tf_op jit(solution)/shard_map/ppermute | solution.py:32
  80.8 1.5 %collective-permute-start.17 = (bf16[128,896]{1,0:T(8,128)(2,1)S(1)}, bf16[128,896]{1,0:T(8,128)(2,1)S(1)}, u32[]{:S(2)}, u32[]{:S(2)}) collective-permute-start(bf16[128,896]{1,0:T(8,128)(2,1)S(1)} %collective-permute-done.15.crossed.second), channel_id=1, source_target_pairs={{0,1},{1,0},{2,3},{3,2},{4,5},{5,4},{6,7},{7,6},{8,9},{9,8},{10,11... | collective-permute-start | bytes 688136 | tf_op jit(solution)/shard_map/ppermute | solution.py:32
  80.8 1.8 %collective-permute-start.18 = (bf16[128,896]{1,0:T(8,128)(2,1)S(1)}, bf16[128,896]{1,0:T(8,128)(2,1)S(1)}, u32[]{:S(2)}, u32[]{:S(2)}) collective-permute-start(bf16[128,896]{1,0:T(8,128)(2,1)S(1)} %collective-permute-done.16.ringed), channel_id=1, source_target_pairs={{0,1},{1,0},{2,3},{3,2},{4,5},{5,4},{6,7},{7,6},{8,9},{9,8},{10,11... | collective-permute-start | bytes 688136 | tf_op jit(solution)/shard_map/ppermute | solution.py:32
  87.4 19.2 %collective-permute-start.19 = (bf16[400,896]{1,0:T(8,128)(2,1)}, bf16[400,896]{1,0:T(8,128)(2,1)}, u32[]{:S(2)}, u32[]{:S(2)}) collective-permute-start(bf16[400,896]{1,0:T(8,128)(2,1)} %get-tuple-element.57), channel_id=1, source_target_pairs={{0,4},{1,5},{2,6},{3,7},{4,0},{5,1},{6,2},{7,3},{8,12},{9,13},{10,... | collective-permute-start | bytes 2150408 | tf_op jit(solution)/shard_map/ppermute | solution.py:32
  92.0 14.7 %collective-permute-start.21 = (bf16[256,896]{1,0:T(8,128)(2,1)S(1)}, bf16[256,896]{1,0:T(8,128)(2,1)S(1)}, u32[]{:S(2)}, u32[]{:S(2)}) collective-permute-start(bf16[256,896]{1,0:T(8,128)(2,1)S(1)} %get-tuple-element.63.own), channel_id=1, source_target_pairs={{2,10},{3,11},{4,12},{5,13},{10,18},{11,19},{12,20},{13,21},{18,26... | collective-permute-start | bytes 1376264 | tf_op jit(solution)/shard_map/ppermute | solution.py:32
  (7 other events, 74.0 us)

commit v6 on v5

--- a/solution.py
+++ b/solution.py
@@ -44,12 +44,12 @@
     return (s, d, y, c) if d != y else None
 
 
-def across_y(s, d, y, c):
-    return (s, d, 1 - y, c) if d != y else None
-
-
-def across_x(s, d, y, c):
-    return (s, 1 - d, y, c) if d == y else None
+def forward(s, d, y, c):
+    return (s, d, 1 - y, c) if d == y else None
+
+
+def swap(s, d, y, c):
+    return (s, d, 1 - y, c)
 
 
 def sibling(s, d, y, c):
@@ -84,75 +84,85 @@
     return pl.BlockSpec(memory_space=pltpu.SMEM)
 
 
-def stage_kernel(place, weight, staged, semaphore):
+def stage_kernel(place, weight, arrived, staged, semaphore):
     copy = pltpu.make_async_copy(weight, staged, semaphore)
     copy.start()
     copy.wait()
 
 
-def stage(place, weight):
+def stage(place, weight, arrived):
     return pl.pallas_call(
         stage_kernel,
-        in_specs=[smem_spec(), any_spec()],
+        in_specs=[smem_spec(), any_spec(), any_spec()],
         out_specs=vmem_spec(),
         out_shape=pltpu.VMEM(weight.shape, weight.dtype),
         scratch_shapes=[pltpu.SemaphoreType.DMA(())],
         compiler_params=pltpu.CompilerParams(vmem_limit_bytes=VMEM_BYTES),
-        cost_estimate=cost(4),
+        cost_estimate=cost(250),
         name="stage",
-    )(place, weight)
-
-
-def project_kernel(place, crossed, ringed, sib_crossed, sib_ringed, gain, weight, *refs):
-    sent, kept, kept_mean, normed = refs
-    rows = normed.shape[0] // 2
-    width = crossed.shape[1]
+    )(place, pltpu.with_memory_space_constraint(weight, pltpu.HBM), arrived)
+
+
+def project_kernel(
+    place, crossed, ringed, sib_crossed, sib_ringed, gain, weight, sent, kept, kept_mean, *scratch
+):
+    normed, out, semaphores = scratch
+    rows, width = crossed.shape
     half = 2 * width
-    core, dp, diagonal = place[0], place[1], place[2]
+    first_core, diagonal = place[0] == 0, place[2] == 1
+    gains = gain[:, pl.ds(pl.multiple_of(place[1] * half, HD), half)].astype(F32)
     means = []
-    for mine, theirs, offset in (
-        (crossed, sib_crossed, diagonal),
-        (ringed, sib_ringed, 1 - diagonal),
-    ):
-        at = pl.ds(pl.multiple_of(offset * rows, rows), rows)
-        pieces = [ref[...].astype(F32) for ref in (mine, theirs)]
+    for i, (mine, theirs) in enumerate(((crossed, sib_crossed), (ringed, sib_ringed))):
+        mine, theirs = mine[...].astype(F32), theirs[...].astype(F32)
+        pieces = jnp.where(first_core, mine, theirs), jnp.where(first_core, theirs, mine)
         squares = sum(jnp.sum(piece * piece, axis=-1, keepdims=True) for piece in pieces)
         mean = squares * (1.0 / half)
         means.append(mean)
         inverse = lax.rsqrt(mean + EPS)
-        for piece, order in zip(pieces, (core, 1 - core)):
-            gains = gain[:, pl.ds(pl.multiple_of(dp * half + order * width, HD), width)]
-            normed[at, pl.ds(pl.multiple_of(order * width, HD), width)] = (
-                piece * inverse * gains.astype(F32)
-            ).astype(BF16)
-    on_diagonal = diagonal == 1
-    sent_mean = jnp.where(on_diagonal, means[1], means[0])
-    kept_mean[...] = jnp.where(on_diagonal, means[0], means[1])
+        for j, piece in enumerate(pieces):
+            at = slice(j * width, (j + 1) * width)
+            normed[i * rows : (i + 1) * rows, at] = (piece * inverse * gains[:, at]).astype(BF16)
+    sent_mean = jnp.where(diagonal, means[1], means[0])
+    kept_mean[...] = jnp.where(diagonal, means[0], means[1])
     row = jnp.transpose(jnp.broadcast_to(sent_mean, (rows, HD)))[:STAT_ROWS]
     high = row.astype(BF16).astype(F32)
     mid = (row - high).astype(BF16).astype(F32)
     low = row - high - mid
     which = lax.broadcasted_iota(jnp.int32, row.shape, 0)
-    stat = jnp.where(which == 0, high, jnp.where(which == 1, mid, low))
+    stat = jnp.where(which == 0, high, jnp.where(which == 1, mid, low)).astype(BF16)
     for begin in range(0, width, rows):
-        sent[3 * rows :, begin : begin + rows] = stat.astype(BF16)
+        out[:STAT_ROWS, begin : begin + rows] = stat
+    copies = []
     for k in range(3):
         product = jnp.dot(normed[...], weight[0, k], preferred_element_type=F32)
-        sent[k * rows : (k + 1) * rows] = product[:rows].astype(BF16)
-        kept[k] = product[rows:]
+        crossed_sums, ringed_sums = product[:rows], product[rows:]
+        begin = STAT_ROWS + k * rows
+        out[begin : begin + rows] = jnp.where(diagonal, ringed_sums, crossed_sums).astype(BF16)
+        kept[k] = jnp.where(diagonal, crossed_sums, ringed_sums)
+        at = pl.ds(begin, rows) if k else pl.ds(0, begin + rows)
+        copies.append(pltpu.make_async_copy(out.at[at], sent.at[at], semaphores.at[k]))
+        copies[-1].start()
+    for copy in copies:
+        copy.wait()
 
 
 def project(rows, place, four, gain, weight, estimate):
     width = four[0].shape[1]
+    sent_shape = (3 * rows + STAT_ROWS, width)
     return pl.pallas_call(
         project_kernel,
         in_specs=[smem_spec()] + [vmem_spec()] * 6,
+        out_specs=[any_spec(), vmem_spec(), vmem_spec()],
         out_shape=[
-            pltpu.VMEM((3 * rows + STAT_ROWS, width), BF16),
+            jax.ShapeDtypeStruct(sent_shape, BF16),
             pltpu.VMEM((3, rows, width), F32),
             pltpu.VMEM((rows, 1), F32),
         ],
-        scratch_shapes=[pltpu.VMEM((2 * rows, 2 * width), BF16)],
+        scratch_shapes=[
+            pltpu.VMEM((2 * rows, 2 * width), BF16),
+            pltpu.VMEM(sent_shape, BF16),
+            pltpu.SemaphoreType.DMA((3,)),
+        ],
         compiler_params=pltpu.CompilerParams(vmem_limit_bytes=VMEM_BYTES),
         cost_estimate=cost(estimate),
         name="project",
@@ -161,7 +171,7 @@
 
 def mix(kept, received, kept_mean, earlier, pairs, put):
     rows, width = kept.shape[1:]
-    stat = received[3 * rows :, :rows].astype(F32)
+    stat = received[:STAT_ROWS, :rows].astype(F32)
     row = stat[0:1] + stat[1:2] + stat[2:3]
     mean_peer = jnp.transpose(jnp.broadcast_to(row, (HD, rows)))[:, :1]
     mean_kept = kept_mean[...]
@@ -177,7 +187,8 @@
         queries, keys, values = (
             (
                 kept[k, :, at] * scale_kept
-                + received[k * rows : (k + 1) * rows, at].astype(F32) * scale_peer
+                + received[STAT_ROWS + k * rows : STAT_ROWS + (k + 1) * rows, at].astype(F32)
+                * scale_peer
             ).astype(BF16)
             for k in range(3)
         )
@@ -265,8 +276,7 @@
         t = lax.axis_index("tensor")
         y, c = t // 2, t % 2
         place = jnp.stack([c, d, (d == y).astype(c.dtype)]).astype(jnp.int32)
-        place, diagonal, weight = lax.optimization_barrier((place, d == y, qkv_weight))
-        weight = stage(place, weight)
+        place, diagonal = lax.optimization_barrier((place, d == y))
 
         def spread(crossed, ringed):
             return (
@@ -283,15 +293,19 @@
         block = inputs[0, 0]
         rows = block.shape[0] // PARTS
         parts = [block[i * rows : (i + 1) * rows] for i in range(PARTS)]
-        pair = permute(parts[0], sections, cross), permute(parts[0], sections, ring)
-        relayed = permute(parts[1], sections, across_y)
-        ringed = permute(parts[1], sections, ring)
-        *pair, weight = lax.optimization_barrier((*pair, weight))
+        ringed = [permute(part, sections, ring) for part in parts]
+        weight = stage(place, qkv_weight, ringed[0])
+        forwarded = permute(ringed[0], sections, forward)
+        crossed = jnp.where(diagonal, parts[0], forwarded)
+        crossed, weight = lax.optimization_barrier((crossed, weight))
         weight = pltpu.with_memory_space_constraint(weight, pltpu.VMEM)
-        sums = [partial(spread(*pair), 3)]
-        crossed = jnp.where(diagonal, parts[1], permute(relayed, sections, across_x))
-        crossed, ringed, _ = lax.optimization_barrier((crossed, ringed, sums[0][2]))
-        sums.append(partial(spread(crossed, ringed), 3))
+        sums = [partial(spread(crossed, ringed[0]), 3)]
+        late, _ = lax.optimization_barrier((ringed[1], weight))
+        forwarded = permute(late, sections, forward)
+        forwarded, late, part, _ = lax.optimization_barrier(
+            (forwarded, late, parts[1], sums[0][2])
+        )
+        sums.append(partial(spread(jnp.where(diagonal, part, forwarded), late), 1))
         width = block.shape[1]
         rows_of = pltpu.VMEM((rows, width), BF16)
         pairs_of = pltpu.VMEM((2, rows, width), BF16)
@@ -304,10 +318,12 @@
             )
             held.append(pairs)
             owns.append(own)
-            pair = permute(own, sections, onward(cross)), permute(own, sections, onward(ring))
-            moved.append(pair[0])
+            moved.append(permute(own, sections, onward(cross)))
             if seconds:
-                pair = lax.optimization_barrier((*pair, seconds[0][2]))[:2]
+                crossed = lax.optimization_barrier((moved[-1], seconds[0][2]))[0]
+                pair = crossed, permute(crossed, sections, swap)
+            else:
+                pair = moved[-1], permute(own, sections, onward(ring))
             seconds.append(partial(spread(*pair), 0.001))
         mixture, pairs, own = call_attend(
             hold_kernel,

time: 111 us -> 120 us (1.081)
  waiting for transfers between devices: 40 us -> 48.8 us
  Pallas kernels: 28.4 us -> 32.6 us
  local copies, waits for them, and re-layouts: 4.88 us -> 1.82 us
    ppermute x22 -> x21, waiting for transfers between devices: 40 us -> 48.8 us  [permute(): return lax.ppermute(array, AXES, pairs)]
    unnamed x18 -> x26, local copies, waits for them, and re-layouts: 3.8 us -> 0.05 us
    pallas_call x1, Pallas kernels: 1.45 us -> 4.31 us  [stage(): pl.pallas_call(stage_kernel, in_specs=[smem_spec(), any_spec(), any_spec(...]
    pallas_call x4, Pallas kernels: 18.6 us -> 19.9 us  [project(): pl.pallas_call(project_kernel, in_specs=[smem_spec()] + [vmem_spec()] * 6...]
    ppermute x22 -> x21, starting transfers between devices: 35.6 us -> 34.8 us  [permute(): return lax.ppermute(array, AXES, pairs)]
  transfers between devices with their start and end apart: 22 -> 21, of which waited for: 13 -> 12; matrix products, arithmetic and copies ran while one was open for 0% -> 1% of each run, Pallas kernels for 23% -> 25%
where the time goes in v6:
time: 120 us
  waiting for transfers between devices  48.8 us (41%)
  starting transfers between devices  34.8 us (29%)
  Pallas kernels  32.6 us (27%)
  local copies, waits for them, and re-layouts  1.82 us (2%)
    ppermute x21, waiting for transfers between devices, permute(): return lax.ppermute(array, AXES, pairs)  48.8 us
    ppermute x21, starting transfers between devices, permute(): return lax.ppermute(array, AXES, pairs)  34.8 us
    pallas_call x4, Pallas kernels, project(): pl.pallas_call(project_kernel, in_specs=[smem_spec()] + [vmem_spec()] * 6...  19.9 us
    pallas_call x4, Pallas kernels, call_attend(): pl.pallas_call(kernel, in_specs=[smem_spec() for _ in scalars] + [vmem_sp...  8.46 us
    pallas_call x1, Pallas kernels, stage(): pl.pallas_call(stage_kernel, in_specs=[smem_spec(), any_spec(), any_spec(...  4.31 us
  transfers between devices with their start and end apart: 21, of which 12 were waited for; matrix products, arithmetic and copies ran while one was open for 1% of the time, Pallas kernels for 25%

profile of v6, /device:TPU:0, one launch (start us, length us, event | category | flops | bytes accessed | tf_op | source)
XLA Modules:
  0.0 120.0 jit_solution(5945235207054632369)
XLA Ops:
  0.0 1.8 %slice_bitcast_fusion = (bf16[128,896]{1,0:T(8,128)(2,1)S(1)}, bf16[128,896]{1,0:T(8,128)(2,1)}) fusion(bf16[1,1,256,896]{3,2,1,0:T(8,128)(2,1)} %param.4), kind=kLoop, calls=%fused_computation | loop fusion | bytes 917504 | tf_op jit(solution)/shard_map/slice | solution.py:295
  1.8 3.0 %collective-permute-start.1 = (bf16[128,896]{1,0:T(8,128)(2,1)S(1)}, bf16[128,896]{1,0:T(8,128)(2,1)}, u32[]{:S(2)}, u32[]{:S(2)}) collective-permute-start(bf16[128,896]{1,0:T(8,128)(2,1)S(1)} %get-tuple-element.63.block), channel_id=1, source_target_pairs={{0,2},{1,3},{2,6},{3,7},{4,0},{5,1},{6,4},{7,5},{8,10},{9,11},{10,... | collective-permute-start | bytes 688136 | tf_op jit(solution)/shard_map/ppermute | solution.py:32
  4.7 1.5 %collective-permute-start = (bf16[128,896]{1,0:T(8,128)(2,1)}, bf16[128,896]{1,0:T(8,128)(2,1)}, u32[]{:S(2)}, u32[]{:S(2)}) collective-permute-start(bf16[128,896]{1,0:T(8,128)(2,1)} %get-tuple-element.50.block), channel_id=1, source_target_pairs={{0,2},{1,3},{2,6},{3,7},{4,0},{5,1},{6,4},{7,5},{8,10},{9,11},{10,... | collective-permute-start | bytes 688136 | tf_op jit(solution)/shard_map/ppermute | solution.py:32
  6.3 4.9 %collective-permute-done.1.arrived.ringed = bf16[128,896]{1,0:T(8,128)(2,1)} collective-permute-done((bf16[128,896]{1,0:T(8,128)(2,1)S(1)}, bf16[128,896]{1,0:T(8,128)(2,1)}, u32[]{:S(2)}, u32[]{:S(2)}) %collective-permute-start.1) | collective-permute-done | bytes 229408 | tf_op jit(solution)/shard_map/ppermute | solution.py:32
  11.2 4.7 %collective-permute-start.2 = (bf16[128,896]{1,0:T(8,128)(2,1)}, bf16[128,896]{1,0:T(8,128)(2,1)}, u32[]{:S(2)}, u32[]{:S(2)}) collective-permute-start(bf16[128,896]{1,0:T(8,128)(2,1)} %collective-permute-done.1.arrived.ringed), channel_id=1, source_target_pairs={{0,2},{1,3},{6,4},{7,5},{8,10},{9,11},{14,12},{15,13},{16,18},{17,... | collective-permute-start | bytes 688136 | tf_op jit(solution)/shard_map/ppermute | solution.py:32
  15.9 4.3 %stage.1.weight = bf16[1,3,1792,896]{3,2,1,0:T(8,128)(2,1)S(1)} custom-call(s32[3]{0:T(128)S(1)} %pad_add_fusion.place, bf16[1,3,1792,896]{3,2,1,0:T(8,128)(2,1)} %weight.1, bf16[128,896]{1,0:T(8,128)(2,1)} %collective-permute-done.1.arrived.ringed), custom_call_target="tpu_custom_call" | custom-call | flops 287500009472 | bytes 1000 | tf_op jit(solution)/shard_map/stage/pallas_call | solution.py:94
  21.2 5.3 %collective-permute-start.3 = (bf16[128,896]{1,0:T(8,128)(2,1)}, bf16[128,896]{1,0:T(8,128)(2,1)S(1)}, u32[]{:S(2)}, u32[]{:S(2)}) collective-permute-start(bf16[128,896]{1,0:T(8,128)(2,1)} %collective-permute-done.ringed), channel_id=1, source_target_pairs={{0,2},{1,3},{6,4},{7,5},{8,10},{9,11},{14,12},{15,13},{16,18},{17,... | collective-permute-start | bytes 688136 | tf_op jit(solution)/shard_map/ppermute | solution.py:32
  26.6 5.7 %project.4 = (bf16[400,896]{1,0:T(8,128)(2,1)S(1)}, f32[3,128,896]{2,1,0:T(8,128)S(1)}, f32[128,1]{1,0:T(8,128)S(1)}) custom-call(s32[3]{0:T(128)S(1)} %pad_add_fusion.place, bf16[128,896]{1,0:T(8,128)(2,1)S(1)} %broadcast_select_fusion.1.crossed, bf16[128,896]{1,0:T(8,128)(2,1)} %collective-permute-done.1.arrived.ringed, ...), custom_call_target="tpu_custom_call" | custom-call | flops 3449999872 | bytes 1000 | tf_op jit(solution)/shard_map/project/pallas_call | solution.py:152
  35.4 5.0 %project.5 = (bf16[400,896]{1,0:T(8,128)(2,1)}, f32[3,128,896]{2,1,0:T(8,128)S(1)}, f32[128,1]{1,0:T(8,128)S(1)}) custom-call(s32[3]{0:T(128)S(1)} %pad_add_fusion.place, bf16[128,896]{1,0:T(8,128)(2,1)S(1)} %broadcast_select_fusion.crossed, bf16[128,896]{1,0:T(8,128)(2,1)} %collective-permute-done.ringed, ...), custom_call_target="tpu_custom_call" | custom-call | flops 1150000000 | bytes 1000 | tf_op jit(solution)/shard_map/project/pallas_call | solution.py:152
  41.9 9.3 %collective-permute-done.9.received = bf16[400,896]{1,0:T(8,128)(2,1)S(1)} collective-permute-done((bf16[400,896]{1,0:T(8,128)(2,1)S(1)}, bf16[400,896]{1,0:T(8,128)(2,1)S(1)}, u32[]{:S(2)}, u32[]{:S(2)}) %collective-permute-start.9) | collective-permute-done | bytes 716832 | tf_op jit(solution)/shard_map/ppermute | solution.py:32
  52.1 2.9 %collective-permute-start.11 = (bf16[128,896]{1,0:T(8,128)(2,1)S(1)}, bf16[128,896]{1,0:T(8,128)(2,1)S(1)}, u32[]{:S(2)}, u32[]{:S(2)}) collective-permute-start(bf16[128,896]{1,0:T(8,128)(2,1)S(1)} %get-tuple-element.48.refs_0_), channel_id=1, source_target_pairs={{0,10},{1,11},{2,14},{3,15},{4,8},{5,9},{6,12},{7,13},{8,18},{9,19... | collective-permute-start | bytes 688136 | tf_op jit(solution)/shard_map/ppermute | solution.py:32
  55.0 3.7 %collective-permute-start.10 = (bf16[128,896]{1,0:T(8,128)(2,1)S(1)}, bf16[128,896]{1,0:T(8,128)(2,1)S(1)}, u32[]{:S(2)}, u32[]{:S(2)}) collective-permute-start(bf16[128,896]{1,0:T(8,128)(2,1)S(1)} %get-tuple-element.48.refs_0_), channel_id=1, source_target_pairs={{0,8},{1,9},{2,12},{3,13},{4,10},{5,11},{6,14},{7,15},{8,16},{9,17... | collective-permute-start | bytes 688136 | tf_op jit(solution)/shard_map/ppermute | solution.py:32
  58.6 2.2 %collective-permute-done.11.ringed = bf16[128,896]{1,0:T(8,128)(2,1)S(1)} collective-permute-done((bf16[128,896]{1,0:T(8,128)(2,1)S(1)}, bf16[128,896]{1,0:T(8,128)(2,1)S(1)}, u32[]{:S(2)}, u32[]{:S(2)}) %collective-permute-start.11) | collective-permute-done | bytes 229408 | tf_op jit(solution)/shard_map/ppermute | solution.py:32
  60.9 3.3 %collective-permute-done.10.crossed.first = bf16[128,896]{1,0:T(8,128)(2,1)S(1)} collective-permute-done((bf16[128,896]{1,0:T(8,128)(2,1)S(1)}, bf16[128,896]{1,0:T(8,128)(2,1)S(1)}, u32[]{:S(2)}, u32[]{:S(2)}) %collective-permute-start.10) | collective-permute-done | bytes 229408 | tf_op jit(solution)/shard_map/ppermute | solution.py:32
  65.6 4.6 %project.6 = (bf16[400,896]{1,0:T(8,128)(2,1)}, f32[3,128,896]{2,1,0:T(8,128)S(1)}, f32[128,1]{1,0:T(8,128)S(1)}) custom-call(s32[3]{0:T(128)S(1)} %copy-done.8, bf16[128,896]{1,0:T(8,128)(2,1)S(1)} %collective-permute-done.10.crossed.first, bf16[128,896]{1,0:T(8,128)(2,1)S(1)} %collective-permute-done.11.ringed, ...), custom_call_target="tpu_custom_call" | custom-call | flops 1150000 | bytes 1000 | tf_op jit(solution)/shard_map/project/pallas_call | solution.py:152
  70.3 1.6 %collective-permute-start.19 = (bf16[400,896]{1,0:T(8,128)(2,1)}, bf16[400,896]{1,0:T(8,128)(2,1)}, u32[]{:S(2)}, u32[]{:S(2)}) collective-permute-start(bf16[400,896]{1,0:T(8,128)(2,1)} %get-tuple-element.58), channel_id=1, source_target_pairs={{0,4},{1,5},{2,6},{3,7},{4,0},{5,1},{6,2},{7,3},{8,12},{9,13},{10,... | collective-permute-start | bytes 2150408 | tf_op jit(solution)/shard_map/ppermute | solution.py:32
  71.8 2.4 %attend.3 = (bf16[128,896]{1,0:T(8,128)(2,1)S(1)}, bf16[2,128,896]{2,1,0:T(8,128)(2,1)}) custom-call(f32[3,128,896]{2,1,0:T(8,128)S(1)} %get-tuple-element.43.kept, bf16[400,896]{1,0:T(8,128)(2,1)} %collective-permute-done.8.received, f32[128,1]{1,0:T(8,128)S(1)} %get-tuple-element.45.kept_mean, bf16[128,896]{1,0:T(8,128)(2,1)} %get-tuple-element.50.block, ...), custom_call_target="tpu_custom_call" | custom-call | flops 287500009472 | bytes 1000 | tf_op jit(solution)/shard_map/attend/pallas_call | solution.py:261
  74.2 8.3 %collective-permute-start.14 = (bf16[128,896]{1,0:T(8,128)(2,1)S(1)}, bf16[128,896]{1,0:T(8,128)(2,1)S(1)}, u32[]{:S(2)}, u32[]{:S(2)}) collective-permute-start(bf16[128,896]{1,0:T(8,128)(2,1)S(1)} %get-tuple-element.52.refs_1_), channel_id=1, source_target_pairs={{0,8},{1,9},{2,12},{3,13},{4,10},{5,11},{6,14},{7,15},{8,16},{9,17... | collective-permute-start | bytes 688136 | tf_op jit(solution)/shard_map/ppermute | solution.py:32
  82.5 3.6 %collective-permute-done.14.crossed.second = bf16[128,896]{1,0:T(8,128)(2,1)S(1)} collective-permute-done((bf16[128,896]{1,0:T(8,128)(2,1)S(1)}, bf16[128,896]{1,0:T(8,128)(2,1)S(1)}, u32[]{:S(2)}, u32[]{:S(2)}) %collective-permute-start.14) | collective-permute-done | bytes 229408 | tf_op jit(solution)/shard_map/ppermute | solution.py:32
  86.7 5.5 %collective-permute-done.15.ringed = bf16[128,896]{1,0:T(8,128)(2,1)S(1)} collective-permute-done((bf16[128,896]{1,0:T(8,128)(2,1)S(1)}, bf16[128,896]{1,0:T(8,128)(2,1)S(1)}, u32[]{:S(2)}, u32[]{:S(2)}) %collective-permute-start.15) | collective-permute-done | bytes 229408 | tf_op jit(solution)/shard_map/ppermute | solution.py:32
  93.7 4.6 %project.7 = (bf16[400,896]{1,0:T(8,128)(2,1)}, f32[3,128,896]{2,1,0:T(8,128)S(1)}, f32[128,1]{1,0:T(8,128)S(1)}) custom-call(s32[3]{0:T(128)S(1)} %copy-done.9, bf16[128,896]{1,0:T(8,128)(2,1)S(1)} %collective-permute-done.14.crossed.second, bf16[128,896]{1,0:T(8,128)(2,1)S(1)} %collective-permute-done.15.ringed, ...), custom_call_target="tpu_custom_call" | custom-call | flops 1150000 | bytes 1000 | tf_op jit(solution)/shard_map/project/pallas_call | solution.py:152
  98.9 2.0 %hold.1 = (f32[128,896]{1,0:T(8,128)S(1)}, bf16[2,128,896]{2,1,0:T(8,128)(2,1)S(1)}, bf16[256,896]{1,0:T(8,128)(2,1)S(1)}) custom-call(f32[3,128,896]{2,1,0:T(8,128)S(1)} %get-tuple-element.57.kept, bf16[400,896]{1,0:T(8,128)(2,1)} %collective-permute-done.19.received, f32[128,1]{1,0:T(8,128)S(1)} %get-tuple-element.49.kept_mean, ...), custom_call_target="tpu_custom_call" | custom-call | flops 287500009472 | bytes 1000 | tf_op jit(solution)/shard_map/hold/pallas_call | solution.py:261
  102.2 14.6 %collective-permute-done.18.received = bf16[400,896]{1,0:T(8,128)(2,1)} collective-permute-done((bf16[400,896]{1,0:T(8,128)(2,1)}, bf16[400,896]{1,0:T(8,128)(2,1)}, u32[]{:S(2)}, u32[]{:S(2)}) %collective-permute-start.18) | collective-permute-done | bytes 716832 | tf_op jit(solution)/shard_map/ppermute | solution.py:32
  116.8 3.2 %final.1 = (bf16[256,896]{1,0:T(8,128)(2,1)}, bf16[2,128,896]{2,1,0:T(8,128)(2,1)}) custom-call(s32[3]{0:T(128)S(1)} %copy-done.9, s32[1]{0:T(128)S(6)} %copy.5.flag, f32[3,128,896]{2,1,0:T(8,128)S(1)} %get-tuple-element.54.kept, bf16[400,896]{1,0:T(8,128)(2,1)} %collective-permute-done.18.received, f32[128,1]{1,0:T(8,128)S(1)} %get-tuple-element.56.kept_mean, ...), custom_call_target="tpu_custom_call" | custom-call | flops 287500009472 | bytes 1000 | tf_op jit(solution)/shard_map/final/pallas_call | solution.py:261
  (57 shorter events, 11.2 us)
Async XLA Ops:
  1.8 9.5 %collective-permute-start.1 = (bf16[128,896]{1,0:T(8,128)(2,1)S(1)}, bf16[128,896]{1,0:T(8,128)(2,1)}, u32[]{:S(2)}, u32[]{:S(2)}) collective-permute-start(bf16[128,896]{1,0:T(8,128)(2,1)S(1)} %get-tuple-element.63.block), channel_id=1, source_target_pairs={{0,2},{1,3},{2,6},{3,7},{4,0},{5,1},{6,4},{7,5},{8,10},{9,11},{10,... | collective-permute-start | bytes 688136 | tf_op jit(solution)/shard_map/ppermute | solution.py:32
  4.7 16.5 %collective-permute-start = (bf16[128,896]{1,0:T(8,128)(2,1)}, bf16[128,896]{1,0:T(8,128)(2,1)}, u32[]{:S(2)}, u32[]{:S(2)}) collective-permute-start(bf16[128,896]{1,0:T(8,128)(2,1)} %get-tuple-element.50.block), channel_id=1, source_target_pairs={{0,2},{1,3},{2,6},{3,7},{4,0},{5,1},{6,4},{7,5},{8,10},{9,11},{10,... | collective-permute-start | bytes 688136 | tf_op jit(solution)/shard_map/ppermute | solution.py:32
  6.3 29.1 %copy-start.7 = (s32[3]{0:T(128)}, s32[3]{0:T(128)S(1)}, u32[]{:S(2)}) copy-start(s32[3]{0:T(128)S(1)} %pad_add_fusion.place) | copy-start | bytes 40
  11.2 15.3 %collective-permute-start.5 = (bf16[128,896]{1,0:T(8,128)(2,1)}, bf16[128,896]{1,0:T(8,128)(2,1)}, u32[]{:S(2)}, u32[]{:S(2)}) collective-permute-start(bf16[128,896]{1,0:T(8,128)(2,1)} %collective-permute-done.1.arrived.ringed), channel_id=1, source_target_pairs={{0,1},{1,0},{2,3},{3,2},{4,5},{5,4},{6,7},{7,6},{8,9},{9,8},{10,11... | collective-permute-start | bytes 688136 | tf_op jit(solution)/shard_map/ppermute | solution.py:32
  11.2 9.8 %collective-permute-start.2 = (bf16[128,896]{1,0:T(8,128)(2,1)}, bf16[128,896]{1,0:T(8,128)(2,1)}, u32[]{:S(2)}, u32[]{:S(2)}) collective-permute-start(bf16[128,896]{1,0:T(8,128)(2,1)} %collective-permute-done.1.arrived.ringed), channel_id=1, source_target_pairs={{0,2},{1,3},{6,4},{7,5},{8,10},{9,11},{14,12},{15,13},{16,18},{17,... | collective-permute-start | bytes 688136 | tf_op jit(solution)/shard_map/ppermute | solution.py:32
  21.1 5.4 %collective-permute-start.4 = (bf16[128,896]{1,0:T(8,128)(2,1)S(1)}, bf16[128,896]{1,0:T(8,128)(2,1)S(1)}, u32[]{:S(2)}, u32[]{:S(2)}) collective-permute-start(bf16[128,896]{1,0:T(8,128)(2,1)S(1)} %broadcast_select_fusion.1.crossed), channel_id=1, source_target_pairs={{0,1},{1,0},{2,3},{3,2},{4,5},{5,4},{6,7},{7,6},{8,9},{9,8},{10,11... | collective-permute-start | bytes 688136 | tf_op jit(solution)/shard_map/ppermute | solution.py:32
  21.2 11.1 %collective-permute-start.3 = (bf16[128,896]{1,0:T(8,128)(2,1)}, bf16[128,896]{1,0:T(8,128)(2,1)S(1)}, u32[]{:S(2)}, u32[]{:S(2)}) collective-permute-start(bf16[128,896]{1,0:T(8,128)(2,1)} %collective-permute-done.ringed), channel_id=1, source_target_pairs={{0,2},{1,3},{6,4},{7,5},{8,10},{9,11},{14,12},{15,13},{16,18},{17,... | collective-permute-start | bytes 688136 | tf_op jit(solution)/shard_map/ppermute | solution.py:32
  32.3 19.0 %collective-permute-start.9 = (bf16[400,896]{1,0:T(8,128)(2,1)S(1)}, bf16[400,896]{1,0:T(8,128)(2,1)S(1)}, u32[]{:S(2)}, u32[]{:S(2)}) collective-permute-start(bf16[400,896]{1,0:T(8,128)(2,1)S(1)} %get-tuple-element.47), channel_id=1, source_target_pairs={{0,4},{1,5},{2,6},{3,7},{4,0},{5,1},{6,2},{7,3},{8,12},{9,13},{10,... | collective-permute-start | bytes 2150408 | tf_op jit(solution)/shard_map/ppermute | solution.py:32
  33.3 1.6 %collective-permute-start.6 = (bf16[128,896]{1,0:T(8,128)(2,1)S(1)}, bf16[128,896]{1,0:T(8,128)(2,1)S(1)}, u32[]{:S(2)}, u32[]{:S(2)}) collective-permute-start(bf16[128,896]{1,0:T(8,128)(2,1)S(1)} %broadcast_select_fusion.crossed), channel_id=1, source_target_pairs={{0,1},{1,0},{2,3},{3,2},{4,5},{5,4},{6,7},{7,6},{8,9},{9,8},{10,11... | collective-permute-start | bytes 688136 | tf_op jit(solution)/shard_map/ppermute | solution.py:32
  33.6 1.8 %collective-permute-start.7 = (bf16[128,896]{1,0:T(8,128)(2,1)}, bf16[128,896]{1,0:T(8,128)(2,1)S(1)}, u32[]{:S(2)}, u32[]{:S(2)}) collective-permute-start(bf16[128,896]{1,0:T(8,128)(2,1)} %collective-permute-done.ringed), channel_id=1, source_target_pairs={{0,1},{1,0},{2,3},{3,2},{4,5},{5,4},{6,7},{7,6},{8,9},{9,8},{10,11... | collective-permute-start | bytes 688136 | tf_op jit(solution)/shard_map/ppermute | solution.py:32
  40.4 31.4 %collective-permute-start.8 = (bf16[400,896]{1,0:T(8,128)(2,1)}, bf16[400,896]{1,0:T(8,128)(2,1)}, u32[]{:S(2)}, u32[]{:S(2)}) collective-permute-start(bf16[400,896]{1,0:T(8,128)(2,1)} %get-tuple-element.44), channel_id=1, source_target_pairs={{0,4},{1,5},{2,6},{3,7},{4,0},{5,1},{6,2},{7,3},{8,12},{9,13},{10,... | collective-permute-start | bytes 2150408 | tf_op jit(solution)/shard_map/ppermute | solution.py:32
  52.1 8.8 %collective-permute-start.11 = (bf16[128,896]{1,0:T(8,128)(2,1)S(1)}, bf16[128,896]{1,0:T(8,128)(2,1)S(1)}, u32[]{:S(2)}, u32[]{:S(2)}) collective-permute-start(bf16[128,896]{1,0:T(8,128)(2,1)S(1)} %get-tuple-element.48.refs_0_), channel_id=1, source_target_pairs={{0,10},{1,11},{2,14},{3,15},{4,8},{5,9},{6,12},{7,13},{8,18},{9,19... | collective-permute-start | bytes 688136 | tf_op jit(solution)/shard_map/ppermute | solution.py:32
  55.0 9.2 %collective-permute-start.10 = (bf16[128,896]{1,0:T(8,128)(2,1)S(1)}, bf16[128,896]{1,0:T(8,128)(2,1)S(1)}, u32[]{:S(2)}, u32[]{:S(2)}) collective-permute-start(bf16[128,896]{1,0:T(8,128)(2,1)S(1)} %get-tuple-element.48.refs_0_), channel_id=1, source_target_pairs={{0,8},{1,9},{2,12},{3,13},{4,10},{5,11},{6,14},{7,15},{8,16},{9,17... | collective-permute-start | bytes 688136 | tf_op jit(solution)/shard_map/ppermute | solution.py:32
  60.9 3.3 %collective-permute-start.13 = (bf16[128,896]{1,0:T(8,128)(2,1)S(1)}, bf16[128,896]{1,0:T(8,128)(2,1)S(1)}, u32[]{:S(2)}, u32[]{:S(2)}) collective-permute-start(bf16[128,896]{1,0:T(8,128)(2,1)S(1)} %collective-permute-done.11.ringed), channel_id=1, source_target_pairs={{0,1},{1,0},{2,3},{3,2},{4,5},{5,4},{6,7},{7,6},{8,9},{9,8},{10,11... | collective-permute-start | bytes 688136 | tf_op jit(solution)/shard_map/ppermute | solution.py:32
  64.1 1.5 %collective-permute-start.12 = (bf16[128,896]{1,0:T(8,128)(2,1)S(1)}, bf16[128,896]{1,0:T(8,128)(2,1)S(1)}, u32[]{:S(2)}, u32[]{:S(2)}) collective-permute-start(bf16[128,896]{1,0:T(8,128)(2,1)S(1)} %collective-permute-done.10.crossed.first), channel_id=1, source_target_pairs={{0,1},{1,0},{2,3},{3,2},{4,5},{5,4},{6,7},{7,6},{8,9},{9,8},{10,11... | collective-permute-start | bytes 688136 | tf_op jit(solution)/shard_map/ppermute | solution.py:32
  70.3 28.6 %collective-permute-start.19 = (bf16[400,896]{1,0:T(8,128)(2,1)}, bf16[400,896]{1,0:T(8,128)(2,1)}, u32[]{:S(2)}, u32[]{:S(2)}) collective-permute-start(bf16[400,896]{1,0:T(8,128)(2,1)} %get-tuple-element.58), channel_id=1, source_target_pairs={{0,4},{1,5},{2,6},{3,7},{4,0},{5,1},{6,2},{7,3},{8,12},{9,13},{10,... | collective-permute-start | bytes 2150408 | tf_op jit(solution)/shard_map/ppermute | solution.py:32
  71.8 21.9 %copy-start.9 = (s32[3]{0:T(128)S(1)}, s32[3]{0:T(128)}, u32[]{:S(2)}) copy-start(s32[3]{0:T(128)} %copy-done.7) | copy-start | bytes 40
  74.2 24.6 %copy-start.11 = (bf16[128,896]{1,0:T(8,128)(2,1)S(1)}, bf16[128,896]{1,0:T(8,128)(2,1)}, u32[]{:S(2)}) copy-start(bf16[128,896]{1,0:T(8,128)(2,1)} %copy-done.10) | copy-start | bytes 688132
  74.2 11.9 %collective-permute-start.14 = (bf16[128,896]{1,0:T(8,128)(2,1)S(1)}, bf16[128,896]{1,0:T(8,128)(2,1)S(1)}, u32[]{:S(2)}, u32[]{:S(2)}) collective-permute-start(bf16[128,896]{1,0:T(8,128)(2,1)S(1)} %get-tuple-element.52.refs_1_), channel_id=1, source_target_pairs={{0,8},{1,9},{2,12},{3,13},{4,10},{5,11},{6,14},{7,15},{8,16},{9,17... | collective-permute-start | bytes 688136 | tf_op jit(solution)/shard_map/ppermute | solution.py:32
  86.2 6.0 %collective-permute-start.15 = (bf16[128,896]{1,0:T(8,128)(2,1)S(1)}, bf16[128,896]{1,0:T(8,128)(2,1)S(1)}, u32[]{:S(2)}, u32[]{:S(2)}) collective-permute-start(bf16[128,896]{1,0:T(8,128)(2,1)S(1)} %collective-permute-done.14.crossed.second), channel_id=1, source_target_pairs={{0,2},{1,3},{2,0},{3,1},{4,6},{5,7},{6,4},{7,5},{8,10},{9,11},{10,... | collective-permute-start | bytes 688136 | tf_op jit(solution)/shard_map/ppermute | solution.py:32
  86.7 5.5 %collective-permute-start.16 = (bf16[128,896]{1,0:T(8,128)(2,1)S(1)}, bf16[128,896]{1,0:T(8,128)(2,1)S(1)}, u32[]{:S(2)}, u32[]{:S(2)}) collective-permute-start(bf16[128,896]{1,0:T(8,128)(2,1)S(1)} %collective-permute-done.14.crossed.second), channel_id=1, source_target_pairs={{0,1},{1,0},{2,3},{3,2},{4,5},{5,4},{6,7},{7,6},{8,9},{9,8},{10,11... | collective-permute-start | bytes 688136 | tf_op jit(solution)/shard_map/ppermute | solution.py:32
  92.2 1.5 %collective-permute-start.17 = (bf16[128,896]{1,0:T(8,128)(2,1)S(1)}, bf16[128,896]{1,0:T(8,128)(2,1)S(1)}, u32[]{:S(2)}, u32[]{:S(2)}) collective-permute-start(bf16[128,896]{1,0:T(8,128)(2,1)S(1)} %collective-permute-done.15.ringed), channel_id=1, source_target_pairs={{0,1},{1,0},{2,3},{3,2},{4,5},{5,4},{6,7},{7,6},{8,9},{9,8},{10,11... | collective-permute-start | bytes 688136 | tf_op jit(solution)/shard_map/ppermute | solution.py:32
  98.3 18.5 %collective-permute-start.18 = (bf16[400,896]{1,0:T(8,128)(2,1)}, bf16[400,896]{1,0:T(8,128)(2,1)}, u32[]{:S(2)}, u32[]{:S(2)}) collective-permute-start(bf16[400,896]{1,0:T(8,128)(2,1)} %get-tuple-element.55), channel_id=1, source_target_pairs={{0,4},{1,5},{2,6},{3,7},{4,0},{5,1},{6,2},{7,3},{8,12},{9,13},{10,... | collective-permute-start | bytes 2150408 | tf_op jit(solution)/shard_map/ppermute | solution.py:32
  100.9 1.3 %collective-permute-start.20 = (bf16[256,896]{1,0:T(8,128)(2,1)S(1)}, bf16[256,896]{1,0:T(8,128)(2,1)S(1)}, u32[]{:S(2)}, u32[]{:S(2)}) collective-permute-start(bf16[256,896]{1,0:T(8,128)(2,1)S(1)} %get-tuple-element.61.own), channel_id=1, source_target_pairs={{2,10},{3,11},{4,12},{5,13},{10,18},{11,19},{12,20},{13,21},{18,26... | collective-permute-start | bytes 1376264 | tf_op jit(solution)/shard_map/ppermute | solution.py:32
  (10 other events, 138.8 us)

commit v7 on v5

--- a/solution.py
+++ b/solution.py
@@ -52,6 +52,10 @@
     return (s, 1 - d, y, c) if d == y else None
 
 
+def swap(s, d, y, c):
+    return (s, d, 1 - y, c)
+
+
 def sibling(s, d, y, c):
     return (s, d, y, 1 - c)
 
@@ -100,11 +104,11 @@
         compiler_params=pltpu.CompilerParams(vmem_limit_bytes=VMEM_BYTES),
         cost_estimate=cost(4),
         name="stage",
-    )(place, weight)
+    )(place, pltpu.with_memory_space_constraint(weight, pltpu.HBM))
 
 
 def project_kernel(place, crossed, ringed, sib_crossed, sib_ringed, gain, weight, *refs):
-    sent, kept, kept_mean, normed = refs
+    sent, kept, kept_mean, normed, out, semaphores = refs
     rows = normed.shape[0] // 2
     width = crossed.shape[1]
     half = 2 * width
@@ -133,26 +137,43 @@
     mid = (row - high).astype(BF16).astype(F32)
     low = row - high - mid
     which = lax.broadcasted_iota(jnp.int32, row.shape, 0)
-    stat = jnp.where(which == 0, high, jnp.where(which == 1, mid, low))
+    stat = jnp.where(which == 0, high, jnp.where(which == 1, mid, low)).astype(BF16)
     for begin in range(0, width, rows):
-        sent[3 * rows :, begin : begin + rows] = stat.astype(BF16)
-    for k in range(3):
-        product = jnp.dot(normed[...], weight[0, k], preferred_element_type=F32)
-        sent[k * rows : (k + 1) * rows] = product[:rows].astype(BF16)
-        kept[k] = product[rows:]
+        out[:STAT_ROWS, begin : begin + rows] = stat
+    split = width // (2 * HD) * HD + HD
+    copies = []
+    for i, (k, begin, end) in enumerate(
+        ((0, 0, width), (1, 0, width), (2, 0, split), (2, split, width))
+    ):
+        columns = slice(begin, end)
+        product = jnp.dot(normed[...], weight[0, k, :, columns], preferred_element_type=F32)
+        top = STAT_ROWS + k * rows
+        out[top : top + rows, columns] = product[:rows].astype(BF16)
+        kept[k, :, columns] = product[rows:]
+        at = (slice(top if k else 0, top + rows), columns)
+        copies.append(pltpu.make_async_copy(out.at[at], sent.at[at], semaphores.at[i]))
+        copies[-1].start()
+    for copy in copies:
+        copy.wait()
 
 
 def project(rows, place, four, gain, weight, estimate):
     width = four[0].shape[1]
+    sent_shape = (3 * rows + STAT_ROWS, width)
     return pl.pallas_call(
         project_kernel,
         in_specs=[smem_spec()] + [vmem_spec()] * 6,
+        out_specs=[any_spec(), vmem_spec(), vmem_spec()],
         out_shape=[
-            pltpu.VMEM((3 * rows + STAT_ROWS, width), BF16),
+            jax.ShapeDtypeStruct(sent_shape, BF16),
             pltpu.VMEM((3, rows, width), F32),
             pltpu.VMEM((rows, 1), F32),
         ],
-        scratch_shapes=[pltpu.VMEM((2 * rows, 2 * width), BF16)],
+        scratch_shapes=[
+            pltpu.VMEM((2 * rows, 2 * width), BF16),
+            pltpu.VMEM(sent_shape, BF16),
+            pltpu.SemaphoreType.DMA((4,)),
+        ],
         compiler_params=pltpu.CompilerParams(vmem_limit_bytes=VMEM_BYTES),
         cost_estimate=cost(estimate),
         name="project",
@@ -161,7 +182,7 @@
 
 def mix(kept, received, kept_mean, earlier, pairs, put):
     rows, width = kept.shape[1:]
-    stat = received[3 * rows :, :rows].astype(F32)
+    stat = received[:STAT_ROWS, :rows].astype(F32)
     row = stat[0:1] + stat[1:2] + stat[2:3]
     mean_peer = jnp.transpose(jnp.broadcast_to(row, (HD, rows)))[:, :1]
     mean_kept = kept_mean[...]
@@ -177,7 +198,8 @@
         queries, keys, values = (
             (
                 kept[k, :, at] * scale_kept
-                + received[k * rows : (k + 1) * rows, at].astype(F32) * scale_peer
+                + received[STAT_ROWS + k * rows : STAT_ROWS + (k + 1) * rows, at].astype(F32)
+                * scale_peer
             ).astype(BF16)
             for k in range(3)
         )
@@ -295,20 +317,26 @@
         width = block.shape[1]
         rows_of = pltpu.VMEM((rows, width), BF16)
         pairs_of = pltpu.VMEM((2, rows, width), BF16)
-        owns, held, moved, seconds = [], [], [], []
-        for part, item in zip(parts, sums):
-            if seconds:
-                part = lax.optimization_barrier((part, seconds[0][2]))[0]
-            own, pairs = call_attend(
+
+        def attend(part, item, held):
+            return call_attend(
                 attend_kernel, "attend", [], [*item, part, *held], [rows_of, pairs_of]
             )
-            held.append(pairs)
-            owns.append(own)
-            pair = permute(own, sections, onward(cross)), permute(own, sections, onward(ring))
-            moved.append(pair[0])
-            if seconds:
-                pair = lax.optimization_barrier((*pair, seconds[0][2]))[:2]
-            seconds.append(partial(spread(*pair), 0.001))
+
+        def carry(own):
+            return permute(own, sections, onward(cross))
+
+        first, pairs = attend(parts[0], sums[0], [])
+        moved = [carry(first)]
+        four = spread(moved[0], permute(moved[0], sections, swap))
+        part = lax.optimization_barrier((parts[1], *four))[0]
+        second, _ = attend(part, sums[1], [pairs])
+        owns = [first, second]
+        moved.append(carry(second))
+        *four, _ = lax.optimization_barrier((*four, second))
+        seconds = [partial(four, 3)]
+        crossed, _ = lax.optimization_barrier((moved[1], seconds[0][2]))
+        seconds.append(partial(spread(crossed, permute(crossed, sections, swap)), 1))
         mixture, pairs, own = call_attend(
             hold_kernel,
             "hold",

time: 111 us -> 112 us (level)
  waiting for transfers between devices: 40 us -> 48 us
  starting transfers between devices: 35.6 us -> 29.7 us
  local copies, waits for them, and re-layouts: 4.88 us -> 1.82 us
  Pallas kernels: 28.4 us -> 31.2 us
    ppermute x22, waiting for transfers between devices: 40 us -> 48 us  [permute(): return lax.ppermute(array, AXES, pairs)]
    ppermute x22, starting transfers between devices: 35.6 us -> 29.7 us  [permute(): return lax.ppermute(array, AXES, pairs)]
    unnamed x18 -> x20, local copies, waits for them, and re-layouts: 3.8 us -> 0.73 us
    pallas_call x1, Pallas kernels: 1.45 us -> 4.31 us  [stage(): pl.pallas_call(stage_kernel, in_specs=[smem_spec(), any_spec()], out_spec...]
    pallas_call x4, Pallas kernels: 8.4 us -> 7.25 us  [call_attend(): pl.pallas_call(kernel, in_specs=[smem_spec() for _ in scalars] + [vmem_sp...]
  transfers between devices with their start and end apart: 22 -> 22, of which waited for: 13 -> 11; matrix products, arithmetic and copies ran while one was open for 0% -> 0% of each run, Pallas kernels for 23% -> 23%
where the time goes in v7:
time: 112 us
  waiting for transfers between devices  48 us (43%)
  Pallas kernels  31.2 us (28%)
  starting transfers between devices  29.7 us (27%)
  local copies, waits for them, and re-layouts  1.82 us (2%)
    ppermute x22, waiting for transfers between devices, permute(): return lax.ppermute(array, AXES, pairs)  48 us
    ppermute x22, starting transfers between devices, permute(): return lax.ppermute(array, AXES, pairs)  29.7 us
    pallas_call x4, Pallas kernels, project(): pl.pallas_call(project_kernel, in_specs=[smem_spec()] + [vmem_spec()] * 6...  19.7 us
    pallas_call x4, Pallas kernels, call_attend(): pl.pallas_call(kernel, in_specs=[smem_spec() for _ in scalars] + [vmem_sp...  7.25 us
    pallas_call x1, Pallas kernels, stage(): pl.pallas_call(stage_kernel, in_specs=[smem_spec(), any_spec()], out_spec...  4.31 us
  transfers between devices with their start and end apart: 22, of which 11 were waited for; matrix products, arithmetic and copies ran while one was open for 0% of the time, Pallas kernels for 23%

profile of v7, /device:TPU:0, one launch (start us, length us, event | category | flops | bytes accessed | tf_op | source)
XLA Modules:
  0.0 111.8 jit_solution(3419176997315314062)
XLA Ops:
  1.8 5.7 %collective-permute-start.4 = (bf16[128,896]{1,0:T(8,128)(2,1)S(1)}, bf16[128,896]{1,0:T(8,128)(2,1)S(1)}, u32[]{:S(2)}, u32[]{:S(2)}) collective-permute-start(bf16[128,896]{1,0:T(8,128)(2,1)S(1)} %get-tuple-element.71.block), channel_id=1, source_target_pairs={{0,2},{1,3},{2,6},{3,7},{4,0},{5,1},{6,4},{7,5},{8,10},{9,11},{10,... | collective-permute-start | bytes 688136 | tf_op jit(solution)/shard_map/ppermute | solution.py:32
  7.5 1.3 %collective-permute-start = (bf16[128,896]{1,0:T(8,128)(2,1)S(1)}, bf16[128,896]{1,0:T(8,128)(2,1)S(1)}, u32[]{:S(2)}, u32[]{:S(2)}) collective-permute-start(bf16[128,896]{1,0:T(8,128)(2,1)S(1)} %get-tuple-element.53.block), channel_id=1, source_target_pairs={{2,0},{3,1},{4,6},{5,7},{10,8},{11,9},{12,14},{13,15},{18,16},{19,... | collective-permute-start | bytes 688136 | tf_op jit(solution)/shard_map/ppermute | solution.py:32
  8.8 4.3 %stage.1.weight = bf16[1,3,1792,896]{3,2,1,0:T(8,128)(2,1)S(1)} custom-call(s32[3]{0:T(128)S(1)} %pad_add_fusion.place, bf16[1,3,1792,896]{3,2,1,0:T(8,128)(2,1)} %weight), custom_call_target="tpu_custom_call" | custom-call | flops 4600000000 | bytes 1000 | tf_op jit(solution)/shard_map/stage/pallas_call | solution.py:98
  13.2 4.5 %collective-permute-done.4.ringed = bf16[128,896]{1,0:T(8,128)(2,1)S(1)} collective-permute-done((bf16[128,896]{1,0:T(8,128)(2,1)S(1)}, bf16[128,896]{1,0:T(8,128)(2,1)S(1)}, u32[]{:S(2)}, u32[]{:S(2)}) %collective-permute-start.4) | collective-permute-done | bytes 229408 | tf_op jit(solution)/shard_map/ppermute | solution.py:32
  18.2 1.4 %collective-permute-start.2 = (bf16[128,896]{1,0:T(8,128)(2,1)S(1)}, bf16[128,896]{1,0:T(8,128)(2,1)S(1)}, u32[]{:S(2)}, u32[]{:S(2)}) collective-permute-start(bf16[128,896]{1,0:T(8,128)(2,1)S(1)} %get-tuple-element.53.block), channel_id=1, source_target_pairs={{0,2},{1,3},{2,6},{3,7},{4,0},{5,1},{6,4},{7,5},{8,10},{9,11},{10,... | collective-permute-start | bytes 688136 | tf_op jit(solution)/shard_map/ppermute | solution.py:32
  19.6 2.5 %collective-permute-start.1 = (bf16[128,896]{1,0:T(8,128)(2,1)S(1)}, bf16[128,896]{1,0:T(8,128)(2,1)S(1)}, u32[]{:S(2)}, u32[]{:S(2)}) collective-permute-start(bf16[128,896]{1,0:T(8,128)(2,1)S(1)} %collective-permute-done), channel_id=1, source_target_pairs={{0,4},{1,5},{6,2},{7,3},{8,12},{9,13},{14,10},{15,11},{16,20},{17,... | collective-permute-start | bytes 688136 | tf_op jit(solution)/shard_map/ppermute | solution.py:32
  22.2 5.2 %project.4 = (bf16[400,896]{1,0:T(8,128)(2,1)S(1)}, f32[3,128,896]{2,1,0:T(8,128)S(1)}, f32[128,1]{1,0:T(8,128)S(1)}) custom-call(s32[3]{0:T(128)S(1)} %pad_add_fusion.place, bf16[128,896]{1,0:T(8,128)(2,1)S(1)} %collective-permute-done.3.crossed, bf16[128,896]{1,0:T(8,128)(2,1)S(1)} %collective-permute-done.4.ringed, ...), custom_call_target="tpu_custom_call" | custom-call | flops 3449999872 | bytes 1000 | tf_op jit(solution)/shard_map/project/pallas_call | solution.py:163
  29.4 4.7 %project.5 = (bf16[400,896]{1,0:T(8,128)(2,1)}, f32[3,128,896]{2,1,0:T(8,128)S(1)}, f32[128,1]{1,0:T(8,128)S(1)}) custom-call(s32[3]{0:T(128)S(1)} %pad_add_fusion.place, bf16[128,896]{1,0:T(8,128)(2,1)S(1)} %broadcast_select_fusion.crossed, bf16[128,896]{1,0:T(8,128)(2,1)S(1)} %collective-permute-done.2.ringed, ...), custom_call_target="tpu_custom_call" | custom-call | flops 3449999872 | bytes 1000 | tf_op jit(solution)/shard_map/project/pallas_call | solution.py:163
  34.1 2.1 %collective-permute-start.9 = (bf16[400,896]{1,0:T(8,128)(2,1)}, bf16[400,896]{1,0:T(8,128)(2,1)}, u32[]{:S(2)}, u32[]{:S(2)}) collective-permute-start(bf16[400,896]{1,0:T(8,128)(2,1)} %get-tuple-element.48), channel_id=1, source_target_pairs={{0,4},{1,5},{2,6},{3,7},{4,0},{5,1},{6,2},{7,3},{8,12},{9,13},{10,... | collective-permute-start | bytes 2150408 | tf_op jit(solution)/shard_map/ppermute | solution.py:32
  36.1 10.3 %collective-permute-done.10.received = bf16[400,896]{1,0:T(8,128)(2,1)S(1)} collective-permute-done((bf16[400,896]{1,0:T(8,128)(2,1)S(1)}, bf16[400,896]{1,0:T(8,128)(2,1)S(1)}, u32[]{:S(2)}, u32[]{:S(2)}) %collective-permute-start.10) | collective-permute-done | bytes 716832 | tf_op jit(solution)/shard_map/ppermute | solution.py:32
  47.3 3.5 %collective-permute-start.11 = (bf16[128,896]{1,0:T(8,128)(2,1)S(1)}, bf16[128,896]{1,0:T(8,128)(2,1)S(1)}, u32[]{:S(2)}, u32[]{:S(2)}) collective-permute-start(bf16[128,896]{1,0:T(8,128)(2,1)S(1)} %get-tuple-element.52.refs_0_), channel_id=1, source_target_pairs={{0,8},{1,9},{2,12},{3,13},{4,10},{5,11},{6,14},{7,15},{8,16},{9,17... | collective-permute-start | bytes 688136 | tf_op jit(solution)/shard_map/ppermute | solution.py:32
  51.5 2.8 %collective-permute-done.11.crossed.first = bf16[128,896]{1,0:T(8,128)(2,1)S(1)} collective-permute-done((bf16[128,896]{1,0:T(8,128)(2,1)S(1)}, bf16[128,896]{1,0:T(8,128)(2,1)S(1)}, u32[]{:S(2)}, u32[]{:S(2)}) %collective-permute-start.11) | collective-permute-done | bytes 229408 | tf_op jit(solution)/shard_map/ppermute | solution.py:32
  55.2 5.1 %collective-permute-done.12.ringed = bf16[128,896]{1,0:T(8,128)(2,1)S(1)} collective-permute-done((bf16[128,896]{1,0:T(8,128)(2,1)S(1)}, bf16[128,896]{1,0:T(8,128)(2,1)S(1)}, u32[]{:S(2)}, u32[]{:S(2)}) %collective-permute-start.12) | collective-permute-done | bytes 229408 | tf_op jit(solution)/shard_map/ppermute | solution.py:32
  60.3 1.5 %collective-permute-done.14.sib_ringed = bf16[128,896]{1,0:T(8,128)(2,1)S(1)} collective-permute-done((bf16[128,896]{1,0:T(8,128)(2,1)S(1)}, bf16[128,896]{1,0:T(8,128)(2,1)S(1)}, u32[]{:S(2)}, u32[]{:S(2)}) %collective-permute-start.14) | collective-permute-done | bytes 229408 | tf_op jit(solution)/shard_map/ppermute | solution.py:32
  61.8 2.4 %attend.3 = (bf16[128,896]{1,0:T(8,128)(2,1)S(1)}, bf16[2,128,896]{2,1,0:T(8,128)(2,1)}) custom-call(f32[3,128,896]{2,1,0:T(8,128)S(1)} %get-tuple-element.47.kept, bf16[400,896]{1,0:T(8,128)(2,1)} %collective-permute-done.9.received, f32[128,1]{1,0:T(8,128)S(1)} %get-tuple-element.49.kept_mean, bf16[128,896]{1,0:T(8,128)(2,1)S(1)} %get-tuple-element.53.block, ...), custom_call_target="tpu_custom_call" | custom-call | flops 287500009472 | bytes 1000 | tf_op jit(solution)/shard_map/attend/pallas_call | solution.py:272
  64.2 7.1 %collective-permute-start.15 = (bf16[128,896]{1,0:T(8,128)(2,1)S(1)}, bf16[128,896]{1,0:T(8,128)(2,1)S(1)}, u32[]{:S(2)}, u32[]{:S(2)}) collective-permute-start(bf16[128,896]{1,0:T(8,128)(2,1)S(1)} %get-tuple-element.55.refs_1_), channel_id=1, source_target_pairs={{0,8},{1,9},{2,12},{3,13},{4,10},{5,11},{6,14},{7,15},{8,16},{9,17... | collective-permute-start | bytes 688136 | tf_op jit(solution)/shard_map/ppermute | solution.py:32
  71.3 5.2 %project.6 = (bf16[400,896]{1,0:T(8,128)(2,1)S(1)}, f32[3,128,896]{2,1,0:T(8,128)S(1)}, f32[128,1]{1,0:T(8,128)S(1)}) custom-call(s32[3]{0:T(128)S(1)} %copy-done.5, bf16[128,896]{1,0:T(8,128)(2,1)S(1)} %collective-permute-done.11.crossed.first, bf16[128,896]{1,0:T(8,128)(2,1)S(1)} %collective-permute-done.12.ringed, ...), custom_call_target="tpu_custom_call" | custom-call | flops 3449999872 | bytes 1000 | tf_op jit(solution)/shard_map/project/pallas_call | solution.py:163
  76.9 1.6 %collective-permute-start.16 = (bf16[128,896]{1,0:T(8,128)(2,1)S(1)}, bf16[128,896]{1,0:T(8,128)(2,1)S(1)}, u32[]{:S(2)}, u32[]{:S(2)}) collective-permute-start(bf16[128,896]{1,0:T(8,128)(2,1)S(1)} %collective-permute-done.15.crossed.second), channel_id=1, source_target_pairs={{0,2},{1,3},{2,0},{3,1},{4,6},{5,7},{6,4},{7,5},{8,10},{9,11},{10,... | collective-permute-start | bytes 688136 | tf_op jit(solution)/shard_map/ppermute | solution.py:32
  78.5 5.4 %collective-permute-done.16.ringed = bf16[128,896]{1,0:T(8,128)(2,1)S(1)} collective-permute-done((bf16[128,896]{1,0:T(8,128)(2,1)S(1)}, bf16[128,896]{1,0:T(8,128)(2,1)S(1)}, u32[]{:S(2)}, u32[]{:S(2)}) %collective-permute-start.16) | collective-permute-done | bytes 229408 | tf_op jit(solution)/shard_map/ppermute | solution.py:32
  83.9 1.5 %collective-permute-done.18.sib_ringed = bf16[128,896]{1,0:T(8,128)(2,1)S(1)} collective-permute-done((bf16[128,896]{1,0:T(8,128)(2,1)S(1)}, bf16[128,896]{1,0:T(8,128)(2,1)S(1)}, u32[]{:S(2)}, u32[]{:S(2)}) %collective-permute-start.18) | collective-permute-done | bytes 229408 | tf_op jit(solution)/shard_map/ppermute | solution.py:32
  85.4 4.7 %project.7 = (bf16[400,896]{1,0:T(8,128)(2,1)}, f32[3,128,896]{2,1,0:T(8,128)S(1)}, f32[128,1]{1,0:T(8,128)S(1)}) custom-call(s32[3]{0:T(128)S(1)} %copy-done.5, bf16[128,896]{1,0:T(8,128)(2,1)S(1)} %collective-permute-done.15.crossed.second, bf16[128,896]{1,0:T(8,128)(2,1)S(1)} %collective-permute-done.16.ringed, ...), custom_call_target="tpu_custom_call" | custom-call | flops 1150000000 | bytes 1000 | tf_op jit(solution)/shard_map/project/pallas_call | solution.py:163
  90.8 2.2 %collective-permute-done.20.received = bf16[400,896]{1,0:T(8,128)(2,1)S(1)} collective-permute-done((bf16[400,896]{1,0:T(8,128)(2,1)S(1)}, bf16[400,896]{1,0:T(8,128)(2,1)S(1)}, u32[]{:S(2)}, u32[]{:S(2)}) %collective-permute-start.20) | collective-permute-done | bytes 716832 | tf_op jit(solution)/shard_map/ppermute | solution.py:32
  95.3 13.3 %collective-permute-done.19.received = bf16[400,896]{1,0:T(8,128)(2,1)} collective-permute-done((bf16[400,896]{1,0:T(8,128)(2,1)}, bf16[400,896]{1,0:T(8,128)(2,1)}, u32[]{:S(2)}, u32[]{:S(2)}) %collective-permute-start.19) | collective-permute-done | bytes 716832 | tf_op jit(solution)/shard_map/ppermute | solution.py:32
  108.6 3.2 %final.1 = (bf16[256,896]{1,0:T(8,128)(2,1)}, bf16[2,128,896]{2,1,0:T(8,128)(2,1)}) custom-call(s32[3]{0:T(128)S(1)} %copy-done.6, s32[1]{0:T(128)S(6)} %copy.5.flag, f32[3,128,896]{2,1,0:T(8,128)S(1)} %get-tuple-element.62.kept, bf16[400,896]{1,0:T(8,128)(2,1)} %collective-permute-done.19.received, f32[128,1]{1,0:T(8,128)S(1)} %get-tuple-element.64.kept_mean, ...), custom_call_target="tpu_custom_call" | custom-call | flops 287500009472 | bytes 1000 | tf_op jit(solution)/shard_map/final/pallas_call | solution.py:272
  (52 shorter events, 9.6 us)
Async XLA Ops:
  1.1 12.1 %collective-permute-start.3 = (bf16[128,896]{1,0:T(8,128)(2,1)S(1)}, bf16[128,896]{1,0:T(8,128)(2,1)S(1)}, u32[]{:S(2)}, u32[]{:S(2)}) collective-permute-start(bf16[128,896]{1,0:T(8,128)(2,1)S(1)} %get-tuple-element.71.block), channel_id=1, source_target_pairs={{0,0},{1,1},{2,4},{3,5},{4,2},{5,3},{6,6},{7,7},{8,8},{9,9},{10,12... | collective-permute-start | bytes 688136 | tf_op jit(solution)/shard_map/ppermute | solution.py:32
  1.8 15.9 %collective-permute-start.4 = (bf16[128,896]{1,0:T(8,128)(2,1)S(1)}, bf16[128,896]{1,0:T(8,128)(2,1)S(1)}, u32[]{:S(2)}, u32[]{:S(2)}) collective-permute-start(bf16[128,896]{1,0:T(8,128)(2,1)S(1)} %get-tuple-element.71.block), channel_id=1, source_target_pairs={{0,2},{1,3},{2,6},{3,7},{4,0},{5,1},{6,4},{7,5},{8,10},{9,11},{10,... | collective-permute-start | bytes 688136 | tf_op jit(solution)/shard_map/ppermute | solution.py:32
  7.5 12.2 %collective-permute-start = (bf16[128,896]{1,0:T(8,128)(2,1)S(1)}, bf16[128,896]{1,0:T(8,128)(2,1)S(1)}, u32[]{:S(2)}, u32[]{:S(2)}) collective-permute-start(bf16[128,896]{1,0:T(8,128)(2,1)S(1)} %get-tuple-element.53.block), channel_id=1, source_target_pairs={{2,0},{3,1},{4,6},{5,7},{10,8},{11,9},{12,14},{13,15},{18,16},{19,... | collective-permute-start | bytes 688136 | tf_op jit(solution)/shard_map/ppermute | solution.py:32
  8.8 20.5 %copy-start.4 = (s32[3]{0:T(128)}, s32[3]{0:T(128)S(1)}, u32[]{:S(2)}) copy-start(s32[3]{0:T(128)S(1)} %pad_add_fusion.place) | copy-start | bytes 40
  17.7 4.5 %collective-permute-start.5 = (bf16[128,896]{1,0:T(8,128)(2,1)S(1)}, bf16[128,896]{1,0:T(8,128)(2,1)S(1)}, u32[]{:S(2)}, u32[]{:S(2)}) collective-permute-start(bf16[128,896]{1,0:T(8,128)(2,1)S(1)} %collective-permute-done.3.crossed), channel_id=1, source_target_pairs={{0,1},{1,0},{2,3},{3,2},{4,5},{5,4},{6,7},{7,6},{8,9},{9,8},{10,11... | collective-permute-start | bytes 688136 | tf_op jit(solution)/shard_map/ppermute | solution.py:32
  17.7 4.5 %collective-permute-start.6 = (bf16[128,896]{1,0:T(8,128)(2,1)S(1)}, bf16[128,896]{1,0:T(8,128)(2,1)S(1)}, u32[]{:S(2)}, u32[]{:S(2)}) collective-permute-start(bf16[128,896]{1,0:T(8,128)(2,1)S(1)} %collective-permute-done.4.ringed), channel_id=1, source_target_pairs={{0,1},{1,0},{2,3},{3,2},{4,5},{5,4},{6,7},{7,6},{8,9},{9,8},{10,11... | collective-permute-start | bytes 688136 | tf_op jit(solution)/shard_map/ppermute | solution.py:32
  18.2 9.3 %collective-permute-start.2 = (bf16[128,896]{1,0:T(8,128)(2,1)S(1)}, bf16[128,896]{1,0:T(8,128)(2,1)S(1)}, u32[]{:S(2)}, u32[]{:S(2)}) collective-permute-start(bf16[128,896]{1,0:T(8,128)(2,1)S(1)} %get-tuple-element.53.block), channel_id=1, source_target_pairs={{0,2},{1,3},{2,6},{3,7},{4,0},{5,1},{6,4},{7,5},{8,10},{9,11},{10,... | collective-permute-start | bytes 688136 | tf_op jit(solution)/shard_map/ppermute | solution.py:32
  19.6 7.8 %collective-permute-start.1 = (bf16[128,896]{1,0:T(8,128)(2,1)S(1)}, bf16[128,896]{1,0:T(8,128)(2,1)S(1)}, u32[]{:S(2)}, u32[]{:S(2)}) collective-permute-start(bf16[128,896]{1,0:T(8,128)(2,1)S(1)} %collective-permute-done), channel_id=1, source_target_pairs={{0,4},{1,5},{6,2},{7,3},{8,12},{9,13},{14,10},{15,11},{16,20},{17,... | collective-permute-start | bytes 688136 | tf_op jit(solution)/shard_map/ppermute | solution.py:32
  27.4 19.1 %collective-permute-start.10 = (bf16[400,896]{1,0:T(8,128)(2,1)S(1)}, bf16[400,896]{1,0:T(8,128)(2,1)S(1)}, u32[]{:S(2)}, u32[]{:S(2)}) collective-permute-start(bf16[400,896]{1,0:T(8,128)(2,1)S(1)} %get-tuple-element.51), channel_id=1, source_target_pairs={{0,4},{1,5},{2,6},{3,7},{4,0},{5,1},{6,2},{7,3},{8,12},{9,13},{10,... | collective-permute-start | bytes 2150408 | tf_op jit(solution)/shard_map/ppermute | solution.py:32
  27.5 1.6 %collective-permute-start.7 = (bf16[128,896]{1,0:T(8,128)(2,1)S(1)}, bf16[128,896]{1,0:T(8,128)(2,1)S(1)}, u32[]{:S(2)}, u32[]{:S(2)}) collective-permute-start(bf16[128,896]{1,0:T(8,128)(2,1)S(1)} %broadcast_select_fusion.crossed), channel_id=1, source_target_pairs={{0,1},{1,0},{2,3},{3,2},{4,5},{5,4},{6,7},{7,6},{8,9},{9,8},{10,11... | collective-permute-start | bytes 688136 | tf_op jit(solution)/shard_map/ppermute | solution.py:32
  27.6 1.8 %collective-permute-start.8 = (bf16[128,896]{1,0:T(8,128)(2,1)S(1)}, bf16[128,896]{1,0:T(8,128)(2,1)S(1)}, u32[]{:S(2)}, u32[]{:S(2)}) collective-permute-start(bf16[128,896]{1,0:T(8,128)(2,1)S(1)} %collective-permute-done.2.ringed), channel_id=1, source_target_pairs={{0,1},{1,0},{2,3},{3,2},{4,5},{5,4},{6,7},{7,6},{8,9},{9,8},{10,11... | collective-permute-start | bytes 688136 | tf_op jit(solution)/shard_map/ppermute | solution.py:32
  34.1 27.7 %collective-permute-start.9 = (bf16[400,896]{1,0:T(8,128)(2,1)}, bf16[400,896]{1,0:T(8,128)(2,1)}, u32[]{:S(2)}, u32[]{:S(2)}) collective-permute-start(bf16[400,896]{1,0:T(8,128)(2,1)} %get-tuple-element.48), channel_id=1, source_target_pairs={{0,4},{1,5},{2,6},{3,7},{4,0},{5,1},{6,2},{7,3},{8,12},{9,13},{10,... | collective-permute-start | bytes 2150408 | tf_op jit(solution)/shard_map/ppermute | solution.py:32
  47.3 7.0 %collective-permute-start.11 = (bf16[128,896]{1,0:T(8,128)(2,1)S(1)}, bf16[128,896]{1,0:T(8,128)(2,1)S(1)}, u32[]{:S(2)}, u32[]{:S(2)}) collective-permute-start(bf16[128,896]{1,0:T(8,128)(2,1)S(1)} %get-tuple-element.52.refs_0_), channel_id=1, source_target_pairs={{0,8},{1,9},{2,12},{3,13},{4,10},{5,11},{6,14},{7,15},{8,16},{9,17... | collective-permute-start | bytes 688136 | tf_op jit(solution)/shard_map/ppermute | solution.py:32
  54.3 6.0 %collective-permute-start.12 = (bf16[128,896]{1,0:T(8,128)(2,1)S(1)}, bf16[128,896]{1,0:T(8,128)(2,1)S(1)}, u32[]{:S(2)}, u32[]{:S(2)}) collective-permute-start(bf16[128,896]{1,0:T(8,128)(2,1)S(1)} %collective-permute-done.11.crossed.first), channel_id=1, source_target_pairs={{0,2},{1,3},{2,0},{3,1},{4,6},{5,7},{6,4},{7,5},{8,10},{9,11},{10,... | collective-permute-start | bytes 688136 | tf_op jit(solution)/shard_map/ppermute | solution.py:32
  55.2 5.1 %collective-permute-start.13 = (bf16[128,896]{1,0:T(8,128)(2,1)S(1)}, bf16[128,896]{1,0:T(8,128)(2,1)S(1)}, u32[]{:S(2)}, u32[]{:S(2)}) collective-permute-start(bf16[128,896]{1,0:T(8,128)(2,1)S(1)} %collective-permute-done.11.crossed.first), channel_id=1, source_target_pairs={{0,1},{1,0},{2,3},{3,2},{4,5},{5,4},{6,7},{7,6},{8,9},{9,8},{10,11... | collective-permute-start | bytes 688136 | tf_op jit(solution)/shard_map/ppermute | solution.py:32
  60.3 1.5 %collective-permute-start.14 = (bf16[128,896]{1,0:T(8,128)(2,1)S(1)}, bf16[128,896]{1,0:T(8,128)(2,1)S(1)}, u32[]{:S(2)}, u32[]{:S(2)}) collective-permute-start(bf16[128,896]{1,0:T(8,128)(2,1)S(1)} %collective-permute-done.12.ringed), channel_id=1, source_target_pairs={{0,1},{1,0},{2,3},{3,2},{4,5},{5,4},{6,7},{7,6},{8,9},{9,8},{10,11... | collective-permute-start | bytes 688136 | tf_op jit(solution)/shard_map/ppermute | solution.py:32
  64.2 12.8 %collective-permute-start.15 = (bf16[128,896]{1,0:T(8,128)(2,1)S(1)}, bf16[128,896]{1,0:T(8,128)(2,1)S(1)}, u32[]{:S(2)}, u32[]{:S(2)}) collective-permute-start(bf16[128,896]{1,0:T(8,128)(2,1)S(1)} %get-tuple-element.55.refs_1_), channel_id=1, source_target_pairs={{0,8},{1,9},{2,12},{3,13},{4,10},{5,11},{6,14},{7,15},{8,16},{9,17... | collective-permute-start | bytes 688136 | tf_op jit(solution)/shard_map/ppermute | solution.py:32
  76.4 16.6 %collective-permute-start.20 = (bf16[400,896]{1,0:T(8,128)(2,1)S(1)}, bf16[400,896]{1,0:T(8,128)(2,1)S(1)}, u32[]{:S(2)}, u32[]{:S(2)}) collective-permute-start(bf16[400,896]{1,0:T(8,128)(2,1)S(1)} %get-tuple-element.66), channel_id=1, source_target_pairs={{0,4},{1,5},{2,6},{3,7},{4,0},{5,1},{6,2},{7,3},{8,12},{9,13},{10,... | collective-permute-start | bytes 2150408 | tf_op jit(solution)/shard_map/ppermute | solution.py:32
  76.9 16.1 %copy-start.8 = (bf16[128,896]{1,0:T(8,128)(2,1)S(1)}, bf16[128,896]{1,0:T(8,128)(2,1)}, u32[]{:S(2)}) copy-start(bf16[128,896]{1,0:T(8,128)(2,1)} %copy-done.7) | copy-start | bytes 688132
  76.9 7.0 %collective-permute-start.16 = (bf16[128,896]{1,0:T(8,128)(2,1)S(1)}, bf16[128,896]{1,0:T(8,128)(2,1)S(1)}, u32[]{:S(2)}, u32[]{:S(2)}) collective-permute-start(bf16[128,896]{1,0:T(8,128)(2,1)S(1)} %collective-permute-done.15.crossed.second), channel_id=1, source_target_pairs={{0,2},{1,3},{2,0},{3,1},{4,6},{5,7},{6,4},{7,5},{8,10},{9,11},{10,... | collective-permute-start | bytes 688136 | tf_op jit(solution)/shard_map/ppermute | solution.py:32
  78.5 5.4 %collective-permute-start.17 = (bf16[128,896]{1,0:T(8,128)(2,1)S(1)}, bf16[128,896]{1,0:T(8,128)(2,1)S(1)}, u32[]{:S(2)}, u32[]{:S(2)}) collective-permute-start(bf16[128,896]{1,0:T(8,128)(2,1)S(1)} %collective-permute-done.15.crossed.second), channel_id=1, source_target_pairs={{0,1},{1,0},{2,3},{3,2},{4,5},{5,4},{6,7},{7,6},{8,9},{9,8},{10,11... | collective-permute-start | bytes 688136 | tf_op jit(solution)/shard_map/ppermute | solution.py:32
  83.9 1.5 %collective-permute-start.18 = (bf16[128,896]{1,0:T(8,128)(2,1)S(1)}, bf16[128,896]{1,0:T(8,128)(2,1)S(1)}, u32[]{:S(2)}, u32[]{:S(2)}) collective-permute-start(bf16[128,896]{1,0:T(8,128)(2,1)S(1)} %collective-permute-done.16.ringed), channel_id=1, source_target_pairs={{0,1},{1,0},{2,3},{3,2},{4,5},{5,4},{6,7},{7,6},{8,9},{9,8},{10,11... | collective-permute-start | bytes 688136 | tf_op jit(solution)/shard_map/ppermute | solution.py:32
  90.1 18.5 %collective-permute-start.19 = (bf16[400,896]{1,0:T(8,128)(2,1)}, bf16[400,896]{1,0:T(8,128)(2,1)}, u32[]{:S(2)}, u32[]{:S(2)}) collective-permute-start(bf16[400,896]{1,0:T(8,128)(2,1)} %get-tuple-element.63), channel_id=1, source_target_pairs={{0,4},{1,5},{2,6},{3,7},{4,0},{5,1},{6,2},{7,3},{8,12},{9,13},{10,... | collective-permute-start | bytes 2150408 | tf_op jit(solution)/shard_map/ppermute | solution.py:32
  93.9 1.3 %collective-permute-start.21 = (bf16[256,896]{1,0:T(8,128)(2,1)S(1)}, bf16[256,896]{1,0:T(8,128)(2,1)S(1)}, u32[]{:S(2)}, u32[]{:S(2)}) collective-permute-start(bf16[256,896]{1,0:T(8,128)(2,1)S(1)} %get-tuple-element.69.own), channel_id=1, source_target_pairs={{2,10},{3,11},{4,12},{5,13},{10,18},{11,19},{12,20},{13,21},{18,26... | collective-permute-start | bytes 1376264 | tf_op jit(solution)/shard_map/ppermute | solution.py:32
  (8 other events, 91.4 us)

commit v8 on v7

--- a/solution.py
+++ b/solution.py
@@ -44,12 +44,8 @@
     return (s, d, y, c) if d != y else None
 
 
-def across_y(s, d, y, c):
-    return (s, d, 1 - y, c) if d != y else None
-
-
-def across_x(s, d, y, c):
-    return (s, 1 - d, y, c) if d == y else None
+def forward(s, d, y, c):
+    return (s, d, 1 - y, c) if d == y else None
 
 
 def swap(s, d, y, c):
@@ -108,7 +104,8 @@
 
 
 def project_kernel(place, crossed, ringed, sib_crossed, sib_ringed, gain, weight, *refs):
-    sent, kept, kept_mean, normed, out, semaphores = refs
+    sent, kept, kept_mean, normed = refs[:4]
+    out, semaphores = refs[4:] or (sent, None)
     rows = normed.shape[0] // 2
     width = crossed.shape[1]
     half = 2 * width
@@ -150,6 +147,8 @@
         top = STAT_ROWS + k * rows
         out[top : top + rows, columns] = product[:rows].astype(BF16)
         kept[k, :, columns] = product[rows:]
+        if semaphores is None:
+            continue
         at = (slice(top if k else 0, top + rows), columns)
         copies.append(pltpu.make_async_copy(out.at[at], sent.at[at], semaphores.at[i]))
         copies[-1].start()
@@ -157,23 +156,20 @@
         copy.wait()
 
 
-def project(rows, place, four, gain, weight, estimate):
+def project(rows, place, four, gain, weight, apart, estimate):
     width = four[0].shape[1]
     sent_shape = (3 * rows + STAT_ROWS, width)
     return pl.pallas_call(
         project_kernel,
         in_specs=[smem_spec()] + [vmem_spec()] * 6,
-        out_specs=[any_spec(), vmem_spec(), vmem_spec()],
+        out_specs=[any_spec() if apart else vmem_spec(), vmem_spec(), vmem_spec()],
         out_shape=[
-            jax.ShapeDtypeStruct(sent_shape, BF16),
+            (pltpu.HBM if apart else pltpu.VMEM)(sent_shape, BF16),
             pltpu.VMEM((3, rows, width), F32),
             pltpu.VMEM((rows, 1), F32),
         ],
-        scratch_shapes=[
-            pltpu.VMEM((2 * rows, 2 * width), BF16),
-            pltpu.VMEM(sent_shape, BF16),
-            pltpu.SemaphoreType.DMA((4,)),
-        ],
+        scratch_shapes=[pltpu.VMEM((2 * rows, 2 * width), BF16)]
+        + [pltpu.VMEM(sent_shape, BF16), pltpu.SemaphoreType.DMA((4,))] * apart,
         compiler_params=pltpu.CompilerParams(vmem_limit_bytes=VMEM_BYTES),
         cost_estimate=cost(estimate),
         name="project",
@@ -298,22 +294,22 @@
                 permute(ringed, sections, sibling),
             )
 
-        def partial(four, estimate):
-            sent, kept, kept_mean = project(rows, place, four, norm_gain, weight, estimate)
+        def partial(four, apart, estimate):
+            sent, kept, kept_mean = project(rows, place, four, norm_gain, weight, apart, estimate)
             return kept, permute(sent, sections, peer), kept_mean
 
         block = inputs[0, 0]
         rows = block.shape[0] // PARTS
         parts = [block[i * rows : (i + 1) * rows] for i in range(PARTS)]
-        pair = permute(parts[0], sections, cross), permute(parts[0], sections, ring)
-        relayed = permute(parts[1], sections, across_y)
-        ringed = permute(parts[1], sections, ring)
-        *pair, weight = lax.optimization_barrier((*pair, weight))
+        ringed = [permute(part, sections, ring) for part in parts]
+        crossed = permute(parts[0], sections, cross)
+        ringed[0], crossed, weight = lax.optimization_barrier((ringed[0], crossed, weight))
         weight = pltpu.with_memory_space_constraint(weight, pltpu.VMEM)
-        sums = [partial(spread(*pair), 3)]
-        crossed = jnp.where(diagonal, parts[1], permute(relayed, sections, across_x))
-        crossed, ringed, _ = lax.optimization_barrier((crossed, ringed, sums[0][2]))
-        sums.append(partial(spread(crossed, ringed), 3))
+        sums = [partial(spread(crossed, ringed[0]), False, 3)]
+        late, _ = lax.optimization_barrier((ringed[1], sums[0][2]))
+        forwarded = permute(late, sections, forward)
+        crossed = jnp.where(diagonal, parts[1], forwarded)
+        sums.append(partial(spread(crossed, late), True, 0.001))
         width = block.shape[1]
         rows_of = pltpu.VMEM((rows, width), BF16)
         pairs_of = pltpu.VMEM((2, rows, width), BF16)
@@ -328,15 +324,18 @@
 
         first, pairs = attend(parts[0], sums[0], [])
         moved = [carry(first)]
-        four = spread(moved[0], permute(moved[0], sections, swap))
-        part = lax.optimization_barrier((parts[1], *four))[0]
+        swapped = permute(moved[0], sections, swap)
+        beside = permute(moved[0], sections, sibling)
+        part = lax.optimization_barrier((parts[1], beside))[0]
         second, _ = attend(part, sums[1], [pairs])
         owns = [first, second]
         moved.append(carry(second))
-        *four, _ = lax.optimization_barrier((*four, second))
-        seconds = [partial(four, 3)]
+        swapped, _ = lax.optimization_barrier((swapped, second))
+        four = moved[0], swapped, beside, permute(swapped, sections, sibling)
+        seconds = [partial(four, False, 3)]
         crossed, _ = lax.optimization_barrier((moved[1], seconds[0][2]))
-        seconds.append(partial(spread(crossed, permute(crossed, sections, swap)), 1))
+        swapped = permute(crossed, sections, swap)
+        seconds.append(partial(spread(crossed, swapped), True, 1))
         mixture, pairs, own = call_attend(
             hold_kernel,
             "hold",

time: 112 us -> 111 us (level)
  starting transfers between devices: 29.7 us -> 33.4 us
  waiting for transfers between devices: 48 us -> 44.4 us
  Pallas kernels: 31.2 us -> 29.5 us
    ppermute x22 -> x21, starting transfers between devices: 29.7 us -> 33.4 us  [permute(): return lax.ppermute(array, AXES, pairs)]
    ppermute x22 -> x21, waiting for transfers between devices: 48 us -> 44.4 us  [permute(): return lax.ppermute(array, AXES, pairs)]
    pallas_call x4, Pallas kernels: 19.7 us -> 17.9 us  [project(): pl.pallas_call(project_kernel, in_specs=[smem_spec()] + [vmem_spec()] * 6...]
  transfers between devices with their start and end apart: 22 -> 21, of which waited for: 11 -> 11; matrix products, arithmetic and copies ran while one was open for 0% -> 0% of each run, Pallas kernels for 23% -> 24%
where the time goes in v8:
time: 111 us; the launch traced here: 110 us
  waiting for transfers between devices  44.4 us (40%)
  starting transfers between devices  33.4 us (30%)
  Pallas kernels  29.5 us (27%)
  local copies, waits for them, and re-layouts  2.06 us (2%)
    ppermute x21, waiting for transfers between devices, permute(): return lax.ppermute(array, AXES, pairs)  44.4 us
    ppermute x21, starting transfers between devices, permute(): return lax.ppermute(array, AXES, pairs)  33.4 us
    pallas_call x4, Pallas kernels, project(): pl.pallas_call(project_kernel, in_specs=[smem_spec()] + [vmem_spec()] * 6...  17.9 us
    pallas_call x4, Pallas kernels, call_attend(): pl.pallas_call(kernel, in_specs=[smem_spec() for _ in scalars] + [vmem_sp...  7.32 us
    pallas_call x1, Pallas kernels, stage(): pl.pallas_call(stage_kernel, in_specs=[smem_spec(), any_spec()], out_spec...  4.31 us
  transfers between devices with their start and end apart: 21, of which 11 were waited for; matrix products, arithmetic and copies ran while one was open for 0% of the time, Pallas kernels for 24%

profile of v8, /device:TPU:0, one launch (start us, length us, event | category | flops | bytes accessed | tf_op | source)
XLA Modules:
  0.0 110.4 jit_solution(4563082088001360060)
XLA Ops:
  1.1 3.0 %collective-permute-start.1 = (bf16[128,896]{1,0:T(8,128)(2,1)S(1)}, bf16[128,896]{1,0:T(8,128)(2,1)S(1)}, u32[]{:S(2)}, u32[]{:S(2)}) collective-permute-start(bf16[128,896]{1,0:T(8,128)(2,1)S(1)} %get-tuple-element.63.block), channel_id=1, source_target_pairs={{0,2},{1,3},{2,6},{3,7},{4,0},{5,1},{6,4},{7,5},{8,10},{9,11},{10,... | collective-permute-start | bytes 688136 | tf_op jit(solution)/shard_map/ppermute | solution.py:32
  4.9 4.3 %stage.1.weight = bf16[1,3,1792,896]{3,2,1,0:T(8,128)(2,1)S(1)} custom-call(s32[3]{0:T(128)S(1)} %pad_add_fusion.place, bf16[1,3,1792,896]{3,2,1,0:T(8,128)(2,1)} %weight), custom_call_target="tpu_custom_call" | custom-call | flops 4600000000 | bytes 1000 | tf_op jit(solution)/shard_map/stage/pallas_call | solution.py:94
  9.2 4.7 %collective-permute-done.1.ringed = bf16[128,896]{1,0:T(8,128)(2,1)S(1)} collective-permute-done((bf16[128,896]{1,0:T(8,128)(2,1)S(1)}, bf16[128,896]{1,0:T(8,128)(2,1)S(1)}, u32[]{:S(2)}, u32[]{:S(2)}) %collective-permute-start.1) | collective-permute-done | bytes 229408 | tf_op jit(solution)/shard_map/ppermute | solution.py:32
  14.4 2.4 %collective-permute-start = (bf16[128,896]{1,0:T(8,128)(2,1)S(1)}, bf16[128,896]{1,0:T(8,128)(2,1)S(1)}, u32[]{:S(2)}, u32[]{:S(2)}) collective-permute-start(bf16[128,896]{1,0:T(8,128)(2,1)S(1)} %get-tuple-element.48.block), channel_id=1, source_target_pairs={{0,2},{1,3},{2,6},{3,7},{4,0},{5,1},{6,4},{7,5},{8,10},{9,11},{10,... | collective-permute-start | bytes 688136 | tf_op jit(solution)/shard_map/ppermute | solution.py:32
  16.9 4.0 %project.4 = (bf16[400,896]{1,0:T(8,128)(2,1)S(1)}, f32[3,128,896]{2,1,0:T(8,128)S(1)}, f32[128,1]{1,0:T(8,128)S(1)}) custom-call(s32[3]{0:T(128)S(1)} %pad_add_fusion.place, bf16[128,896]{1,0:T(8,128)(2,1)S(1)} %collective-permute-done.2.crossed, bf16[128,896]{1,0:T(8,128)(2,1)S(1)} %collective-permute-done.1.ringed, ...), custom_call_target="tpu_custom_call" | custom-call | flops 3449999872 | bytes 1000 | tf_op jit(solution)/shard_map/project/pallas_call | solution.py:162
  20.9 2.3 %collective-permute-start.9 = (bf16[400,896]{1,0:T(8,128)(2,1)S(1)}, bf16[400,896]{1,0:T(8,128)(2,1)S(1)}, u32[]{:S(2)}, u32[]{:S(2)}) collective-permute-start(bf16[400,896]{1,0:T(8,128)(2,1)S(1)} %get-tuple-element.46), channel_id=1, source_target_pairs={{0,4},{1,5},{2,6},{3,7},{4,0},{5,1},{6,2},{7,3},{8,12},{9,13},{10,... | collective-permute-start | bytes 2150408 | tf_op jit(solution)/shard_map/ppermute | solution.py:32
  23.6 2.7 %collective-permute-start.5 = (bf16[128,896]{1,0:T(8,128)(2,1)S(1)}, bf16[128,896]{1,0:T(8,128)(2,1)S(1)}, u32[]{:S(2)}, u32[]{:S(2)}) collective-permute-start(bf16[128,896]{1,0:T(8,128)(2,1)S(1)} %collective-permute-done.ringed), channel_id=1, source_target_pairs={{0,2},{1,3},{6,4},{7,5},{8,10},{9,11},{14,12},{15,13},{16,18},{17,... | collective-permute-start | bytes 688136 | tf_op jit(solution)/shard_map/ppermute | solution.py:32
  26.4 4.1 %collective-permute-done.5 = bf16[128,896]{1,0:T(8,128)(2,1)S(1)} collective-permute-done((bf16[128,896]{1,0:T(8,128)(2,1)S(1)}, bf16[128,896]{1,0:T(8,128)(2,1)S(1)}, u32[]{:S(2)}, u32[]{:S(2)}) %collective-permute-start.5) | collective-permute-done | bytes 229408 | tf_op jit(solution)/shard_map/ppermute | solution.py:32
  32.0 4.7 %project.5 = (bf16[400,896]{1,0:T(8,128)(2,1)}, f32[3,128,896]{2,1,0:T(8,128)S(1)}, f32[128,1]{1,0:T(8,128)S(1)}) custom-call(s32[3]{0:T(128)S(1)} %pad_add_fusion.place, bf16[128,896]{1,0:T(8,128)(2,1)S(1)} %broadcast_select_fusion.crossed, bf16[128,896]{1,0:T(8,128)(2,1)S(1)} %collective-permute-done.ringed, ...), custom_call_target="tpu_custom_call" | custom-call | flops 1150000 | bytes 1000 | tf_op jit(solution)/shard_map/project/pallas_call | solution.py:162
  36.7 3.5 %collective-permute-start.8 = (bf16[400,896]{1,0:T(8,128)(2,1)}, bf16[400,896]{1,0:T(8,128)(2,1)}, u32[]{:S(2)}, u32[]{:S(2)}) collective-permute-start(bf16[400,896]{1,0:T(8,128)(2,1)} %get-tuple-element.43), channel_id=1, source_target_pairs={{0,4},{1,5},{2,6},{3,7},{4,0},{5,1},{6,2},{7,3},{8,12},{9,13},{10,... | collective-permute-start | bytes 2150408 | tf_op jit(solution)/shard_map/ppermute | solution.py:32
  41.1 4.2 %collective-permute-start.10 = (bf16[128,896]{1,0:T(8,128)(2,1)S(1)}, bf16[128,896]{1,0:T(8,128)(2,1)}, u32[]{:S(2)}, u32[]{:S(2)}) collective-permute-start(bf16[128,896]{1,0:T(8,128)(2,1)S(1)} %get-tuple-element.47.refs_0_), channel_id=1, source_target_pairs={{0,8},{1,9},{2,12},{3,13},{4,10},{5,11},{6,14},{7,15},{8,16},{9,17... | collective-permute-start | bytes 688136 | tf_op jit(solution)/shard_map/ppermute | solution.py:32
  45.3 4.1 %collective-permute-done.10.crossed.first = bf16[128,896]{1,0:T(8,128)(2,1)} collective-permute-done((bf16[128,896]{1,0:T(8,128)(2,1)S(1)}, bf16[128,896]{1,0:T(8,128)(2,1)}, u32[]{:S(2)}, u32[]{:S(2)}) %collective-permute-start.10) | collective-permute-done | bytes 229408 | tf_op jit(solution)/shard_map/ppermute | solution.py:32
  49.4 1.6 %collective-permute-start.13 = (bf16[128,896]{1,0:T(8,128)(2,1)}, bf16[128,896]{1,0:T(8,128)(2,1)}, u32[]{:S(2)}, u32[]{:S(2)}) collective-permute-start(bf16[128,896]{1,0:T(8,128)(2,1)} %collective-permute-done.10.crossed.first), channel_id=1, source_target_pairs={{0,2},{1,3},{2,0},{3,1},{4,6},{5,7},{6,4},{7,5},{8,10},{9,11},{10,... | collective-permute-start | bytes 688136 | tf_op jit(solution)/shard_map/ppermute | solution.py:32
  51.1 5.7 %collective-permute-done.8.received = bf16[400,896]{1,0:T(8,128)(2,1)} collective-permute-done((bf16[400,896]{1,0:T(8,128)(2,1)}, bf16[400,896]{1,0:T(8,128)(2,1)}, u32[]{:S(2)}, u32[]{:S(2)}) %collective-permute-start.8) | collective-permute-done | bytes 716832 | tf_op jit(solution)/shard_map/ppermute | solution.py:32
  56.9 2.4 %attend.3 = (bf16[128,896]{1,0:T(8,128)(2,1)S(1)}, bf16[2,128,896]{2,1,0:T(8,128)(2,1)}) custom-call(f32[3,128,896]{2,1,0:T(8,128)S(1)} %get-tuple-element.42.kept, bf16[400,896]{1,0:T(8,128)(2,1)} %collective-permute-done.8.received, f32[128,1]{1,0:T(8,128)S(1)} %get-tuple-element.44.kept_mean, bf16[128,896]{1,0:T(8,128)(2,1)S(1)} %get-tuple-element.48.block, ...), custom_call_target="tpu_custom_call" | custom-call | flops 287500009472 | bytes 1000 | tf_op jit(solution)/shard_map/attend/pallas_call | solution.py:268
  59.3 8.6 %collective-permute-start.12 = (bf16[128,896]{1,0:T(8,128)(2,1)S(1)}, bf16[128,896]{1,0:T(8,128)(2,1)S(1)}, u32[]{:S(2)}, u32[]{:S(2)}) collective-permute-start(bf16[128,896]{1,0:T(8,128)(2,1)S(1)} %get-tuple-element.50.refs_1_), channel_id=1, source_target_pairs={{0,8},{1,9},{2,12},{3,13},{4,10},{5,11},{6,14},{7,15},{8,16},{9,17... | collective-permute-start | bytes 688136 | tf_op jit(solution)/shard_map/ppermute | solution.py:32
  68.9 4.5 %project.6 = (bf16[400,896]{1,0:T(8,128)(2,1)S(1)}, f32[3,128,896]{2,1,0:T(8,128)S(1)}, f32[128,1]{1,0:T(8,128)S(1)}) custom-call(s32[3]{0:T(128)S(1)} %copy-done.5, bf16[128,896]{1,0:T(8,128)(2,1)} %collective-permute-done.10.crossed.first, bf16[128,896]{1,0:T(8,128)(2,1)} %collective-permute-done.13.ringed, bf16[128,896]{1,0:T(8,128)(2,1)S(1)} %copy-done.10, ...), custom_call_target="tpu_custom_call" | custom-call | flops 3449999872 | bytes 1000 | tf_op jit(solution)/shard_map/project/pallas_call | solution.py:162
  74.8 6.5 %collective-permute-done.15.ringed = bf16[128,896]{1,0:T(8,128)(2,1)S(1)} collective-permute-done((bf16[128,896]{1,0:T(8,128)(2,1)S(1)}, bf16[128,896]{1,0:T(8,128)(2,1)S(1)}, u32[]{:S(2)}, u32[]{:S(2)}) %collective-permute-start.15) | collective-permute-done | bytes 229408 | tf_op jit(solution)/shard_map/ppermute | solution.py:32
  81.3 1.5 %collective-permute-done.17.sib_ringed = bf16[128,896]{1,0:T(8,128)(2,1)S(1)} collective-permute-done((bf16[128,896]{1,0:T(8,128)(2,1)S(1)}, bf16[128,896]{1,0:T(8,128)(2,1)S(1)}, u32[]{:S(2)}, u32[]{:S(2)}) %collective-permute-start.17) | collective-permute-done | bytes 229408 | tf_op jit(solution)/shard_map/ppermute | solution.py:32
  82.8 4.7 %project.7 = (bf16[400,896]{1,0:T(8,128)(2,1)}, f32[3,128,896]{2,1,0:T(8,128)S(1)}, f32[128,1]{1,0:T(8,128)S(1)}) custom-call(s32[3]{0:T(128)S(1)} %copy-done.5, bf16[128,896]{1,0:T(8,128)(2,1)S(1)} %collective-permute-done.12.crossed.second, bf16[128,896]{1,0:T(8,128)(2,1)S(1)} %collective-permute-done.15.ringed, ...), custom_call_target="tpu_custom_call" | custom-call | flops 1150000000 | bytes 1000 | tf_op jit(solution)/shard_map/project/pallas_call | solution.py:162
  87.5 1.7 %collective-permute-start.18 = (bf16[400,896]{1,0:T(8,128)(2,1)}, bf16[400,896]{1,0:T(8,128)(2,1)}, u32[]{:S(2)}, u32[]{:S(2)}) collective-permute-start(bf16[400,896]{1,0:T(8,128)(2,1)} %get-tuple-element.55), channel_id=1, source_target_pairs={{0,4},{1,5},{2,6},{3,7},{4,0},{5,1},{6,2},{7,3},{8,12},{9,13},{10,... | collective-permute-start | bytes 2150408 | tf_op jit(solution)/shard_map/ppermute | solution.py:32
  89.2 3.2 %collective-permute-done.19.received = bf16[400,896]{1,0:T(8,128)(2,1)S(1)} collective-permute-done((bf16[400,896]{1,0:T(8,128)(2,1)S(1)}, bf16[400,896]{1,0:T(8,128)(2,1)S(1)}, u32[]{:S(2)}, u32[]{:S(2)}) %collective-permute-start.19) | collective-permute-done | bytes 716832 | tf_op jit(solution)/shard_map/ppermute | solution.py:32
  94.6 12.5 %collective-permute-done.18.received = bf16[400,896]{1,0:T(8,128)(2,1)} collective-permute-done((bf16[400,896]{1,0:T(8,128)(2,1)}, bf16[400,896]{1,0:T(8,128)(2,1)}, u32[]{:S(2)}, u32[]{:S(2)}) %collective-permute-start.18) | collective-permute-done | bytes 716832 | tf_op jit(solution)/shard_map/ppermute | solution.py:32
  107.1 3.3 %final.1 = (bf16[256,896]{1,0:T(8,128)(2,1)}, bf16[2,128,896]{2,1,0:T(8,128)(2,1)}) custom-call(s32[3]{0:T(128)S(1)} %copy-done.6, s32[1]{0:T(128)S(6)} %copy.5.flag, f32[3,128,896]{2,1,0:T(8,128)S(1)} %get-tuple-element.54.kept, bf16[400,896]{1,0:T(8,128)(2,1)} %collective-permute-done.18.received, f32[128,1]{1,0:T(8,128)S(1)} %get-tuple-element.56.kept_mean, ...), custom_call_target="tpu_custom_call" | custom-call | flops 287500009472 | bytes 1000 | tf_op jit(solution)/shard_map/final/pallas_call | solution.py:268
  (54 shorter events, 9.3 us)
Async XLA Ops:
  1.1 12.8 %collective-permute-start.1 = (bf16[128,896]{1,0:T(8,128)(2,1)S(1)}, bf16[128,896]{1,0:T(8,128)(2,1)S(1)}, u32[]{:S(2)}, u32[]{:S(2)}) collective-permute-start(bf16[128,896]{1,0:T(8,128)(2,1)S(1)} %get-tuple-element.63.block), channel_id=1, source_target_pairs={{0,2},{1,3},{2,6},{3,7},{4,0},{5,1},{6,4},{7,5},{8,10},{9,11},{10,... | collective-permute-start | bytes 688136 | tf_op jit(solution)/shard_map/ppermute | solution.py:32
  4.1 9.8 %collective-permute-start.2 = (bf16[128,896]{1,0:T(8,128)(2,1)S(1)}, bf16[128,896]{1,0:T(8,128)(2,1)S(1)}, u32[]{:S(2)}, u32[]{:S(2)}) collective-permute-start(bf16[128,896]{1,0:T(8,128)(2,1)S(1)} %get-tuple-element.63.block), channel_id=1, source_target_pairs={{0,0},{1,1},{2,4},{3,5},{4,2},{5,3},{6,6},{7,7},{8,8},{9,9},{10,12... | collective-permute-start | bytes 688136 | tf_op jit(solution)/shard_map/ppermute | solution.py:32
  4.9 27.2 %copy-start.4 = (s32[3]{0:T(128)}, s32[3]{0:T(128)S(1)}, u32[]{:S(2)}) copy-start(s32[3]{0:T(128)S(1)} %pad_add_fusion.place) | copy-start | bytes 40
  13.9 3.0 %collective-permute-start.3 = (bf16[128,896]{1,0:T(8,128)(2,1)S(1)}, bf16[128,896]{1,0:T(8,128)(2,1)S(1)}, u32[]{:S(2)}, u32[]{:S(2)}) collective-permute-start(bf16[128,896]{1,0:T(8,128)(2,1)S(1)} %collective-permute-done.2.crossed), channel_id=1, source_target_pairs={{0,1},{1,0},{2,3},{3,2},{4,5},{5,4},{6,7},{7,6},{8,9},{9,8},{10,11... | collective-permute-start | bytes 688136 | tf_op jit(solution)/shard_map/ppermute | solution.py:32
  13.9 3.0 %collective-permute-start.4 = (bf16[128,896]{1,0:T(8,128)(2,1)S(1)}, bf16[128,896]{1,0:T(8,128)(2,1)S(1)}, u32[]{:S(2)}, u32[]{:S(2)}) collective-permute-start(bf16[128,896]{1,0:T(8,128)(2,1)S(1)} %collective-permute-done.1.ringed), channel_id=1, source_target_pairs={{0,1},{1,0},{2,3},{3,2},{4,5},{5,4},{6,7},{7,6},{8,9},{9,8},{10,11... | collective-permute-start | bytes 688136 | tf_op jit(solution)/shard_map/ppermute | solution.py:32
  14.4 9.1 %collective-permute-start = (bf16[128,896]{1,0:T(8,128)(2,1)S(1)}, bf16[128,896]{1,0:T(8,128)(2,1)S(1)}, u32[]{:S(2)}, u32[]{:S(2)}) collective-permute-start(bf16[128,896]{1,0:T(8,128)(2,1)S(1)} %get-tuple-element.48.block), channel_id=1, source_target_pairs={{0,2},{1,3},{2,6},{3,7},{4,0},{5,1},{6,4},{7,5},{8,10},{9,11},{10,... | collective-permute-start | bytes 688136 | tf_op jit(solution)/shard_map/ppermute | solution.py:32
  20.9 19.3 %collective-permute-start.9 = (bf16[400,896]{1,0:T(8,128)(2,1)S(1)}, bf16[400,896]{1,0:T(8,128)(2,1)S(1)}, u32[]{:S(2)}, u32[]{:S(2)}) collective-permute-start(bf16[400,896]{1,0:T(8,128)(2,1)S(1)} %get-tuple-element.46), channel_id=1, source_target_pairs={{0,4},{1,5},{2,6},{3,7},{4,0},{5,1},{6,2},{7,3},{8,12},{9,13},{10,... | collective-permute-start | bytes 2150408 | tf_op jit(solution)/shard_map/ppermute | solution.py:32
  23.6 6.9 %collective-permute-start.5 = (bf16[128,896]{1,0:T(8,128)(2,1)S(1)}, bf16[128,896]{1,0:T(8,128)(2,1)S(1)}, u32[]{:S(2)}, u32[]{:S(2)}) collective-permute-start(bf16[128,896]{1,0:T(8,128)(2,1)S(1)} %collective-permute-done.ringed), channel_id=1, source_target_pairs={{0,2},{1,3},{6,4},{7,5},{8,10},{9,11},{14,12},{15,13},{16,18},{17,... | collective-permute-start | bytes 688136 | tf_op jit(solution)/shard_map/ppermute | solution.py:32
  26.3 4.3 %collective-permute-start.7 = (bf16[128,896]{1,0:T(8,128)(2,1)S(1)}, bf16[128,896]{1,0:T(8,128)(2,1)S(1)}, u32[]{:S(2)}, u32[]{:S(2)}) collective-permute-start(bf16[128,896]{1,0:T(8,128)(2,1)S(1)} %collective-permute-done.ringed), channel_id=1, source_target_pairs={{0,1},{1,0},{2,3},{3,2},{4,5},{5,4},{6,7},{7,6},{8,9},{9,8},{10,11... | collective-permute-start | bytes 688136 | tf_op jit(solution)/shard_map/ppermute | solution.py:32
  30.5 1.6 %collective-permute-start.6 = (bf16[128,896]{1,0:T(8,128)(2,1)S(1)}, bf16[128,896]{1,0:T(8,128)(2,1)S(1)}, u32[]{:S(2)}, u32[]{:S(2)}) collective-permute-start(bf16[128,896]{1,0:T(8,128)(2,1)S(1)} %broadcast_select_fusion.crossed), channel_id=1, source_target_pairs={{0,1},{1,0},{2,3},{3,2},{4,5},{5,4},{6,7},{7,6},{8,9},{9,8},{10,11... | collective-permute-start | bytes 688136 | tf_op jit(solution)/shard_map/ppermute | solution.py:32
  36.7 20.1 %collective-permute-start.8 = (bf16[400,896]{1,0:T(8,128)(2,1)}, bf16[400,896]{1,0:T(8,128)(2,1)}, u32[]{:S(2)}, u32[]{:S(2)}) collective-permute-start(bf16[400,896]{1,0:T(8,128)(2,1)} %get-tuple-element.43), channel_id=1, source_target_pairs={{0,4},{1,5},{2,6},{3,7},{4,0},{5,1},{6,2},{7,3},{8,12},{9,13},{10,... | collective-permute-start | bytes 2150408 | tf_op jit(solution)/shard_map/ppermute | solution.py:32
  41.1 18.2 %copy-start.7 = (bf16[128,896]{1,0:T(8,128)(2,1)}, bf16[128,896]{1,0:T(8,128)(2,1)S(1)}, u32[]{:S(2)}) copy-start(bf16[128,896]{1,0:T(8,128)(2,1)S(1)} %get-tuple-element.47.refs_0_) | copy-start | bytes 688132
  41.1 8.4 %collective-permute-start.10 = (bf16[128,896]{1,0:T(8,128)(2,1)S(1)}, bf16[128,896]{1,0:T(8,128)(2,1)}, u32[]{:S(2)}, u32[]{:S(2)}) collective-permute-start(bf16[128,896]{1,0:T(8,128)(2,1)S(1)} %get-tuple-element.47.refs_0_), channel_id=1, source_target_pairs={{0,8},{1,9},{2,12},{3,13},{4,10},{5,11},{6,14},{7,15},{8,16},{9,17... | collective-permute-start | bytes 688136 | tf_op jit(solution)/shard_map/ppermute | solution.py:32
  49.4 1.7 %collective-permute-start.11 = (bf16[128,896]{1,0:T(8,128)(2,1)}, bf16[128,896]{1,0:T(8,128)(2,1)S(1)}, u32[]{:S(2)}, u32[]{:S(2)}) collective-permute-start(bf16[128,896]{1,0:T(8,128)(2,1)} %collective-permute-done.10.crossed.first), channel_id=1, source_target_pairs={{0,1},{1,0},{2,3},{3,2},{4,5},{5,4},{6,7},{7,6},{8,9},{9,8},{10,11... | collective-permute-start | bytes 688136 | tf_op jit(solution)/shard_map/ppermute | solution.py:32
  49.4 9.8 %collective-permute-start.13 = (bf16[128,896]{1,0:T(8,128)(2,1)}, bf16[128,896]{1,0:T(8,128)(2,1)}, u32[]{:S(2)}, u32[]{:S(2)}) collective-permute-start(bf16[128,896]{1,0:T(8,128)(2,1)} %collective-permute-done.10.crossed.first), channel_id=1, source_target_pairs={{0,2},{1,3},{2,0},{3,1},{4,6},{5,7},{6,4},{7,5},{8,10},{9,11},{10,... | collective-permute-start | bytes 688136 | tf_op jit(solution)/shard_map/ppermute | solution.py:32
  59.3 8.7 %collective-permute-start.14 = (bf16[128,896]{1,0:T(8,128)(2,1)}, bf16[128,896]{1,0:T(8,128)(2,1)S(1)}, u32[]{:S(2)}, u32[]{:S(2)}) collective-permute-start(bf16[128,896]{1,0:T(8,128)(2,1)} %collective-permute-done.13.ringed), channel_id=1, source_target_pairs={{0,1},{1,0},{2,3},{3,2},{4,5},{5,4},{6,7},{7,6},{8,9},{9,8},{10,11... | collective-permute-start | bytes 688136 | tf_op jit(solution)/shard_map/ppermute | solution.py:32
  59.3 14.2 %collective-permute-start.12 = (bf16[128,896]{1,0:T(8,128)(2,1)S(1)}, bf16[128,896]{1,0:T(8,128)(2,1)S(1)}, u32[]{:S(2)}, u32[]{:S(2)}) collective-permute-start(bf16[128,896]{1,0:T(8,128)(2,1)S(1)} %get-tuple-element.50.refs_1_), channel_id=1, source_target_pairs={{0,8},{1,9},{2,12},{3,13},{4,10},{5,11},{6,14},{7,15},{8,16},{9,17... | collective-permute-start | bytes 688136 | tf_op jit(solution)/shard_map/ppermute | solution.py:32
  73.4 19.0 %collective-permute-start.19 = (bf16[400,896]{1,0:T(8,128)(2,1)S(1)}, bf16[400,896]{1,0:T(8,128)(2,1)S(1)}, u32[]{:S(2)}, u32[]{:S(2)}) collective-permute-start(bf16[400,896]{1,0:T(8,128)(2,1)S(1)} %get-tuple-element.58), channel_id=1, source_target_pairs={{0,4},{1,5},{2,6},{3,7},{4,0},{5,1},{6,2},{7,3},{8,12},{9,13},{10,... | collective-permute-start | bytes 2150408 | tf_op jit(solution)/shard_map/ppermute | solution.py:32
  73.5 18.9 %copy-start.8 = (bf16[128,896]{1,0:T(8,128)(2,1)S(1)}, bf16[128,896]{1,0:T(8,128)(2,1)}, u32[]{:S(2)}) copy-start(bf16[128,896]{1,0:T(8,128)(2,1)} %copy-done.7) | copy-start | bytes 688132
  73.6 7.8 %collective-permute-start.15 = (bf16[128,896]{1,0:T(8,128)(2,1)S(1)}, bf16[128,896]{1,0:T(8,128)(2,1)S(1)}, u32[]{:S(2)}, u32[]{:S(2)}) collective-permute-start(bf16[128,896]{1,0:T(8,128)(2,1)S(1)} %collective-permute-done.12.crossed.second), channel_id=1, source_target_pairs={{0,2},{1,3},{2,0},{3,1},{4,6},{5,7},{6,4},{7,5},{8,10},{9,11},{10,... | collective-permute-start | bytes 688136 | tf_op jit(solution)/shard_map/ppermute | solution.py:32
  74.8 6.5 %collective-permute-start.16 = (bf16[128,896]{1,0:T(8,128)(2,1)S(1)}, bf16[128,896]{1,0:T(8,128)(2,1)S(1)}, u32[]{:S(2)}, u32[]{:S(2)}) collective-permute-start(bf16[128,896]{1,0:T(8,128)(2,1)S(1)} %collective-permute-done.12.crossed.second), channel_id=1, source_target_pairs={{0,1},{1,0},{2,3},{3,2},{4,5},{5,4},{6,7},{7,6},{8,9},{9,8},{10,11... | collective-permute-start | bytes 688136 | tf_op jit(solution)/shard_map/ppermute | solution.py:32
  81.3 1.5 %collective-permute-start.17 = (bf16[128,896]{1,0:T(8,128)(2,1)S(1)}, bf16[128,896]{1,0:T(8,128)(2,1)S(1)}, u32[]{:S(2)}, u32[]{:S(2)}) collective-permute-start(bf16[128,896]{1,0:T(8,128)(2,1)S(1)} %collective-permute-done.15.ringed), channel_id=1, source_target_pairs={{0,1},{1,0},{2,3},{3,2},{4,5},{5,4},{6,7},{7,6},{8,9},{9,8},{10,11... | collective-permute-start | bytes 688136 | tf_op jit(solution)/shard_map/ppermute | solution.py:32
  87.5 19.6 %collective-permute-start.18 = (bf16[400,896]{1,0:T(8,128)(2,1)}, bf16[400,896]{1,0:T(8,128)(2,1)}, u32[]{:S(2)}, u32[]{:S(2)}) collective-permute-start(bf16[400,896]{1,0:T(8,128)(2,1)} %get-tuple-element.55), channel_id=1, source_target_pairs={{0,4},{1,5},{2,6},{3,7},{4,0},{5,1},{6,2},{7,3},{8,12},{9,13},{10,... | collective-permute-start | bytes 2150408 | tf_op jit(solution)/shard_map/ppermute | solution.py:32
  93.2 1.3 %collective-permute-start.20 = (bf16[256,896]{1,0:T(8,128)(2,1)S(1)}, bf16[256,896]{1,0:T(8,128)(2,1)S(1)}, u32[]{:S(2)}, u32[]{:S(2)}) collective-permute-start(bf16[256,896]{1,0:T(8,128)(2,1)S(1)} %get-tuple-element.61.own), channel_id=1, source_target_pairs={{2,10},{3,11},{4,12},{5,13},{10,18},{11,19},{12,20},{13,21},{18,26... | collective-permute-start | bytes 1376264 | tf_op jit(solution)/shard_map/ppermute | solution.py:32
  (9 other events, 102.7 us)

commit v9 on v8

--- a/solution.py
+++ b/solution.py
@@ -13,9 +13,12 @@
 AXES = ("section", "dp", "tensor")
 F32 = jnp.float32
 BF16 = jnp.bfloat16
-PARTS = 2
 VMEM_BYTES = 16 * 1024 * 1024
 STAT_ROWS = 16
+
+
+def chunk_rows(length):
+    return [length * 7 // 16, length * 5 // 16, length // 4]
 
 
 def permute(array, sections, hop):
@@ -103,7 +106,7 @@
     )(place, pltpu.with_memory_space_constraint(weight, pltpu.HBM))
 
 
-def project_kernel(place, crossed, ringed, sib_crossed, sib_ringed, gain, weight, *refs):
+def project_kernel(start, place, crossed, ringed, sib_crossed, sib_ringed, gain, weight, *refs):
     sent, kept, kept_mean, normed = refs[:4]
     out, semaphores = refs[4:] or (sent, None)
     rows = normed.shape[0] // 2
@@ -116,7 +119,7 @@
         (ringed, sib_ringed, 1 - diagonal),
     ):
         at = pl.ds(pl.multiple_of(offset * rows, rows), rows)
-        pieces = [ref[...].astype(F32) for ref in (mine, theirs)]
+        pieces = [ref[start : start + rows].astype(F32) for ref in (mine, theirs)]
         squares = sum(jnp.sum(piece * piece, axis=-1, keepdims=True) for piece in pieces)
         mean = squares * (1.0 / half)
         means.append(mean)
@@ -129,14 +132,17 @@
     on_diagonal = diagonal == 1
     sent_mean = jnp.where(on_diagonal, means[1], means[0])
     kept_mean[...] = jnp.where(on_diagonal, means[0], means[1])
-    row = jnp.transpose(jnp.broadcast_to(sent_mean, (rows, HD)))[:STAT_ROWS]
+    wide = jnp.broadcast_to(sent_mean, (rows, HD))
+    if rows < HD:
+        wide = jnp.concatenate([wide, jnp.zeros((HD - rows, HD), F32)])
+    row = jnp.transpose(wide)[:STAT_ROWS]
     high = row.astype(BF16).astype(F32)
     mid = (row - high).astype(BF16).astype(F32)
     low = row - high - mid
     which = lax.broadcasted_iota(jnp.int32, row.shape, 0)
     stat = jnp.where(which == 0, high, jnp.where(which == 1, mid, low)).astype(BF16)
-    for begin in range(0, width, rows):
-        out[:STAT_ROWS, begin : begin + rows] = stat
+    for begin in range(0, width, HD):
+        out[:STAT_ROWS, begin : begin + HD] = stat
     split = width // (2 * HD) * HD + HD
     copies = []
     for i, (k, begin, end) in enumerate(
@@ -156,11 +162,11 @@
         copy.wait()
 
 
-def project(rows, place, four, gain, weight, apart, estimate):
+def project(start, rows, place, four, gain, weight, apart, estimate):
     width = four[0].shape[1]
     sent_shape = (3 * rows + STAT_ROWS, width)
     return pl.pallas_call(
-        project_kernel,
+        functools.partial(project_kernel, start),
         in_specs=[smem_spec()] + [vmem_spec()] * 6,
         out_specs=[any_spec() if apart else vmem_spec(), vmem_spec(), vmem_spec()],
         out_shape=[
@@ -178,16 +184,26 @@
 
 def mix(kept, received, kept_mean, earlier, pairs, put):
     rows, width = kept.shape[1:]
-    stat = received[:STAT_ROWS, :rows].astype(F32)
+    stat = received[:STAT_ROWS, :HD].astype(F32)
     row = stat[0:1] + stat[1:2] + stat[2:3]
-    mean_peer = jnp.transpose(jnp.broadcast_to(row, (HD, rows)))[:, :1]
+    mean_peer = jnp.transpose(jnp.broadcast_to(row, (HD, HD)))[:rows, :1]
     mean_kept = kept_mean[...]
     inverse = lax.rsqrt((mean_kept + mean_peer) * 0.5 + EPS)
     scale_kept = inverse * jnp.sqrt(mean_kept + EPS)
     scale_peer = inverse * jnp.sqrt(mean_peer + EPS)
-    causal = lax.broadcasted_iota(jnp.int32, (rows, rows), 0) >= lax.broadcasted_iota(
-        jnp.int32, (rows, rows), 1
+    start = sum(ref.shape[1] for ref in earlier)
+    padding = -(start + rows) % HD
+    shape = (rows, start + rows + padding)
+    causal = lax.broadcasted_iota(jnp.int32, shape, 0) + start >= lax.broadcasted_iota(
+        jnp.int32, shape, 1
     )
+
+    def together(k, at, last):
+        pieces = [ref[k, :, at] for ref in earlier] + [last]
+        if padding:
+            pieces.append(jnp.zeros((padding, HD), BF16))
+        return jnp.concatenate(pieces) if len(pieces) > 1 else last
+
     heads = [slice(begin, begin + HD) for begin in range(0, width, HD)]
     held, scores = [], []
     for at in heads:
@@ -201,27 +217,16 @@
         )
         pairs[0, :, at] = keys
         pairs[1, :, at] = values
-        held.append([(ref[0, :, at], ref[1, :, at]) for ref in earlier] + [(keys, values)])
-        scores.append(
-            [
-                lax.dot_general(queries, key, (((1,), (1,)), ((), ())), preferred_element_type=F32)
-                * (1.0 / math.sqrt(HD))
-                for key, _ in held[-1]
-            ]
+        held.append(together(1, at, values))
+        score = lax.dot_general(
+            queries, together(0, at, keys), (((1,), (1,)), ((), ())), preferred_element_type=F32
         )
-        scores[-1][-1] = jnp.where(causal, scores[-1][-1], F32(-1e30))
-    tops = [
-        functools.reduce(jnp.maximum, [jnp.max(item, axis=-1, keepdims=True) for item in score])
-        for score in scores
-    ]
-    raised = [[jnp.exp(item - top) for item in score] for score, top in zip(scores, tops)]
-    overs = [1.0 / sum(jnp.sum(item, axis=-1, keepdims=True) for item in items) for items in raised]
-    for at, items, over, pair in zip(heads, raised, overs, held):
-        mixture = sum(
-            jnp.dot((item * over).astype(BF16), value, preferred_element_type=F32)
-            for item, (_, value) in zip(items, pair)
-        )
-        put(at, mixture)
+        scores.append(jnp.where(causal, score * (1.0 / math.sqrt(HD)), F32(-1e30)))
+    tops = [jnp.max(score, axis=-1, keepdims=True) for score in scores]
+    raised = [jnp.exp(score - top) for score, top in zip(scores, tops)]
+    overs = [1.0 / jnp.sum(item, axis=-1, keepdims=True) for item in raised]
+    for at, item, over, values in zip(heads, raised, overs, held):
+        put(at, jnp.dot((item * over).astype(BF16), values, preferred_element_type=F32))
 
 
 def attend_kernel(kept, received, kept_mean, block, *refs):
@@ -233,35 +238,43 @@
     mix(kept, received, kept_mean, earlier, pairs, put)
 
 
-def hold_kernel(kept, received, kept_mean, *refs):
-    owns, (held, pairs, whole) = refs[:-3], refs[-3:]
-    rows = kept.shape[1]
+def hold_kernel(count, kept, received, kept_mean, *refs):
+    earlier = refs[:count]
+    if count:
+        owns, (held, pairs) = (), refs[count:]
+    else:
+        owns, (held, pairs, whole) = refs[:-3], refs[-3:]
 
     def put(at, mixture):
         held[:, at] = mixture
 
-    mix(kept, received, kept_mean, (), pairs, put)
-    for i, own in enumerate(owns):
-        whole[i * rows : (i + 1) * rows] = own[...]
-
-
-def final_kernel(
-    place, flag, kept, received, kept_mean, earlier, held, first, second, before, own, out, pairs
-):
-    rows = kept.shape[1]
+    mix(kept, received, kept_mean, earlier, pairs, put)
+    begin = 0
+    for own in owns:
+        whole[begin : begin + own.shape[0]] = own[...]
+        begin += own.shape[0]
+
+
+def final_kernel(count, place, flag, kept, received, kept_mean, *refs):
+    earlier, mixtures, crossed = refs[:count], refs[count : 2 * count], refs[2 * count : -4]
+    before, own, out, pairs = refs[-4:]
     diagonal, shadow = place[2] == 1, flag[0] == 1
 
-    def settle(start, crossed, at, mixture):
-        here = slice(start, start + rows)
-        residual = jnp.where(diagonal, crossed[:, at].astype(F32), before[here, at].astype(F32))
+    def settle(start, arrived, at, mixture):
+        here = slice(start, start + arrived.shape[0])
+        residual = jnp.where(diagonal, arrived[:, at].astype(F32), before[here, at].astype(F32))
         result = jnp.where(shadow, residual + mixture, own[here, at].astype(F32))
         out[here, at] = result.astype(BF16)
 
+    begin = 0
+    for arrived, mixture in zip(crossed, mixtures):
+        settle(begin, arrived, slice(None), mixture[...])
+        begin += arrived.shape[0]
+
     def put(at, mixture):
-        settle(rows, second, at, mixture)
-
-    settle(0, first, slice(None), held[...])
-    mix(kept, received, kept_mean, (earlier,), pairs, put)
+        settle(begin, crossed[-1], at, mixture)
+
+    mix(kept, received, kept_mean, earlier, pairs, put)
 
 
 def call_attend(kernel, name, scalars, arrays, out_shape):
@@ -294,62 +307,105 @@
                 permute(ringed, sections, sibling),
             )
 
-        def partial(four, apart, estimate):
-            sent, kept, kept_mean = project(rows, place, four, norm_gain, weight, apart, estimate)
+        def partial(start, rows, four, apart, estimate):
+            sent, kept, kept_mean = project(
+                start, rows, place, four, norm_gain, weight, apart, estimate
+            )
             return kept, permute(sent, sections, peer), kept_mean
 
         block = inputs[0, 0]
-        rows = block.shape[0] // PARTS
-        parts = [block[i * rows : (i + 1) * rows] for i in range(PARTS)]
-        ringed = [permute(part, sections, ring) for part in parts]
+        length, width = block.shape
+        sizes = chunk_rows(length)
+        begins = [sum(sizes[:i]) for i in range(len(sizes))]
+        parts = [block[begin : begin + size] for begin, size in zip(begins, sizes)]
+        ringed = permute(parts[0], sections, ring)
         crossed = permute(parts[0], sections, cross)
-        ringed[0], crossed, weight = lax.optimization_barrier((ringed[0], crossed, weight))
+        others = block[sizes[0] :]
+        late = permute(others, sections, ring)
+        crossed, ringed, weight = lax.optimization_barrier((crossed, ringed, weight))
         weight = pltpu.with_memory_space_constraint(weight, pltpu.VMEM)
-        sums = [partial(spread(crossed, ringed[0]), False, 3)]
-        late, _ = lax.optimization_barrier((ringed[1], sums[0][2]))
-        forwarded = permute(late, sections, forward)
-        crossed = jnp.where(diagonal, parts[1], forwarded)
-        sums.append(partial(spread(crossed, late), True, 0.001))
-        width = block.shape[1]
-        rows_of = pltpu.VMEM((rows, width), BF16)
-        pairs_of = pltpu.VMEM((2, rows, width), BF16)
-
-        def attend(part, item, held):
+        sums = [partial(0, sizes[0], spread(crossed, ringed), False, 3)]
+        late, _ = lax.optimization_barrier((late, sums[0][2]))
+        crossed = jnp.where(diagonal, others, permute(late, sections, forward))
+        four = spread(crossed, late)
+        for begin, size in zip(begins[1:-1], sizes[1:-1]):
+            *four, _ = lax.optimization_barrier((*four, sums[-1][2]))
+            sums.append(partial(begin - sizes[0], size, four, True, 0.001))
+
+        def pairs_of(size):
+            return pltpu.VMEM((2, size, width), BF16)
+
+        def attend(i, part, held):
             return call_attend(
-                attend_kernel, "attend", [], [*item, part, *held], [rows_of, pairs_of]
+                attend_kernel,
+                "attend",
+                [],
+                [*sums[i], part, *held],
+                [pltpu.VMEM((sizes[i], width), BF16), pairs_of(sizes[i])],
             )
 
-        def carry(own):
-            return permute(own, sections, onward(cross))
-
-        first, pairs = attend(parts[0], sums[0], [])
-        moved = [carry(first)]
-        swapped = permute(moved[0], sections, swap)
-        beside = permute(moved[0], sections, sibling)
-        part = lax.optimization_barrier((parts[1], beside))[0]
-        second, _ = attend(part, sums[1], [pairs])
-        owns = [first, second]
-        moved.append(carry(second))
-        swapped, _ = lax.optimization_barrier((swapped, second))
-        four = moved[0], swapped, beside, permute(swapped, sections, sibling)
-        seconds = [partial(four, False, 3)]
-        crossed, _ = lax.optimization_barrier((moved[1], seconds[0][2]))
-        swapped = permute(crossed, sections, swap)
-        seconds.append(partial(spread(crossed, swapped), True, 1))
-        mixture, pairs, own = call_attend(
-            hold_kernel,
-            "hold",
-            [],
-            [*seconds[0], *owns],
-            [pltpu.VMEM((rows, width), F32), pairs_of, pltpu.VMEM(block.shape, BF16)],
-        )
-        before = permute(own, sections, onward(direct))
+        part, _ = lax.optimization_barrier((parts[0], sums[-1][2]))
+        own, pairs = attend(0, part, [])
+        owns, held = [own], [pairs]
+        moved = [permute(own, sections, onward(cross))]
+        *four, _ = lax.optimization_barrier((*four, own))
+        sums.append(partial(begins[-1] - sizes[0], sizes[-1], four, True, 0.001))
+
+        mixtures, mixed, seconds = [], [], []
+
+        def hold(i, after):
+            shapes = [pltpu.VMEM((sizes[i], width), F32), pairs_of(sizes[i])]
+            if not i:
+                shapes.append(pltpu.VMEM(block.shape, BF16))
+            kept, received, kept_mean = seconds[i]
+            kept, _ = lax.optimization_barrier((kept, after))
+            mixture, pairs, *first = call_attend(
+                functools.partial(hold_kernel, i),
+                "hold",
+                [],
+                [kept, received, kept_mean, *mixed, *(owns if not i else [])],
+                shapes,
+            )
+            mixtures.append(mixture)
+            mixed.append(pairs)
+            return first
+
+        for i, size in enumerate(sizes):
+            crossed = moved[i]
+            last = i + 1 == len(sizes)
+            if not i:
+                crossed, _ = lax.optimization_barrier((crossed, sums[-1][2]))
+            else:
+                if last:
+                    (whole,) = hold(0, seconds[-1][2])
+                    after = mixtures[0]
+                else:
+                    part, _ = lax.optimization_barrier((parts[i + 1], seconds[-1][2]))
+                    own, pairs = attend(i + 1, part, held)
+                    after = own
+                crossed, _ = lax.optimization_barrier((crossed, after))
+            swapped = permute(crossed, sections, swap)
+            beside = permute(crossed, sections, sibling)
+            if not i:
+                part, _, _ = lax.optimization_barrier((parts[1], beside, sums[-1][2]))
+                own, pairs = attend(1, part, held)
+            if not last:
+                owns.append(own)
+                held.append(pairs)
+                on_its_way, _ = lax.optimization_barrier((own, beside))
+                moved.append(permute(on_its_way, sections, onward(cross)))
+                swapped, _ = lax.optimization_barrier((swapped, own))
+            four = crossed, swapped, beside, permute(swapped, sections, sibling)
+            seconds.append(partial(0, size, four, bool(i), 0.001 if i else 3))
+        for i in range(1, len(sizes) - 1):
+            hold(i, seconds[-1][2])
+        before = permute(whole, sections, onward(direct))
         out, _ = call_attend(
-            final_kernel,
+            functools.partial(final_kernel, len(mixtures)),
             "final",
             [place, preempted],
-            [*seconds[1], pairs, mixture, *moved, before, own],
-            [jax.ShapeDtypeStruct(block.shape, BF16), pairs_of],
+            [*seconds[-1], *mixed, *mixtures, *moved, before, whole],
+            [jax.ShapeDtypeStruct(block.shape, BF16), pairs_of(sizes[-1])],
         )
         return out[None, None]
 

time: 111 us -> 121 us (1.090)
  Pallas kernels: 29.5 us -> 40.2 us
  waiting for transfers between devices: 44.4 us -> 35.6 us
  starting transfers between devices: 33.4 us -> 39.6 us
  local copies, waits for them, and re-layouts: 2.06 us -> 3.55 us
    ppermute x21 -> x27, waiting for transfers between devices: 44.4 us -> 35.6 us  [permute(): return lax.ppermute(array, AXES, pairs)]
    pallas_call x4 -> x6, Pallas kernels: 7.32 us -> 13.6 us  [call_attend(): pl.pallas_call(kernel, in_specs=[smem_spec() for _ in scalars] + [vmem_sp...]
    ppermute x21 -> x27, starting transfers between devices: 33.4 us -> 39.6 us  [permute(): return lax.ppermute(array, AXES, pairs)]
    pallas_call x4 -> x6, Pallas kernels: 17.9 us -> 22.2 us  [project(): pl.pallas_call(functools.partial(project_kernel, start), in_specs=[smem_s...]
    slice x1 -> x4, local copies, waits for them, and re-layouts: 1.09 us -> 2.8 us  [the longest x3 2.78 us: local(): parts = [block[begin:begin + size] for begin, size in zip(begins, sizes)]]
  transfers between devices with their start and end apart: 21 -> 27, of which waited for: 11 -> 9; matrix products, arithmetic and copies ran while one was open for 0% -> 2% of each run, Pallas kernels for 24% -> 31%
where the time goes in v9:
time: 121 us; the launch traced here: 120 us
  Pallas kernels  40.2 us (33%)
  starting transfers between devices  39.6 us (33%)
  waiting for transfers between devices  35.6 us (29%)
  local copies, waits for them, and re-layouts  3.55 us (3%)
    ppermute x27, starting transfers between devices, permute(): return lax.ppermute(array, AXES, pairs)  39.6 us
    ppermute x27, waiting for transfers between devices, permute(): return lax.ppermute(array, AXES, pairs)  35.6 us
    pallas_call x6, Pallas kernels, project(): pl.pallas_call(functools.partial(project_kernel, start), in_specs=[smem_s...  22.2 us
    pallas_call x6, Pallas kernels, call_attend(): pl.pallas_call(kernel, in_specs=[smem_spec() for _ in scalars] + [vmem_sp...  13.6 us
    pallas_call x1, Pallas kernels, stage(): pl.pallas_call(stage_kernel, in_specs=[smem_spec(), any_spec()], out_spec...  4.31 us
    slice x3, local copies, waits for them, and re-layouts, local(): parts = [block[begin:begin + size] for begin, size in zip(begins, sizes)]  2.78 us
  transfers between devices with their start and end apart: 27, of which 9 were waited for; matrix products, arithmetic and copies ran while one was open for 2% of the time, Pallas kernels for 31%

profile of v9, /device:TPU:0, one launch (start us, length us, event | category | flops | bytes accessed | tf_op | source)
XLA Modules:
  0.0 120.0 jit_solution(1373292469816801975)
XLA Ops:
  0.9 3.0 %collective-permute-start.2 = (bf16[112,896]{1,0:T(8,128)(2,1)S(1)}, bf16[112,896]{1,0:T(8,128)(2,1)S(1)}, u32[]{:S(2)}, u32[]{:S(2)}) collective-permute-start(bf16[112,896]{1,0:T(8,128)(2,1)S(1)} %slice_bitcast_fusion.1.block), channel_id=1, source_target_pairs={{0,2},{1,3},{2,6},{3,7},{4,0},{5,1},{6,4},{7,5},{8,10},{9,11},{10,... | collective-permute-start | bytes 602120 | tf_op jit(solution)/shard_map/ppermute | solution.py:35
  4.7 4.3 %stage.1.weight = bf16[1,3,1792,896]{3,2,1,0:T(8,128)(2,1)S(1)} custom-call(s32[3]{0:T(128)S(1)} %pad_add_fusion.place, bf16[1,3,1792,896]{3,2,1,0:T(8,128)(2,1)} %weight), custom_call_target="tpu_custom_call" | custom-call | flops 4600000000 | bytes 1000 | tf_op jit(solution)/shard_map/stage/pallas_call | solution.py:97
  9.1 3.5 %collective-permute-done.2.ringed = bf16[112,896]{1,0:T(8,128)(2,1)S(1)} collective-permute-done((bf16[112,896]{1,0:T(8,128)(2,1)S(1)}, bf16[112,896]{1,0:T(8,128)(2,1)S(1)}, u32[]{:S(2)}, u32[]{:S(2)}) %collective-permute-start.2) | collective-permute-done | bytes 200736 | tf_op jit(solution)/shard_map/ppermute | solution.py:35
  15.6 3.6 %project.6 = (bf16[352,896]{1,0:T(8,128)(2,1)S(1)}, f32[3,112,896]{2,1,0:T(8,128)S(1)}, f32[112,1]{1,0:T(8,128)S(1)}) custom-call(s32[3]{0:T(128)S(1)} %pad_add_fusion.place, bf16[112,896]{1,0:T(8,128)(2,1)S(1)} %collective-permute-done.1.crossed, bf16[112,896]{1,0:T(8,128)(2,1)S(1)} %collective-permute-done.2.ringed, ...), custom_call_target="tpu_custom_call" | custom-call | flops 3449999872 | bytes 1000 | tf_op jit(solution)/shard_map/project/pallas_call | solution.py:168
  19.3 3.6 %collective-permute-done.ringed = bf16[144,896]{1,0:T(8,128)(2,1)S(1)} collective-permute-done((bf16[144,896]{1,0:T(8,128)(2,1)S(1)}, bf16[144,896]{1,0:T(8,128)(2,1)S(1)}, u32[]{:S(2)}, u32[]{:S(2)}) %collective-permute-start) | collective-permute-done | bytes 258080 | tf_op jit(solution)/shard_map/ppermute | solution.py:35
  22.9 2.7 %collective-permute-start.5 = (bf16[144,896]{1,0:T(8,128)(2,1)S(1)}, bf16[144,896]{1,0:T(8,128)(2,1)S(1)}, u32[]{:S(2)}, u32[]{:S(2)}) collective-permute-start(bf16[144,896]{1,0:T(8,128)(2,1)S(1)} %collective-permute-done.ringed), channel_id=1, source_target_pairs={{0,2},{1,3},{6,4},{7,5},{8,10},{9,11},{14,12},{15,13},{16,18},{17,... | collective-permute-start | bytes 774152 | tf_op jit(solution)/shard_map/ppermute | solution.py:35
  26.0 4.4 %collective-permute-done.5 = bf16[144,896]{1,0:T(8,128)(2,1)S(1)} collective-permute-done((bf16[144,896]{1,0:T(8,128)(2,1)S(1)}, bf16[144,896]{1,0:T(8,128)(2,1)S(1)}, u32[]{:S(2)}, u32[]{:S(2)}) %collective-permute-start.5) | collective-permute-done | bytes 258080 | tf_op jit(solution)/shard_map/ppermute | solution.py:35
  32.0 3.4 %project.7 = (bf16[256,896]{1,0:T(8,128)(2,1)}, f32[3,80,896]{2,1,0:T(8,128)S(1)}, f32[80,1]{1,0:T(8,128)S(1)}) custom-call(s32[3]{0:T(128)S(1)} %pad_add_fusion.place, bf16[144,896]{1,0:T(8,128)(2,1)S(1)} %broadcast_select_fusion.crossed, bf16[144,896]{1,0:T(8,128)(2,1)S(1)} %collective-permute-done.ringed, ...), custom_call_target="tpu_custom_call" | custom-call | flops 1150000 | bytes 1000 | tf_op jit(solution)/shard_map/project/pallas_call | solution.py:168
  35.5 3.5 %collective-permute-start.12 = (bf16[256,896]{1,0:T(8,128)(2,1)}, bf16[256,896]{1,0:T(8,128)(2,1)}, u32[]{:S(2)}, u32[]{:S(2)}) collective-permute-start(bf16[256,896]{1,0:T(8,128)(2,1)} %get-tuple-element.87), channel_id=1, source_target_pairs={{0,4},{1,5},{2,6},{3,7},{4,0},{5,1},{6,2},{7,3},{8,12},{9,13},{10,... | collective-permute-start | bytes 1376264 | tf_op jit(solution)/shard_map/ppermute | solution.py:35
  42.1 4.2 %collective-permute-start.10 = (bf16[112,896]{1,0:T(8,128)(2,1)S(1)}, bf16[112,896]{1,0:T(8,128)(2,1)}, u32[]{:S(2)}, u32[]{:S(2)}) collective-permute-start(bf16[112,896]{1,0:T(8,128)(2,1)S(1)} %get-tuple-element.77.refs_0_), channel_id=1, source_target_pairs={{0,8},{1,9},{2,12},{3,13},{4,10},{5,11},{6,14},{7,15},{8,16},{9,17... | collective-permute-start | bytes 602120 | tf_op jit(solution)/shard_map/ppermute | solution.py:35
  46.3 3.0 %project.8 = (bf16[208,896]{1,0:T(8,128)(2,1)}, f32[3,64,896]{2,1,0:T(8,128)S(1)}, f32[64,1]{1,0:T(8,128)S(1)}) custom-call(s32[3]{0:T(128)S(1)} %copy-done.11, bf16[144,896]{1,0:T(8,128)(2,1)S(1)} %broadcast_select_fusion.crossed, bf16[144,896]{1,0:T(8,128)(2,1)S(1)} %copy-done.1, bf16[144,896]{1,0:T(8,128)(2,1)S(1)} %copy-done.5, ...), custom_call_target="tpu_custom_call" | custom-call | flops 1150000 | bytes 1000 | tf_op jit(solution)/shard_map/project/pallas_call | solution.py:168
  50.3 3.1 %collective-permute-start.9 = (bf16[208,896]{1,0:T(8,128)(2,1)}, bf16[208,896]{1,0:T(8,128)(2,1)}, u32[]{:S(2)}, u32[]{:S(2)}) collective-permute-start(bf16[208,896]{1,0:T(8,128)(2,1)} %get-tuple-element.83), channel_id=1, source_target_pairs={{0,4},{1,5},{2,6},{3,7},{4,0},{5,1},{6,2},{7,3},{8,12},{9,13},{10,... | collective-permute-start | bytes 1118216 | tf_op jit(solution)/shard_map/ppermute | solution.py:35
  61.8 4.4 %collective-permute-start.15 = (bf16[80,896]{1,0:T(8,128)(2,1)}, bf16[80,896]{1,0:T(8,128)(2,1)}, u32[]{:S(2)}, u32[]{:S(2)}) collective-permute-start(bf16[80,896]{1,0:T(8,128)(2,1)} %get-tuple-element.96.refs_1_), channel_id=1, source_target_pairs={{0,8},{1,9},{2,12},{3,13},{4,10},{5,11},{6,14},{7,15},{8,16},{9,17... | collective-permute-start | bytes 430088 | tf_op jit(solution)/shard_map/ppermute | solution.py:35
  66.2 5.0 %project.9 = (bf16[352,896]{1,0:T(8,128)(2,1)}, f32[3,112,896]{2,1,0:T(8,128)S(1)}, f32[112,1]{1,0:T(8,128)S(1)}) custom-call(s32[3]{0:T(128)S(1)} %copy-done.12, bf16[112,896]{1,0:T(8,128)(2,1)} %collective-permute-done.10.crossed.refs_4_, bf16[112,896]{1,0:T(8,128)(2,1)} %collective-permute-done.11.ringed, bf16[112,896]{1,0:T(8,128)(2,1)S(1)} %copy-done.17, ...), custom_call_target="tpu_custom_call" | custom-call | flops 3449999872 | bytes 1000 | tf_op jit(solution)/shard_map/project/pallas_call | solution.py:168
  71.1 2.6 %collective-permute-start.20 = (bf16[352,896]{1,0:T(8,128)(2,1)}, bf16[352,896]{1,0:T(8,128)(2,1)}, u32[]{:S(2)}, u32[]{:S(2)}) collective-permute-start(bf16[352,896]{1,0:T(8,128)(2,1)} %get-tuple-element.103), channel_id=1, source_target_pairs={{0,4},{1,5},{2,6},{3,7},{4,0},{5,1},{6,2},{7,3},{8,12},{9,13},{10,... | collective-permute-start | bytes 1892360 | tf_op jit(solution)/shard_map/ppermute | solution.py:35
  76.7 5.3 %collective-permute-done.18.ringed = bf16[80,896]{1,0:T(8,128)(2,1)S(1)} collective-permute-done((bf16[80,896]{1,0:T(8,128)(2,1)}, bf16[80,896]{1,0:T(8,128)(2,1)S(1)}, u32[]{:S(2)}, u32[]{:S(2)}) %collective-permute-start.18) | collective-permute-done | bytes 143392 | tf_op jit(solution)/shard_map/ppermute | solution.py:35
  82.0 3.7 %collective-permute-start.17 = (bf16[64,896]{1,0:T(8,128)(2,1)}, bf16[64,896]{1,0:T(8,128)(2,1)}, u32[]{:S(2)}, u32[]{:S(2)}) collective-permute-start(bf16[64,896]{1,0:T(8,128)(2,1)} %get-tuple-element.98.refs_2_), channel_id=1, source_target_pairs={{0,8},{1,9},{2,12},{3,13},{4,10},{5,11},{6,14},{7,15},{8,16},{9,17... | collective-permute-start | bytes 344072 | tf_op jit(solution)/shard_map/ppermute | solution.py:35
  85.7 3.8 %project.10 = (bf16[256,896]{1,0:T(8,128)(2,1)}, f32[3,80,896]{2,1,0:T(8,128)S(1)}, f32[80,1]{1,0:T(8,128)S(1)}) custom-call(s32[3]{0:T(128)S(1)} %copy-done.12, bf16[80,896]{1,0:T(8,128)(2,1)} %collective-permute-done.15.crossed.refs_5_, bf16[80,896]{1,0:T(8,128)(2,1)S(1)} %collective-permute-done.18.ringed, ...), custom_call_target="tpu_custom_call" | custom-call | flops 1150000 | bytes 1000 | tf_op jit(solution)/shard_map/project/pallas_call | solution.py:168
  91.0 2.7 %hold.2 = (f32[112,896]{1,0:T(8,128)S(1)}, bf16[2,112,896]{2,1,0:T(8,128)(2,1)S(1)}, bf16[256,896]{1,0:T(8,128)(2,1)}) custom-call(f32[3,112,896]{2,1,0:T(8,128)S(1)} %get-tuple-element.102.kept, bf16[352,896]{1,0:T(8,128)(2,1)} %collective-permute-done.20.received, f32[112,1]{1,0:T(8,128)S(1)} %get-tuple-element.92.kept_mean, ...), custom_call_target="tpu_custom_call" | custom-call | flops 287500009472 | bytes 1000 | tf_op jit(solution)/shard_map/hold/pallas_call | solution.py:281
  94.0 4.9 %collective-permute-done.21.ringed = bf16[64,896]{1,0:T(8,128)(2,1)S(1)} collective-permute-done((bf16[64,896]{1,0:T(8,128)(2,1)}, bf16[64,896]{1,0:T(8,128)(2,1)S(1)}, u32[]{:S(2)}, u32[]{:S(2)}) %collective-permute-start.21) | collective-permute-done | bytes 114720 | tf_op jit(solution)/shard_map/ppermute | solution.py:35
  101.1 3.4 %project.11 = (bf16[208,896]{1,0:T(8,128)(2,1)}, f32[3,64,896]{2,1,0:T(8,128)S(1)}, f32[64,1]{1,0:T(8,128)S(1)}) custom-call(s32[3]{0:T(128)S(1)} %copy-done.13, bf16[64,896]{1,0:T(8,128)(2,1)} %collective-permute-done.17.crossed.refs_6_, bf16[64,896]{1,0:T(8,128)(2,1)S(1)} %collective-permute-done.21.ringed, ...), custom_call_target="tpu_custom_call" | custom-call | flops 1150000 | bytes 1000 | tf_op jit(solution)/shard_map/project/pallas_call | solution.py:168
  104.5 2.8 %collective-permute-start.24 = (bf16[208,896]{1,0:T(8,128)(2,1)}, bf16[208,896]{1,0:T(8,128)(2,1)}, u32[]{:S(2)}, u32[]{:S(2)}) collective-permute-start(bf16[208,896]{1,0:T(8,128)(2,1)} %get-tuple-element.107), channel_id=1, source_target_pairs={{0,4},{1,5},{2,6},{3,7},{4,0},{5,1},{6,2},{7,3},{8,12},{9,13},{10,... | collective-permute-start | bytes 1118216 | tf_op jit(solution)/shard_map/ppermute | solution.py:35
  109.2 7.5 %collective-permute-done.24.received = bf16[208,896]{1,0:T(8,128)(2,1)} collective-permute-done((bf16[208,896]{1,0:T(8,128)(2,1)}, bf16[208,896]{1,0:T(8,128)(2,1)}, u32[]{:S(2)}, u32[]{:S(2)}) %collective-permute-start.24) | collective-permute-done | bytes 372768 | tf_op jit(solution)/shard_map/ppermute | solution.py:35
  116.7 3.3 %final.1 = (bf16[256,896]{1,0:T(8,128)(2,1)}, bf16[2,64,896]{2,1,0:T(8,128)(2,1)}) custom-call(s32[3]{0:T(128)S(1)} %copy-done.13, s32[1]{0:T(128)S(6)} %copy.5.flag, f32[3,64,896]{2,1,0:T(8,128)S(1)} %get-tuple-element.106.kept, bf16[208,896]{1,0:T(8,128)(2,1)} %collective-permute-done.24.received, f32[64,1]{1,0:T(8,128)S(1)} %get-tuple-element.108.kept_mean, ...), custom_call_target="tpu_custom_call" | custom-call | flops 287500009472 | bytes 1000 | tf_op jit(solution)/shard_map/final/pallas_call | solution.py:281
  (87 shorter events, 27.2 us)
Async XLA Ops:
  0.9 11.6 %collective-permute-start.2 = (bf16[112,896]{1,0:T(8,128)(2,1)S(1)}, bf16[112,896]{1,0:T(8,128)(2,1)S(1)}, u32[]{:S(2)}, u32[]{:S(2)}) collective-permute-start(bf16[112,896]{1,0:T(8,128)(2,1)S(1)} %slice_bitcast_fusion.1.block), channel_id=1, source_target_pairs={{0,2},{1,3},{2,6},{3,7},{4,0},{5,1},{6,4},{7,5},{8,10},{9,11},{10,... | collective-permute-start | bytes 602120 | tf_op jit(solution)/shard_map/ppermute | solution.py:35
  4.0 8.6 %collective-permute-start.1 = (bf16[112,896]{1,0:T(8,128)(2,1)S(1)}, bf16[112,896]{1,0:T(8,128)(2,1)S(1)}, u32[]{:S(2)}, u32[]{:S(2)}) collective-permute-start(bf16[112,896]{1,0:T(8,128)(2,1)S(1)} %slice_bitcast_fusion.1.block), channel_id=1, source_target_pairs={{0,0},{1,1},{2,4},{3,5},{4,2},{5,3},{6,6},{7,7},{8,8},{9,9},{10,12... | collective-permute-start | bytes 602120 | tf_op jit(solution)/shard_map/ppermute | solution.py:35
  12.6 3.0 %collective-permute-start.3 = (bf16[112,896]{1,0:T(8,128)(2,1)S(1)}, bf16[112,896]{1,0:T(8,128)(2,1)S(1)}, u32[]{:S(2)}, u32[]{:S(2)}) collective-permute-start(bf16[112,896]{1,0:T(8,128)(2,1)S(1)} %collective-permute-done.1.crossed), channel_id=1, source_target_pairs={{0,1},{1,0},{2,3},{3,2},{4,5},{5,4},{6,7},{7,6},{8,9},{9,8},{10,11... | collective-permute-start | bytes 602120 | tf_op jit(solution)/shard_map/ppermute | solution.py:35
  13.1 9.8 %collective-permute-start = (bf16[144,896]{1,0:T(8,128)(2,1)S(1)}, bf16[144,896]{1,0:T(8,128)(2,1)S(1)}, u32[]{:S(2)}, u32[]{:S(2)}) collective-permute-start(bf16[144,896]{1,0:T(8,128)(2,1)S(1)} %slice_bitcast_fusion), channel_id=1, source_target_pairs={{0,2},{1,3},{2,6},{3,7},{4,0},{5,1},{6,4},{7,5},{8,10},{9,11},{10,... | collective-permute-start | bytes 774152 | tf_op jit(solution)/shard_map/ppermute | solution.py:35
  22.9 7.5 %collective-permute-start.5 = (bf16[144,896]{1,0:T(8,128)(2,1)S(1)}, bf16[144,896]{1,0:T(8,128)(2,1)S(1)}, u32[]{:S(2)}, u32[]{:S(2)}) collective-permute-start(bf16[144,896]{1,0:T(8,128)(2,1)S(1)} %collective-permute-done.ringed), channel_id=1, source_target_pairs={{0,2},{1,3},{6,4},{7,5},{8,10},{9,11},{14,12},{15,13},{16,18},{17,... | collective-permute-start | bytes 774152 | tf_op jit(solution)/shard_map/ppermute | solution.py:35
  25.6 15.5 %collective-permute-start.8 = (bf16[352,896]{1,0:T(8,128)(2,1)S(1)}, bf16[352,896]{1,0:T(8,128)(2,1)S(1)}, u32[]{:S(2)}, u32[]{:S(2)}) collective-permute-start(bf16[352,896]{1,0:T(8,128)(2,1)S(1)} %get-tuple-element.74), channel_id=1, source_target_pairs={{0,4},{1,5},{2,6},{3,7},{4,0},{5,1},{6,2},{7,3},{8,12},{9,13},{10,... | collective-permute-start | bytes 1892360 | tf_op jit(solution)/shard_map/ppermute | solution.py:35
  26.0 4.5 %collective-permute-start.7 = (bf16[144,896]{1,0:T(8,128)(2,1)S(1)}, bf16[144,896]{1,0:T(8,128)(2,1)S(1)}, u32[]{:S(2)}, u32[]{:S(2)}) collective-permute-start(bf16[144,896]{1,0:T(8,128)(2,1)S(1)} %collective-permute-done.ringed), channel_id=1, source_target_pairs={{0,1},{1,0},{2,3},{3,2},{4,5},{5,4},{6,7},{7,6},{8,9},{9,8},{10,11... | collective-permute-start | bytes 774152 | tf_op jit(solution)/shard_map/ppermute | solution.py:35
  35.5 20.3 %collective-permute-start.12 = (bf16[256,896]{1,0:T(8,128)(2,1)}, bf16[256,896]{1,0:T(8,128)(2,1)}, u32[]{:S(2)}, u32[]{:S(2)}) collective-permute-start(bf16[256,896]{1,0:T(8,128)(2,1)} %get-tuple-element.87), channel_id=1, source_target_pairs={{0,4},{1,5},{2,6},{3,7},{4,0},{5,1},{6,2},{7,3},{8,12},{9,13},{10,... | collective-permute-start | bytes 1376264 | tf_op jit(solution)/shard_map/ppermute | solution.py:35
  42.1 7.2 %collective-permute-start.10 = (bf16[112,896]{1,0:T(8,128)(2,1)S(1)}, bf16[112,896]{1,0:T(8,128)(2,1)}, u32[]{:S(2)}, u32[]{:S(2)}) collective-permute-start(bf16[112,896]{1,0:T(8,128)(2,1)S(1)} %get-tuple-element.77.refs_0_), channel_id=1, source_target_pairs={{0,8},{1,9},{2,12},{3,13},{4,10},{5,11},{6,14},{7,15},{8,16},{9,17... | collective-permute-start | bytes 602120 | tf_op jit(solution)/shard_map/ppermute | solution.py:35
  49.3 5.7 %collective-permute-start.13 = (bf16[112,896]{1,0:T(8,128)(2,1)}, bf16[112,896]{1,0:T(8,128)(2,1)S(1)}, u32[]{:S(2)}, u32[]{:S(2)}) collective-permute-start(bf16[112,896]{1,0:T(8,128)(2,1)} %collective-permute-done.10.crossed.refs_4_), channel_id=1, source_target_pairs={{0,1},{1,0},{2,3},{3,2},{4,5},{5,4},{6,7},{7,6},{8,9},{9,8},{10,11... | collective-permute-start | bytes 602120 | tf_op jit(solution)/shard_map/ppermute | solution.py:35
  50.3 23.5 %collective-permute-start.9 = (bf16[208,896]{1,0:T(8,128)(2,1)}, bf16[208,896]{1,0:T(8,128)(2,1)}, u32[]{:S(2)}, u32[]{:S(2)}) collective-permute-start(bf16[208,896]{1,0:T(8,128)(2,1)} %get-tuple-element.83), channel_id=1, source_target_pairs={{0,4},{1,5},{2,6},{3,7},{4,0},{5,1},{6,2},{7,3},{8,12},{9,13},{10,... | collective-permute-start | bytes 1118216 | tf_op jit(solution)/shard_map/ppermute | solution.py:35
  53.4 7.4 %collective-permute-start.11 = (bf16[112,896]{1,0:T(8,128)(2,1)}, bf16[112,896]{1,0:T(8,128)(2,1)}, u32[]{:S(2)}, u32[]{:S(2)}) collective-permute-start(bf16[112,896]{1,0:T(8,128)(2,1)} %collective-permute-done.10.crossed.refs_4_), channel_id=1, source_target_pairs={{0,2},{1,3},{2,0},{3,1},{4,6},{5,7},{6,4},{7,5},{8,10},{9,11},{10,... | collective-permute-start | bytes 602120 | tf_op jit(solution)/shard_map/ppermute | solution.py:35
  60.9 5.3 %collective-permute-start.14 = (bf16[112,896]{1,0:T(8,128)(2,1)}, bf16[112,896]{1,0:T(8,128)(2,1)S(1)}, u32[]{:S(2)}, u32[]{:S(2)}) collective-permute-start(bf16[112,896]{1,0:T(8,128)(2,1)} %collective-permute-done.11.ringed), channel_id=1, source_target_pairs={{0,1},{1,0},{2,3},{3,2},{4,5},{5,4},{6,7},{7,6},{8,9},{9,8},{10,11... | collective-permute-start | bytes 602120 | tf_op jit(solution)/shard_map/ppermute | solution.py:35
  61.8 14.4 %collective-permute-start.15 = (bf16[80,896]{1,0:T(8,128)(2,1)}, bf16[80,896]{1,0:T(8,128)(2,1)}, u32[]{:S(2)}, u32[]{:S(2)}) collective-permute-start(bf16[80,896]{1,0:T(8,128)(2,1)} %get-tuple-element.96.refs_1_), channel_id=1, source_target_pairs={{0,8},{1,9},{2,12},{3,13},{4,10},{5,11},{6,14},{7,15},{8,16},{9,17... | collective-permute-start | bytes 430088 | tf_op jit(solution)/shard_map/ppermute | solution.py:35
  71.1 19.9 %collective-permute-start.20 = (bf16[352,896]{1,0:T(8,128)(2,1)}, bf16[352,896]{1,0:T(8,128)(2,1)}, u32[]{:S(2)}, u32[]{:S(2)}) collective-permute-start(bf16[352,896]{1,0:T(8,128)(2,1)} %get-tuple-element.103), channel_id=1, source_target_pairs={{0,4},{1,5},{2,6},{3,7},{4,0},{5,1},{6,2},{7,3},{8,12},{9,13},{10,... | collective-permute-start | bytes 1892360 | tf_op jit(solution)/shard_map/ppermute | solution.py:35
  76.2 5.8 %collective-permute-start.18 = (bf16[80,896]{1,0:T(8,128)(2,1)}, bf16[80,896]{1,0:T(8,128)(2,1)S(1)}, u32[]{:S(2)}, u32[]{:S(2)}) collective-permute-start(bf16[80,896]{1,0:T(8,128)(2,1)} %collective-permute-done.15.crossed.refs_5_), channel_id=1, source_target_pairs={{0,2},{1,3},{2,0},{3,1},{4,6},{5,7},{6,4},{7,5},{8,10},{9,11},{10,... | collective-permute-start | bytes 430088 | tf_op jit(solution)/shard_map/ppermute | solution.py:35
  76.7 5.3 %collective-permute-start.16 = (bf16[80,896]{1,0:T(8,128)(2,1)}, bf16[80,896]{1,0:T(8,128)(2,1)S(1)}, u32[]{:S(2)}, u32[]{:S(2)}) collective-permute-start(bf16[80,896]{1,0:T(8,128)(2,1)} %collective-permute-done.15.crossed.refs_5_), channel_id=1, source_target_pairs={{0,1},{1,0},{2,3},{3,2},{4,5},{5,4},{6,7},{7,6},{8,9},{9,8},{10,11... | collective-permute-start | bytes 430088 | tf_op jit(solution)/shard_map/ppermute | solution.py:35
  82.0 3.7 %collective-permute-start.19 = (bf16[80,896]{1,0:T(8,128)(2,1)S(1)}, bf16[80,896]{1,0:T(8,128)(2,1)S(1)}, u32[]{:S(2)}, u32[]{:S(2)}) collective-permute-start(bf16[80,896]{1,0:T(8,128)(2,1)S(1)} %collective-permute-done.18.ringed), channel_id=1, source_target_pairs={{0,1},{1,0},{2,3},{3,2},{4,5},{5,4},{6,7},{7,6},{8,9},{9,8},{10,11... | collective-permute-start | bytes 430088 | tf_op jit(solution)/shard_map/ppermute | solution.py:35
  82.0 11.7 %collective-permute-start.17 = (bf16[64,896]{1,0:T(8,128)(2,1)}, bf16[64,896]{1,0:T(8,128)(2,1)}, u32[]{:S(2)}, u32[]{:S(2)}) collective-permute-start(bf16[64,896]{1,0:T(8,128)(2,1)} %get-tuple-element.98.refs_2_), channel_id=1, source_target_pairs={{0,8},{1,9},{2,12},{3,13},{4,10},{5,11},{6,14},{7,15},{8,16},{9,17... | collective-permute-start | bytes 344072 | tf_op jit(solution)/shard_map/ppermute | solution.py:35
  89.5 17.8 %collective-permute-start.25 = (bf16[256,896]{1,0:T(8,128)(2,1)}, bf16[256,896]{1,0:T(8,128)(2,1)}, u32[]{:S(2)}, u32[]{:S(2)}) collective-permute-start(bf16[256,896]{1,0:T(8,128)(2,1)} %get-tuple-element.112), channel_id=1, source_target_pairs={{0,4},{1,5},{2,6},{3,7},{4,0},{5,1},{6,2},{7,3},{8,12},{9,13},{10,... | collective-permute-start | bytes 1376264 | tf_op jit(solution)/shard_map/ppermute | solution.py:35
  93.8 5.2 %collective-permute-start.21 = (bf16[64,896]{1,0:T(8,128)(2,1)}, bf16[64,896]{1,0:T(8,128)(2,1)S(1)}, u32[]{:S(2)}, u32[]{:S(2)}) collective-permute-start(bf16[64,896]{1,0:T(8,128)(2,1)} %collective-permute-done.17.crossed.refs_6_), channel_id=1, source_target_pairs={{0,2},{1,3},{2,0},{3,1},{4,6},{5,7},{6,4},{7,5},{8,10},{9,11},{10,... | collective-permute-start | bytes 344072 | tf_op jit(solution)/shard_map/ppermute | solution.py:35
  94.0 7.0 %collective-permute-start.22 = (bf16[64,896]{1,0:T(8,128)(2,1)}, bf16[64,896]{1,0:T(8,128)(2,1)S(1)}, u32[]{:S(2)}, u32[]{:S(2)}) collective-permute-start(bf16[64,896]{1,0:T(8,128)(2,1)} %collective-permute-done.17.crossed.refs_6_), channel_id=1, source_target_pairs={{0,1},{1,0},{2,3},{3,2},{4,5},{5,4},{6,7},{7,6},{8,9},{9,8},{10,11... | collective-permute-start | bytes 344072 | tf_op jit(solution)/shard_map/ppermute | solution.py:35
  99.6 9.6 %collective-permute-start.26 = (bf16[256,896]{1,0:T(8,128)(2,1)}, bf16[256,896]{1,0:T(8,128)(2,1)}, u32[]{:S(2)}, u32[]{:S(2)}) collective-permute-start(bf16[256,896]{1,0:T(8,128)(2,1)} %get-tuple-element.115.refs_8_), channel_id=1, source_target_pairs={{2,10},{3,11},{4,12},{5,13},{10,18},{11,19},{12,20},{13,21},{18,26... | collective-permute-start | bytes 1376264 | tf_op jit(solution)/shard_map/ppermute | solution.py:35
  104.5 12.2 %collective-permute-start.24 = (bf16[208,896]{1,0:T(8,128)(2,1)}, bf16[208,896]{1,0:T(8,128)(2,1)}, u32[]{:S(2)}, u32[]{:S(2)}) collective-permute-start(bf16[208,896]{1,0:T(8,128)(2,1)} %get-tuple-element.107), channel_id=1, source_target_pairs={{0,4},{1,5},{2,6},{3,7},{4,0},{5,1},{6,2},{7,3},{8,12},{9,13},{10,... | collective-permute-start | bytes 1118216 | tf_op jit(solution)/shard_map/ppermute | solution.py:35
  (22 other events, 190.7 us)

commit v10 on v8

--- a/solution.py
+++ b/solution.py
@@ -44,8 +44,12 @@
     return (s, d, y, c) if d != y else None
 
 
-def forward(s, d, y, c):
-    return (s, d, 1 - y, c) if d == y else None
+def across_y(s, d, y, c):
+    return (s, d, 1 - y, c) if d != y else None
+
+
+def across_x(s, d, y, c):
+    return (s, 1 - d, y, c) if d == y else None
 
 
 def swap(s, d, y, c):
@@ -103,9 +107,12 @@
     )(place, pltpu.with_memory_space_constraint(weight, pltpu.HBM))
 
 
-def project_kernel(place, crossed, ringed, sib_crossed, sib_ringed, gain, weight, *refs):
-    sent, kept, kept_mean, normed = refs[:4]
-    out, semaphores = refs[4:] or (sent, None)
+def project_kernel(
+    cuts, apart, place, crossed, ringed, sib_crossed, sib_ringed, gain, weight, *refs
+):
+    count = len(cuts)
+    sents, (kept, kept_mean, normed) = refs[:count], refs[count : count + 3]
+    outs = refs[count + 3 : -1] if apart else sents
     rows = normed.shape[0] // 2
     width = crossed.shape[1]
     half = 2 * width
@@ -135,49 +142,48 @@
     low = row - high - mid
     which = lax.broadcasted_iota(jnp.int32, row.shape, 0)
     stat = jnp.where(which == 0, high, jnp.where(which == 1, mid, low)).astype(BF16)
-    for begin in range(0, width, rows):
-        out[:STAT_ROWS, begin : begin + rows] = stat
-    split = width // (2 * HD) * HD + HD
     copies = []
-    for i, (k, begin, end) in enumerate(
-        ((0, 0, width), (1, 0, width), (2, 0, split), (2, split, width))
-    ):
-        columns = slice(begin, end)
-        product = jnp.dot(normed[...], weight[0, k, :, columns], preferred_element_type=F32)
-        top = STAT_ROWS + k * rows
-        out[top : top + rows, columns] = product[:rows].astype(BF16)
-        kept[k, :, columns] = product[rows:]
-        if semaphores is None:
-            continue
-        at = (slice(top if k else 0, top + rows), columns)
-        copies.append(pltpu.make_async_copy(out.at[at], sent.at[at], semaphores.at[i]))
-        copies[-1].start()
+    for (begin, end), out, sent in zip(cuts, outs, sents):
+        for column in range(0, end - begin, rows):
+            out[:STAT_ROWS, column : column + rows] = stat
+        for k in range(3):
+            product = jnp.dot(normed[...], weight[0, k, :, begin:end], preferred_element_type=F32)
+            top = STAT_ROWS + k * rows
+            out[top : top + rows] = product[:rows].astype(BF16)
+            kept[k, :, begin:end] = product[rows:]
+            if apart:
+                at = pl.ds(top, rows) if k else pl.ds(0, top + rows)
+                copies.append(
+                    pltpu.make_async_copy(out.at[at], sent.at[at], refs[-1].at[len(copies)])
+                )
+                copies[-1].start()
     for copy in copies:
         copy.wait()
 
 
-def project(rows, place, four, gain, weight, apart, estimate):
+def project(rows, place, four, gain, weight, cuts, apart, estimate):
     width = four[0].shape[1]
-    sent_shape = (3 * rows + STAT_ROWS, width)
+    shapes = [(3 * rows + STAT_ROWS, end - begin) for begin, end in cuts]
+    scratch = [pltpu.VMEM((2 * rows, 2 * width), BF16)]
+    if apart:
+        scratch += [pltpu.VMEM(shape, BF16) for shape in shapes]
+        scratch.append(pltpu.SemaphoreType.DMA((3 * len(cuts),)))
     return pl.pallas_call(
-        project_kernel,
+        functools.partial(project_kernel, cuts, apart),
         in_specs=[smem_spec()] + [vmem_spec()] * 6,
-        out_specs=[any_spec() if apart else vmem_spec(), vmem_spec(), vmem_spec()],
-        out_shape=[
-            (pltpu.HBM if apart else pltpu.VMEM)(sent_shape, BF16),
-            pltpu.VMEM((3, rows, width), F32),
-            pltpu.VMEM((rows, 1), F32),
-        ],
-        scratch_shapes=[pltpu.VMEM((2 * rows, 2 * width), BF16)]
-        + [pltpu.VMEM(sent_shape, BF16), pltpu.SemaphoreType.DMA((4,))] * apart,
+        out_specs=[any_spec() if apart else vmem_spec() for _ in cuts] + [vmem_spec()] * 2,
+        out_shape=[(pltpu.HBM if apart else pltpu.VMEM)(shape, BF16) for shape in shapes]
+        + [pltpu.VMEM((3, rows, width), F32), pltpu.VMEM((rows, 1), F32)],
+        scratch_shapes=scratch,
         compiler_params=pltpu.CompilerParams(vmem_limit_bytes=VMEM_BYTES),
         cost_estimate=cost(estimate),
         name="project",
     )(place, *four, gain, weight)
 
 
-def mix(kept, received, kept_mean, earlier, pairs, put):
-    rows, width = kept.shape[1:]
+def mix(kept, received, kept_mean, earlier, pairs, put, first=0):
+    rows = kept.shape[1]
+    last = first + received.shape[1]
     stat = received[:STAT_ROWS, :rows].astype(F32)
     row = stat[0:1] + stat[1:2] + stat[2:3]
     mean_peer = jnp.transpose(jnp.broadcast_to(row, (HD, rows)))[:, :1]
@@ -188,19 +194,23 @@
     causal = lax.broadcasted_iota(jnp.int32, (rows, rows), 0) >= lax.broadcasted_iota(
         jnp.int32, (rows, rows), 1
     )
-    heads = [slice(begin, begin + HD) for begin in range(0, width, HD)]
+    heads = [slice(begin, begin + HD) for begin in range(first, last, HD)]
     held, scores = [], []
     for at in heads:
         queries, keys, values = (
             (
                 kept[k, :, at] * scale_kept
-                + received[STAT_ROWS + k * rows : STAT_ROWS + (k + 1) * rows, at].astype(F32)
+                + received[
+                    STAT_ROWS + k * rows : STAT_ROWS + (k + 1) * rows,
+                    at.start - first : at.stop - first,
+                ].astype(F32)
                 * scale_peer
             ).astype(BF16)
             for k in range(3)
         )
-        pairs[0, :, at] = keys
-        pairs[1, :, at] = values
+        if pairs is not None:
+            pairs[0, :, at] = keys
+            pairs[1, :, at] = values
         held.append([(ref[0, :, at], ref[1, :, at]) for ref in earlier] + [(keys, values)])
         scores.append(
             [
@@ -225,10 +235,11 @@
 
 
 def attend_kernel(kept, received, kept_mean, block, *refs):
-    earlier, (out, pairs) = refs[:-2], refs[-2:]
+    earlier, (out, again, pairs) = refs[:-3], refs[-3:]
 
     def put(at, mixture):
         out[:, at] = (block[:, at].astype(F32) + mixture).astype(BF16)
+        again[:, at] = out[:, at]
 
     mix(kept, received, kept_mean, earlier, pairs, put)
 
@@ -245,8 +256,15 @@
         whole[i * rows : (i + 1) * rows] = own[...]
 
 
+def part_kernel(kept, received, kept_mean, earlier, held):
+    def put(at, mixture):
+        held[:, at] = mixture
+
+    mix(kept, received, kept_mean, (earlier,), None, put)
+
+
 def final_kernel(
-    place, flag, kept, received, kept_mean, earlier, held, first, second, before, own, out, pairs
+    place, flag, kept, received, kept_mean, earlier, held, part, first, second, before, own, out
 ):
     rows = kept.shape[1]
     diagonal, shadow = place[2] == 1, flag[0] == 1
@@ -260,8 +278,10 @@
     def put(at, mixture):
         settle(rows, second, at, mixture)
 
+    done = part.shape[1]
     settle(0, first, slice(None), held[...])
-    mix(kept, received, kept_mean, (earlier,), pairs, put)
+    settle(rows, second, slice(0, done), part[...])
+    mix(kept, received, kept_mean, (earlier,), None, put, done)
 
 
 def call_attend(kernel, name, scalars, arrays, out_shape):
@@ -294,48 +314,59 @@
                 permute(ringed, sections, sibling),
             )
 
-        def partial(four, apart, estimate):
-            sent, kept, kept_mean = project(rows, place, four, norm_gain, weight, apart, estimate)
-            return kept, permute(sent, sections, peer), kept_mean
+        def partial(four, apart, estimate, cuts=None):
+            width = four[0].shape[1]
+            *sents, kept, kept_mean = project(
+                rows, place, four, norm_gain, weight, cuts or [(0, width)], apart, estimate
+            )
+            received = [permute(sent, sections, peer) for sent in sents]
+            return kept, received if cuts else received[0], kept_mean
 
         block = inputs[0, 0]
         rows = block.shape[0] // PARTS
         parts = [block[i * rows : (i + 1) * rows] for i in range(PARTS)]
-        ringed = [permute(part, sections, ring) for part in parts]
+        ringed = permute(parts[0], sections, ring)
         crossed = permute(parts[0], sections, cross)
-        ringed[0], crossed, weight = lax.optimization_barrier((ringed[0], crossed, weight))
+        relayed = permute(parts[1], sections, across_y)
+        ringed, crossed, weight = lax.optimization_barrier((ringed, crossed, weight))
         weight = pltpu.with_memory_space_constraint(weight, pltpu.VMEM)
-        sums = [partial(spread(crossed, ringed[0]), False, 3)]
-        late, _ = lax.optimization_barrier((ringed[1], sums[0][2]))
-        forwarded = permute(late, sections, forward)
-        crossed = jnp.where(diagonal, parts[1], forwarded)
-        sums.append(partial(spread(crossed, late), True, 0.001))
+        sums = [partial(spread(crossed, ringed), False, 3)]
+        crossed = jnp.where(diagonal, parts[1], permute(relayed, sections, across_x))
+        crossed, _ = lax.optimization_barrier((crossed, sums[0][2]))
+        swapped = permute(crossed, sections, swap)
+        sums.append(partial(spread(crossed, swapped), True, 0.001))
         width = block.shape[1]
         rows_of = pltpu.VMEM((rows, width), BF16)
         pairs_of = pltpu.VMEM((2, rows, width), BF16)
 
         def attend(part, item, held):
             return call_attend(
-                attend_kernel, "attend", [], [*item, part, *held], [rows_of, pairs_of]
+                attend_kernel,
+                "attend",
+                [],
+                [*item, part, *held],
+                [rows_of, pltpu.HBM((rows, width), BF16), pairs_of],
             )
 
         def carry(own):
             return permute(own, sections, onward(cross))
 
-        first, pairs = attend(parts[0], sums[0], [])
+        first, first_again, pairs = attend(parts[0], sums[0], [])
         moved = [carry(first)]
         swapped = permute(moved[0], sections, swap)
         beside = permute(moved[0], sections, sibling)
         part = lax.optimization_barrier((parts[1], beside))[0]
-        second, _ = attend(part, sums[1], [pairs])
-        owns = [first, second]
+        second, second_again, _ = attend(part, sums[1], [pairs])
+        owns = [first_again, second_again]
         moved.append(carry(second))
         swapped, _ = lax.optimization_barrier((swapped, second))
         four = moved[0], swapped, beside, permute(swapped, sections, sibling)
         seconds = [partial(four, False, 3)]
         crossed, _ = lax.optimization_barrier((moved[1], seconds[0][2]))
         swapped = permute(crossed, sections, swap)
-        seconds.append(partial(spread(crossed, swapped), True, 1))
+        cut = (width // HD + 1) // 2 * HD
+        cuts = [(0, cut), (cut, width)]
+        kept, received, kept_mean = partial(spread(crossed, swapped), True, 1, cuts)
         mixture, pairs, own = call_attend(
             hold_kernel,
             "hold",
@@ -344,12 +375,19 @@
             [pltpu.VMEM((rows, width), F32), pairs_of, pltpu.VMEM(block.shape, BF16)],
         )
         before = permute(own, sections, onward(direct))
-        out, _ = call_attend(
+        (part,) = call_attend(
+            part_kernel,
+            "part",
+            [],
+            [kept, received[0], kept_mean, pairs],
+            [pltpu.VMEM((rows, cut), F32)],
+        )
+        (out,) = call_attend(
             final_kernel,
             "final",
             [place, preempted],
-            [*seconds[1], pairs, mixture, *moved, before, own],
-            [jax.ShapeDtypeStruct(block.shape, BF16), pairs_of],
+            [kept, received[1], kept_mean, pairs, mixture, part, *moved, before, own],
+            [jax.ShapeDtypeStruct(block.shape, BF16)],
         )
         return out[None, None]
 

time: 111 us -> 110 us (level)
  waiting for transfers between devices: 44.4 us -> 38.9 us
  Pallas kernels: 29.5 us -> 33.4 us
  starting transfers between devices: 33.4 us -> 35.5 us
    ppermute x21 -> x23, waiting for transfers between devices: 44.4 us -> 38.9 us  [permute(): return lax.ppermute(array, AXES, pairs)]
    pallas_call x4 -> x5, Pallas kernels: 7.32 us -> 11.2 us  [call_attend(): pl.pallas_call(kernel, in_specs=[smem_spec() for _ in scalars] + [vmem_sp...]
    ppermute x21 -> x23, starting transfers between devices: 33.4 us -> 35.5 us  [permute(): return lax.ppermute(array, AXES, pairs)]
  transfers between devices with their start and end apart: 21 -> 23, of which waited for: 11 -> 13; matrix products, arithmetic and copies ran while one was open for 0% -> 0% of each run, Pallas kernels for 24% -> 28%
where the time goes in v10:
time: 110 us
  waiting for transfers between devices  38.9 us (35%)
  starting transfers between devices  35.5 us (32%)
  Pallas kernels  33.4 us (30%)
  local copies, waits for them, and re-layouts  1.13 us (1%)
    ppermute x23, waiting for transfers between devices, permute(): return lax.ppermute(array, AXES, pairs)  38.9 us
    ppermute x23, starting transfers between devices, permute(): return lax.ppermute(array, AXES, pairs)  35.5 us
    pallas_call x4, Pallas kernels, project(): pl.pallas_call(functools.partial(project_kernel, cuts, apart), in_specs=[...  17.9 us
    pallas_call x5, Pallas kernels, call_attend(): pl.pallas_call(kernel, in_specs=[smem_spec() for _ in scalars] + [vmem_sp...  11.2 us
    pallas_call x1, Pallas kernels, stage(): pl.pallas_call(stage_kernel, in_specs=[smem_spec(), any_spec()], out_spec...  4.31 us
  transfers between devices with their start and end apart: 23, of which 13 were waited for; matrix products, arithmetic and copies ran while one was open for 0% of the time, Pallas kernels for 28%

profile of v10, /device:TPU:0, one launch (start us, length us, event | category | flops | bytes accessed | tf_op | source)
XLA Modules:
  0.0 110.0 jit_solution(14443098368814676308)
XLA Ops:
  1.1 3.0 %collective-permute-start.2 = (bf16[128,896]{1,0:T(8,128)(2,1)S(1)}, bf16[128,896]{1,0:T(8,128)(2,1)S(1)}, u32[]{:S(2)}, u32[]{:S(2)}) collective-permute-start(bf16[128,896]{1,0:T(8,128)(2,1)S(1)} %get-tuple-element.67.block), channel_id=1, source_target_pairs={{0,2},{1,3},{2,6},{3,7},{4,0},{5,1},{6,4},{7,5},{8,10},{9,11},{10,... | collective-permute-start | bytes 688136 | tf_op jit(solution)/shard_map/ppermute | solution.py:32
  6.2 4.3 %stage.1.weight = bf16[1,3,1792,896]{3,2,1,0:T(8,128)(2,1)S(1)} custom-call(s32[3]{0:T(128)S(1)} %pad_add_fusion.place, bf16[1,3,1792,896]{3,2,1,0:T(8,128)(2,1)} %weight), custom_call_target="tpu_custom_call" | custom-call | flops 4600000000 | bytes 1000 | tf_op jit(solution)/shard_map/stage/pallas_call | solution.py:98
  10.5 3.4 %collective-permute-done.2.ringed = bf16[128,896]{1,0:T(8,128)(2,1)S(1)} collective-permute-done((bf16[128,896]{1,0:T(8,128)(2,1)S(1)}, bf16[128,896]{1,0:T(8,128)(2,1)S(1)}, u32[]{:S(2)}, u32[]{:S(2)}) %collective-permute-start.2) | collective-permute-done | bytes 229408 | tf_op jit(solution)/shard_map/ppermute | solution.py:32
  14.4 5.3 %collective-permute-start.1 = (bf16[128,896]{1,0:T(8,128)(2,1)S(1)}, bf16[128,896]{1,0:T(8,128)(2,1)S(1)}, u32[]{:S(2)}, u32[]{:S(2)}) collective-permute-start(bf16[128,896]{1,0:T(8,128)(2,1)S(1)} %collective-permute-done), channel_id=1, source_target_pairs={{0,4},{1,5},{6,2},{7,3},{8,12},{9,13},{14,10},{15,11},{16,20},{17,... | collective-permute-start | bytes 688136 | tf_op jit(solution)/shard_map/ppermute | solution.py:32
  19.8 4.0 %project.4 = (bf16[400,896]{1,0:T(8,128)(2,1)S(1)}, f32[3,128,896]{2,1,0:T(8,128)S(1)}, f32[128,1]{1,0:T(8,128)S(1)}) custom-call(s32[3]{0:T(128)S(1)} %pad_add_fusion.place, bf16[128,896]{1,0:T(8,128)(2,1)S(1)} %collective-permute-done.3.crossed, bf16[128,896]{1,0:T(8,128)(2,1)S(1)} %collective-permute-done.2.ringed, ...), custom_call_target="tpu_custom_call" | custom-call | flops 3449999872 | bytes 1000 | tf_op jit(solution)/shard_map/project/pallas_call | solution.py:171
  25.5 1.6 %collective-permute-start.6 = (bf16[128,896]{1,0:T(8,128)(2,1)S(1)}, bf16[128,896]{1,0:T(8,128)(2,1)S(1)}, u32[]{:S(2)}, u32[]{:S(2)}) collective-permute-start(bf16[128,896]{1,0:T(8,128)(2,1)S(1)} %broadcast_select_fusion.crossed), channel_id=1, source_target_pairs={{0,2},{1,3},{2,0},{3,1},{4,6},{5,7},{6,4},{7,5},{8,10},{9,11},{10,... | collective-permute-start | bytes 688136 | tf_op jit(solution)/shard_map/ppermute | solution.py:32
  27.1 4.5 %collective-permute-done.6.ringed = bf16[128,896]{1,0:T(8,128)(2,1)S(1)} collective-permute-done((bf16[128,896]{1,0:T(8,128)(2,1)S(1)}, bf16[128,896]{1,0:T(8,128)(2,1)S(1)}, u32[]{:S(2)}, u32[]{:S(2)}) %collective-permute-start.6) | collective-permute-done | bytes 229408 | tf_op jit(solution)/shard_map/ppermute | solution.py:32
  33.0 4.7 %project.5 = (bf16[400,896]{1,0:T(8,128)(2,1)}, f32[3,128,896]{2,1,0:T(8,128)S(1)}, f32[128,1]{1,0:T(8,128)S(1)}) custom-call(s32[3]{0:T(128)S(1)} %pad_add_fusion.place, bf16[128,896]{1,0:T(8,128)(2,1)S(1)} %broadcast_select_fusion.crossed, bf16[128,896]{1,0:T(8,128)(2,1)S(1)} %collective-permute-done.6.ringed, ...), custom_call_target="tpu_custom_call" | custom-call | flops 1150000 | bytes 1000 | tf_op jit(solution)/shard_map/project/pallas_call | solution.py:171
  37.7 2.5 %collective-permute-start.9 = (bf16[400,896]{1,0:T(8,128)(2,1)}, bf16[400,896]{1,0:T(8,128)(2,1)}, u32[]{:S(2)}, u32[]{:S(2)}) collective-permute-start(bf16[400,896]{1,0:T(8,128)(2,1)} %get-tuple-element.45), channel_id=1, source_target_pairs={{0,4},{1,5},{2,6},{3,7},{4,0},{5,1},{6,2},{7,3},{8,12},{9,13},{10,... | collective-permute-start | bytes 2150408 | tf_op jit(solution)/shard_map/ppermute | solution.py:32
  43.1 4.2 %collective-permute-start.11 = (bf16[128,896]{1,0:T(8,128)(2,1)S(1)}, bf16[128,896]{1,0:T(8,128)(2,1)}, u32[]{:S(2)}, u32[]{:S(2)}) collective-permute-start(bf16[128,896]{1,0:T(8,128)(2,1)S(1)} %get-tuple-element.49), channel_id=1, source_target_pairs={{0,8},{1,9},{2,12},{3,13},{4,10},{5,11},{6,14},{7,15},{8,16},{9,17... | collective-permute-start | bytes 688136 | tf_op jit(solution)/shard_map/ppermute | solution.py:32
  47.3 3.2 %collective-permute-done.11.crossed.first = bf16[128,896]{1,0:T(8,128)(2,1)} collective-permute-done((bf16[128,896]{1,0:T(8,128)(2,1)S(1)}, bf16[128,896]{1,0:T(8,128)(2,1)}, u32[]{:S(2)}, u32[]{:S(2)}) %collective-permute-start.11) | collective-permute-done | bytes 229408 | tf_op jit(solution)/shard_map/ppermute | solution.py:32
  50.4 2.6 %collective-permute-start.14 = (bf16[128,896]{1,0:T(8,128)(2,1)}, bf16[128,896]{1,0:T(8,128)(2,1)}, u32[]{:S(2)}, u32[]{:S(2)}) collective-permute-start(bf16[128,896]{1,0:T(8,128)(2,1)} %collective-permute-done.11.crossed.first), channel_id=1, source_target_pairs={{0,2},{1,3},{2,0},{3,1},{4,6},{5,7},{6,4},{7,5},{8,10},{9,11},{10,... | collective-permute-start | bytes 688136 | tf_op jit(solution)/shard_map/ppermute | solution.py:32
  53.0 4.0 %collective-permute-done.9.received = bf16[400,896]{1,0:T(8,128)(2,1)} collective-permute-done((bf16[400,896]{1,0:T(8,128)(2,1)}, bf16[400,896]{1,0:T(8,128)(2,1)}, u32[]{:S(2)}, u32[]{:S(2)}) %collective-permute-start.9) | collective-permute-done | bytes 716832 | tf_op jit(solution)/shard_map/ppermute | solution.py:32
  57.0 3.0 %attend.3 = (bf16[128,896]{1,0:T(8,128)(2,1)S(1)}, bf16[128,896]{1,0:T(8,128)(2,1)}, bf16[2,128,896]{2,1,0:T(8,128)(2,1)}) custom-call(f32[3,128,896]{2,1,0:T(8,128)S(1)} %get-tuple-element.44.kept, bf16[400,896]{1,0:T(8,128)(2,1)} %collective-permute-done.9.received, f32[128,1]{1,0:T(8,128)S(1)} %get-tuple-element.46.kept_mean, ...), custom_call_target="tpu_custom_call" | custom-call | flops 287500009472 | bytes 1000 | tf_op jit(solution)/shard_map/attend/pallas_call | solution.py:288
  60.0 8.6 %collective-permute-start.13 = (bf16[128,896]{1,0:T(8,128)(2,1)S(1)}, bf16[128,896]{1,0:T(8,128)(2,1)S(1)}, u32[]{:S(2)}, u32[]{:S(2)}) collective-permute-start(bf16[128,896]{1,0:T(8,128)(2,1)S(1)} %get-tuple-element.52), channel_id=1, source_target_pairs={{0,8},{1,9},{2,12},{3,13},{4,10},{5,11},{6,14},{7,15},{8,16},{9,17... | collective-permute-start | bytes 688136 | tf_op jit(solution)/shard_map/ppermute | solution.py:32
  68.6 4.5 %project.6 = (bf16[400,896]{1,0:T(8,128)(2,1)S(1)}, f32[3,128,896]{2,1,0:T(8,128)S(1)}, f32[128,1]{1,0:T(8,128)S(1)}) custom-call(s32[3]{0:T(128)S(1)} %copy-done.5, bf16[128,896]{1,0:T(8,128)(2,1)} %collective-permute-done.11.crossed.first, bf16[128,896]{1,0:T(8,128)(2,1)} %collective-permute-done.14.ringed, ...), custom_call_target="tpu_custom_call" | custom-call | flops 3449999872 | bytes 1000 | tf_op jit(solution)/shard_map/project/pallas_call | solution.py:171
  75.2 6.0 %collective-permute-done.16.ringed = bf16[128,896]{1,0:T(8,128)(2,1)S(1)} collective-permute-done((bf16[128,896]{1,0:T(8,128)(2,1)S(1)}, bf16[128,896]{1,0:T(8,128)(2,1)S(1)}, u32[]{:S(2)}, u32[]{:S(2)}) %collective-permute-start.16) | collective-permute-done | bytes 229408 | tf_op jit(solution)/shard_map/ppermute | solution.py:32
  82.6 4.7 %project.7 = (bf16[400,512]{1,0:T(8,128)(2,1)}, bf16[400,384]{1,0:T(8,128)(2,1)}, f32[3,128,896]{2,1,0:T(8,128)S(1)}, f32[128,1]{1,0:T(8,128)S(1)}) custom-call(s32[3]{0:T(128)S(1)} %copy-done.5, bf16[128,896]{1,0:T(8,128)(2,1)S(1)} %collective-permute-done.13.crossed.second, bf16[128,896]{1,0:T(8,128)(2,1)S(1)} %collective-permute-done.16.ringed, ...), custom_call_target="tpu_custom_call" | custom-call | flops 1150000000 | bytes 1000 | tf_op jit(solution)/shard_map/project/pallas_call | solution.py:171
  87.3 1.6 %collective-permute-start.21 = (bf16[400,512]{1,0:T(8,128)(2,1)}, bf16[400,512]{1,0:T(8,128)(2,1)}, u32[]{:S(2)}, u32[]{:S(2)}) collective-permute-start(bf16[400,512]{1,0:T(8,128)(2,1)} %get-tuple-element.65), channel_id=1, source_target_pairs={{0,4},{1,5},{2,6},{3,7},{4,0},{5,1},{6,2},{7,3},{8,12},{9,13},{10,... | collective-permute-start | bytes 1228808 | tf_op jit(solution)/shard_map/ppermute | solution.py:32
  89.4 2.7 %collective-permute-done.20.received = bf16[400,896]{1,0:T(8,128)(2,1)S(1)} collective-permute-done((bf16[400,896]{1,0:T(8,128)(2,1)S(1)}, bf16[400,896]{1,0:T(8,128)(2,1)S(1)}, u32[]{:S(2)}, u32[]{:S(2)}) %collective-permute-start.20) | collective-permute-done | bytes 716832 | tf_op jit(solution)/shard_map/ppermute | solution.py:32
  95.1 5.9 %collective-permute-done.21.received = bf16[400,512]{1,0:T(8,128)(2,1)} collective-permute-done((bf16[400,512]{1,0:T(8,128)(2,1)}, bf16[400,512]{1,0:T(8,128)(2,1)}, u32[]{:S(2)}, u32[]{:S(2)}) %collective-permute-start.21) | collective-permute-done | bytes 409632 | tf_op jit(solution)/shard_map/ppermute | solution.py:32
  101.0 1.9 %part.1 = f32[128,512]{1,0:T(8,128)S(1)} custom-call(f32[3,128,896]{2,1,0:T(8,128)S(1)} %get-tuple-element.56.kept, bf16[400,512]{1,0:T(8,128)(2,1)} %collective-permute-done.21.received, f32[128,1]{1,0:T(8,128)S(1)} %get-tuple-element.58.kept_mean, bf16[2,128,896]{2,1,0:T(8,128)(2,1)S(1)} %get-tuple-element.63.earlier), custom_call_target="tpu_custom_call" | custom-call | flops 287500009472 | bytes 1000 | tf_op jit(solution)/shard_map/part/pallas_call | solution.py:288
  102.9 4.0 %collective-permute-done.19.received = bf16[400,384]{1,0:T(8,128)(2,1)} collective-permute-done((bf16[400,384]{1,0:T(8,128)(2,1)}, bf16[400,384]{1,0:T(8,128)(2,1)}, u32[]{:S(2)}, u32[]{:S(2)}) %collective-permute-start.19) | collective-permute-done | bytes 307232 | tf_op jit(solution)/shard_map/ppermute | solution.py:32
  106.9 3.2 %final.1 = bf16[256,896]{1,0:T(8,128)(2,1)} custom-call(s32[3]{0:T(128)S(1)} %copy-done.6, s32[1]{0:T(128)S(6)} %copy.5.flag, f32[3,128,896]{2,1,0:T(8,128)S(1)} %get-tuple-element.56.kept, bf16[400,384]{1,0:T(8,128)(2,1)} %collective-permute-done.19.received, f32[128,1]{1,0:T(8,128)S(1)} %get-tuple-element.58.kept_mean, ...), custom_call_target="tpu_custom_call" | custom-call | flops 287500009472 | bytes 1000 | tf_op jit(solution)/shard_map/final/pallas_call | solution.py:288
  (55 shorter events, 15.9 us)
Async XLA Ops:
  1.1 12.8 %collective-permute-start.2 = (bf16[128,896]{1,0:T(8,128)(2,1)S(1)}, bf16[128,896]{1,0:T(8,128)(2,1)S(1)}, u32[]{:S(2)}, u32[]{:S(2)}) collective-permute-start(bf16[128,896]{1,0:T(8,128)(2,1)S(1)} %get-tuple-element.67.block), channel_id=1, source_target_pairs={{0,2},{1,3},{2,6},{3,7},{4,0},{5,1},{6,4},{7,5},{8,10},{9,11},{10,... | collective-permute-start | bytes 688136 | tf_op jit(solution)/shard_map/ppermute | solution.py:32
  4.1 9.8 %collective-permute-start.3 = (bf16[128,896]{1,0:T(8,128)(2,1)S(1)}, bf16[128,896]{1,0:T(8,128)(2,1)S(1)}, u32[]{:S(2)}, u32[]{:S(2)}) collective-permute-start(bf16[128,896]{1,0:T(8,128)(2,1)S(1)} %get-tuple-element.67.block), channel_id=1, source_target_pairs={{0,0},{1,1},{2,4},{3,5},{4,2},{5,3},{6,6},{7,7},{8,8},{9,9},{10,12... | collective-permute-start | bytes 688136 | tf_op jit(solution)/shard_map/ppermute | solution.py:32
  4.8 9.7 %collective-permute-start = (bf16[128,896]{1,0:T(8,128)(2,1)S(1)}, bf16[128,896]{1,0:T(8,128)(2,1)S(1)}, u32[]{:S(2)}, u32[]{:S(2)}) collective-permute-start(bf16[128,896]{1,0:T(8,128)(2,1)S(1)} %get-tuple-element.50.block), channel_id=1, source_target_pairs={{2,0},{3,1},{4,6},{5,7},{10,8},{11,9},{12,14},{13,15},{18,16},{19,... | collective-permute-start | bytes 688136 | tf_op jit(solution)/shard_map/ppermute | solution.py:32
  6.2 26.9 %copy-start.4 = (s32[3]{0:T(128)}, s32[3]{0:T(128)S(1)}, u32[]{:S(2)}) copy-start(s32[3]{0:T(128)S(1)} %pad_add_fusion.place) | copy-start | bytes 40
  13.9 5.8 %collective-permute-start.4 = (bf16[128,896]{1,0:T(8,128)(2,1)S(1)}, bf16[128,896]{1,0:T(8,128)(2,1)S(1)}, u32[]{:S(2)}, u32[]{:S(2)}) collective-permute-start(bf16[128,896]{1,0:T(8,128)(2,1)S(1)} %collective-permute-done.3.crossed), channel_id=1, source_target_pairs={{0,1},{1,0},{2,3},{3,2},{4,5},{5,4},{6,7},{7,6},{8,9},{9,8},{10,11... | collective-permute-start | bytes 688136 | tf_op jit(solution)/shard_map/ppermute | solution.py:32
  13.9 5.8 %collective-permute-start.5 = (bf16[128,896]{1,0:T(8,128)(2,1)S(1)}, bf16[128,896]{1,0:T(8,128)(2,1)S(1)}, u32[]{:S(2)}, u32[]{:S(2)}) collective-permute-start(bf16[128,896]{1,0:T(8,128)(2,1)S(1)} %collective-permute-done.2.ringed), channel_id=1, source_target_pairs={{0,1},{1,0},{2,3},{3,2},{4,5},{5,4},{6,7},{7,6},{8,9},{9,8},{10,11... | collective-permute-start | bytes 688136 | tf_op jit(solution)/shard_map/ppermute | solution.py:32
  14.4 11.0 %collective-permute-start.1 = (bf16[128,896]{1,0:T(8,128)(2,1)S(1)}, bf16[128,896]{1,0:T(8,128)(2,1)S(1)}, u32[]{:S(2)}, u32[]{:S(2)}) collective-permute-start(bf16[128,896]{1,0:T(8,128)(2,1)S(1)} %collective-permute-done), channel_id=1, source_target_pairs={{0,4},{1,5},{6,2},{7,3},{8,12},{9,13},{14,10},{15,11},{16,20},{17,... | collective-permute-start | bytes 688136 | tf_op jit(solution)/shard_map/ppermute | solution.py:32
  23.8 17.7 %collective-permute-start.10 = (bf16[400,896]{1,0:T(8,128)(2,1)S(1)}, bf16[400,896]{1,0:T(8,128)(2,1)S(1)}, u32[]{:S(2)}, u32[]{:S(2)}) collective-permute-start(bf16[400,896]{1,0:T(8,128)(2,1)S(1)} %get-tuple-element.48), channel_id=1, source_target_pairs={{0,4},{1,5},{2,6},{3,7},{4,0},{5,1},{6,2},{7,3},{8,12},{9,13},{10,... | collective-permute-start | bytes 2150408 | tf_op jit(solution)/shard_map/ppermute | solution.py:32
  25.5 6.1 %collective-permute-start.6 = (bf16[128,896]{1,0:T(8,128)(2,1)S(1)}, bf16[128,896]{1,0:T(8,128)(2,1)S(1)}, u32[]{:S(2)}, u32[]{:S(2)}) collective-permute-start(bf16[128,896]{1,0:T(8,128)(2,1)S(1)} %broadcast_select_fusion.crossed), channel_id=1, source_target_pairs={{0,2},{1,3},{2,0},{3,1},{4,6},{5,7},{6,4},{7,5},{8,10},{9,11},{10,... | collective-permute-start | bytes 688136 | tf_op jit(solution)/shard_map/ppermute | solution.py:32
  27.1 4.5 %collective-permute-start.7 = (bf16[128,896]{1,0:T(8,128)(2,1)S(1)}, bf16[128,896]{1,0:T(8,128)(2,1)S(1)}, u32[]{:S(2)}, u32[]{:S(2)}) collective-permute-start(bf16[128,896]{1,0:T(8,128)(2,1)S(1)} %broadcast_select_fusion.crossed), channel_id=1, source_target_pairs={{0,1},{1,0},{2,3},{3,2},{4,5},{5,4},{6,7},{7,6},{8,9},{9,8},{10,11... | collective-permute-start | bytes 688136 | tf_op jit(solution)/shard_map/ppermute | solution.py:32
  31.5 1.5 %collective-permute-start.8 = (bf16[128,896]{1,0:T(8,128)(2,1)S(1)}, bf16[128,896]{1,0:T(8,128)(2,1)S(1)}, u32[]{:S(2)}, u32[]{:S(2)}) collective-permute-start(bf16[128,896]{1,0:T(8,128)(2,1)S(1)} %collective-permute-done.6.ringed), channel_id=1, source_target_pairs={{0,1},{1,0},{2,3},{3,2},{4,5},{5,4},{6,7},{7,6},{8,9},{9,8},{10,11... | collective-permute-start | bytes 688136 | tf_op jit(solution)/shard_map/ppermute | solution.py:32
  37.7 19.2 %collective-permute-start.9 = (bf16[400,896]{1,0:T(8,128)(2,1)}, bf16[400,896]{1,0:T(8,128)(2,1)}, u32[]{:S(2)}, u32[]{:S(2)}) collective-permute-start(bf16[400,896]{1,0:T(8,128)(2,1)} %get-tuple-element.45), channel_id=1, source_target_pairs={{0,4},{1,5},{2,6},{3,7},{4,0},{5,1},{6,2},{7,3},{8,12},{9,13},{10,... | collective-permute-start | bytes 2150408 | tf_op jit(solution)/shard_map/ppermute | solution.py:32
  43.1 7.3 %collective-permute-start.11 = (bf16[128,896]{1,0:T(8,128)(2,1)S(1)}, bf16[128,896]{1,0:T(8,128)(2,1)}, u32[]{:S(2)}, u32[]{:S(2)}) collective-permute-start(bf16[128,896]{1,0:T(8,128)(2,1)S(1)} %get-tuple-element.49), channel_id=1, source_target_pairs={{0,8},{1,9},{2,12},{3,13},{4,10},{5,11},{6,14},{7,15},{8,16},{9,17... | collective-permute-start | bytes 688136 | tf_op jit(solution)/shard_map/ppermute | solution.py:32
  50.4 2.6 %collective-permute-start.12 = (bf16[128,896]{1,0:T(8,128)(2,1)}, bf16[128,896]{1,0:T(8,128)(2,1)S(1)}, u32[]{:S(2)}, u32[]{:S(2)}) collective-permute-start(bf16[128,896]{1,0:T(8,128)(2,1)} %collective-permute-done.11.crossed.first), channel_id=1, source_target_pairs={{0,1},{1,0},{2,3},{3,2},{4,5},{5,4},{6,7},{7,6},{8,9},{9,8},{10,11... | collective-permute-start | bytes 688136 | tf_op jit(solution)/shard_map/ppermute | solution.py:32
  50.4 9.6 %collective-permute-start.14 = (bf16[128,896]{1,0:T(8,128)(2,1)}, bf16[128,896]{1,0:T(8,128)(2,1)}, u32[]{:S(2)}, u32[]{:S(2)}) collective-permute-start(bf16[128,896]{1,0:T(8,128)(2,1)} %collective-permute-done.11.crossed.first), channel_id=1, source_target_pairs={{0,2},{1,3},{2,0},{3,1},{4,6},{5,7},{6,4},{7,5},{8,10},{9,11},{10,... | collective-permute-start | bytes 688136 | tf_op jit(solution)/shard_map/ppermute | solution.py:32
  60.0 8.6 %collective-permute-start.15 = (bf16[128,896]{1,0:T(8,128)(2,1)}, bf16[128,896]{1,0:T(8,128)(2,1)S(1)}, u32[]{:S(2)}, u32[]{:S(2)}) collective-permute-start(bf16[128,896]{1,0:T(8,128)(2,1)} %collective-permute-done.14.ringed), channel_id=1, source_target_pairs={{0,1},{1,0},{2,3},{3,2},{4,5},{5,4},{6,7},{7,6},{8,9},{9,8},{10,11... | collective-permute-start | bytes 688136 | tf_op jit(solution)/shard_map/ppermute | solution.py:32
  60.0 13.9 %collective-permute-start.13 = (bf16[128,896]{1,0:T(8,128)(2,1)S(1)}, bf16[128,896]{1,0:T(8,128)(2,1)S(1)}, u32[]{:S(2)}, u32[]{:S(2)}) collective-permute-start(bf16[128,896]{1,0:T(8,128)(2,1)S(1)} %get-tuple-element.52), channel_id=1, source_target_pairs={{0,8},{1,9},{2,12},{3,13},{4,10},{5,11},{6,14},{7,15},{8,16},{9,17... | collective-permute-start | bytes 688136 | tf_op jit(solution)/shard_map/ppermute | solution.py:32
  73.1 18.9 %collective-permute-start.20 = (bf16[400,896]{1,0:T(8,128)(2,1)S(1)}, bf16[400,896]{1,0:T(8,128)(2,1)S(1)}, u32[]{:S(2)}, u32[]{:S(2)}) collective-permute-start(bf16[400,896]{1,0:T(8,128)(2,1)S(1)} %get-tuple-element.60), channel_id=1, source_target_pairs={{0,4},{1,5},{2,6},{3,7},{4,0},{5,1},{6,2},{7,3},{8,12},{9,13},{10,... | collective-permute-start | bytes 2150408 | tf_op jit(solution)/shard_map/ppermute | solution.py:32
  73.9 7.2 %collective-permute-start.16 = (bf16[128,896]{1,0:T(8,128)(2,1)S(1)}, bf16[128,896]{1,0:T(8,128)(2,1)S(1)}, u32[]{:S(2)}, u32[]{:S(2)}) collective-permute-start(bf16[128,896]{1,0:T(8,128)(2,1)S(1)} %collective-permute-done.13.crossed.second), channel_id=1, source_target_pairs={{0,2},{1,3},{2,0},{3,1},{4,6},{5,7},{6,4},{7,5},{8,10},{9,11},{10,... | collective-permute-start | bytes 688136 | tf_op jit(solution)/shard_map/ppermute | solution.py:32
  75.2 6.6 %collective-permute-start.17 = (bf16[128,896]{1,0:T(8,128)(2,1)S(1)}, bf16[128,896]{1,0:T(8,128)(2,1)S(1)}, u32[]{:S(2)}, u32[]{:S(2)}) collective-permute-start(bf16[128,896]{1,0:T(8,128)(2,1)S(1)} %collective-permute-done.13.crossed.second), channel_id=1, source_target_pairs={{0,1},{1,0},{2,3},{3,2},{4,5},{5,4},{6,7},{7,6},{8,9},{9,8},{10,11... | collective-permute-start | bytes 688136 | tf_op jit(solution)/shard_map/ppermute | solution.py:32
  81.1 1.5 %collective-permute-start.18 = (bf16[128,896]{1,0:T(8,128)(2,1)S(1)}, bf16[128,896]{1,0:T(8,128)(2,1)S(1)}, u32[]{:S(2)}, u32[]{:S(2)}) collective-permute-start(bf16[128,896]{1,0:T(8,128)(2,1)S(1)} %collective-permute-done.16.ringed), channel_id=1, source_target_pairs={{0,1},{1,0},{2,3},{3,2},{4,5},{5,4},{6,7},{7,6},{8,9},{9,8},{10,11... | collective-permute-start | bytes 688136 | tf_op jit(solution)/shard_map/ppermute | solution.py:32
  87.3 13.7 %collective-permute-start.21 = (bf16[400,512]{1,0:T(8,128)(2,1)}, bf16[400,512]{1,0:T(8,128)(2,1)}, u32[]{:S(2)}, u32[]{:S(2)}) collective-permute-start(bf16[400,512]{1,0:T(8,128)(2,1)} %get-tuple-element.65), channel_id=1, source_target_pairs={{0,4},{1,5},{2,6},{3,7},{4,0},{5,1},{6,2},{7,3},{8,12},{9,13},{10,... | collective-permute-start | bytes 1228808 | tf_op jit(solution)/shard_map/ppermute | solution.py:32
  88.9 17.9 %collective-permute-start.19 = (bf16[400,384]{1,0:T(8,128)(2,1)}, bf16[400,384]{1,0:T(8,128)(2,1)}, u32[]{:S(2)}, u32[]{:S(2)}) collective-permute-start(bf16[400,384]{1,0:T(8,128)(2,1)} %get-tuple-element.57), channel_id=1, source_target_pairs={{0,4},{1,5},{2,6},{3,7},{4,0},{5,1},{6,2},{7,3},{8,12},{9,13},{10,... | collective-permute-start | bytes 921608 | tf_op jit(solution)/shard_map/ppermute | solution.py:32
  93.7 13.2 %collective-permute-start.22 = (bf16[256,896]{1,0:T(8,128)(2,1)}, bf16[256,896]{1,0:T(8,128)(2,1)}, u32[]{:S(2)}, u32[]{:S(2)}) collective-permute-start(bf16[256,896]{1,0:T(8,128)(2,1)} %get-tuple-element.66.own), channel_id=1, source_target_pairs={{2,10},{3,11},{4,12},{5,13},{10,18},{11,19},{12,20},{13,21},{18,26... | collective-permute-start | bytes 1376264 | tf_op jit(solution)/shard_map/ppermute | solution.py:32
  (9 other events, 97.5 us)

commit v11 on v10

--- a/solution.py
+++ b/solution.py
@@ -41,15 +41,11 @@
 
 
 def direct(s, d, y, c):
-    return (s, d, y, c) if d != y else None
-
-
-def across_y(s, d, y, c):
-    return (s, d, 1 - y, c) if d != y else None
-
-
-def across_x(s, d, y, c):
-    return (s, 1 - d, y, c) if d == y else None
+    return (s, d, y, c)
+
+
+def forward(s, d, y, c):
+    return (s, d, 1 - y, c) if d == y else None
 
 
 def swap(s, d, y, c):
@@ -108,11 +104,27 @@
 
 
 def project_kernel(
-    cuts, apart, place, crossed, ringed, sib_crossed, sib_ringed, gain, weight, *refs
+    cuts, apart, owned, place, crossed, ringed, sib_crossed, sib_ringed, gain, weight, *refs
 ):
     count = len(cuts)
-    sents, (kept, kept_mean, normed) = refs[:count], refs[count : count + 3]
-    outs = refs[count + 3 : -1] if apart else sents
+    semaphores = refs[-1]
+    owns, refs = refs[:owned], refs[owned:-1]
+    sents, (kept, kept_mean, *whole), (normed, *outs) = (
+        refs[:count],
+        refs[count : count + 2 + bool(owned)],
+        refs[count + 2 + bool(owned) :],
+    )
+    copies = []
+
+    def copy(source, target):
+        copies.append(pltpu.make_async_copy(source, target, semaphores.at[len(copies)]))
+        copies[-1].start()
+
+    begin = 0
+    for own in owns:
+        copy(own, whole[0].at[pl.ds(begin, own.shape[0])])
+        begin += own.shape[0]
+    outs = outs if apart else sents
     rows = normed.shape[0] // 2
     width = crossed.shape[1]
     half = 2 * width
@@ -142,7 +154,6 @@
     low = row - high - mid
     which = lax.broadcasted_iota(jnp.int32, row.shape, 0)
     stat = jnp.where(which == 0, high, jnp.where(which == 1, mid, low)).astype(BF16)
-    copies = []
     for (begin, end), out, sent in zip(cuts, outs, sents):
         for column in range(0, end - begin, rows):
             out[:STAT_ROWS, column : column + rows] = stat
@@ -153,32 +164,33 @@
             kept[k, :, begin:end] = product[rows:]
             if apart:
                 at = pl.ds(top, rows) if k else pl.ds(0, top + rows)
-                copies.append(
-                    pltpu.make_async_copy(out.at[at], sent.at[at], refs[-1].at[len(copies)])
-                )
-                copies[-1].start()
-    for copy in copies:
-        copy.wait()
-
-
-def project(rows, place, four, gain, weight, cuts, apart, estimate):
+                copy(out.at[at], sent.at[at])
+    for item in copies:
+        item.wait()
+
+
+def project(rows, place, four, gain, weight, cuts, apart, owns, estimate):
     width = four[0].shape[1]
     shapes = [(3 * rows + STAT_ROWS, end - begin) for begin, end in cuts]
     scratch = [pltpu.VMEM((2 * rows, 2 * width), BF16)]
     if apart:
         scratch += [pltpu.VMEM(shape, BF16) for shape in shapes]
-        scratch.append(pltpu.SemaphoreType.DMA((3 * len(cuts),)))
+    scratch.append(pltpu.SemaphoreType.DMA((3 * len(cuts) + len(owns),)))
+    whole = (sum(own.shape[0] for own in owns), width)
     return pl.pallas_call(
-        functools.partial(project_kernel, cuts, apart),
-        in_specs=[smem_spec()] + [vmem_spec()] * 6,
-        out_specs=[any_spec() if apart else vmem_spec() for _ in cuts] + [vmem_spec()] * 2,
+        functools.partial(project_kernel, cuts, apart, len(owns)),
+        in_specs=[smem_spec()] + [vmem_spec() for _ in range(6 + len(owns))],
+        out_specs=[any_spec() if apart else vmem_spec() for _ in cuts]
+        + [vmem_spec()] * 2
+        + [any_spec()] * bool(owns),
         out_shape=[(pltpu.HBM if apart else pltpu.VMEM)(shape, BF16) for shape in shapes]
-        + [pltpu.VMEM((3, rows, width), F32), pltpu.VMEM((rows, 1), F32)],
+        + [pltpu.VMEM((3, rows, width), F32), pltpu.VMEM((rows, 1), F32)]
+        + [pltpu.HBM(whole, BF16)] * bool(owns),
         scratch_shapes=scratch,
         compiler_params=pltpu.CompilerParams(vmem_limit_bytes=VMEM_BYTES),
         cost_estimate=cost(estimate),
         name="project",
-    )(place, *four, gain, weight)
+    )(place, *four, gain, weight, *owns)
 
 
 def mix(kept, received, kept_mean, earlier, pairs, put, first=0):
@@ -234,26 +246,20 @@
         put(at, mixture)
 
 
-def attend_kernel(kept, received, kept_mean, block, *refs):
-    earlier, (out, again, pairs) = refs[:-3], refs[-3:]
+def attend_kernel(first, kept, received, kept_mean, block, *refs):
+    earlier, out, pairs = ((), *refs) if first else (refs[:1], refs[1], None)
 
     def put(at, mixture):
         out[:, at] = (block[:, at].astype(F32) + mixture).astype(BF16)
-        again[:, at] = out[:, at]
 
     mix(kept, received, kept_mean, earlier, pairs, put)
 
 
-def hold_kernel(kept, received, kept_mean, *refs):
-    owns, (held, pairs, whole) = refs[:-3], refs[-3:]
-    rows = kept.shape[1]
-
+def hold_kernel(kept, received, kept_mean, held, pairs):
     def put(at, mixture):
         held[:, at] = mixture
 
     mix(kept, received, kept_mean, (), pairs, put)
-    for i, own in enumerate(owns):
-        whole[i * rows : (i + 1) * rows] = own[...]
 
 
 def part_kernel(kept, received, kept_mean, earlier, held):
@@ -263,25 +269,42 @@
     mix(kept, received, kept_mean, (earlier,), None, put)
 
 
+def settle_kernel(flag, held, part, before, own, out, rest, rest_own):
+    rows, done = part.shape
+    shadow = flag[0] == 1
+
+    def settle(here, at, mixture):
+        result = jnp.where(
+            shadow, before[here, at].astype(F32) + mixture, own[here, at].astype(F32)
+        )
+        out[here, at] = result.astype(BF16)
+
+    upper, lower = slice(0, rows), slice(rows, 2 * rows)
+    settle(upper, slice(None), held[...])
+    settle(lower, slice(0, done), part[...])
+    out[lower, done:] = own[lower, done:]
+    rest[...] = before[lower, done:]
+    rest_own[...] = own[lower, done:]
+
+
 def final_kernel(
-    place, flag, kept, received, kept_mean, earlier, held, part, first, second, before, own, out
+    flag, kept, received, kept_mean, earlier, rest, rest_own, settled, out, piece, semaphore
 ):
-    rows = kept.shape[1]
-    diagonal, shadow = place[2] == 1, flag[0] == 1
-
-    def settle(start, crossed, at, mixture):
-        here = slice(start, start + rows)
-        residual = jnp.where(diagonal, crossed[:, at].astype(F32), before[here, at].astype(F32))
-        result = jnp.where(shadow, residual + mixture, own[here, at].astype(F32))
-        out[here, at] = result.astype(BF16)
+    rows, width = kept.shape[1:]
+    done = width - rest.shape[1]
+    shadow = flag[0] == 1
 
     def put(at, mixture):
-        settle(rows, second, at, mixture)
-
-    done = part.shape[1]
-    settle(0, first, slice(None), held[...])
-    settle(rows, second, slice(0, done), part[...])
+        here = slice(at.start - done, at.stop - done)
+        result = rest[:, here].astype(F32) + mixture
+        piece[:, here] = jnp.where(shadow, result, rest_own[:, here].astype(F32)).astype(BF16)
+
     mix(kept, received, kept_mean, (earlier,), None, put, done)
+    copy = pltpu.make_async_copy(
+        piece, out.at[pl.ds(rows, rows), pl.ds(done, width - done)], semaphore
+    )
+    copy.start()
+    copy.wait()
 
 
 def call_attend(kernel, name, scalars, arrays, out_shape):
@@ -314,66 +337,63 @@
                 permute(ringed, sections, sibling),
             )
 
-        def partial(four, apart, estimate, cuts=None):
+        def partial(four, apart, estimate, cuts=None, owns=()):
             width = four[0].shape[1]
-            *sents, kept, kept_mean = project(
-                rows, place, four, norm_gain, weight, cuts or [(0, width)], apart, estimate
+            cuts_in = cuts or [(0, width)]
+            results = project(
+                rows, place, four, norm_gain, weight, cuts_in, apart, owns, estimate
             )
-            received = [permute(sent, sections, peer) for sent in sents]
-            return kept, received if cuts else received[0], kept_mean
+            received = [permute(sent, sections, peer) for sent in results[: len(cuts_in)]]
+            kept, kept_mean, *whole = results[len(cuts_in) :]
+            return (kept, received if cuts else received[0], kept_mean, *whole)
 
         block = inputs[0, 0]
         rows = block.shape[0] // PARTS
         parts = [block[i * rows : (i + 1) * rows] for i in range(PARTS)]
-        ringed = permute(parts[0], sections, ring)
+        ringed = [permute(part, sections, ring) for part in parts]
         crossed = permute(parts[0], sections, cross)
-        relayed = permute(parts[1], sections, across_y)
-        ringed, crossed, weight = lax.optimization_barrier((ringed, crossed, weight))
+        ringed[0], crossed, weight = lax.optimization_barrier((ringed[0], crossed, weight))
         weight = pltpu.with_memory_space_constraint(weight, pltpu.VMEM)
-        sums = [partial(spread(crossed, ringed), False, 3)]
-        crossed = jnp.where(diagonal, parts[1], permute(relayed, sections, across_x))
-        crossed, _ = lax.optimization_barrier((crossed, sums[0][2]))
-        swapped = permute(crossed, sections, swap)
-        sums.append(partial(spread(crossed, swapped), True, 0.001))
+        sums = [partial(spread(crossed, ringed[0]), False, 3)]
+        late, _ = lax.optimization_barrier((ringed[1], sums[0][2]))
+        forwarded = permute(late, sections, forward)
+        crossed = jnp.where(diagonal, parts[1], forwarded)
+        sums.append(partial(spread(crossed, late), True, 0.001))
         width = block.shape[1]
         rows_of = pltpu.VMEM((rows, width), BF16)
         pairs_of = pltpu.VMEM((2, rows, width), BF16)
 
         def attend(part, item, held):
             return call_attend(
-                attend_kernel,
+                functools.partial(attend_kernel, not held),
                 "attend",
                 [],
                 [*item, part, *held],
-                [rows_of, pltpu.HBM((rows, width), BF16), pairs_of],
+                [rows_of] if held else [rows_of, pairs_of],
             )
 
         def carry(own):
             return permute(own, sections, onward(cross))
 
-        first, first_again, pairs = attend(parts[0], sums[0], [])
+        first, pairs = attend(parts[0], sums[0], [])
         moved = [carry(first)]
         swapped = permute(moved[0], sections, swap)
         beside = permute(moved[0], sections, sibling)
         part = lax.optimization_barrier((parts[1], beside))[0]
-        second, second_again, _ = attend(part, sums[1], [pairs])
-        owns = [first_again, second_again]
+        (second,) = attend(part, sums[1], [pairs])
         moved.append(carry(second))
         swapped, _ = lax.optimization_barrier((swapped, second))
         four = moved[0], swapped, beside, permute(swapped, sections, sibling)
-        seconds = [partial(four, False, 3)]
-        crossed, _ = lax.optimization_barrier((moved[1], seconds[0][2]))
+        *upper, own = partial(four, False, 3, None, [first, second])
+        crossed, _ = lax.optimization_barrier((moved[1], upper[2]))
         swapped = permute(crossed, sections, swap)
         cut = (width // HD + 1) // 2 * HD
         cuts = [(0, cut), (cut, width)]
         kept, received, kept_mean = partial(spread(crossed, swapped), True, 1, cuts)
-        mixture, pairs, own = call_attend(
-            hold_kernel,
-            "hold",
-            [],
-            [*seconds[0], *owns],
-            [pltpu.VMEM((rows, width), F32), pairs_of, pltpu.VMEM(block.shape, BF16)],
-        )
+        mixture, pairs = call_attend(
+            hold_kernel, "hold", [], upper, [pltpu.VMEM((rows, width), F32), pairs_of]
+        )
+        own, _ = lax.optimization_barrier((own, mixture))
         before = permute(own, sections, onward(direct))
         (part,) = call_attend(
             part_kernel,
@@ -382,13 +402,29 @@
             [kept, received[0], kept_mean, pairs],
             [pltpu.VMEM((rows, cut), F32)],
         )
-        (out,) = call_attend(
+        rest_of = pltpu.VMEM((rows, width - cut), BF16)
+        out, *rest = call_attend(
+            settle_kernel,
+            "settle",
+            [preempted],
+            [mixture, part, before, own],
+            [jax.ShapeDtypeStruct(block.shape, BF16), rest_of, rest_of],
+        )
+        last = [kept, received[1], kept_mean, pairs, *rest]
+        out = pl.pallas_call(
             final_kernel,
-            "final",
-            [place, preempted],
-            [kept, received[1], kept_mean, pairs, mixture, part, *moved, before, own],
-            [jax.ShapeDtypeStruct(block.shape, BF16)],
-        )
+            in_specs=[smem_spec()] + [vmem_spec() for _ in last] + [any_spec()],
+            out_specs=any_spec(),
+            out_shape=jax.ShapeDtypeStruct(block.shape, BF16),
+            input_output_aliases={1 + len(last): 0},
+            scratch_shapes=[
+                pltpu.VMEM((rows, width - cut), BF16),
+                pltpu.SemaphoreType.DMA(()),
+            ],
+            compiler_params=pltpu.CompilerParams(vmem_limit_bytes=VMEM_BYTES),
+            cost_estimate=cost(250),
+            name="final",
+        )(preempted, *last, out)
         return out[None, None]
 
     placed = (

time: 110 us -> 110 us (level)
  waiting for transfers between devices: 38.9 us -> 36.4 us
  local copies, waits for them, and re-layouts: 1.13 us -> 2.48 us
  starting transfers between devices: 35.5 us -> 36.6 us
    pallas_call x5, Pallas kernels: 11.2 us -> 8 us  [call_attend(): pl.pallas_call(kernel, in_specs=[smem_spec() for _ in scalars] + [vmem_sp...]
    ppermute x23 -> x22, waiting for transfers between devices: 38.9 us -> 36.4 us  [permute(): return lax.ppermute(array, AXES, pairs)]
    pallas_call x4 -> x5, Pallas kernels: 17.9 us -> 20.4 us  [the longest x4 18 us: project(): pl.pallas_call(functools.partial(project_kernel, cuts, apart, len(owns)),...]
    unnamed x20 -> x22, local copies, waits for them, and re-layouts: 0.04 us -> 1.4 us
    ppermute x23 -> x22, starting transfers between devices: 35.5 us -> 36.6 us  [permute(): return lax.ppermute(array, AXES, pairs)]
  transfers between devices with their start and end apart: 23 -> 22, of which waited for: 13 -> 13; matrix products, arithmetic and copies ran while one was open for 0% -> 0% of each run, Pallas kernels for 28% -> 28%
where the time goes in v11:
time: 110 us; the launch traced here: 109 us
  starting transfers between devices  36.6 us (33%)
  waiting for transfers between devices  36.4 us (33%)
  Pallas kernels  32.7 us (30%)
  local copies, waits for them, and re-layouts  2.48 us (2%)
    ppermute x22, starting transfers between devices, permute(): return lax.ppermute(array, AXES, pairs)  36.6 us
    ppermute x22, waiting for transfers between devices, permute(): return lax.ppermute(array, AXES, pairs)  36.4 us
    pallas_call x4, Pallas kernels, project(): pl.pallas_call(functools.partial(project_kernel, cuts, apart, len(owns)),...  18 us
    pallas_call x5, Pallas kernels, call_attend(): pl.pallas_call(kernel, in_specs=[smem_spec() for _ in scalars] + [vmem_sp...  8 us
    pallas_call x1, Pallas kernels, stage(): pl.pallas_call(stage_kernel, in_specs=[smem_spec(), any_spec()], out_spec...  4.29 us
    pallas_call x1, Pallas kernels, local(): pl.pallas_call(final_kernel, in_specs=[smem_spec()] + [vmem_spec() for _...  2.39 us
  transfers between devices with their start and end apart: 22, of which 13 were waited for; matrix products, arithmetic and copies ran while one was open for 0% of the time, Pallas kernels for 28%

profile of v11, /device:TPU:0, one launch (start us, length us, event | category | flops | bytes accessed | tf_op | source)
XLA Modules:
  0.0 109.3 jit_solution(11817582766306627683)
XLA Ops:
  1.1 3.0 %collective-permute-start.1 = (bf16[128,896]{1,0:T(8,128)(2,1)S(1)}, bf16[128,896]{1,0:T(8,128)(2,1)S(1)}, u32[]{:S(2)}, u32[]{:S(2)}) collective-permute-start(bf16[128,896]{1,0:T(8,128)(2,1)S(1)} %get-tuple-element.69.block), channel_id=1, source_target_pairs={{0,2},{1,3},{2,6},{3,7},{4,0},{5,1},{6,4},{7,5},{8,10},{9,11},{10,... | collective-permute-start | bytes 688136 | tf_op jit(solution)/shard_map/ppermute | solution.py:32
  4.9 4.3 %stage.1.weight = bf16[1,3,1792,896]{3,2,1,0:T(8,128)(2,1)S(1)} custom-call(s32[3]{0:T(128)S(1)} %pad_add_fusion.place, bf16[1,3,1792,896]{3,2,1,0:T(8,128)(2,1)} %weight), custom_call_target="tpu_custom_call" | custom-call | flops 4600000000 | bytes 1000 | tf_op jit(solution)/shard_map/stage/pallas_call | solution.py:94
  9.2 4.7 %collective-permute-done.1.ringed = bf16[128,896]{1,0:T(8,128)(2,1)S(1)} collective-permute-done((bf16[128,896]{1,0:T(8,128)(2,1)S(1)}, bf16[128,896]{1,0:T(8,128)(2,1)S(1)}, u32[]{:S(2)}, u32[]{:S(2)}) %collective-permute-start.1) | collective-permute-done | bytes 229408 | tf_op jit(solution)/shard_map/ppermute | solution.py:32
  14.4 2.4 %collective-permute-start = (bf16[128,896]{1,0:T(8,128)(2,1)S(1)}, bf16[128,896]{1,0:T(8,128)(2,1)S(1)}, u32[]{:S(2)}, u32[]{:S(2)}) collective-permute-start(bf16[128,896]{1,0:T(8,128)(2,1)S(1)} %get-tuple-element.51.block), channel_id=1, source_target_pairs={{0,2},{1,3},{2,6},{3,7},{4,0},{5,1},{6,4},{7,5},{8,10},{9,11},{10,... | collective-permute-start | bytes 688136 | tf_op jit(solution)/shard_map/ppermute | solution.py:32
  16.9 4.0 %project.4 = (bf16[400,896]{1,0:T(8,128)(2,1)S(1)}, f32[3,128,896]{2,1,0:T(8,128)S(1)}, f32[128,1]{1,0:T(8,128)S(1)}) custom-call(s32[3]{0:T(128)S(1)} %pad_add_fusion.place, bf16[128,896]{1,0:T(8,128)(2,1)S(1)} %collective-permute-done.2.crossed, bf16[128,896]{1,0:T(8,128)(2,1)S(1)} %collective-permute-done.1.ringed, ...), custom_call_target="tpu_custom_call" | custom-call | flops 3449999872 | bytes 1000 | tf_op jit(solution)/shard_map/project/pallas_call | solution.py:180
  20.9 2.3 %collective-permute-start.9 = (bf16[400,896]{1,0:T(8,128)(2,1)S(1)}, bf16[400,896]{1,0:T(8,128)(2,1)S(1)}, u32[]{:S(2)}, u32[]{:S(2)}) collective-permute-start(bf16[400,896]{1,0:T(8,128)(2,1)S(1)} %get-tuple-element.49), channel_id=1, source_target_pairs={{0,4},{1,5},{2,6},{3,7},{4,0},{5,1},{6,2},{7,3},{8,12},{9,13},{10,... | collective-permute-start | bytes 2150408 | tf_op jit(solution)/shard_map/ppermute | solution.py:32
  23.6 2.7 %collective-permute-start.5 = (bf16[128,896]{1,0:T(8,128)(2,1)S(1)}, bf16[128,896]{1,0:T(8,128)(2,1)S(1)}, u32[]{:S(2)}, u32[]{:S(2)}) collective-permute-start(bf16[128,896]{1,0:T(8,128)(2,1)S(1)} %collective-permute-done.ringed), channel_id=1, source_target_pairs={{0,2},{1,3},{6,4},{7,5},{8,10},{9,11},{14,12},{15,13},{16,18},{17,... | collective-permute-start | bytes 688136 | tf_op jit(solution)/shard_map/ppermute | solution.py:32
  26.4 4.1 %collective-permute-done.5 = bf16[128,896]{1,0:T(8,128)(2,1)S(1)} collective-permute-done((bf16[128,896]{1,0:T(8,128)(2,1)S(1)}, bf16[128,896]{1,0:T(8,128)(2,1)S(1)}, u32[]{:S(2)}, u32[]{:S(2)}) %collective-permute-start.5) | collective-permute-done | bytes 229408 | tf_op jit(solution)/shard_map/ppermute | solution.py:32
  32.1 4.7 %project.5 = (bf16[400,896]{1,0:T(8,128)(2,1)}, f32[3,128,896]{2,1,0:T(8,128)S(1)}, f32[128,1]{1,0:T(8,128)S(1)}) custom-call(s32[3]{0:T(128)S(1)} %pad_add_fusion.place, bf16[128,896]{1,0:T(8,128)(2,1)S(1)} %broadcast_select_fusion.crossed, bf16[128,896]{1,0:T(8,128)(2,1)S(1)} %collective-permute-done.ringed, ...), custom_call_target="tpu_custom_call" | custom-call | flops 1150000 | bytes 1000 | tf_op jit(solution)/shard_map/project/pallas_call | solution.py:180
  36.8 3.5 %collective-permute-start.8 = (bf16[400,896]{1,0:T(8,128)(2,1)}, bf16[400,896]{1,0:T(8,128)(2,1)}, u32[]{:S(2)}, u32[]{:S(2)}) collective-permute-start(bf16[400,896]{1,0:T(8,128)(2,1)} %get-tuple-element.46), channel_id=1, source_target_pairs={{0,4},{1,5},{2,6},{3,7},{4,0},{5,1},{6,2},{7,3},{8,12},{9,13},{10,... | collective-permute-start | bytes 2150408 | tf_op jit(solution)/shard_map/ppermute | solution.py:32
  41.1 4.2 %collective-permute-start.10 = (bf16[128,896]{1,0:T(8,128)(2,1)S(1)}, bf16[128,896]{1,0:T(8,128)(2,1)}, u32[]{:S(2)}, u32[]{:S(2)}) collective-permute-start(bf16[128,896]{1,0:T(8,128)(2,1)S(1)} %get-tuple-element.50.refs_0_), channel_id=1, source_target_pairs={{0,8},{1,9},{2,12},{3,13},{4,10},{5,11},{6,14},{7,15},{8,16},{9,17... | collective-permute-start | bytes 688136 | tf_op jit(solution)/shard_map/ppermute | solution.py:32
  46.0 3.5 %collective-permute-done.10.crossed = bf16[128,896]{1,0:T(8,128)(2,1)} collective-permute-done((bf16[128,896]{1,0:T(8,128)(2,1)S(1)}, bf16[128,896]{1,0:T(8,128)(2,1)}, u32[]{:S(2)}, u32[]{:S(2)}) %collective-permute-start.10) | collective-permute-done | bytes 229408 | tf_op jit(solution)/shard_map/ppermute | solution.py:32
  51.9 5.1 %collective-permute-done.8.received = bf16[400,896]{1,0:T(8,128)(2,1)} collective-permute-done((bf16[400,896]{1,0:T(8,128)(2,1)}, bf16[400,896]{1,0:T(8,128)(2,1)}, u32[]{:S(2)}, u32[]{:S(2)}) %collective-permute-start.8) | collective-permute-done | bytes 716832 | tf_op jit(solution)/shard_map/ppermute | solution.py:32
  56.9 2.4 %attend.3.refs_1_ = bf16[128,896]{1,0:T(8,128)(2,1)S(1)} custom-call(f32[3,128,896]{2,1,0:T(8,128)S(1)} %get-tuple-element.45.kept, bf16[400,896]{1,0:T(8,128)(2,1)} %collective-permute-done.8.received, f32[128,1]{1,0:T(8,128)S(1)} %get-tuple-element.47.kept_mean, bf16[128,896]{1,0:T(8,128)(2,1)S(1)} %get-tuple-element.51.block, ...), custom_call_target="tpu_custom_call" | custom-call | flops 287500009472 | bytes 1000 | tf_op jit(solution)/shard_map/attend/pallas_call | solution.py:311
  59.4 8.7 %collective-permute-start.12 = (bf16[128,896]{1,0:T(8,128)(2,1)S(1)}, bf16[128,896]{1,0:T(8,128)(2,1)S(1)}, u32[]{:S(2)}, u32[]{:S(2)}) collective-permute-start(bf16[128,896]{1,0:T(8,128)(2,1)S(1)} %attend.3.refs_1_), channel_id=1, source_target_pairs={{0,8},{1,9},{2,12},{3,13},{4,10},{5,11},{6,14},{7,15},{8,16},{9,17... | collective-permute-start | bytes 688136 | tf_op jit(solution)/shard_map/ppermute | solution.py:32
  68.2 4.6 %project.6 = (bf16[400,896]{1,0:T(8,128)(2,1)S(1)}, f32[3,128,896]{2,1,0:T(8,128)S(1)}, f32[128,1]{1,0:T(8,128)S(1)}, bf16[256,896]{1,0:T(8,128)(2,1)}) custom-call(s32[3]{0:T(128)S(1)} %copy-done.5, bf16[128,896]{1,0:T(8,128)(2,1)} %collective-permute-done.10.crossed, bf16[128,896]{1,0:T(8,128)(2,1)} %collective-permute-done.13.ringed, ...), custom_call_target="tpu_custom_call" | custom-call | flops 3449999872 | bytes 1000 | tf_op jit(solution)/shard_map/project/pallas_call | solution.py:180
  74.2 6.4 %collective-permute-done.15.ringed = bf16[128,896]{1,0:T(8,128)(2,1)S(1)} collective-permute-done((bf16[128,896]{1,0:T(8,128)(2,1)S(1)}, bf16[128,896]{1,0:T(8,128)(2,1)S(1)}, u32[]{:S(2)}, u32[]{:S(2)}) %collective-permute-start.15) | collective-permute-done | bytes 229408 | tf_op jit(solution)/shard_map/ppermute | solution.py:32
  82.0 4.7 %project.7 = (bf16[400,512]{1,0:T(8,128)(2,1)}, bf16[400,384]{1,0:T(8,128)(2,1)}, f32[3,128,896]{2,1,0:T(8,128)S(1)}, f32[128,1]{1,0:T(8,128)S(1)}) custom-call(s32[3]{0:T(128)S(1)} %copy-done.5, bf16[128,896]{1,0:T(8,128)(2,1)S(1)} %collective-permute-done.12.crossed, bf16[128,896]{1,0:T(8,128)(2,1)S(1)} %collective-permute-done.15.ringed, ...), custom_call_target="tpu_custom_call" | custom-call | flops 1150000000 | bytes 1000 | tf_op jit(solution)/shard_map/project/pallas_call | solution.py:180
  88.8 3.0 %collective-permute-done.19.received = bf16[400,896]{1,0:T(8,128)(2,1)S(1)} collective-permute-done((bf16[400,896]{1,0:T(8,128)(2,1)S(1)}, bf16[400,896]{1,0:T(8,128)(2,1)S(1)}, u32[]{:S(2)}, u32[]{:S(2)}) %collective-permute-start.19) | collective-permute-done | bytes 716832 | tf_op jit(solution)/shard_map/ppermute | solution.py:32
  92.6 3.8 %collective-permute-start.21 = (bf16[256,896]{1,0:T(8,128)(2,1)}, bf16[256,896]{1,0:T(8,128)(2,1)}, u32[]{:S(2)}, u32[]{:S(2)}) collective-permute-start(bf16[256,896]{1,0:T(8,128)(2,1)} %get-tuple-element.65.own), channel_id=1, source_target_pairs={{0,8},{1,9},{2,10},{3,11},{4,12},{5,13},{6,14},{7,15},{8,16},{9,17... | collective-permute-start | bytes 1376264 | tf_op jit(solution)/shard_map/ppermute | solution.py:32
  96.4 4.3 %collective-permute-done.20.received = bf16[400,512]{1,0:T(8,128)(2,1)} collective-permute-done((bf16[400,512]{1,0:T(8,128)(2,1)}, bf16[400,512]{1,0:T(8,128)(2,1)}, u32[]{:S(2)}, u32[]{:S(2)}) %collective-permute-start.20) | collective-permute-done | bytes 409632 | tf_op jit(solution)/shard_map/ppermute | solution.py:32
  102.5 2.2 %collective-permute-done.21.before = bf16[256,896]{1,0:T(8,128)(2,1)} collective-permute-done((bf16[256,896]{1,0:T(8,128)(2,1)}, bf16[256,896]{1,0:T(8,128)(2,1)}, u32[]{:S(2)}, u32[]{:S(2)}) %collective-permute-start.21) | collective-permute-done | bytes 458784 | tf_op jit(solution)/shard_map/ppermute | solution.py:32
  104.7 2.0 %settle.1 = (bf16[256,896]{1,0:T(8,128)(2,1)}, bf16[128,384]{1,0:T(8,128)(2,1)S(1)}, bf16[128,384]{1,0:T(8,128)(2,1)S(1)}) custom-call(s32[1]{0:T(128)S(6)} %copy.7.flag, f32[128,896]{1,0:T(8,128)S(1)} %get-tuple-element.62.held, f32[128,512]{1,0:T(8,128)S(1)} %part.1, bf16[256,896]{1,0:T(8,128)(2,1)} %collective-permute-done.21.before, ...), custom_call_target="tpu_custom_call" | custom-call | flops 287500009472 | bytes 1000 | tf_op jit(solution)/shard_map/settle/pallas_call | solution.py:311
  106.8 2.4 %final.1 = bf16[256,896]{1,0:T(8,128)(2,1)} custom-call(s32[1]{0:T(128)S(6)} %copy.7.flag, f32[3,128,896]{2,1,0:T(8,128)S(1)} %get-tuple-element.56.kept, bf16[400,384]{1,0:T(8,128)(2,1)} %collective-permute-done.18.received, f32[128,1]{1,0:T(8,128)S(1)} %get-tuple-element.58.kept_mean, ...), custom_call_target="tpu_custom_call", output_to_operand_aliasing={{}: (7, {})} | custom-call | flops 287500009472 | bytes 1000 | tf_op jit(solution)/shard_map/final/pallas_call | solution.py:414
  (56 shorter events, 15.3 us)
Async XLA Ops:
  1.1 12.8 %collective-permute-start.1 = (bf16[128,896]{1,0:T(8,128)(2,1)S(1)}, bf16[128,896]{1,0:T(8,128)(2,1)S(1)}, u32[]{:S(2)}, u32[]{:S(2)}) collective-permute-start(bf16[128,896]{1,0:T(8,128)(2,1)S(1)} %get-tuple-element.69.block), channel_id=1, source_target_pairs={{0,2},{1,3},{2,6},{3,7},{4,0},{5,1},{6,4},{7,5},{8,10},{9,11},{10,... | collective-permute-start | bytes 688136 | tf_op jit(solution)/shard_map/ppermute | solution.py:32
  4.1 9.8 %collective-permute-start.2 = (bf16[128,896]{1,0:T(8,128)(2,1)S(1)}, bf16[128,896]{1,0:T(8,128)(2,1)S(1)}, u32[]{:S(2)}, u32[]{:S(2)}) collective-permute-start(bf16[128,896]{1,0:T(8,128)(2,1)S(1)} %get-tuple-element.69.block), channel_id=1, source_target_pairs={{0,0},{1,1},{2,4},{3,5},{4,2},{5,3},{6,6},{7,7},{8,8},{9,9},{10,12... | collective-permute-start | bytes 688136 | tf_op jit(solution)/shard_map/ppermute | solution.py:32
  4.9 27.2 %copy-start.4 = (s32[3]{0:T(128)}, s32[3]{0:T(128)S(1)}, u32[]{:S(2)}) copy-start(s32[3]{0:T(128)S(1)} %pad_add_fusion.place) | copy-start | bytes 40
  9.2 22.9 %copy-start = (bf16[1,3,1792,896]{3,2,1,0:T(8,128)(2,1)}, bf16[1,3,1792,896]{3,2,1,0:T(8,128)(2,1)S(1)}, u32[]{:S(2)}) copy-start(bf16[1,3,1792,896]{3,2,1,0:T(8,128)(2,1)S(1)} %stage.1.weight) | copy-start | bytes 28901380
  13.9 3.0 %collective-permute-start.3 = (bf16[128,896]{1,0:T(8,128)(2,1)S(1)}, bf16[128,896]{1,0:T(8,128)(2,1)S(1)}, u32[]{:S(2)}, u32[]{:S(2)}) collective-permute-start(bf16[128,896]{1,0:T(8,128)(2,1)S(1)} %collective-permute-done.2.crossed), channel_id=1, source_target_pairs={{0,1},{1,0},{2,3},{3,2},{4,5},{5,4},{6,7},{7,6},{8,9},{9,8},{10,11... | collective-permute-start | bytes 688136 | tf_op jit(solution)/shard_map/ppermute | solution.py:32
  13.9 3.0 %collective-permute-start.4 = (bf16[128,896]{1,0:T(8,128)(2,1)S(1)}, bf16[128,896]{1,0:T(8,128)(2,1)S(1)}, u32[]{:S(2)}, u32[]{:S(2)}) collective-permute-start(bf16[128,896]{1,0:T(8,128)(2,1)S(1)} %collective-permute-done.1.ringed), channel_id=1, source_target_pairs={{0,1},{1,0},{2,3},{3,2},{4,5},{5,4},{6,7},{7,6},{8,9},{9,8},{10,11... | collective-permute-start | bytes 688136 | tf_op jit(solution)/shard_map/ppermute | solution.py:32
  14.4 9.1 %collective-permute-start = (bf16[128,896]{1,0:T(8,128)(2,1)S(1)}, bf16[128,896]{1,0:T(8,128)(2,1)S(1)}, u32[]{:S(2)}, u32[]{:S(2)}) collective-permute-start(bf16[128,896]{1,0:T(8,128)(2,1)S(1)} %get-tuple-element.51.block), channel_id=1, source_target_pairs={{0,2},{1,3},{2,6},{3,7},{4,0},{5,1},{6,4},{7,5},{8,10},{9,11},{10,... | collective-permute-start | bytes 688136 | tf_op jit(solution)/shard_map/ppermute | solution.py:32
  20.9 19.3 %collective-permute-start.9 = (bf16[400,896]{1,0:T(8,128)(2,1)S(1)}, bf16[400,896]{1,0:T(8,128)(2,1)S(1)}, u32[]{:S(2)}, u32[]{:S(2)}) collective-permute-start(bf16[400,896]{1,0:T(8,128)(2,1)S(1)} %get-tuple-element.49), channel_id=1, source_target_pairs={{0,4},{1,5},{2,6},{3,7},{4,0},{5,1},{6,2},{7,3},{8,12},{9,13},{10,... | collective-permute-start | bytes 2150408 | tf_op jit(solution)/shard_map/ppermute | solution.py:32
  23.6 6.9 %collective-permute-start.5 = (bf16[128,896]{1,0:T(8,128)(2,1)S(1)}, bf16[128,896]{1,0:T(8,128)(2,1)S(1)}, u32[]{:S(2)}, u32[]{:S(2)}) collective-permute-start(bf16[128,896]{1,0:T(8,128)(2,1)S(1)} %collective-permute-done.ringed), channel_id=1, source_target_pairs={{0,2},{1,3},{6,4},{7,5},{8,10},{9,11},{14,12},{15,13},{16,18},{17,... | collective-permute-start | bytes 688136 | tf_op jit(solution)/shard_map/ppermute | solution.py:32
  26.3 4.3 %collective-permute-start.7 = (bf16[128,896]{1,0:T(8,128)(2,1)S(1)}, bf16[128,896]{1,0:T(8,128)(2,1)S(1)}, u32[]{:S(2)}, u32[]{:S(2)}) collective-permute-start(bf16[128,896]{1,0:T(8,128)(2,1)S(1)} %collective-permute-done.ringed), channel_id=1, source_target_pairs={{0,1},{1,0},{2,3},{3,2},{4,5},{5,4},{6,7},{7,6},{8,9},{9,8},{10,11... | collective-permute-start | bytes 688136 | tf_op jit(solution)/shard_map/ppermute | solution.py:32
  30.5 1.6 %collective-permute-start.6 = (bf16[128,896]{1,0:T(8,128)(2,1)S(1)}, bf16[128,896]{1,0:T(8,128)(2,1)S(1)}, u32[]{:S(2)}, u32[]{:S(2)}) collective-permute-start(bf16[128,896]{1,0:T(8,128)(2,1)S(1)} %broadcast_select_fusion.crossed), channel_id=1, source_target_pairs={{0,1},{1,0},{2,3},{3,2},{4,5},{5,4},{6,7},{7,6},{8,9},{9,8},{10,11... | collective-permute-start | bytes 688136 | tf_op jit(solution)/shard_map/ppermute | solution.py:32
  36.8 20.1 %collective-permute-start.8 = (bf16[400,896]{1,0:T(8,128)(2,1)}, bf16[400,896]{1,0:T(8,128)(2,1)}, u32[]{:S(2)}, u32[]{:S(2)}) collective-permute-start(bf16[400,896]{1,0:T(8,128)(2,1)} %get-tuple-element.46), channel_id=1, source_target_pairs={{0,4},{1,5},{2,6},{3,7},{4,0},{5,1},{6,2},{7,3},{8,12},{9,13},{10,... | collective-permute-start | bytes 2150408 | tf_op jit(solution)/shard_map/ppermute | solution.py:32
  41.1 8.4 %collective-permute-start.10 = (bf16[128,896]{1,0:T(8,128)(2,1)S(1)}, bf16[128,896]{1,0:T(8,128)(2,1)}, u32[]{:S(2)}, u32[]{:S(2)}) collective-permute-start(bf16[128,896]{1,0:T(8,128)(2,1)S(1)} %get-tuple-element.50.refs_0_), channel_id=1, source_target_pairs={{0,8},{1,9},{2,12},{3,13},{4,10},{5,11},{6,14},{7,15},{8,16},{9,17... | collective-permute-start | bytes 688136 | tf_op jit(solution)/shard_map/ppermute | solution.py:32
  49.5 1.7 %collective-permute-start.11 = (bf16[128,896]{1,0:T(8,128)(2,1)}, bf16[128,896]{1,0:T(8,128)(2,1)S(1)}, u32[]{:S(2)}, u32[]{:S(2)}) collective-permute-start(bf16[128,896]{1,0:T(8,128)(2,1)} %collective-permute-done.10.crossed), channel_id=1, source_target_pairs={{0,1},{1,0},{2,3},{3,2},{4,5},{5,4},{6,7},{7,6},{8,9},{9,8},{10,11... | collective-permute-start | bytes 688136 | tf_op jit(solution)/shard_map/ppermute | solution.py:32
  49.5 9.9 %collective-permute-start.13 = (bf16[128,896]{1,0:T(8,128)(2,1)}, bf16[128,896]{1,0:T(8,128)(2,1)}, u32[]{:S(2)}, u32[]{:S(2)}) collective-permute-start(bf16[128,896]{1,0:T(8,128)(2,1)} %collective-permute-done.10.crossed), channel_id=1, source_target_pairs={{0,2},{1,3},{2,0},{3,1},{4,6},{5,7},{6,4},{7,5},{8,10},{9,11},{10,... | collective-permute-start | bytes 688136 | tf_op jit(solution)/shard_map/ppermute | solution.py:32
  59.3 8.8 %collective-permute-start.14 = (bf16[128,896]{1,0:T(8,128)(2,1)}, bf16[128,896]{1,0:T(8,128)(2,1)S(1)}, u32[]{:S(2)}, u32[]{:S(2)}) collective-permute-start(bf16[128,896]{1,0:T(8,128)(2,1)} %collective-permute-done.13.ringed), channel_id=1, source_target_pairs={{0,1},{1,0},{2,3},{3,2},{4,5},{5,4},{6,7},{7,6},{8,9},{9,8},{10,11... | collective-permute-start | bytes 688136 | tf_op jit(solution)/shard_map/ppermute | solution.py:32
  59.4 13.9 %collective-permute-start.12 = (bf16[128,896]{1,0:T(8,128)(2,1)S(1)}, bf16[128,896]{1,0:T(8,128)(2,1)S(1)}, u32[]{:S(2)}, u32[]{:S(2)}) collective-permute-start(bf16[128,896]{1,0:T(8,128)(2,1)S(1)} %attend.3.refs_1_), channel_id=1, source_target_pairs={{0,8},{1,9},{2,12},{3,13},{4,10},{5,11},{6,14},{7,15},{8,16},{9,17... | collective-permute-start | bytes 688136 | tf_op jit(solution)/shard_map/ppermute | solution.py:32
  72.8 19.0 %collective-permute-start.19 = (bf16[400,896]{1,0:T(8,128)(2,1)S(1)}, bf16[400,896]{1,0:T(8,128)(2,1)S(1)}, u32[]{:S(2)}, u32[]{:S(2)}) collective-permute-start(bf16[400,896]{1,0:T(8,128)(2,1)S(1)} %get-tuple-element.60), channel_id=1, source_target_pairs={{0,4},{1,5},{2,6},{3,7},{4,0},{5,1},{6,2},{7,3},{8,12},{9,13},{10,... | collective-permute-start | bytes 2150408 | tf_op jit(solution)/shard_map/ppermute | solution.py:32
  73.3 7.2 %collective-permute-start.15 = (bf16[128,896]{1,0:T(8,128)(2,1)S(1)}, bf16[128,896]{1,0:T(8,128)(2,1)S(1)}, u32[]{:S(2)}, u32[]{:S(2)}) collective-permute-start(bf16[128,896]{1,0:T(8,128)(2,1)S(1)} %collective-permute-done.12.crossed), channel_id=1, source_target_pairs={{0,2},{1,3},{2,0},{3,1},{4,6},{5,7},{6,4},{7,5},{8,10},{9,11},{10,... | collective-permute-start | bytes 688136 | tf_op jit(solution)/shard_map/ppermute | solution.py:32
  74.2 7.0 %collective-permute-start.16 = (bf16[128,896]{1,0:T(8,128)(2,1)S(1)}, bf16[128,896]{1,0:T(8,128)(2,1)S(1)}, u32[]{:S(2)}, u32[]{:S(2)}) collective-permute-start(bf16[128,896]{1,0:T(8,128)(2,1)S(1)} %collective-permute-done.12.crossed), channel_id=1, source_target_pairs={{0,1},{1,0},{2,3},{3,2},{4,5},{5,4},{6,7},{7,6},{8,9},{9,8},{10,11... | collective-permute-start | bytes 688136 | tf_op jit(solution)/shard_map/ppermute | solution.py:32
  80.5 1.5 %collective-permute-start.17 = (bf16[128,896]{1,0:T(8,128)(2,1)S(1)}, bf16[128,896]{1,0:T(8,128)(2,1)S(1)}, u32[]{:S(2)}, u32[]{:S(2)}) collective-permute-start(bf16[128,896]{1,0:T(8,128)(2,1)S(1)} %collective-permute-done.15.ringed), channel_id=1, source_target_pairs={{0,1},{1,0},{2,3},{3,2},{4,5},{5,4},{6,7},{7,6},{8,9},{9,8},{10,11... | collective-permute-start | bytes 688136 | tf_op jit(solution)/shard_map/ppermute | solution.py:32
  86.7 14.0 %collective-permute-start.20 = (bf16[400,512]{1,0:T(8,128)(2,1)}, bf16[400,512]{1,0:T(8,128)(2,1)}, u32[]{:S(2)}, u32[]{:S(2)}) collective-permute-start(bf16[400,512]{1,0:T(8,128)(2,1)} %get-tuple-element.63), channel_id=1, source_target_pairs={{0,4},{1,5},{2,6},{3,7},{4,0},{5,1},{6,2},{7,3},{8,12},{9,13},{10,... | collective-permute-start | bytes 1228808 | tf_op jit(solution)/shard_map/ppermute | solution.py:32
  88.4 18.3 %collective-permute-start.18 = (bf16[400,384]{1,0:T(8,128)(2,1)}, bf16[400,384]{1,0:T(8,128)(2,1)}, u32[]{:S(2)}, u32[]{:S(2)}) collective-permute-start(bf16[400,384]{1,0:T(8,128)(2,1)} %get-tuple-element.57), channel_id=1, source_target_pairs={{0,4},{1,5},{2,6},{3,7},{4,0},{5,1},{6,2},{7,3},{8,12},{9,13},{10,... | collective-permute-start | bytes 921608 | tf_op jit(solution)/shard_map/ppermute | solution.py:32
  92.6 12.1 %collective-permute-start.21 = (bf16[256,896]{1,0:T(8,128)(2,1)}, bf16[256,896]{1,0:T(8,128)(2,1)}, u32[]{:S(2)}, u32[]{:S(2)}) collective-permute-start(bf16[256,896]{1,0:T(8,128)(2,1)} %get-tuple-element.65.own), channel_id=1, source_target_pairs={{0,8},{1,9},{2,10},{3,11},{4,12},{5,13},{6,14},{7,15},{8,16},{9,17... | collective-permute-start | bytes 1376264 | tf_op jit(solution)/shard_map/ppermute | solution.py:32
  (9 other events, 85.8 us)

commit v12 on v11

--- a/solution.py
+++ b/solution.py
@@ -13,9 +13,13 @@
 AXES = ("section", "dp", "tensor")
 F32 = jnp.float32
 BF16 = jnp.bfloat16
-PARTS = 2
 VMEM_BYTES = 16 * 1024 * 1024
 STAT_ROWS = 16
+
+
+def chunk_rows(length):
+    first = length * 9 // 16
+    return [first, length - first]
 
 
 def permute(array, sections, hop):
@@ -101,6 +105,24 @@
         cost_estimate=cost(4),
         name="stage",
     )(place, pltpu.with_memory_space_constraint(weight, pltpu.HBM))
+
+
+def to_lanes(column):
+    rows = column.shape[0]
+    wide = jnp.broadcast_to(column, (rows, HD))
+    if rows % HD:
+        wide = jnp.concatenate([wide, jnp.zeros((-rows % HD, HD), F32)])
+    tiles = [jnp.transpose(wide[i : i + HD])[:STAT_ROWS] for i in range(0, wide.shape[0], HD)]
+    return jnp.concatenate(tiles, axis=1) if len(tiles) > 1 else tiles[0]
+
+
+def to_column(row, rows):
+    tiles = [
+        jnp.transpose(jnp.broadcast_to(row[:, i : i + HD], (HD, HD)))
+        for i in range(0, row.shape[1], HD)
+    ]
+    column = jnp.concatenate(tiles) if len(tiles) > 1 else tiles[0]
+    return column[:rows, :1]
 
 
 def project_kernel(
@@ -148,15 +170,15 @@
     on_diagonal = diagonal == 1
     sent_mean = jnp.where(on_diagonal, means[1], means[0])
     kept_mean[...] = jnp.where(on_diagonal, means[0], means[1])
-    row = jnp.transpose(jnp.broadcast_to(sent_mean, (rows, HD)))[:STAT_ROWS]
+    row = to_lanes(sent_mean)
     high = row.astype(BF16).astype(F32)
     mid = (row - high).astype(BF16).astype(F32)
     low = row - high - mid
     which = lax.broadcasted_iota(jnp.int32, row.shape, 0)
     stat = jnp.where(which == 0, high, jnp.where(which == 1, mid, low)).astype(BF16)
     for (begin, end), out, sent in zip(cuts, outs, sents):
-        for column in range(0, end - begin, rows):
-            out[:STAT_ROWS, column : column + rows] = stat
+        out[:STAT_ROWS] = jnp.zeros((STAT_ROWS, end - begin), BF16)
+        out[:STAT_ROWS, : stat.shape[1]] = stat
         for k in range(3):
             product = jnp.dot(normed[...], weight[0, k, :, begin:end], preferred_element_type=F32)
             top = STAT_ROWS + k * rows
@@ -196,16 +218,25 @@
 def mix(kept, received, kept_mean, earlier, pairs, put, first=0):
     rows = kept.shape[1]
     last = first + received.shape[1]
-    stat = received[:STAT_ROWS, :rows].astype(F32)
-    row = stat[0:1] + stat[1:2] + stat[2:3]
-    mean_peer = jnp.transpose(jnp.broadcast_to(row, (HD, rows)))[:, :1]
+    stat = received[:STAT_ROWS, : rows + -rows % HD].astype(F32)
+    mean_peer = to_column(stat[0:1] + stat[1:2] + stat[2:3], rows)
     mean_kept = kept_mean[...]
     inverse = lax.rsqrt((mean_kept + mean_peer) * 0.5 + EPS)
     scale_kept = inverse * jnp.sqrt(mean_kept + EPS)
     scale_peer = inverse * jnp.sqrt(mean_peer + EPS)
-    causal = lax.broadcasted_iota(jnp.int32, (rows, rows), 0) >= lax.broadcasted_iota(
-        jnp.int32, (rows, rows), 1
+    start = sum(ref.shape[1] for ref in earlier)
+    padding = -(start + rows) % HD
+    shape = (rows, start + rows + padding)
+    causal = lax.broadcasted_iota(jnp.int32, shape, 0) + start >= lax.broadcasted_iota(
+        jnp.int32, shape, 1
     )
+
+    def together(k, at, mine):
+        pieces = [ref[k, :, at] for ref in earlier] + [mine]
+        if padding:
+            pieces.append(jnp.zeros((padding, HD), BF16))
+        return jnp.concatenate(pieces) if len(pieces) > 1 else mine
+
     heads = [slice(begin, begin + HD) for begin in range(first, last, HD)]
     held, scores = [], []
     for at in heads:
@@ -223,27 +254,16 @@
         if pairs is not None:
             pairs[0, :, at] = keys
             pairs[1, :, at] = values
-        held.append([(ref[0, :, at], ref[1, :, at]) for ref in earlier] + [(keys, values)])
-        scores.append(
-            [
-                lax.dot_general(queries, key, (((1,), (1,)), ((), ())), preferred_element_type=F32)
-                * (1.0 / math.sqrt(HD))
-                for key, _ in held[-1]
-            ]
-        )
-        scores[-1][-1] = jnp.where(causal, scores[-1][-1], F32(-1e30))
-    tops = [
-        functools.reduce(jnp.maximum, [jnp.max(item, axis=-1, keepdims=True) for item in score])
-        for score in scores
-    ]
-    raised = [[jnp.exp(item - top) for item in score] for score, top in zip(scores, tops)]
-    overs = [1.0 / sum(jnp.sum(item, axis=-1, keepdims=True) for item in items) for items in raised]
-    for at, items, over, pair in zip(heads, raised, overs, held):
-        mixture = sum(
-            jnp.dot((item * over).astype(BF16), value, preferred_element_type=F32)
-            for item, (_, value) in zip(items, pair)
-        )
-        put(at, mixture)
+        held.append(together(1, at, values))
+        score = lax.dot_general(
+            queries, together(0, at, keys), (((1,), (1,)), ((), ())), preferred_element_type=F32
+        )
+        scores.append(jnp.where(causal, score * (1.0 / math.sqrt(HD)), F32(-1e30)))
+    tops = [jnp.max(score, axis=-1, keepdims=True) for score in scores]
+    raised = [jnp.exp(score - top) for score, top in zip(scores, tops)]
+    overs = [1.0 / jnp.sum(item, axis=-1, keepdims=True) for item in raised]
+    for at, item, over, values in zip(heads, raised, overs, held):
+        put(at, jnp.dot((item * over).astype(BF16), values, preferred_element_type=F32))
 
 
 def attend_kernel(first, kept, received, kept_mean, block, *refs):
@@ -270,7 +290,7 @@
 
 
 def settle_kernel(flag, held, part, before, own, out, rest, rest_own):
-    rows, done = part.shape
+    rows, done = held.shape[0], part.shape[1]
     shadow = flag[0] == 1
 
     def settle(here, at, mixture):
@@ -279,7 +299,7 @@
         )
         out[here, at] = result.astype(BF16)
 
-    upper, lower = slice(0, rows), slice(rows, 2 * rows)
+    upper, lower = slice(0, rows), slice(rows, rows + part.shape[0])
     settle(upper, slice(None), held[...])
     settle(lower, slice(0, done), part[...])
     out[lower, done:] = own[lower, done:]
@@ -301,7 +321,7 @@
 
     mix(kept, received, kept_mean, (earlier,), None, put, done)
     copy = pltpu.make_async_copy(
-        piece, out.at[pl.ds(rows, rows), pl.ds(done, width - done)], semaphore
+        piece, out.at[pl.ds(out.shape[0] - rows, rows), pl.ds(done, width - done)], semaphore
     )
     copy.start()
     copy.wait()
@@ -338,7 +358,7 @@
             )
 
         def partial(four, apart, estimate, cuts=None, owns=()):
-            width = four[0].shape[1]
+            rows, width = four[0].shape
             cuts_in = cuts or [(0, width)]
             results = project(
                 rows, place, four, norm_gain, weight, cuts_in, apart, owns, estimate
@@ -348,8 +368,8 @@
             return (kept, received if cuts else received[0], kept_mean, *whole)
 
         block = inputs[0, 0]
-        rows = block.shape[0] // PARTS
-        parts = [block[i * rows : (i + 1) * rows] for i in range(PARTS)]
+        above, below = chunk_rows(block.shape[0])
+        parts = [block[:above], block[above:]]
         ringed = [permute(part, sections, ring) for part in parts]
         crossed = permute(parts[0], sections, cross)
         ringed[0], crossed, weight = lax.optimization_barrier((ringed[0], crossed, weight))
@@ -360,8 +380,7 @@
         crossed = jnp.where(diagonal, parts[1], forwarded)
         sums.append(partial(spread(crossed, late), True, 0.001))
         width = block.shape[1]
-        rows_of = pltpu.VMEM((rows, width), BF16)
-        pairs_of = pltpu.VMEM((2, rows, width), BF16)
+        pairs_of = pltpu.VMEM((2, above, width), BF16)
 
         def attend(part, item, held):
             return call_attend(
@@ -369,7 +388,7 @@
                 "attend",
                 [],
                 [*item, part, *held],
-                [rows_of] if held else [rows_of, pairs_of],
+                [pltpu.VMEM(part.shape, BF16)] + [pairs_of] * (not held),
             )
 
         def carry(own):
@@ -389,20 +408,20 @@
         swapped = permute(crossed, sections, swap)
         cut = (width // HD + 1) // 2 * HD
         cuts = [(0, cut), (cut, width)]
-        kept, received, kept_mean = partial(spread(crossed, swapped), True, 1, cuts)
+        kept, received, kept_mean = partial(spread(crossed, swapped), True, 2, cuts)
+        before = permute(own, sections, onward(direct))
+        before, *upper = lax.optimization_barrier((before, *upper))
         mixture, pairs = call_attend(
-            hold_kernel, "hold", [], upper, [pltpu.VMEM((rows, width), F32), pairs_of]
-        )
-        own, _ = lax.optimization_barrier((own, mixture))
-        before = permute(own, sections, onward(direct))
+            hold_kernel, "hold", [], upper, [pltpu.VMEM((above, width), F32), pairs_of]
+        )
         (part,) = call_attend(
             part_kernel,
             "part",
             [],
             [kept, received[0], kept_mean, pairs],
-            [pltpu.VMEM((rows, cut), F32)],
-        )
-        rest_of = pltpu.VMEM((rows, width - cut), BF16)
+            [pltpu.VMEM((below, cut), F32)],
+        )
+        rest_of = pltpu.VMEM((below, width - cut), BF16)
         out, *rest = call_attend(
             settle_kernel,
             "settle",
@@ -418,7 +437,7 @@
             out_shape=jax.ShapeDtypeStruct(block.shape, BF16),
             input_output_aliases={1 + len(last): 0},
             scratch_shapes=[
-                pltpu.VMEM((rows, width - cut), BF16),
+                pltpu.VMEM((below, width - cut), BF16),
                 pltpu.SemaphoreType.DMA(()),
             ],
             compiler_params=pltpu.CompilerParams(vmem_limit_bytes=VMEM_BYTES),

time: 110 us -> 110 us (level)
  waiting for transfers between devices: 36.4 us -> 40.1 us
  local copies, waits for them, and re-layouts: 2.48 us -> 1.03 us
  Pallas kernels: 32.7 us -> 31.5 us
  starting transfers between devices: 36.6 us -> 35.4 us
    ppermute x22, waiting for transfers between devices: 36.4 us -> 40.1 us  [permute(): return lax.ppermute(array, AXES, pairs)]
    unnamed x22 -> x20, local copies, waits for them, and re-layouts: 1.4 us -> 0.04 us
    pallas_call x5, Pallas kernels: 8 us -> 6.76 us  [call_attend(): pl.pallas_call(kernel, in_specs=[smem_spec() for _ in scalars] + [vmem_sp...]
    ppermute x22, starting transfers between devices: 36.6 us -> 35.4 us  [permute(): return lax.ppermute(array, AXES, pairs)]
  transfers between devices with their start and end apart: 22 -> 22, of which waited for: 13 -> 12; matrix products, arithmetic and copies ran while one was open for 0% -> 0% of each run, Pallas kernels for 28% -> 27%
where the time goes in v12:
time: 110 us; the launch traced here: 109 us
  waiting for transfers between devices  40.1 us (36%)
  starting transfers between devices  35.4 us (32%)
  Pallas kernels  31.5 us (29%)
    ppermute x22, waiting for transfers between devices, permute(): return lax.ppermute(array, AXES, pairs)  40.1 us
    ppermute x22, starting transfers between devices, permute(): return lax.ppermute(array, AXES, pairs)  35.4 us
    pallas_call x4, Pallas kernels, project(): pl.pallas_call(functools.partial(project_kernel, cuts, apart, len(owns)),...  18.2 us
    pallas_call x5, Pallas kernels, call_attend(): pl.pallas_call(kernel, in_specs=[smem_spec() for _ in scalars] + [vmem_sp...  6.76 us
    pallas_call x1, Pallas kernels, stage(): pl.pallas_call(stage_kernel, in_specs=[smem_spec(), any_spec()], out_spec...  4.29 us
    pallas_call x1, Pallas kernels, local(): pl.pallas_call(final_kernel, in_specs=[smem_spec()] + [vmem_spec() for _...  2.32 us
  transfers between devices with their start and end apart: 22, of which 12 were waited for; matrix products, arithmetic and copies ran while one was open for 0% of the time, Pallas kernels for 27%

profile of v12, /device:TPU:0, one launch (start us, length us, event | category | flops | bytes accessed | tf_op | source)
XLA Modules:
  0.0 109.2 jit_solution(3641208713861075109)
XLA Ops:
  1.0 3.0 %collective-permute-start.1 = (bf16[144,896]{1,0:T(8,128)(2,1)S(1)}, bf16[144,896]{1,0:T(8,128)(2,1)S(1)}, u32[]{:S(2)}, u32[]{:S(2)}) collective-permute-start(bf16[144,896]{1,0:T(8,128)(2,1)S(1)} %slice_bitcast_fusion.block), channel_id=1, source_target_pairs={{0,2},{1,3},{2,6},{3,7},{4,0},{5,1},{6,4},{7,5},{8,10},{9,11},{10,... | collective-permute-start | bytes 774152 | tf_op jit(solution)/shard_map/ppermute | solution.py:36
  4.8 4.3 %stage.1.weight = bf16[1,3,1792,896]{3,2,1,0:T(8,128)(2,1)S(1)} custom-call(s32[3]{0:T(128)S(1)} %pad_add_fusion.place, bf16[1,3,1792,896]{3,2,1,0:T(8,128)(2,1)} %weight), custom_call_target="tpu_custom_call" | custom-call | flops 4600000000 | bytes 1000 | tf_op jit(solution)/shard_map/stage/pallas_call | solution.py:98
  9.1 6.0 %collective-permute-done.1.ringed = bf16[144,896]{1,0:T(8,128)(2,1)S(1)} collective-permute-done((bf16[144,896]{1,0:T(8,128)(2,1)S(1)}, bf16[144,896]{1,0:T(8,128)(2,1)S(1)}, u32[]{:S(2)}, u32[]{:S(2)}) %collective-permute-start.1) | collective-permute-done | bytes 258080 | tf_op jit(solution)/shard_map/ppermute | solution.py:36
  15.6 2.5 %collective-permute-start = (bf16[112,896]{1,0:T(8,128)(2,1)S(1)}, bf16[112,896]{1,0:T(8,128)(2,1)S(1)}, u32[]{:S(2)}, u32[]{:S(2)}) collective-permute-start(bf16[112,896]{1,0:T(8,128)(2,1)S(1)} %slice_bitcast_fusion.1.block), channel_id=1, source_target_pairs={{0,2},{1,3},{2,6},{3,7},{4,0},{5,1},{6,4},{7,5},{8,10},{9,11},{10,... | collective-permute-start | bytes 602120 | tf_op jit(solution)/shard_map/ppermute | solution.py:36
  18.1 4.5 %project.4 = (bf16[448,896]{1,0:T(8,128)(2,1)S(1)}, f32[3,144,896]{2,1,0:T(8,128)S(1)}, f32[144,1]{1,0:T(8,128)S(1)}) custom-call(s32[3]{0:T(128)S(1)} %pad_add_fusion.place, bf16[144,896]{1,0:T(8,128)(2,1)S(1)} %collective-permute-done.2.crossed, bf16[144,896]{1,0:T(8,128)(2,1)S(1)} %collective-permute-done.1.ringed, ...), custom_call_target="tpu_custom_call" | custom-call | flops 3449999872 | bytes 1000 | tf_op jit(solution)/shard_map/project/pallas_call | solution.py:202
  22.6 2.3 %collective-permute-start.9 = (bf16[448,896]{1,0:T(8,128)(2,1)S(1)}, bf16[448,896]{1,0:T(8,128)(2,1)S(1)}, u32[]{:S(2)}, u32[]{:S(2)}) collective-permute-start(bf16[448,896]{1,0:T(8,128)(2,1)S(1)} %get-tuple-element.52), channel_id=1, source_target_pairs={{0,4},{1,5},{2,6},{3,7},{4,0},{5,1},{6,2},{7,3},{8,12},{9,13},{10,... | collective-permute-start | bytes 2408456 | tf_op jit(solution)/shard_map/ppermute | solution.py:36
  24.9 2.6 %collective-permute-start.5 = (bf16[112,896]{1,0:T(8,128)(2,1)S(1)}, bf16[112,896]{1,0:T(8,128)(2,1)S(1)}, u32[]{:S(2)}, u32[]{:S(2)}) collective-permute-start(bf16[112,896]{1,0:T(8,128)(2,1)S(1)} %collective-permute-done.ringed), channel_id=1, source_target_pairs={{0,2},{1,3},{6,4},{7,5},{8,10},{9,11},{14,12},{15,13},{16,18},{17,... | collective-permute-start | bytes 602120 | tf_op jit(solution)/shard_map/ppermute | solution.py:36
  27.6 3.7 %collective-permute-done.5 = bf16[112,896]{1,0:T(8,128)(2,1)S(1)} collective-permute-done((bf16[112,896]{1,0:T(8,128)(2,1)S(1)}, bf16[112,896]{1,0:T(8,128)(2,1)S(1)}, u32[]{:S(2)}, u32[]{:S(2)}) %collective-permute-start.5) | collective-permute-done | bytes 200736 | tf_op jit(solution)/shard_map/ppermute | solution.py:36
  32.9 4.3 %project.5 = (bf16[352,896]{1,0:T(8,128)(2,1)}, f32[3,112,896]{2,1,0:T(8,128)S(1)}, f32[112,1]{1,0:T(8,128)S(1)}) custom-call(s32[3]{0:T(128)S(1)} %pad_add_fusion.place, bf16[112,896]{1,0:T(8,128)(2,1)S(1)} %broadcast_select_fusion.crossed, bf16[112,896]{1,0:T(8,128)(2,1)S(1)} %collective-permute-done.ringed, ...), custom_call_target="tpu_custom_call" | custom-call | flops 1150000 | bytes 1000 | tf_op jit(solution)/shard_map/project/pallas_call | solution.py:202
  37.3 2.5 %collective-permute-start.8 = (bf16[352,896]{1,0:T(8,128)(2,1)}, bf16[352,896]{1,0:T(8,128)(2,1)}, u32[]{:S(2)}, u32[]{:S(2)}) collective-permute-start(bf16[352,896]{1,0:T(8,128)(2,1)} %get-tuple-element.49), channel_id=1, source_target_pairs={{0,4},{1,5},{2,6},{3,7},{4,0},{5,1},{6,2},{7,3},{8,12},{9,13},{10,... | collective-permute-start | bytes 1892360 | tf_op jit(solution)/shard_map/ppermute | solution.py:36
  39.8 3.8 %collective-permute-done.9.received = bf16[448,896]{1,0:T(8,128)(2,1)S(1)} collective-permute-done((bf16[448,896]{1,0:T(8,128)(2,1)S(1)}, bf16[448,896]{1,0:T(8,128)(2,1)S(1)}, u32[]{:S(2)}, u32[]{:S(2)}) %collective-permute-start.9) | collective-permute-done | bytes 802848 | tf_op jit(solution)/shard_map/ppermute | solution.py:36
  44.6 4.2 %collective-permute-start.10 = (bf16[144,896]{1,0:T(8,128)(2,1)S(1)}, bf16[144,896]{1,0:T(8,128)(2,1)}, u32[]{:S(2)}, u32[]{:S(2)}) collective-permute-start(bf16[144,896]{1,0:T(8,128)(2,1)S(1)} %get-tuple-element.53.refs_0_), channel_id=1, source_target_pairs={{0,8},{1,9},{2,12},{3,13},{4,10},{5,11},{6,14},{7,15},{8,16},{9,17... | collective-permute-start | bytes 774152 | tf_op jit(solution)/shard_map/ppermute | solution.py:36
  48.7 4.1 %collective-permute-done.10.crossed = bf16[144,896]{1,0:T(8,128)(2,1)} collective-permute-done((bf16[144,896]{1,0:T(8,128)(2,1)S(1)}, bf16[144,896]{1,0:T(8,128)(2,1)}, u32[]{:S(2)}, u32[]{:S(2)}) %collective-permute-start.10) | collective-permute-done | bytes 258080 | tf_op jit(solution)/shard_map/ppermute | solution.py:36
  52.8 2.4 %collective-permute-start.13 = (bf16[144,896]{1,0:T(8,128)(2,1)}, bf16[144,896]{1,0:T(8,128)(2,1)}, u32[]{:S(2)}, u32[]{:S(2)}) collective-permute-start(bf16[144,896]{1,0:T(8,128)(2,1)} %collective-permute-done.10.crossed), channel_id=1, source_target_pairs={{0,2},{1,3},{2,0},{3,1},{4,6},{5,7},{6,4},{7,5},{8,10},{9,11},{10,... | collective-permute-start | bytes 774152 | tf_op jit(solution)/shard_map/ppermute | solution.py:36
  56.7 2.1 %attend.3.refs_1_ = bf16[112,896]{1,0:T(8,128)(2,1)S(1)} custom-call(f32[3,112,896]{2,1,0:T(8,128)S(1)} %get-tuple-element.48.kept, bf16[352,896]{1,0:T(8,128)(2,1)} %collective-permute-done.8.received, f32[112,1]{1,0:T(8,128)S(1)} %get-tuple-element.50.kept_mean, bf16[112,896]{1,0:T(8,128)(2,1)S(1)} %copy-done.3, ...), custom_call_target="tpu_custom_call" | custom-call | flops 287500009472 | bytes 1000 | tf_op jit(solution)/shard_map/attend/pallas_call | solution.py:331
  58.8 3.5 %collective-permute-done.13.ringed = bf16[144,896]{1,0:T(8,128)(2,1)} collective-permute-done((bf16[144,896]{1,0:T(8,128)(2,1)}, bf16[144,896]{1,0:T(8,128)(2,1)}, u32[]{:S(2)}, u32[]{:S(2)}) %collective-permute-start.13) | collective-permute-done | bytes 258080 | tf_op jit(solution)/shard_map/ppermute | solution.py:36
  62.4 5.7 %collective-permute-start.12 = (bf16[112,896]{1,0:T(8,128)(2,1)S(1)}, bf16[112,896]{1,0:T(8,128)(2,1)S(1)}, u32[]{:S(2)}, u32[]{:S(2)}) collective-permute-start(bf16[112,896]{1,0:T(8,128)(2,1)S(1)} %attend.3.refs_1_), channel_id=1, source_target_pairs={{0,8},{1,9},{2,12},{3,13},{4,10},{5,11},{6,14},{7,15},{8,16},{9,17... | collective-permute-start | bytes 602120 | tf_op jit(solution)/shard_map/ppermute | solution.py:36
  68.1 5.1 %project.6 = (bf16[448,896]{1,0:T(8,128)(2,1)S(1)}, f32[3,144,896]{2,1,0:T(8,128)S(1)}, f32[144,1]{1,0:T(8,128)S(1)}, bf16[256,896]{1,0:T(8,128)(2,1)}) custom-call(s32[3]{0:T(128)S(1)} %copy-done.7, bf16[144,896]{1,0:T(8,128)(2,1)} %collective-permute-done.10.crossed, bf16[144,896]{1,0:T(8,128)(2,1)} %collective-permute-done.13.ringed, ...), custom_call_target="tpu_custom_call" | custom-call | flops 3449999872 | bytes 1000 | tf_op jit(solution)/shard_map/project/pallas_call | solution.py:202
  75.8 4.2 %collective-permute-start.19 = (bf16[256,896]{1,0:T(8,128)(2,1)}, bf16[256,896]{1,0:T(8,128)(2,1)S(1)}, u32[]{:S(2)}, u32[]{:S(2)}) collective-permute-start(bf16[256,896]{1,0:T(8,128)(2,1)} %get-tuple-element.62.own), channel_id=1, source_target_pairs={{0,8},{1,9},{2,10},{3,11},{4,12},{5,13},{6,14},{7,15},{8,16},{9,17... | collective-permute-start | bytes 1376264 | tf_op jit(solution)/shard_map/ppermute | solution.py:36
  83.0 4.3 %project.7 = (bf16[352,512]{1,0:T(8,128)(2,1)}, bf16[352,384]{1,0:T(8,128)(2,1)}, f32[3,112,896]{2,1,0:T(8,128)S(1)}, f32[112,1]{1,0:T(8,128)S(1)}) custom-call(s32[3]{0:T(128)S(1)} %copy-done.7, bf16[112,896]{1,0:T(8,128)(2,1)S(1)} %collective-permute-done.12.crossed, bf16[112,896]{1,0:T(8,128)(2,1)S(1)} %collective-permute-done.15.ringed, ...), custom_call_target="tpu_custom_call" | custom-call | flops 2300000000 | bytes 1000 | tf_op jit(solution)/shard_map/project/pallas_call | solution.py:202
  89.4 4.6 %collective-permute-done.20.received = bf16[448,896]{1,0:T(8,128)(2,1)S(1)} collective-permute-done((bf16[448,896]{1,0:T(8,128)(2,1)S(1)}, bf16[448,896]{1,0:T(8,128)(2,1)S(1)}, u32[]{:S(2)}, u32[]{:S(2)}) %collective-permute-start.20) | collective-permute-done | bytes 802848 | tf_op jit(solution)/shard_map/ppermute | solution.py:36
  95.0 6.9 %collective-permute-done.21.received = bf16[352,512]{1,0:T(8,128)(2,1)} collective-permute-done((bf16[352,512]{1,0:T(8,128)(2,1)}, bf16[352,512]{1,0:T(8,128)(2,1)}, u32[]{:S(2)}, u32[]{:S(2)}) %collective-permute-start.21) | collective-permute-done | bytes 360480 | tf_op jit(solution)/shard_map/ppermute | solution.py:36
  104.5 2.2 %collective-permute-done.18.received = bf16[352,384]{1,0:T(8,128)(2,1)} collective-permute-done((bf16[352,384]{1,0:T(8,128)(2,1)}, bf16[352,384]{1,0:T(8,128)(2,1)}, u32[]{:S(2)}, u32[]{:S(2)}) %collective-permute-start.18) | collective-permute-done | bytes 270368 | tf_op jit(solution)/shard_map/ppermute | solution.py:36
  106.7 2.3 %final.1 = bf16[256,896]{1,0:T(8,128)(2,1)} custom-call(s32[1]{0:T(128)S(6)} %copy.7.flag, f32[3,112,896]{2,1,0:T(8,128)S(1)} %get-tuple-element.59.kept, bf16[352,384]{1,0:T(8,128)(2,1)} %collective-permute-done.18.received, f32[112,1]{1,0:T(8,128)S(1)} %get-tuple-element.61.kept_mean, ...), custom_call_target="tpu_custom_call", output_to_operand_aliasing={{}: (7, {})} | custom-call | flops 287500009472 | bytes 1000 | tf_op jit(solution)/shard_map/final/pallas_call | solution.py:433
  (55 shorter events, 17.1 us)
Async XLA Ops:
  1.0 14.1 %collective-permute-start.1 = (bf16[144,896]{1,0:T(8,128)(2,1)S(1)}, bf16[144,896]{1,0:T(8,128)(2,1)S(1)}, u32[]{:S(2)}, u32[]{:S(2)}) collective-permute-start(bf16[144,896]{1,0:T(8,128)(2,1)S(1)} %slice_bitcast_fusion.block), channel_id=1, source_target_pairs={{0,2},{1,3},{2,6},{3,7},{4,0},{5,1},{6,4},{7,5},{8,10},{9,11},{10,... | collective-permute-start | bytes 774152 | tf_op jit(solution)/shard_map/ppermute | solution.py:36
  4.0 11.0 %collective-permute-start.2 = (bf16[144,896]{1,0:T(8,128)(2,1)S(1)}, bf16[144,896]{1,0:T(8,128)(2,1)S(1)}, u32[]{:S(2)}, u32[]{:S(2)}) collective-permute-start(bf16[144,896]{1,0:T(8,128)(2,1)S(1)} %slice_bitcast_fusion.block), channel_id=1, source_target_pairs={{0,0},{1,1},{2,4},{3,5},{4,2},{5,3},{6,6},{7,7},{8,8},{9,9},{10,12... | collective-permute-start | bytes 774152 | tf_op jit(solution)/shard_map/ppermute | solution.py:36
  4.8 28.2 %copy-start.6 = (s32[3]{0:T(128)}, s32[3]{0:T(128)S(1)}, u32[]{:S(2)}) copy-start(s32[3]{0:T(128)S(1)} %pad_add_fusion.place) | copy-start | bytes 40
  9.1 23.9 %copy-start = (bf16[1,3,1792,896]{3,2,1,0:T(8,128)(2,1)}, bf16[1,3,1792,896]{3,2,1,0:T(8,128)(2,1)S(1)}, u32[]{:S(2)}) copy-start(bf16[1,3,1792,896]{3,2,1,0:T(8,128)(2,1)S(1)} %stage.1.weight) | copy-start | bytes 28901380
  15.0 3.1 %collective-permute-start.3 = (bf16[144,896]{1,0:T(8,128)(2,1)S(1)}, bf16[144,896]{1,0:T(8,128)(2,1)S(1)}, u32[]{:S(2)}, u32[]{:S(2)}) collective-permute-start(bf16[144,896]{1,0:T(8,128)(2,1)S(1)} %collective-permute-done.2.crossed), channel_id=1, source_target_pairs={{0,1},{1,0},{2,3},{3,2},{4,5},{5,4},{6,7},{7,6},{8,9},{9,8},{10,11... | collective-permute-start | bytes 774152 | tf_op jit(solution)/shard_map/ppermute | solution.py:36
  15.0 3.1 %collective-permute-start.4 = (bf16[144,896]{1,0:T(8,128)(2,1)S(1)}, bf16[144,896]{1,0:T(8,128)(2,1)S(1)}, u32[]{:S(2)}, u32[]{:S(2)}) collective-permute-start(bf16[144,896]{1,0:T(8,128)(2,1)S(1)} %collective-permute-done.1.ringed), channel_id=1, source_target_pairs={{0,1},{1,0},{2,3},{3,2},{4,5},{5,4},{6,7},{7,6},{8,9},{9,8},{10,11... | collective-permute-start | bytes 774152 | tf_op jit(solution)/shard_map/ppermute | solution.py:36
  15.6 9.3 %collective-permute-start = (bf16[112,896]{1,0:T(8,128)(2,1)S(1)}, bf16[112,896]{1,0:T(8,128)(2,1)S(1)}, u32[]{:S(2)}, u32[]{:S(2)}) collective-permute-start(bf16[112,896]{1,0:T(8,128)(2,1)S(1)} %slice_bitcast_fusion.1.block), channel_id=1, source_target_pairs={{0,2},{1,3},{2,6},{3,7},{4,0},{5,1},{6,4},{7,5},{8,10},{9,11},{10,... | collective-permute-start | bytes 602120 | tf_op jit(solution)/shard_map/ppermute | solution.py:36
  22.6 21.0 %collective-permute-start.9 = (bf16[448,896]{1,0:T(8,128)(2,1)S(1)}, bf16[448,896]{1,0:T(8,128)(2,1)S(1)}, u32[]{:S(2)}, u32[]{:S(2)}) collective-permute-start(bf16[448,896]{1,0:T(8,128)(2,1)S(1)} %get-tuple-element.52), channel_id=1, source_target_pairs={{0,4},{1,5},{2,6},{3,7},{4,0},{5,1},{6,2},{7,3},{8,12},{9,13},{10,... | collective-permute-start | bytes 2408456 | tf_op jit(solution)/shard_map/ppermute | solution.py:36
  24.9 6.5 %collective-permute-start.5 = (bf16[112,896]{1,0:T(8,128)(2,1)S(1)}, bf16[112,896]{1,0:T(8,128)(2,1)S(1)}, u32[]{:S(2)}, u32[]{:S(2)}) collective-permute-start(bf16[112,896]{1,0:T(8,128)(2,1)S(1)} %collective-permute-done.ringed), channel_id=1, source_target_pairs={{0,2},{1,3},{6,4},{7,5},{8,10},{9,11},{14,12},{15,13},{16,18},{17,... | collective-permute-start | bytes 602120 | tf_op jit(solution)/shard_map/ppermute | solution.py:36
  27.5 3.9 %collective-permute-start.7 = (bf16[112,896]{1,0:T(8,128)(2,1)S(1)}, bf16[112,896]{1,0:T(8,128)(2,1)S(1)}, u32[]{:S(2)}, u32[]{:S(2)}) collective-permute-start(bf16[112,896]{1,0:T(8,128)(2,1)S(1)} %collective-permute-done.ringed), channel_id=1, source_target_pairs={{0,1},{1,0},{2,3},{3,2},{4,5},{5,4},{6,7},{7,6},{8,9},{9,8},{10,11... | collective-permute-start | bytes 602120 | tf_op jit(solution)/shard_map/ppermute | solution.py:36
  31.4 1.5 %collective-permute-start.6 = (bf16[112,896]{1,0:T(8,128)(2,1)S(1)}, bf16[112,896]{1,0:T(8,128)(2,1)S(1)}, u32[]{:S(2)}, u32[]{:S(2)}) collective-permute-start(bf16[112,896]{1,0:T(8,128)(2,1)S(1)} %broadcast_select_fusion.crossed), channel_id=1, source_target_pairs={{0,1},{1,0},{2,3},{3,2},{4,5},{5,4},{6,7},{7,6},{8,9},{9,8},{10,11... | collective-permute-start | bytes 602120 | tf_op jit(solution)/shard_map/ppermute | solution.py:36
  37.3 19.5 %collective-permute-start.8 = (bf16[352,896]{1,0:T(8,128)(2,1)}, bf16[352,896]{1,0:T(8,128)(2,1)}, u32[]{:S(2)}, u32[]{:S(2)}) collective-permute-start(bf16[352,896]{1,0:T(8,128)(2,1)} %get-tuple-element.49), channel_id=1, source_target_pairs={{0,4},{1,5},{2,6},{3,7},{4,0},{5,1},{6,2},{7,3},{8,12},{9,13},{10,... | collective-permute-start | bytes 1892360 | tf_op jit(solution)/shard_map/ppermute | solution.py:36
  44.6 8.3 %collective-permute-start.10 = (bf16[144,896]{1,0:T(8,128)(2,1)S(1)}, bf16[144,896]{1,0:T(8,128)(2,1)}, u32[]{:S(2)}, u32[]{:S(2)}) collective-permute-start(bf16[144,896]{1,0:T(8,128)(2,1)S(1)} %get-tuple-element.53.refs_0_), channel_id=1, source_target_pairs={{0,8},{1,9},{2,12},{3,13},{4,10},{5,11},{6,14},{7,15},{8,16},{9,17... | collective-permute-start | bytes 774152 | tf_op jit(solution)/shard_map/ppermute | solution.py:36
  52.8 2.4 %collective-permute-start.11 = (bf16[144,896]{1,0:T(8,128)(2,1)}, bf16[144,896]{1,0:T(8,128)(2,1)S(1)}, u32[]{:S(2)}, u32[]{:S(2)}) collective-permute-start(bf16[144,896]{1,0:T(8,128)(2,1)} %collective-permute-done.10.crossed), channel_id=1, source_target_pairs={{0,1},{1,0},{2,3},{3,2},{4,5},{5,4},{6,7},{7,6},{8,9},{9,8},{10,11... | collective-permute-start | bytes 774152 | tf_op jit(solution)/shard_map/ppermute | solution.py:36
  52.8 9.6 %collective-permute-start.13 = (bf16[144,896]{1,0:T(8,128)(2,1)}, bf16[144,896]{1,0:T(8,128)(2,1)}, u32[]{:S(2)}, u32[]{:S(2)}) collective-permute-start(bf16[144,896]{1,0:T(8,128)(2,1)} %collective-permute-done.10.crossed), channel_id=1, source_target_pairs={{0,2},{1,3},{2,0},{3,1},{4,6},{5,7},{6,4},{7,5},{8,10},{9,11},{10,... | collective-permute-start | bytes 774152 | tf_op jit(solution)/shard_map/ppermute | solution.py:36
  62.4 5.7 %collective-permute-start.14 = (bf16[144,896]{1,0:T(8,128)(2,1)}, bf16[144,896]{1,0:T(8,128)(2,1)S(1)}, u32[]{:S(2)}, u32[]{:S(2)}) collective-permute-start(bf16[144,896]{1,0:T(8,128)(2,1)} %collective-permute-done.13.ringed), channel_id=1, source_target_pairs={{0,1},{1,0},{2,3},{3,2},{4,5},{5,4},{6,7},{7,6},{8,9},{9,8},{10,11... | collective-permute-start | bytes 774152 | tf_op jit(solution)/shard_map/ppermute | solution.py:36
  62.4 12.3 %collective-permute-start.12 = (bf16[112,896]{1,0:T(8,128)(2,1)S(1)}, bf16[112,896]{1,0:T(8,128)(2,1)S(1)}, u32[]{:S(2)}, u32[]{:S(2)}) collective-permute-start(bf16[112,896]{1,0:T(8,128)(2,1)S(1)} %attend.3.refs_1_), channel_id=1, source_target_pairs={{0,8},{1,9},{2,12},{3,13},{4,10},{5,11},{6,14},{7,15},{8,16},{9,17... | collective-permute-start | bytes 602120 | tf_op jit(solution)/shard_map/ppermute | solution.py:36
  73.2 20.8 %collective-permute-start.20 = (bf16[448,896]{1,0:T(8,128)(2,1)S(1)}, bf16[448,896]{1,0:T(8,128)(2,1)S(1)}, u32[]{:S(2)}, u32[]{:S(2)}) collective-permute-start(bf16[448,896]{1,0:T(8,128)(2,1)S(1)} %get-tuple-element.64), channel_id=1, source_target_pairs={{0,4},{1,5},{2,6},{3,7},{4,0},{5,1},{6,2},{7,3},{8,12},{9,13},{10,... | collective-permute-start | bytes 2408456 | tf_op jit(solution)/shard_map/ppermute | solution.py:36
  74.7 6.8 %collective-permute-start.15 = (bf16[112,896]{1,0:T(8,128)(2,1)S(1)}, bf16[112,896]{1,0:T(8,128)(2,1)S(1)}, u32[]{:S(2)}, u32[]{:S(2)}) collective-permute-start(bf16[112,896]{1,0:T(8,128)(2,1)S(1)} %collective-permute-done.12.crossed), channel_id=1, source_target_pairs={{0,2},{1,3},{2,0},{3,1},{4,6},{5,7},{6,4},{7,5},{8,10},{9,11},{10,... | collective-permute-start | bytes 602120 | tf_op jit(solution)/shard_map/ppermute | solution.py:36
  75.8 13.7 %collective-permute-start.19 = (bf16[256,896]{1,0:T(8,128)(2,1)}, bf16[256,896]{1,0:T(8,128)(2,1)S(1)}, u32[]{:S(2)}, u32[]{:S(2)}) collective-permute-start(bf16[256,896]{1,0:T(8,128)(2,1)} %get-tuple-element.62.own), channel_id=1, source_target_pairs={{0,8},{1,9},{2,10},{3,11},{4,12},{5,13},{6,14},{7,15},{8,16},{9,17... | collective-permute-start | bytes 1376264 | tf_op jit(solution)/shard_map/ppermute | solution.py:36
  79.9 2.3 %collective-permute-start.16 = (bf16[112,896]{1,0:T(8,128)(2,1)S(1)}, bf16[112,896]{1,0:T(8,128)(2,1)S(1)}, u32[]{:S(2)}, u32[]{:S(2)}) collective-permute-start(bf16[112,896]{1,0:T(8,128)(2,1)S(1)} %collective-permute-done.12.crossed), channel_id=1, source_target_pairs={{0,1},{1,0},{2,3},{3,2},{4,5},{5,4},{6,7},{7,6},{8,9},{9,8},{10,11... | collective-permute-start | bytes 602120 | tf_op jit(solution)/shard_map/ppermute | solution.py:36
  81.6 1.4 %collective-permute-start.17 = (bf16[112,896]{1,0:T(8,128)(2,1)S(1)}, bf16[112,896]{1,0:T(8,128)(2,1)S(1)}, u32[]{:S(2)}, u32[]{:S(2)}) collective-permute-start(bf16[112,896]{1,0:T(8,128)(2,1)S(1)} %collective-permute-done.15.ringed), channel_id=1, source_target_pairs={{0,1},{1,0},{2,3},{3,2},{4,5},{5,4},{6,7},{7,6},{8,9},{9,8},{10,11... | collective-permute-start | bytes 602120 | tf_op jit(solution)/shard_map/ppermute | solution.py:36
  87.3 14.5 %collective-permute-start.21 = (bf16[352,512]{1,0:T(8,128)(2,1)}, bf16[352,512]{1,0:T(8,128)(2,1)}, u32[]{:S(2)}, u32[]{:S(2)}) collective-permute-start(bf16[352,512]{1,0:T(8,128)(2,1)} %get-tuple-element.70), channel_id=1, source_target_pairs={{0,4},{1,5},{2,6},{3,7},{4,0},{5,1},{6,2},{7,3},{8,12},{9,13},{10,... | collective-permute-start | bytes 1081352 | tf_op jit(solution)/shard_map/ppermute | solution.py:36
  88.6 18.1 %collective-permute-start.18 = (bf16[352,384]{1,0:T(8,128)(2,1)}, bf16[352,384]{1,0:T(8,128)(2,1)}, u32[]{:S(2)}, u32[]{:S(2)}) collective-permute-start(bf16[352,384]{1,0:T(8,128)(2,1)} %get-tuple-element.60), channel_id=1, source_target_pairs={{0,4},{1,5},{2,6},{3,7},{4,0},{5,1},{6,2},{7,3},{8,12},{9,13},{10,... | collective-permute-start | bytes 811016 | tf_op jit(solution)/shard_map/ppermute | solution.py:36
  (8 other events, 80.3 us)

commit v13 on v12

--- a/solution.py
+++ b/solution.py
@@ -18,7 +18,7 @@
 
 
 def chunk_rows(length):
-    first = length * 9 // 16
+    first = length // 2
     return [first, length - first]
 
 
@@ -125,94 +125,172 @@
     return column[:rows, :1]
 
 
+def normalize(mine, theirs, place, gain, normed, at):
+    width = mine.shape[1]
+    half = 2 * width
+    core, dp = place[0], place[1]
+    pieces = [ref[...].astype(F32) for ref in (mine, theirs)]
+    squares = sum(jnp.sum(piece * piece, axis=-1, keepdims=True) for piece in pieces)
+    mean = squares * (1.0 / half)
+    inverse = lax.rsqrt(mean + EPS)
+    for piece, order in zip(pieces, (core, 1 - core)):
+        gains = gain[:, pl.ds(pl.multiple_of(dp * half + order * width, HD), width)]
+        normed[at, pl.ds(pl.multiple_of(order * width, HD), width)] = (
+            piece * inverse * gains.astype(F32)
+        ).astype(BF16)
+    return mean
+
+
+def statistics(mean):
+    row = to_lanes(mean)
+    high = row.astype(BF16).astype(F32)
+    mid = (row - high).astype(BF16).astype(F32)
+    low = row - high - mid
+    which = lax.broadcasted_iota(jnp.int32, row.shape, 0)
+    return jnp.where(which == 0, high, jnp.where(which == 1, mid, low)).astype(BF16)
+
+
+def put_statistics(out, stat):
+    out[:STAT_ROWS] = jnp.zeros((STAT_ROWS, out.shape[1]), BF16)
+    out[:STAT_ROWS, : stat.shape[1]] = stat
+
+
+class Copies:
+    def __init__(self, semaphores):
+        self.semaphores, self.started = semaphores, []
+
+    def start(self, source, target):
+        copy = pltpu.make_async_copy(source, target, self.semaphores.at[len(self.started)])
+        copy.start()
+        self.started.append(copy)
+
+    def wait(self):
+        for copy in self.started:
+            copy.wait()
+
+
+def piece_of(k, rows):
+    top = STAT_ROWS + k * rows
+    return pl.ds(top, rows) if k else pl.ds(0, top + rows)
+
+
 def project_kernel(
-    cuts, apart, owned, place, crossed, ringed, sib_crossed, sib_ringed, gain, weight, *refs
+    apart, place, crossed, ringed, sib_crossed, sib_ringed, gain, weight, sent, kept, kept_mean, *refs
 ):
-    count = len(cuts)
-    semaphores = refs[-1]
-    owns, refs = refs[:owned], refs[owned:-1]
-    sents, (kept, kept_mean, *whole), (normed, *outs) = (
-        refs[:count],
-        refs[count : count + 2 + bool(owned)],
-        refs[count + 2 + bool(owned) :],
-    )
-    copies = []
-
-    def copy(source, target):
-        copies.append(pltpu.make_async_copy(source, target, semaphores.at[len(copies)]))
-        copies[-1].start()
-
-    begin = 0
-    for own in owns:
-        copy(own, whole[0].at[pl.ds(begin, own.shape[0])])
-        begin += own.shape[0]
-    outs = outs if apart else sents
+    normed, *out, semaphores = refs
     rows = normed.shape[0] // 2
-    width = crossed.shape[1]
-    half = 2 * width
-    core, dp, diagonal = place[0], place[1], place[2]
+    diagonal = place[2]
+    copies = Copies(semaphores)
+    out = out[0] if apart else sent
     means = []
     for mine, theirs, offset in (
         (crossed, sib_crossed, diagonal),
         (ringed, sib_ringed, 1 - diagonal),
     ):
         at = pl.ds(pl.multiple_of(offset * rows, rows), rows)
-        pieces = [ref[...].astype(F32) for ref in (mine, theirs)]
-        squares = sum(jnp.sum(piece * piece, axis=-1, keepdims=True) for piece in pieces)
-        mean = squares * (1.0 / half)
-        means.append(mean)
-        inverse = lax.rsqrt(mean + EPS)
-        for piece, order in zip(pieces, (core, 1 - core)):
-            gains = gain[:, pl.ds(pl.multiple_of(dp * half + order * width, HD), width)]
-            normed[at, pl.ds(pl.multiple_of(order * width, HD), width)] = (
-                piece * inverse * gains.astype(F32)
-            ).astype(BF16)
-    on_diagonal = diagonal == 1
-    sent_mean = jnp.where(on_diagonal, means[1], means[0])
-    kept_mean[...] = jnp.where(on_diagonal, means[0], means[1])
-    row = to_lanes(sent_mean)
-    high = row.astype(BF16).astype(F32)
-    mid = (row - high).astype(BF16).astype(F32)
-    low = row - high - mid
-    which = lax.broadcasted_iota(jnp.int32, row.shape, 0)
-    stat = jnp.where(which == 0, high, jnp.where(which == 1, mid, low)).astype(BF16)
-    for (begin, end), out, sent in zip(cuts, outs, sents):
-        out[:STAT_ROWS] = jnp.zeros((STAT_ROWS, end - begin), BF16)
-        out[:STAT_ROWS, : stat.shape[1]] = stat
-        for k in range(3):
-            product = jnp.dot(normed[...], weight[0, k, :, begin:end], preferred_element_type=F32)
-            top = STAT_ROWS + k * rows
-            out[top : top + rows] = product[:rows].astype(BF16)
-            kept[k, :, begin:end] = product[rows:]
-            if apart:
-                at = pl.ds(top, rows) if k else pl.ds(0, top + rows)
-                copy(out.at[at], sent.at[at])
-    for item in copies:
-        item.wait()
-
-
-def project(rows, place, four, gain, weight, cuts, apart, owns, estimate):
-    width = four[0].shape[1]
-    shapes = [(3 * rows + STAT_ROWS, end - begin) for begin, end in cuts]
-    scratch = [pltpu.VMEM((2 * rows, 2 * width), BF16)]
-    if apart:
-        scratch += [pltpu.VMEM(shape, BF16) for shape in shapes]
-    scratch.append(pltpu.SemaphoreType.DMA((3 * len(cuts) + len(owns),)))
-    whole = (sum(own.shape[0] for own in owns), width)
+        means.append(normalize(mine, theirs, place, gain, normed, at))
+    kept_mean[...] = jnp.where(diagonal == 1, means[0], means[1])
+    put_statistics(out, statistics(jnp.where(diagonal == 1, means[1], means[0])))
+    for k in range(3):
+        product = jnp.dot(normed[...], weight[0, k], preferred_element_type=F32)
+        top = STAT_ROWS + k * rows
+        out[top : top + rows] = product[:rows].astype(BF16)
+        kept[k] = product[rows:]
+        if apart:
+            copies.start(out.at[piece_of(k, rows)], sent.at[piece_of(k, rows)])
+    copies.wait()
+
+
+def project(place, four, gain, weight, apart, estimate):
+    rows, width = four[0].shape
+    shape = (3 * rows + STAT_ROWS, width)
     return pl.pallas_call(
-        functools.partial(project_kernel, cuts, apart, len(owns)),
-        in_specs=[smem_spec()] + [vmem_spec() for _ in range(6 + len(owns))],
-        out_specs=[any_spec() if apart else vmem_spec() for _ in cuts]
-        + [vmem_spec()] * 2
-        + [any_spec()] * bool(owns),
-        out_shape=[(pltpu.HBM if apart else pltpu.VMEM)(shape, BF16) for shape in shapes]
-        + [pltpu.VMEM((3, rows, width), F32), pltpu.VMEM((rows, 1), F32)]
-        + [pltpu.HBM(whole, BF16)] * bool(owns),
-        scratch_shapes=scratch,
+        functools.partial(project_kernel, apart),
+        in_specs=[smem_spec()] + [vmem_spec()] * 6,
+        out_specs=[any_spec() if apart else vmem_spec()] + [vmem_spec()] * 2,
+        out_shape=[
+            (pltpu.HBM if apart else pltpu.VMEM)(shape, BF16),
+            pltpu.VMEM((3, rows, width), F32),
+            pltpu.VMEM((rows, 1), F32),
+        ],
+        scratch_shapes=[pltpu.VMEM((2 * rows, 2 * width), BF16)]
+        + [pltpu.VMEM(shape, BF16)] * apart
+        + [pltpu.SemaphoreType.DMA((3,))],
         compiler_params=pltpu.CompilerParams(vmem_limit_bytes=VMEM_BYTES),
         cost_estimate=cost(estimate),
         name="project",
-    )(place, *four, gain, weight, *owns)
+    )(place, *four, gain, weight)
+
+
+def early_kernel(count, place, mine, theirs, gain, weight, *refs):
+    owns, (product, mean), kept = refs[:count], refs[count : count + 2], refs[count + 2 : -2]
+    normed, semaphores = refs[-2:]
+    copies = Copies(semaphores)
+    for source, target in zip(owns, kept):
+        copies.start(source, target)
+    mean[...] = normalize(mine, theirs, place, gain, normed, slice(None))
+    for k in range(3):
+        product[k] = jnp.dot(normed[...], weight[0, k], preferred_element_type=F32)
+    copies.wait()
+
+
+def early(place, mine, theirs, gain, weight, owns, estimate):
+    rows, width = mine.shape
+    return pl.pallas_call(
+        functools.partial(early_kernel, len(owns)),
+        in_specs=[smem_spec()] + [vmem_spec() for _ in range(4 + len(owns))],
+        out_specs=[vmem_spec(), vmem_spec()] + [any_spec() for _ in owns],
+        out_shape=[pltpu.VMEM((3, rows, width), F32), pltpu.VMEM((rows, 1), F32)]
+        + [pltpu.HBM(own.shape, BF16) for own in owns],
+        scratch_shapes=[
+            pltpu.VMEM((rows, 2 * width), BF16),
+            pltpu.SemaphoreType.DMA((max(len(owns), 1),)),
+        ],
+        compiler_params=pltpu.CompilerParams(vmem_limit_bytes=VMEM_BYTES),
+        cost_estimate=cost(estimate),
+        name="early",
+    )(place, mine, theirs, gain, weight, *owns)
+
+
+def late_kernel(cuts, apart, place, mine, theirs, gain, weight, product, mean, *refs):
+    count = len(cuts)
+    sents, (kept, kept_mean, normed) = refs[:count], refs[count : count + 3]
+    outs, semaphores = refs[count + 3 : -1] if apart else sents, refs[-1]
+    rows = normed.shape[0]
+    diagonal = place[2] == 1
+    copies = Copies(semaphores)
+    swapped_mean = normalize(mine, theirs, place, gain, normed, slice(None))
+    kept_mean[...] = jnp.where(diagonal, mean[...], swapped_mean)
+    stat = statistics(jnp.where(diagonal, swapped_mean, mean[...]))
+    for (begin, end), out, sent in zip(cuts, outs, sents):
+        put_statistics(out, stat)
+        for k in range(3):
+            swapped = jnp.dot(normed[...], weight[0, k, :, begin:end], preferred_element_type=F32)
+            crossed = product[k, :, begin:end]
+            top = STAT_ROWS + k * rows
+            out[top : top + rows] = jnp.where(diagonal, swapped, crossed).astype(BF16)
+            kept[k, :, begin:end] = jnp.where(diagonal, crossed, swapped)
+            if apart:
+                copies.start(out.at[piece_of(k, rows)], sent.at[piece_of(k, rows)])
+    copies.wait()
+
+
+def late(place, mine, theirs, gain, weight, product, mean, cuts, apart, estimate):
+    rows, width = mine.shape
+    shapes = [(3 * rows + STAT_ROWS, end - begin) for begin, end in cuts]
+    return pl.pallas_call(
+        functools.partial(late_kernel, cuts, apart),
+        in_specs=[smem_spec()] + [vmem_spec()] * 6,
+        out_specs=[any_spec() if apart else vmem_spec() for _ in cuts] + [vmem_spec()] * 2,
+        out_shape=[(pltpu.HBM if apart else pltpu.VMEM)(shape, BF16) for shape in shapes]
+        + [pltpu.VMEM((3, rows, width), F32), pltpu.VMEM((rows, 1), F32)],
+        scratch_shapes=[pltpu.VMEM((rows, 2 * width), BF16)]
+        + [pltpu.VMEM(shape, BF16) for shape in shapes] * apart
+        + [pltpu.SemaphoreType.DMA((3 * len(cuts),))],
+        compiler_params=pltpu.CompilerParams(vmem_limit_bytes=VMEM_BYTES),
+        cost_estimate=cost(estimate),
+        name="late",
+    )(place, mine, theirs, gain, weight, product, mean)
 
 
 def mix(kept, received, kept_mean, earlier, pairs, put, first=0):
@@ -289,22 +367,19 @@
     mix(kept, received, kept_mean, (earlier,), None, put)
 
 
-def settle_kernel(flag, held, part, before, own, out, rest, rest_own):
+def settle_kernel(flag, held, part, before, before_last, own, own_last, out, rest, rest_own):
     rows, done = held.shape[0], part.shape[1]
     shadow = flag[0] == 1
 
-    def settle(here, at, mixture):
-        result = jnp.where(
-            shadow, before[here, at].astype(F32) + mixture, own[here, at].astype(F32)
-        )
-        out[here, at] = result.astype(BF16)
-
-    upper, lower = slice(0, rows), slice(rows, rows + part.shape[0])
-    settle(upper, slice(None), held[...])
-    settle(lower, slice(0, done), part[...])
-    out[lower, done:] = own[lower, done:]
-    rest[...] = before[lower, done:]
-    rest_own[...] = own[lower, done:]
+    def settle(mixture, before, own):
+        result = jnp.where(shadow, before.astype(F32) + mixture, own.astype(F32))
+        return result.astype(BF16)
+
+    out[:rows] = settle(held[...], before[...], own[...])
+    out[rows:, :done] = settle(part[...], before_last[:, :done], own_last[:, :done])
+    out[rows:, done:] = own_last[:, done:]
+    rest[...] = before_last[:, done:]
+    rest_own[...] = own_last[:, done:]
 
 
 def final_kernel(
@@ -357,15 +432,9 @@
                 permute(ringed, sections, sibling),
             )
 
-        def partial(four, apart, estimate, cuts=None, owns=()):
-            rows, width = four[0].shape
-            cuts_in = cuts or [(0, width)]
-            results = project(
-                rows, place, four, norm_gain, weight, cuts_in, apart, owns, estimate
-            )
-            received = [permute(sent, sections, peer) for sent in results[: len(cuts_in)]]
-            kept, kept_mean, *whole = results[len(cuts_in) :]
-            return (kept, received if cuts else received[0], kept_mean, *whole)
+        def partial(four, apart, estimate):
+            sent, kept, kept_mean = project(place, four, norm_gain, weight, apart, estimate)
+            return kept, permute(sent, sections, peer), kept_mean
 
         block = inputs[0, 0]
         above, below = chunk_rows(block.shape[0])
@@ -375,10 +444,10 @@
         ringed[0], crossed, weight = lax.optimization_barrier((ringed[0], crossed, weight))
         weight = pltpu.with_memory_space_constraint(weight, pltpu.VMEM)
         sums = [partial(spread(crossed, ringed[0]), False, 3)]
-        late, _ = lax.optimization_barrier((ringed[1], sums[0][2]))
-        forwarded = permute(late, sections, forward)
+        behind, _ = lax.optimization_barrier((ringed[1], sums[0][2]))
+        forwarded = permute(behind, sections, forward)
         crossed = jnp.where(diagonal, parts[1], forwarded)
-        sums.append(partial(spread(crossed, late), True, 0.001))
+        sums.append(partial(spread(crossed, behind), True, 0.001))
         width = block.shape[1]
         pairs_of = pltpu.VMEM((2, above, width), BF16)
 
@@ -394,26 +463,61 @@
         def carry(own):
             return permute(own, sections, onward(cross))
 
-        first, pairs = attend(parts[0], sums[0], [])
-        moved = [carry(first)]
-        swapped = permute(moved[0], sections, swap)
-        beside = permute(moved[0], sections, sibling)
-        part = lax.optimization_barrier((parts[1], beside))[0]
+        part, _ = lax.optimization_barrier((parts[0], sums[1][2]))
+        first, pairs = attend(part, sums[0], [])
+        crossed = carry(first)
+        swapped = permute(crossed, sections, swap)
+        beside = permute(crossed, sections, sibling)
+        product, mean = early(place, crossed, beside, norm_gain, weight, [], 0.001)
+        part, _ = lax.optimization_barrier((parts[1], mean))
         (second,) = attend(part, sums[1], [pairs])
-        moved.append(carry(second))
+        later = carry(second)
         swapped, _ = lax.optimization_barrier((swapped, second))
-        four = moved[0], swapped, beside, permute(swapped, sections, sibling)
-        *upper, own = partial(four, False, 3, None, [first, second])
-        crossed, _ = lax.optimization_barrier((moved[1], upper[2]))
+        sent, *upper = late(
+            place,
+            swapped,
+            permute(swapped, sections, sibling),
+            norm_gain,
+            weight,
+            product,
+            mean,
+            [(0, width)],
+            False,
+            3,
+        )
+        arrived = permute(sent, sections, peer)
+        crossed, _ = lax.optimization_barrier((later, upper[1]))
         swapped = permute(crossed, sections, swap)
+        beside = permute(crossed, sections, sibling)
+        product, mean, own, own_last = early(
+            place, crossed, beside, norm_gain, weight, [first, second], 3
+        )
         cut = (width // HD + 1) // 2 * HD
         cuts = [(0, cut), (cut, width)]
-        kept, received, kept_mean = partial(spread(crossed, swapped), True, 2, cuts)
-        before = permute(own, sections, onward(direct))
-        before, *upper = lax.optimization_barrier((before, *upper))
+        *sents, kept, kept_mean = late(
+            place,
+            swapped,
+            permute(swapped, sections, sibling),
+            norm_gain,
+            weight,
+            product,
+            mean,
+            cuts,
+            True,
+            1,
+        )
+        received = [permute(sent, sections, peer) for sent in sents]
+        before = permute(first, sections, onward(direct))
+        before, arrived, _ = lax.optimization_barrier((before, arrived, kept_mean))
         mixture, pairs = call_attend(
-            hold_kernel, "hold", [], upper, [pltpu.VMEM((above, width), F32), pairs_of]
-        )
+            hold_kernel,
+            "hold",
+            [],
+            [upper[0], arrived, upper[1]],
+            [pltpu.VMEM((above, width), F32), pairs_of],
+        )
+        own_last, _ = lax.optimization_barrier((own_last, arrived))
+        before_last = permute(own_last, sections, onward(direct))
         (part,) = call_attend(
             part_kernel,
             "part",
@@ -426,7 +530,7 @@
             settle_kernel,
             "settle",
             [preempted],
-            [mixture, part, before, own],
+            [mixture, part, before, before_last, own, own_last],
             [jax.ShapeDtypeStruct(block.shape, BF16), rest_of, rest_of],
         )
         last = [kept, received[1], kept_mean, pairs, *rest]

time: 110 us -> 107 us (0.973)
  waiting for transfers between devices: 40.1 us -> 28.1 us
  starting transfers between devices: 35.4 us -> 41.6 us
  Pallas kernels: 31.5 us -> 34.2 us
    ppermute x22 -> x23, waiting for transfers between devices: 40.1 us -> 28.1 us  [permute(): return lax.ppermute(array, AXES, pairs)]
    ppermute x22 -> x23, starting transfers between devices: 35.4 us -> 41.6 us  [permute(): return lax.ppermute(array, AXES, pairs)]
    pallas_call x4 -> x6, Pallas kernels: 18.2 us -> 19.9 us  [the longest x2 8.7 us: project(): pl.pallas_call(functools.partial(project_kernel, apart), in_specs=[smem_s...]
  transfers between devices with their start and end apart: 22 -> 23, of which waited for: 12 -> 12; matrix products, arithmetic and copies ran while one was open for 0% -> 0% of each run, Pallas kernels for 27% -> 30%
where the time goes in v13:
time: 107 us
  starting transfers between devices  41.6 us (39%)
  Pallas kernels  34.2 us (32%)
  waiting for transfers between devices  28.1 us (26%)
  local copies, waits for them, and re-layouts  1.86 us (2%)
  between operations  1.15 us (1%)
    ppermute x23, starting transfers between devices, permute(): return lax.ppermute(array, AXES, pairs)  41.6 us
    ppermute x23, waiting for transfers between devices, permute(): return lax.ppermute(array, AXES, pairs)  28.1 us
    pallas_call x2, Pallas kernels, project(): pl.pallas_call(functools.partial(project_kernel, apart), in_specs=[smem_s...  8.7 us
    pallas_call x5, Pallas kernels, call_attend(): pl.pallas_call(kernel, in_specs=[smem_spec() for _ in scalars] + [vmem_sp...  7.67 us
    pallas_call x2, Pallas kernels, late(): pl.pallas_call(functools.partial(late_kernel, cuts, apart), in_specs=[sme...  6.02 us
    pallas_call x2, Pallas kernels, early(): pl.pallas_call(functools.partial(early_kernel, len(owns)), in_specs=[smem...  5.18 us
    pallas_call x1, Pallas kernels, stage(): pl.pallas_call(stage_kernel, in_specs=[smem_spec(), any_spec()], out_spec...  4.29 us
    pallas_call x1, Pallas kernels, local(): pl.pallas_call(final_kernel, in_specs=[smem_spec()] + [vmem_spec() for _...  2.36 us
  transfers between devices with their start and end apart: 23, of which 12 were waited for; matrix products, arithmetic and copies ran while one was open for 0% of the time, Pallas kernels for 30%

profile of v13, /device:TPU:0, one launch (start us, length us, event | category | flops | bytes accessed | tf_op | source)
XLA Modules:
  0.0 107.0 jit_solution(10680866499320333756)
XLA Ops:
  1.1 3.0 %collective-permute-start.1 = (bf16[128,896]{1,0:T(8,128)(2,1)S(1)}, bf16[128,896]{1,0:T(8,128)(2,1)S(1)}, u32[]{:S(2)}, u32[]{:S(2)}) collective-permute-start(bf16[128,896]{1,0:T(8,128)(2,1)S(1)} %get-tuple-element.58.block), channel_id=1, source_target_pairs={{0,2},{1,3},{2,6},{3,7},{4,0},{5,1},{6,4},{7,5},{8,10},{9,11},{10,... | collective-permute-start | bytes 688136 | tf_op jit(solution)/shard_map/ppermute | solution.py:36
  4.9 4.3 %stage.1.weight = bf16[1,3,1792,896]{3,2,1,0:T(8,128)(2,1)S(1)} custom-call(s32[3]{0:T(128)S(1)} %pad_add_fusion.place, bf16[1,3,1792,896]{3,2,1,0:T(8,128)(2,1)} %weight), custom_call_target="tpu_custom_call" | custom-call | flops 4600000000 | bytes 1000 | tf_op jit(solution)/shard_map/stage/pallas_call | solution.py:98
  9.2 4.7 %collective-permute-done.1.ringed = bf16[128,896]{1,0:T(8,128)(2,1)S(1)} collective-permute-done((bf16[128,896]{1,0:T(8,128)(2,1)S(1)}, bf16[128,896]{1,0:T(8,128)(2,1)S(1)}, u32[]{:S(2)}, u32[]{:S(2)}) %collective-permute-start.1) | collective-permute-done | bytes 229408 | tf_op jit(solution)/shard_map/ppermute | solution.py:36
  14.4 2.4 %collective-permute-start = (bf16[128,896]{1,0:T(8,128)(2,1)S(1)}, bf16[128,896]{1,0:T(8,128)(2,1)S(1)}, u32[]{:S(2)}, u32[]{:S(2)}) collective-permute-start(bf16[128,896]{1,0:T(8,128)(2,1)S(1)} %get-tuple-element.61.block), channel_id=1, source_target_pairs={{0,2},{1,3},{2,6},{3,7},{4,0},{5,1},{6,4},{7,5},{8,10},{9,11},{10,... | collective-permute-start | bytes 688136 | tf_op jit(solution)/shard_map/ppermute | solution.py:36
  16.9 4.0 %project.2 = (bf16[400,896]{1,0:T(8,128)(2,1)S(1)}, f32[3,128,896]{2,1,0:T(8,128)S(1)}, f32[128,1]{1,0:T(8,128)S(1)}) custom-call(s32[3]{0:T(128)S(1)} %pad_add_fusion.place, bf16[128,896]{1,0:T(8,128)(2,1)S(1)} %collective-permute-done.2.crossed, bf16[128,896]{1,0:T(8,128)(2,1)S(1)} %collective-permute-done.1.ringed, ...), custom_call_target="tpu_custom_call" | custom-call | flops 3449999872 | bytes 1000 | tf_op jit(solution)/shard_map/project/pallas_call | solution.py:207
  20.9 2.3 %collective-permute-start.9 = (bf16[400,896]{1,0:T(8,128)(2,1)S(1)}, bf16[400,896]{1,0:T(8,128)(2,1)S(1)}, u32[]{:S(2)}, u32[]{:S(2)}) collective-permute-start(bf16[400,896]{1,0:T(8,128)(2,1)S(1)} %get-tuple-element.57), channel_id=1, source_target_pairs={{0,4},{1,5},{2,6},{3,7},{4,0},{5,1},{6,2},{7,3},{8,12},{9,13},{10,... | collective-permute-start | bytes 2150408 | tf_op jit(solution)/shard_map/ppermute | solution.py:36
  23.6 2.7 %collective-permute-start.5 = (bf16[128,896]{1,0:T(8,128)(2,1)S(1)}, bf16[128,896]{1,0:T(8,128)(2,1)S(1)}, u32[]{:S(2)}, u32[]{:S(2)}) collective-permute-start(bf16[128,896]{1,0:T(8,128)(2,1)S(1)} %collective-permute-done.ringed), channel_id=1, source_target_pairs={{0,2},{1,3},{6,4},{7,5},{8,10},{9,11},{14,12},{15,13},{16,18},{17,... | collective-permute-start | bytes 688136 | tf_op jit(solution)/shard_map/ppermute | solution.py:36
  26.4 4.1 %collective-permute-done.5 = bf16[128,896]{1,0:T(8,128)(2,1)S(1)} collective-permute-done((bf16[128,896]{1,0:T(8,128)(2,1)S(1)}, bf16[128,896]{1,0:T(8,128)(2,1)S(1)}, u32[]{:S(2)}, u32[]{:S(2)}) %collective-permute-start.5) | collective-permute-done | bytes 229408 | tf_op jit(solution)/shard_map/ppermute | solution.py:36
  32.1 4.7 %project.3 = (bf16[400,896]{1,0:T(8,128)(2,1)}, f32[3,128,896]{2,1,0:T(8,128)S(1)}, f32[128,1]{1,0:T(8,128)S(1)}) custom-call(s32[3]{0:T(128)S(1)} %pad_add_fusion.place, bf16[128,896]{1,0:T(8,128)(2,1)S(1)} %broadcast_select_fusion.crossed, bf16[128,896]{1,0:T(8,128)(2,1)S(1)} %collective-permute-done.ringed, ...), custom_call_target="tpu_custom_call" | custom-call | flops 1150000 | bytes 1000 | tf_op jit(solution)/shard_map/project/pallas_call | solution.py:207
  36.7 3.5 %collective-permute-start.8 = (bf16[400,896]{1,0:T(8,128)(2,1)}, bf16[400,896]{1,0:T(8,128)(2,1)}, u32[]{:S(2)}, u32[]{:S(2)}) collective-permute-start(bf16[400,896]{1,0:T(8,128)(2,1)} %get-tuple-element.54), channel_id=1, source_target_pairs={{0,4},{1,5},{2,6},{3,7},{4,0},{5,1},{6,2},{7,3},{8,12},{9,13},{10,... | collective-permute-start | bytes 2150408 | tf_op jit(solution)/shard_map/ppermute | solution.py:36
  41.1 4.2 %collective-permute-start.10 = (bf16[128,896]{1,0:T(8,128)(2,1)S(1)}, bf16[128,896]{1,0:T(8,128)(2,1)}, u32[]{:S(2)}, u32[]{:S(2)}) collective-permute-start(bf16[128,896]{1,0:T(8,128)(2,1)S(1)} %get-tuple-element.59.refs_0_), channel_id=1, source_target_pairs={{0,8},{1,9},{2,12},{3,13},{4,10},{5,11},{6,14},{7,15},{8,16},{9,17... | collective-permute-start | bytes 688136 | tf_op jit(solution)/shard_map/ppermute | solution.py:36
  45.3 4.2 %collective-permute-done.10.mine = bf16[128,896]{1,0:T(8,128)(2,1)} collective-permute-done((bf16[128,896]{1,0:T(8,128)(2,1)S(1)}, bf16[128,896]{1,0:T(8,128)(2,1)}, u32[]{:S(2)}, u32[]{:S(2)}) %collective-permute-start.10) | collective-permute-done | bytes 229408 | tf_op jit(solution)/shard_map/ppermute | solution.py:36
  51.1 2.8 %early.2 = (f32[3,128,896]{2,1,0:T(8,128)S(1)}, f32[128,1]{1,0:T(8,128)S(1)}) custom-call(s32[3]{0:T(128)S(1)} %copy-done.6, bf16[128,896]{1,0:T(8,128)(2,1)} %collective-permute-done.10.mine, bf16[128,896]{1,0:T(8,128)(2,1)S(1)} %collective-permute-done.11.theirs, bf16[1,3584]{1,0:T(2,128)(2,1)S(1)} %copy-done.3, bf16[1,3,1792,896]{3,2,1,0:T(8,128)(2,1)S(1)} %stage.1.weight), custom_call_target="tpu_custom_call" | custom-call | flops 1150000 | bytes 1000 | tf_op jit(solution)/shard_map/early/pallas_call | solution.py:239
  54.0 2.9 %collective-permute-done.8.received = bf16[400,896]{1,0:T(8,128)(2,1)} collective-permute-done((bf16[400,896]{1,0:T(8,128)(2,1)}, bf16[400,896]{1,0:T(8,128)(2,1)}, u32[]{:S(2)}, u32[]{:S(2)}) %collective-permute-start.8) | collective-permute-done | bytes 716832 | tf_op jit(solution)/shard_map/ppermute | solution.py:36
  56.9 2.2 %attend.3.refs_1_ = bf16[128,896]{1,0:T(8,128)(2,1)S(1)} custom-call(f32[3,128,896]{2,1,0:T(8,128)S(1)} %get-tuple-element.53.kept, bf16[400,896]{1,0:T(8,128)(2,1)} %collective-permute-done.8.received, f32[128,1]{1,0:T(8,128)S(1)} %get-tuple-element.55.kept_mean, bf16[128,896]{1,0:T(8,128)(2,1)S(1)} %get-tuple-element.61.block, ...), custom_call_target="tpu_custom_call" | custom-call | flops 287500009472 | bytes 1000 | tf_op jit(solution)/shard_map/attend/pallas_call | solution.py:406
  59.1 8.7 %collective-permute-start.12 = (bf16[128,896]{1,0:T(8,128)(2,1)S(1)}, bf16[128,896]{1,0:T(8,128)(2,1)S(1)}, u32[]{:S(2)}, u32[]{:S(2)}) collective-permute-start(bf16[128,896]{1,0:T(8,128)(2,1)S(1)} %attend.3.refs_1_), channel_id=1, source_target_pairs={{0,8},{1,9},{2,12},{3,13},{4,10},{5,11},{6,14},{7,15},{8,16},{9,17... | collective-permute-start | bytes 688136 | tf_op jit(solution)/shard_map/ppermute | solution.py:36
  67.9 2.9 %late.2 = (bf16[400,896]{1,0:T(8,128)(2,1)S(1)}, f32[3,128,896]{2,1,0:T(8,128)S(1)}, f32[128,1]{1,0:T(8,128)S(1)}) custom-call(s32[3]{0:T(128)S(1)} %copy-done.7, bf16[128,896]{1,0:T(8,128)(2,1)} %collective-permute-done.13.mine, bf16[128,896]{1,0:T(8,128)(2,1)S(1)} %collective-permute-done.14.theirs, bf16[1,3584]{1,0:T(2,128)(2,1)S(1)} %copy-done.4, ...), custom_call_target="tpu_custom_call" | custom-call | flops 3449999872 | bytes 1000 | tf_op jit(solution)/shard_map/late/pallas_call | solution.py:281
  74.1 4.6 %collective-permute-start.19 = (bf16[128,896]{1,0:T(8,128)(2,1)S(1)}, bf16[128,896]{1,0:T(8,128)(2,1)S(1)}, u32[]{:S(2)}, u32[]{:S(2)}) collective-permute-start(bf16[128,896]{1,0:T(8,128)(2,1)S(1)} %copy-done.9), channel_id=1, source_target_pairs={{0,8},{1,9},{2,10},{3,11},{4,12},{5,13},{6,14},{7,15},{8,16},{9,17... | collective-permute-start | bytes 688136 | tf_op jit(solution)/shard_map/ppermute | solution.py:36
  80.1 2.4 %early.3 = (f32[3,128,896]{2,1,0:T(8,128)S(1)}, f32[128,1]{1,0:T(8,128)S(1)}, bf16[128,896]{1,0:T(8,128)(2,1)}, bf16[128,896]{1,0:T(8,128)(2,1)}) custom-call(s32[3]{0:T(128)S(1)} %copy-done.7, bf16[128,896]{1,0:T(8,128)(2,1)S(1)} %collective-permute-done.12.mine, bf16[128,896]{1,0:T(8,128)(2,1)S(1)} %collective-permute-done.17.theirs, ...), custom_call_target="tpu_custom_call" | custom-call | flops 3449999872 | bytes 1000 | tf_op jit(solution)/shard_map/early/pallas_call | solution.py:239
  82.5 3.1 %late.3 = (bf16[400,512]{1,0:T(8,128)(2,1)}, bf16[400,384]{1,0:T(8,128)(2,1)}, f32[3,128,896]{2,1,0:T(8,128)S(1)}, f32[128,1]{1,0:T(8,128)S(1)}) custom-call(s32[3]{0:T(128)S(1)} %copy-done.7, bf16[128,896]{1,0:T(8,128)(2,1)S(1)} %collective-permute-done.15.mine, bf16[128,896]{1,0:T(8,128)(2,1)S(1)} %collective-permute-done.16.theirs, ...), custom_call_target="tpu_custom_call" | custom-call | flops 1150000000 | bytes 1000 | tf_op jit(solution)/shard_map/late/pallas_call | solution.py:281
  88.9 4.6 %collective-permute-start.22 = (bf16[128,896]{1,0:T(8,128)(2,1)}, bf16[128,896]{1,0:T(8,128)(2,1)}, u32[]{:S(2)}, u32[]{:S(2)}) collective-permute-start(bf16[128,896]{1,0:T(8,128)(2,1)} %get-tuple-element.80.own_last), channel_id=1, source_target_pairs={{0,8},{1,9},{2,10},{3,11},{4,12},{5,13},{6,14},{7,15},{8,16},{9,17... | collective-permute-start | bytes 688136 | tf_op jit(solution)/shard_map/ppermute | solution.py:36
  94.4 3.9 %collective-permute-done.21.received = bf16[400,512]{1,0:T(8,128)(2,1)} collective-permute-done((bf16[400,512]{1,0:T(8,128)(2,1)}, bf16[400,512]{1,0:T(8,128)(2,1)}, u32[]{:S(2)}, u32[]{:S(2)}) %collective-permute-start.21) | collective-permute-done | bytes 409632 | tf_op jit(solution)/shard_map/ppermute | solution.py:36
  102.2 2.3 %collective-permute-done.18.received = bf16[400,384]{1,0:T(8,128)(2,1)} collective-permute-done((bf16[400,384]{1,0:T(8,128)(2,1)}, bf16[400,384]{1,0:T(8,128)(2,1)}, u32[]{:S(2)}, u32[]{:S(2)}) %collective-permute-start.18) | collective-permute-done | bytes 307232 | tf_op jit(solution)/shard_map/ppermute | solution.py:36
  104.5 2.4 %final.1 = bf16[256,896]{1,0:T(8,128)(2,1)} custom-call(s32[1]{0:T(128)S(6)} %copy.7.flag, f32[3,128,896]{2,1,0:T(8,128)S(1)} %get-tuple-element.69.kept, bf16[400,384]{1,0:T(8,128)(2,1)} %collective-permute-done.18.received, f32[128,1]{1,0:T(8,128)S(1)} %get-tuple-element.71.kept_mean, ...), custom_call_target="tpu_custom_call", output_to_operand_aliasing={{}: (7, {})} | custom-call | flops 287500009472 | bytes 1000 | tf_op jit(solution)/shard_map/final/pallas_call | solution.py:537
  (70 shorter events, 19.0 us)
Async XLA Ops:
  1.1 12.8 %collective-permute-start.1 = (bf16[128,896]{1,0:T(8,128)(2,1)S(1)}, bf16[128,896]{1,0:T(8,128)(2,1)S(1)}, u32[]{:S(2)}, u32[]{:S(2)}) collective-permute-start(bf16[128,896]{1,0:T(8,128)(2,1)S(1)} %get-tuple-element.58.block), channel_id=1, source_target_pairs={{0,2},{1,3},{2,6},{3,7},{4,0},{5,1},{6,4},{7,5},{8,10},{9,11},{10,... | collective-permute-start | bytes 688136 | tf_op jit(solution)/shard_map/ppermute | solution.py:36
  4.1 9.8 %collective-permute-start.2 = (bf16[128,896]{1,0:T(8,128)(2,1)S(1)}, bf16[128,896]{1,0:T(8,128)(2,1)S(1)}, u32[]{:S(2)}, u32[]{:S(2)}) collective-permute-start(bf16[128,896]{1,0:T(8,128)(2,1)S(1)} %get-tuple-element.58.block), channel_id=1, source_target_pairs={{0,0},{1,1},{2,4},{3,5},{4,2},{5,3},{6,6},{7,7},{8,8},{9,9},{10,12... | collective-permute-start | bytes 688136 | tf_op jit(solution)/shard_map/ppermute | solution.py:36
  9.2 42.0 %copy-start = (bf16[1,3,1792,896]{3,2,1,0:T(8,128)(2,1)}, bf16[1,3,1792,896]{3,2,1,0:T(8,128)(2,1)S(1)}, u32[]{:S(2)}) copy-start(bf16[1,3,1792,896]{3,2,1,0:T(8,128)(2,1)S(1)} %stage.1.weight) | copy-start | bytes 28901380
  13.9 3.0 %collective-permute-start.3 = (bf16[128,896]{1,0:T(8,128)(2,1)S(1)}, bf16[128,896]{1,0:T(8,128)(2,1)S(1)}, u32[]{:S(2)}, u32[]{:S(2)}) collective-permute-start(bf16[128,896]{1,0:T(8,128)(2,1)S(1)} %collective-permute-done.2.crossed), channel_id=1, source_target_pairs={{0,1},{1,0},{2,3},{3,2},{4,5},{5,4},{6,7},{7,6},{8,9},{9,8},{10,11... | collective-permute-start | bytes 688136 | tf_op jit(solution)/shard_map/ppermute | solution.py:36
  13.9 3.0 %collective-permute-start.4 = (bf16[128,896]{1,0:T(8,128)(2,1)S(1)}, bf16[128,896]{1,0:T(8,128)(2,1)S(1)}, u32[]{:S(2)}, u32[]{:S(2)}) collective-permute-start(bf16[128,896]{1,0:T(8,128)(2,1)S(1)} %collective-permute-done.1.ringed), channel_id=1, source_target_pairs={{0,1},{1,0},{2,3},{3,2},{4,5},{5,4},{6,7},{7,6},{8,9},{9,8},{10,11... | collective-permute-start | bytes 688136 | tf_op jit(solution)/shard_map/ppermute | solution.py:36
  14.4 9.1 %collective-permute-start = (bf16[128,896]{1,0:T(8,128)(2,1)S(1)}, bf16[128,896]{1,0:T(8,128)(2,1)S(1)}, u32[]{:S(2)}, u32[]{:S(2)}) collective-permute-start(bf16[128,896]{1,0:T(8,128)(2,1)S(1)} %get-tuple-element.61.block), channel_id=1, source_target_pairs={{0,2},{1,3},{2,6},{3,7},{4,0},{5,1},{6,4},{7,5},{8,10},{9,11},{10,... | collective-permute-start | bytes 688136 | tf_op jit(solution)/shard_map/ppermute | solution.py:36
  20.9 19.3 %collective-permute-start.9 = (bf16[400,896]{1,0:T(8,128)(2,1)S(1)}, bf16[400,896]{1,0:T(8,128)(2,1)S(1)}, u32[]{:S(2)}, u32[]{:S(2)}) collective-permute-start(bf16[400,896]{1,0:T(8,128)(2,1)S(1)} %get-tuple-element.57), channel_id=1, source_target_pairs={{0,4},{1,5},{2,6},{3,7},{4,0},{5,1},{6,2},{7,3},{8,12},{9,13},{10,... | collective-permute-start | bytes 2150408 | tf_op jit(solution)/shard_map/ppermute | solution.py:36
  23.6 6.9 %collective-permute-start.5 = (bf16[128,896]{1,0:T(8,128)(2,1)S(1)}, bf16[128,896]{1,0:T(8,128)(2,1)S(1)}, u32[]{:S(2)}, u32[]{:S(2)}) collective-permute-start(bf16[128,896]{1,0:T(8,128)(2,1)S(1)} %collective-permute-done.ringed), channel_id=1, source_target_pairs={{0,2},{1,3},{6,4},{7,5},{8,10},{9,11},{14,12},{15,13},{16,18},{17,... | collective-permute-start | bytes 688136 | tf_op jit(solution)/shard_map/ppermute | solution.py:36
  26.3 4.3 %collective-permute-start.7 = (bf16[128,896]{1,0:T(8,128)(2,1)S(1)}, bf16[128,896]{1,0:T(8,128)(2,1)S(1)}, u32[]{:S(2)}, u32[]{:S(2)}) collective-permute-start(bf16[128,896]{1,0:T(8,128)(2,1)S(1)} %collective-permute-done.ringed), channel_id=1, source_target_pairs={{0,1},{1,0},{2,3},{3,2},{4,5},{5,4},{6,7},{7,6},{8,9},{9,8},{10,11... | collective-permute-start | bytes 688136 | tf_op jit(solution)/shard_map/ppermute | solution.py:36
  30.5 1.6 %collective-permute-start.6 = (bf16[128,896]{1,0:T(8,128)(2,1)S(1)}, bf16[128,896]{1,0:T(8,128)(2,1)S(1)}, u32[]{:S(2)}, u32[]{:S(2)}) collective-permute-start(bf16[128,896]{1,0:T(8,128)(2,1)S(1)} %broadcast_select_fusion.crossed), channel_id=1, source_target_pairs={{0,1},{1,0},{2,3},{3,2},{4,5},{5,4},{6,7},{7,6},{8,9},{9,8},{10,11... | collective-permute-start | bytes 688136 | tf_op jit(solution)/shard_map/ppermute | solution.py:36
  36.7 20.1 %collective-permute-start.8 = (bf16[400,896]{1,0:T(8,128)(2,1)}, bf16[400,896]{1,0:T(8,128)(2,1)}, u32[]{:S(2)}, u32[]{:S(2)}) collective-permute-start(bf16[400,896]{1,0:T(8,128)(2,1)} %get-tuple-element.54), channel_id=1, source_target_pairs={{0,4},{1,5},{2,6},{3,7},{4,0},{5,1},{6,2},{7,3},{8,12},{9,13},{10,... | collective-permute-start | bytes 2150408 | tf_op jit(solution)/shard_map/ppermute | solution.py:36
  41.1 8.4 %collective-permute-start.10 = (bf16[128,896]{1,0:T(8,128)(2,1)S(1)}, bf16[128,896]{1,0:T(8,128)(2,1)}, u32[]{:S(2)}, u32[]{:S(2)}) collective-permute-start(bf16[128,896]{1,0:T(8,128)(2,1)S(1)} %get-tuple-element.59.refs_0_), channel_id=1, source_target_pairs={{0,8},{1,9},{2,12},{3,13},{4,10},{5,11},{6,14},{7,15},{8,16},{9,17... | collective-permute-start | bytes 688136 | tf_op jit(solution)/shard_map/ppermute | solution.py:36
  49.4 1.7 %collective-permute-start.11 = (bf16[128,896]{1,0:T(8,128)(2,1)}, bf16[128,896]{1,0:T(8,128)(2,1)S(1)}, u32[]{:S(2)}, u32[]{:S(2)}) collective-permute-start(bf16[128,896]{1,0:T(8,128)(2,1)} %collective-permute-done.10.mine), channel_id=1, source_target_pairs={{0,1},{1,0},{2,3},{3,2},{4,5},{5,4},{6,7},{7,6},{8,9},{9,8},{10,11... | collective-permute-start | bytes 688136 | tf_op jit(solution)/shard_map/ppermute | solution.py:36
  49.4 9.6 %collective-permute-start.13 = (bf16[128,896]{1,0:T(8,128)(2,1)}, bf16[128,896]{1,0:T(8,128)(2,1)}, u32[]{:S(2)}, u32[]{:S(2)}) collective-permute-start(bf16[128,896]{1,0:T(8,128)(2,1)} %collective-permute-done.10.mine), channel_id=1, source_target_pairs={{0,2},{1,3},{2,0},{3,1},{4,6},{5,7},{6,4},{7,5},{8,10},{9,11},{10,... | collective-permute-start | bytes 688136 | tf_op jit(solution)/shard_map/ppermute | solution.py:36
  59.1 8.8 %collective-permute-start.14 = (bf16[128,896]{1,0:T(8,128)(2,1)}, bf16[128,896]{1,0:T(8,128)(2,1)S(1)}, u32[]{:S(2)}, u32[]{:S(2)}) collective-permute-start(bf16[128,896]{1,0:T(8,128)(2,1)} %collective-permute-done.13.mine), channel_id=1, source_target_pairs={{0,1},{1,0},{2,3},{3,2},{4,5},{5,4},{6,7},{7,6},{8,9},{9,8},{10,11... | collective-permute-start | bytes 688136 | tf_op jit(solution)/shard_map/ppermute | solution.py:36
  59.1 13.9 %collective-permute-start.12 = (bf16[128,896]{1,0:T(8,128)(2,1)S(1)}, bf16[128,896]{1,0:T(8,128)(2,1)S(1)}, u32[]{:S(2)}, u32[]{:S(2)}) collective-permute-start(bf16[128,896]{1,0:T(8,128)(2,1)S(1)} %attend.3.refs_1_), channel_id=1, source_target_pairs={{0,8},{1,9},{2,12},{3,13},{4,10},{5,11},{6,14},{7,15},{8,16},{9,17... | collective-permute-start | bytes 688136 | tf_op jit(solution)/shard_map/ppermute | solution.py:36
  70.8 18.1 %collective-permute-start.20 = (bf16[400,896]{1,0:T(8,128)(2,1)S(1)}, bf16[400,896]{1,0:T(8,128)(2,1)S(1)}, u32[]{:S(2)}, u32[]{:S(2)}) collective-permute-start(bf16[400,896]{1,0:T(8,128)(2,1)S(1)} %get-tuple-element.73), channel_id=1, source_target_pairs={{0,4},{1,5},{2,6},{3,7},{4,0},{5,1},{6,2},{7,3},{8,12},{9,13},{10,... | collective-permute-start | bytes 2150408 | tf_op jit(solution)/shard_map/ppermute | solution.py:36
  73.0 7.1 %collective-permute-start.15 = (bf16[128,896]{1,0:T(8,128)(2,1)S(1)}, bf16[128,896]{1,0:T(8,128)(2,1)S(1)}, u32[]{:S(2)}, u32[]{:S(2)}) collective-permute-start(bf16[128,896]{1,0:T(8,128)(2,1)S(1)} %collective-permute-done.12.mine), channel_id=1, source_target_pairs={{0,2},{1,3},{2,0},{3,1},{4,6},{5,7},{6,4},{7,5},{8,10},{9,11},{10,... | collective-permute-start | bytes 688136 | tf_op jit(solution)/shard_map/ppermute | solution.py:36
  73.5 6.6 %collective-permute-start.17 = (bf16[128,896]{1,0:T(8,128)(2,1)S(1)}, bf16[128,896]{1,0:T(8,128)(2,1)S(1)}, u32[]{:S(2)}, u32[]{:S(2)}) collective-permute-start(bf16[128,896]{1,0:T(8,128)(2,1)S(1)} %collective-permute-done.12.mine), channel_id=1, source_target_pairs={{0,1},{1,0},{2,3},{3,2},{4,5},{5,4},{6,7},{7,6},{8,9},{9,8},{10,11... | collective-permute-start | bytes 688136 | tf_op jit(solution)/shard_map/ppermute | solution.py:36
  74.1 13.6 %collective-permute-start.19 = (bf16[128,896]{1,0:T(8,128)(2,1)S(1)}, bf16[128,896]{1,0:T(8,128)(2,1)S(1)}, u32[]{:S(2)}, u32[]{:S(2)}) collective-permute-start(bf16[128,896]{1,0:T(8,128)(2,1)S(1)} %copy-done.9), channel_id=1, source_target_pairs={{0,8},{1,9},{2,10},{3,11},{4,12},{5,13},{6,14},{7,15},{8,16},{9,17... | collective-permute-start | bytes 688136 | tf_op jit(solution)/shard_map/ppermute | solution.py:36
  80.1 2.4 %collective-permute-start.16 = (bf16[128,896]{1,0:T(8,128)(2,1)S(1)}, bf16[128,896]{1,0:T(8,128)(2,1)S(1)}, u32[]{:S(2)}, u32[]{:S(2)}) collective-permute-start(bf16[128,896]{1,0:T(8,128)(2,1)S(1)} %collective-permute-done.15.mine), channel_id=1, source_target_pairs={{0,1},{1,0},{2,3},{3,2},{4,5},{5,4},{6,7},{7,6},{8,9},{9,8},{10,11... | collective-permute-start | bytes 688136 | tf_op jit(solution)/shard_map/ppermute | solution.py:36
  85.7 12.6 %collective-permute-start.21 = (bf16[400,512]{1,0:T(8,128)(2,1)}, bf16[400,512]{1,0:T(8,128)(2,1)}, u32[]{:S(2)}, u32[]{:S(2)}) collective-permute-start(bf16[400,512]{1,0:T(8,128)(2,1)} %get-tuple-element.77), channel_id=1, source_target_pairs={{0,4},{1,5},{2,6},{3,7},{4,0},{5,1},{6,2},{7,3},{8,12},{9,13},{10,... | collective-permute-start | bytes 1228808 | tf_op jit(solution)/shard_map/ppermute | solution.py:36
  85.8 18.7 %collective-permute-start.18 = (bf16[400,384]{1,0:T(8,128)(2,1)}, bf16[400,384]{1,0:T(8,128)(2,1)}, u32[]{:S(2)}, u32[]{:S(2)}) collective-permute-start(bf16[400,384]{1,0:T(8,128)(2,1)} %get-tuple-element.70), channel_id=1, source_target_pairs={{0,4},{1,5},{2,6},{3,7},{4,0},{5,1},{6,2},{7,3},{8,12},{9,13},{10,... | collective-permute-start | bytes 921608 | tf_op jit(solution)/shard_map/ppermute | solution.py:36
  88.9 11.2 %collective-permute-start.22 = (bf16[128,896]{1,0:T(8,128)(2,1)}, bf16[128,896]{1,0:T(8,128)(2,1)}, u32[]{:S(2)}, u32[]{:S(2)}) collective-permute-start(bf16[128,896]{1,0:T(8,128)(2,1)} %get-tuple-element.80.own_last), channel_id=1, source_target_pairs={{0,8},{1,9},{2,10},{3,11},{4,12},{5,13},{6,14},{7,15},{8,16},{9,17... | collective-permute-start | bytes 688136 | tf_op jit(solution)/shard_map/ppermute | solution.py:36
  (15 other events, 143.7 us)

commit v14 on v13

--- a/solution.py
+++ b/solution.py
@@ -169,19 +169,23 @@
             copy.wait()
 
 
-def piece_of(k, rows):
-    top = STAT_ROWS + k * rows
-    return pl.ds(top, rows) if k else pl.ds(0, top + rows)
+def piece_of(k, rows, top):
+    return pl.ds(top + k * rows, rows) if k else pl.ds(0, top + rows)
+
+
+def tops_of(cuts):
+    return [STAT_ROWS] + [0] * (len(cuts) - 1)
 
 
 def project_kernel(
-    apart, place, crossed, ringed, sib_crossed, sib_ringed, gain, weight, sent, kept, kept_mean, *refs
+    cuts, apart, place, crossed, ringed, sib_crossed, sib_ringed, gain, weight, *refs
 ):
-    normed, *out, semaphores = refs
+    count = len(cuts)
+    sents, (kept, kept_mean, normed) = refs[:count], refs[count : count + 3]
+    outs, semaphores = refs[count + 3 : -1] if apart else sents, refs[-1]
     rows = normed.shape[0] // 2
     diagonal = place[2]
     copies = Copies(semaphores)
-    out = out[0] if apart else sent
     means = []
     for mine, theirs, offset in (
         (crossed, sib_crossed, diagonal),
@@ -190,32 +194,30 @@
         at = pl.ds(pl.multiple_of(offset * rows, rows), rows)
         means.append(normalize(mine, theirs, place, gain, normed, at))
     kept_mean[...] = jnp.where(diagonal == 1, means[0], means[1])
-    put_statistics(out, statistics(jnp.where(diagonal == 1, means[1], means[0])))
-    for k in range(3):
-        product = jnp.dot(normed[...], weight[0, k], preferred_element_type=F32)
-        top = STAT_ROWS + k * rows
-        out[top : top + rows] = product[:rows].astype(BF16)
-        kept[k] = product[rows:]
-        if apart:
-            copies.start(out.at[piece_of(k, rows)], sent.at[piece_of(k, rows)])
+    put_statistics(outs[0], statistics(jnp.where(diagonal == 1, means[1], means[0])))
+    for (begin, end), out, sent, top in zip(cuts, outs, sents, tops_of(cuts)):
+        for k in range(3):
+            product = jnp.dot(normed[...], weight[0, k, :, begin:end], preferred_element_type=F32)
+            out[top + k * rows : top + (k + 1) * rows] = product[:rows].astype(BF16)
+            kept[k, :, begin:end] = product[rows:]
+            if apart:
+                at = piece_of(k, rows, top)
+                copies.start(out.at[at], sent.at[at])
     copies.wait()
 
 
-def project(place, four, gain, weight, apart, estimate):
+def project(place, four, gain, weight, cuts, apart, estimate):
     rows, width = four[0].shape
-    shape = (3 * rows + STAT_ROWS, width)
+    shapes = [(top + 3 * rows, end - begin) for (begin, end), top in zip(cuts, tops_of(cuts))]
     return pl.pallas_call(
-        functools.partial(project_kernel, apart),
+        functools.partial(project_kernel, cuts, apart),
         in_specs=[smem_spec()] + [vmem_spec()] * 6,
-        out_specs=[any_spec() if apart else vmem_spec()] + [vmem_spec()] * 2,
-        out_shape=[
-            (pltpu.HBM if apart else pltpu.VMEM)(shape, BF16),
-            pltpu.VMEM((3, rows, width), F32),
-            pltpu.VMEM((rows, 1), F32),
-        ],
+        out_specs=[any_spec() if apart else vmem_spec() for _ in cuts] + [vmem_spec()] * 2,
+        out_shape=[(pltpu.HBM if apart else pltpu.VMEM)(shape, BF16) for shape in shapes]
+        + [pltpu.VMEM((3, rows, width), F32), pltpu.VMEM((rows, 1), F32)],
         scratch_shapes=[pltpu.VMEM((2 * rows, 2 * width), BF16)]
-        + [pltpu.VMEM(shape, BF16)] * apart
-        + [pltpu.SemaphoreType.DMA((3,))],
+        + [pltpu.VMEM(shape, BF16) for shape in shapes] * apart
+        + [pltpu.SemaphoreType.DMA((3 * len(cuts),))],
         compiler_params=pltpu.CompilerParams(vmem_limit_bytes=VMEM_BYTES),
         cost_estimate=cost(estimate),
         name="project",
@@ -262,22 +264,24 @@
     swapped_mean = normalize(mine, theirs, place, gain, normed, slice(None))
     kept_mean[...] = jnp.where(diagonal, mean[...], swapped_mean)
     stat = statistics(jnp.where(diagonal, swapped_mean, mean[...]))
-    for (begin, end), out, sent in zip(cuts, outs, sents):
-        put_statistics(out, stat)
+    put_statistics(outs[0], stat)
+    for (begin, end), out, sent, top in zip(cuts, outs, sents, tops_of(cuts)):
         for k in range(3):
             swapped = jnp.dot(normed[...], weight[0, k, :, begin:end], preferred_element_type=F32)
             crossed = product[k, :, begin:end]
-            top = STAT_ROWS + k * rows
-            out[top : top + rows] = jnp.where(diagonal, swapped, crossed).astype(BF16)
+            out[top + k * rows : top + (k + 1) * rows] = jnp.where(
+                diagonal, swapped, crossed
+            ).astype(BF16)
             kept[k, :, begin:end] = jnp.where(diagonal, crossed, swapped)
             if apart:
-                copies.start(out.at[piece_of(k, rows)], sent.at[piece_of(k, rows)])
+                at = piece_of(k, rows, top)
+                copies.start(out.at[at], sent.at[at])
     copies.wait()
 
 
 def late(place, mine, theirs, gain, weight, product, mean, cuts, apart, estimate):
     rows, width = mine.shape
-    shapes = [(3 * rows + STAT_ROWS, end - begin) for begin, end in cuts]
+    shapes = [(top + 3 * rows, end - begin) for (begin, end), top in zip(cuts, tops_of(cuts))]
     return pl.pallas_call(
         functools.partial(late_kernel, cuts, apart),
         in_specs=[smem_spec()] + [vmem_spec()] * 6,
@@ -293,15 +297,21 @@
     )(place, mine, theirs, gain, weight, product, mean)
 
 
-def mix(kept, received, kept_mean, earlier, pairs, put, first=0):
-    rows = kept.shape[1]
-    last = first + received.shape[1]
+def scales_of(received, kept_mean):
+    rows = kept_mean.shape[0]
     stat = received[:STAT_ROWS, : rows + -rows % HD].astype(F32)
     mean_peer = to_column(stat[0:1] + stat[1:2] + stat[2:3], rows)
     mean_kept = kept_mean[...]
     inverse = lax.rsqrt((mean_kept + mean_peer) * 0.5 + EPS)
     scale_kept = inverse * jnp.sqrt(mean_kept + EPS)
     scale_peer = inverse * jnp.sqrt(mean_peer + EPS)
+    return scale_kept, scale_peer
+
+
+def mix(kept, received, scales, earlier, pairs, put, first=0, top=STAT_ROWS):
+    rows = kept.shape[1]
+    last = first + received.shape[1]
+    scale_kept, scale_peer = scales
     start = sum(ref.shape[1] for ref in earlier)
     padding = -(start + rows) % HD
     shape = (rows, start + rows + padding)
@@ -322,7 +332,7 @@
             (
                 kept[k, :, at] * scale_kept
                 + received[
-                    STAT_ROWS + k * rows : STAT_ROWS + (k + 1) * rows,
+                    top + k * rows : top + (k + 1) * rows,
                     at.start - first : at.stop - first,
                 ].astype(F32)
                 * scale_peer
@@ -344,27 +354,35 @@
         put(at, jnp.dot((item * over).astype(BF16), values, preferred_element_type=F32))
 
 
-def attend_kernel(first, kept, received, kept_mean, block, *refs):
-    earlier, out, pairs = ((), *refs) if first else (refs[:1], refs[1], None)
-
+def attend_kernel(kept, received, kept_mean, block, out, pairs):
     def put(at, mixture):
         out[:, at] = (block[:, at].astype(F32) + mixture).astype(BF16)
 
-    mix(kept, received, kept_mean, earlier, pairs, put)
+    mix(kept, received, scales_of(received, kept_mean), (), pairs, put)
 
 
 def hold_kernel(kept, received, kept_mean, held, pairs):
     def put(at, mixture):
         held[:, at] = mixture
 
-    mix(kept, received, kept_mean, (), pairs, put)
-
-
-def part_kernel(kept, received, kept_mean, earlier, held):
+    mix(kept, received, scales_of(received, kept_mean), (), pairs, put)
+
+
+def part_kernel(kept, received, kept_mean, earlier, held, *scales):
     def put(at, mixture):
         held[:, at] = mixture
 
-    mix(kept, received, kept_mean, (earlier,), None, put)
+    found = scales_of(received, kept_mean)
+    for ref, scale in zip(scales, found):
+        ref[...] = scale
+    mix(kept, received, found, (earlier,), None, put)
+
+
+def next_kernel(kept, received, kept_mean, block, earlier, out):
+    def put(at, mixture):
+        out[:, at] = (block[:, at].astype(F32) + mixture).astype(BF16)
+
+    mix(kept, received, scales_of(received, kept_mean), (earlier,), None, put)
 
 
 def settle_kernel(flag, held, part, before, before_last, own, own_last, out, rest, rest_own):
@@ -383,7 +401,18 @@
 
 
 def final_kernel(
-    flag, kept, received, kept_mean, earlier, rest, rest_own, settled, out, piece, semaphore
+    flag,
+    kept,
+    received,
+    scale_kept,
+    scale_peer,
+    earlier,
+    rest,
+    rest_own,
+    settled,
+    out,
+    piece,
+    semaphore,
 ):
     rows, width = kept.shape[1:]
     done = width - rest.shape[1]
@@ -394,7 +423,7 @@
         result = rest[:, here].astype(F32) + mixture
         piece[:, here] = jnp.where(shadow, result, rest_own[:, here].astype(F32)).astype(BF16)
 
-    mix(kept, received, kept_mean, (earlier,), None, put, done)
+    mix(kept, received, (scale_kept[...], scale_peer[...]), (earlier,), None, put, done, 0)
     copy = pltpu.make_async_copy(
         piece, out.at[pl.ds(out.shape[0] - rows, rows), pl.ds(done, width - done)], semaphore
     )
@@ -432,9 +461,8 @@
                 permute(ringed, sections, sibling),
             )
 
-        def partial(four, apart, estimate):
-            sent, kept, kept_mean = project(place, four, norm_gain, weight, apart, estimate)
-            return kept, permute(sent, sections, peer), kept_mean
+        def send(sents):
+            return [permute(sent, sections, peer) for sent in sents]
 
         block = inputs[0, 0]
         above, below = chunk_rows(block.shape[0])
@@ -443,34 +471,54 @@
         crossed = permute(parts[0], sections, cross)
         ringed[0], crossed, weight = lax.optimization_barrier((ringed[0], crossed, weight))
         weight = pltpu.with_memory_space_constraint(weight, pltpu.VMEM)
-        sums = [partial(spread(crossed, ringed[0]), False, 3)]
-        behind, _ = lax.optimization_barrier((ringed[1], sums[0][2]))
+        width = block.shape[1]
+        heads = width // HD
+        sent, *sums = project(
+            place, spread(crossed, ringed[0]), norm_gain, weight, [(0, width)], False, 3
+        )
+        (received,) = send([sent])
+        behind, _ = lax.optimization_barrier((ringed[1], sums[1]))
         forwarded = permute(behind, sections, forward)
         crossed = jnp.where(diagonal, parts[1], forwarded)
-        sums.append(partial(spread(crossed, behind), True, 0.001))
-        width = block.shape[1]
-        pairs_of = pltpu.VMEM((2, above, width), BF16)
-
-        def attend(part, item, held):
-            return call_attend(
-                functools.partial(attend_kernel, not held),
-                "attend",
-                [],
-                [*item, part, *held],
-                [pltpu.VMEM(part.shape, BF16)] + [pairs_of] * (not held),
-            )
+        sent, *behind_sums = project(
+            place, spread(crossed, behind), norm_gain, weight, [(0, width)], True, 0.001
+        )
+        (received_behind,) = send([sent])
 
         def carry(own):
             return permute(own, sections, onward(cross))
 
-        part, _ = lax.optimization_barrier((parts[0], sums[1][2]))
-        first, pairs = attend(part, sums[0], [])
+        def start_part(kept, received, kept_mean, earlier, part):
+            column = pltpu.VMEM((below, 1), F32)
+            return call_attend(
+                part_kernel,
+                "part",
+                [],
+                [kept, received, kept_mean, earlier],
+                [pltpu.VMEM((below, part), F32), column, column],
+            )
+
+        pairs_of = pltpu.VMEM((2, above, width), BF16)
+        part, _ = lax.optimization_barrier((parts[0], behind_sums[1]))
+        first, pairs = call_attend(
+            attend_kernel,
+            "attend",
+            [],
+            [sums[0], received, sums[1], part],
+            [pltpu.VMEM(part.shape, BF16), pairs_of],
+        )
         crossed = carry(first)
         swapped = permute(crossed, sections, swap)
         beside = permute(crossed, sections, sibling)
         product, mean = early(place, crossed, beside, norm_gain, weight, [], 0.001)
         part, _ = lax.optimization_barrier((parts[1], mean))
-        (second,) = attend(part, sums[1], [pairs])
+        (second,) = call_attend(
+            next_kernel,
+            "attend",
+            [],
+            [behind_sums[0], received_behind, behind_sums[1], part, pairs],
+            [pltpu.VMEM(part.shape, BF16)],
+        )
         later = carry(second)
         swapped, _ = lax.optimization_barrier((swapped, second))
         sent, *upper = late(
@@ -492,7 +540,7 @@
         product, mean, own, own_last = early(
             place, crossed, beside, norm_gain, weight, [first, second], 3
         )
-        cut = (width // HD + 1) // 2 * HD
+        cut = (heads * 2 + 2) // 3 * HD
         cuts = [(0, cut), (cut, width)]
         *sents, kept, kept_mean = late(
             place,
@@ -506,7 +554,7 @@
             True,
             1,
         )
-        received = [permute(sent, sections, peer) for sent in sents]
+        received = send(sents)
         before = permute(first, sections, onward(direct))
         before, arrived, _ = lax.optimization_barrier((before, arrived, kept_mean))
         mixture, pairs = call_attend(
@@ -518,13 +566,7 @@
         )
         own_last, _ = lax.optimization_barrier((own_last, arrived))
         before_last = permute(own_last, sections, onward(direct))
-        (part,) = call_attend(
-            part_kernel,
-            "part",
-            [],
-            [kept, received[0], kept_mean, pairs],
-            [pltpu.VMEM((below, cut), F32)],
-        )
+        part, *scales = start_part(kept, received[0], kept_mean, pairs, cut)
         rest_of = pltpu.VMEM((below, width - cut), BF16)
         out, *rest = call_attend(
             settle_kernel,
@@ -533,7 +575,7 @@
             [mixture, part, before, before_last, own, own_last],
             [jax.ShapeDtypeStruct(block.shape, BF16), rest_of, rest_of],
         )
-        last = [kept, received[1], kept_mean, pairs, *rest]
+        last = [kept, received[1], *scales, pairs, *rest]
         out = pl.pallas_call(
             final_kernel,
             in_specs=[smem_spec()] + [vmem_spec() for _ in last] + [any_spec()],

time: 107 us -> 107 us (level)
  transfers between devices with their start and end apart: 23 -> 23, of which waited for: 12 -> 11; matrix products, arithmetic and copies ran while one was open for 0% -> 0% of each run, Pallas kernels for 30% -> 30%
where the time goes in v14:
time: 107 us
  starting transfers between devices  41.6 us (39%)
  Pallas kernels  34.1 us (32%)
  waiting for transfers between devices  28 us (26%)
  local copies, waits for them, and re-layouts  1.83 us (2%)
  between operations  1.15 us (1%)
    ppermute x23, starting transfers between devices, permute(): return lax.ppermute(array, AXES, pairs)  41.6 us
    ppermute x23, waiting for transfers between devices, permute(): return lax.ppermute(array, AXES, pairs)  28 us
    pallas_call x2, Pallas kernels, project(): pl.pallas_call(functools.partial(project_kernel, cuts, apart), in_specs=[...  8.71 us
    pallas_call x5, Pallas kernels, call_attend(): pl.pallas_call(kernel, in_specs=[smem_spec() for _ in scalars] + [vmem_sp...  7.77 us
    pallas_call x2, Pallas kernels, late(): pl.pallas_call(functools.partial(late_kernel, cuts, apart), in_specs=[sme...  6.04 us
    pallas_call x2, Pallas kernels, early(): pl.pallas_call(functools.partial(early_kernel, len(owns)), in_specs=[smem...  5.18 us
    pallas_call x1, Pallas kernels, stage(): pl.pallas_call(stage_kernel, in_specs=[smem_spec(), any_spec()], out_spec...  4.29 us
  transfers between devices with their start and end apart: 23, of which 11 were waited for; matrix products, arithmetic and copies ran while one was open for 0% of the time, Pallas kernels for 30%

profile of v14, /device:TPU:0, one launch (start us, length us, event | category | flops | bytes accessed | tf_op | source)
XLA Modules:
  0.0 106.8 jit_solution(4403578951496691386)
XLA Ops:
  1.1 3.0 %collective-permute-start.1 = (bf16[128,896]{1,0:T(8,128)(2,1)S(1)}, bf16[128,896]{1,0:T(8,128)(2,1)S(1)}, u32[]{:S(2)}, u32[]{:S(2)}) collective-permute-start(bf16[128,896]{1,0:T(8,128)(2,1)S(1)} %get-tuple-element.61.block), channel_id=1, source_target_pairs={{0,2},{1,3},{2,6},{3,7},{4,0},{5,1},{6,4},{7,5},{8,10},{9,11},{10,... | collective-permute-start | bytes 688136 | tf_op jit(solution)/shard_map/ppermute | solution.py:36
  4.9 4.3 %stage.1.weight = bf16[1,3,1792,896]{3,2,1,0:T(8,128)(2,1)S(1)} custom-call(s32[3]{0:T(128)S(1)} %pad_add_fusion.place, bf16[1,3,1792,896]{3,2,1,0:T(8,128)(2,1)} %weight), custom_call_target="tpu_custom_call" | custom-call | flops 4600000000 | bytes 1000 | tf_op jit(solution)/shard_map/stage/pallas_call | solution.py:98
  9.2 4.7 %collective-permute-done.1.ringed = bf16[128,896]{1,0:T(8,128)(2,1)S(1)} collective-permute-done((bf16[128,896]{1,0:T(8,128)(2,1)S(1)}, bf16[128,896]{1,0:T(8,128)(2,1)S(1)}, u32[]{:S(2)}, u32[]{:S(2)}) %collective-permute-start.1) | collective-permute-done | bytes 229408 | tf_op jit(solution)/shard_map/ppermute | solution.py:36
  14.4 2.4 %collective-permute-start = (bf16[128,896]{1,0:T(8,128)(2,1)S(1)}, bf16[128,896]{1,0:T(8,128)(2,1)S(1)}, u32[]{:S(2)}, u32[]{:S(2)}) collective-permute-start(bf16[128,896]{1,0:T(8,128)(2,1)S(1)} %get-tuple-element.64.block), channel_id=1, source_target_pairs={{0,2},{1,3},{2,6},{3,7},{4,0},{5,1},{6,4},{7,5},{8,10},{9,11},{10,... | collective-permute-start | bytes 688136 | tf_op jit(solution)/shard_map/ppermute | solution.py:36
  16.9 4.0 %project.2 = (bf16[400,896]{1,0:T(8,128)(2,1)S(1)}, f32[3,128,896]{2,1,0:T(8,128)S(1)}, f32[128,1]{1,0:T(8,128)S(1)}) custom-call(s32[3]{0:T(128)S(1)} %pad_add_fusion.place, bf16[128,896]{1,0:T(8,128)(2,1)S(1)} %collective-permute-done.2.crossed, bf16[128,896]{1,0:T(8,128)(2,1)S(1)} %collective-permute-done.1.ringed, ...), custom_call_target="tpu_custom_call" | custom-call | flops 3449999872 | bytes 1000 | tf_op jit(solution)/shard_map/project/pallas_call | solution.py:212
  20.9 2.3 %collective-permute-start.9 = (bf16[400,896]{1,0:T(8,128)(2,1)S(1)}, bf16[400,896]{1,0:T(8,128)(2,1)S(1)}, u32[]{:S(2)}, u32[]{:S(2)}) collective-permute-start(bf16[400,896]{1,0:T(8,128)(2,1)S(1)} %get-tuple-element.60), channel_id=1, source_target_pairs={{0,4},{1,5},{2,6},{3,7},{4,0},{5,1},{6,2},{7,3},{8,12},{9,13},{10,... | collective-permute-start | bytes 2150408 | tf_op jit(solution)/shard_map/ppermute | solution.py:36
  23.6 2.7 %collective-permute-start.5 = (bf16[128,896]{1,0:T(8,128)(2,1)S(1)}, bf16[128,896]{1,0:T(8,128)(2,1)S(1)}, u32[]{:S(2)}, u32[]{:S(2)}) collective-permute-start(bf16[128,896]{1,0:T(8,128)(2,1)S(1)} %collective-permute-done.ringed), channel_id=1, source_target_pairs={{0,2},{1,3},{6,4},{7,5},{8,10},{9,11},{14,12},{15,13},{16,18},{17,... | collective-permute-start | bytes 688136 | tf_op jit(solution)/shard_map/ppermute | solution.py:36
  26.4 4.1 %collective-permute-done.5 = bf16[128,896]{1,0:T(8,128)(2,1)S(1)} collective-permute-done((bf16[128,896]{1,0:T(8,128)(2,1)S(1)}, bf16[128,896]{1,0:T(8,128)(2,1)S(1)}, u32[]{:S(2)}, u32[]{:S(2)}) %collective-permute-start.5) | collective-permute-done | bytes 229408 | tf_op jit(solution)/shard_map/ppermute | solution.py:36
  32.1 4.7 %project.3 = (bf16[400,896]{1,0:T(8,128)(2,1)}, f32[3,128,896]{2,1,0:T(8,128)S(1)}, f32[128,1]{1,0:T(8,128)S(1)}) custom-call(s32[3]{0:T(128)S(1)} %pad_add_fusion.place, bf16[128,896]{1,0:T(8,128)(2,1)S(1)} %broadcast_select_fusion.crossed, bf16[128,896]{1,0:T(8,128)(2,1)S(1)} %collective-permute-done.ringed, ...), custom_call_target="tpu_custom_call" | custom-call | flops 1150000 | bytes 1000 | tf_op jit(solution)/shard_map/project/pallas_call | solution.py:212
  36.7 3.5 %collective-permute-start.8 = (bf16[400,896]{1,0:T(8,128)(2,1)}, bf16[400,896]{1,0:T(8,128)(2,1)}, u32[]{:S(2)}, u32[]{:S(2)}) collective-permute-start(bf16[400,896]{1,0:T(8,128)(2,1)} %get-tuple-element.57), channel_id=1, source_target_pairs={{0,4},{1,5},{2,6},{3,7},{4,0},{5,1},{6,2},{7,3},{8,12},{9,13},{10,... | collective-permute-start | bytes 2150408 | tf_op jit(solution)/shard_map/ppermute | solution.py:36
  41.1 4.2 %collective-permute-start.10 = (bf16[128,896]{1,0:T(8,128)(2,1)S(1)}, bf16[128,896]{1,0:T(8,128)(2,1)}, u32[]{:S(2)}, u32[]{:S(2)}) collective-permute-start(bf16[128,896]{1,0:T(8,128)(2,1)S(1)} %get-tuple-element.62.refs_0_), channel_id=1, source_target_pairs={{0,8},{1,9},{2,12},{3,13},{4,10},{5,11},{6,14},{7,15},{8,16},{9,17... | collective-permute-start | bytes 688136 | tf_op jit(solution)/shard_map/ppermute | solution.py:36
  45.3 4.2 %collective-permute-done.10.mine = bf16[128,896]{1,0:T(8,128)(2,1)} collective-permute-done((bf16[128,896]{1,0:T(8,128)(2,1)S(1)}, bf16[128,896]{1,0:T(8,128)(2,1)}, u32[]{:S(2)}, u32[]{:S(2)}) %collective-permute-start.10) | collective-permute-done | bytes 229408 | tf_op jit(solution)/shard_map/ppermute | solution.py:36
  51.2 2.8 %early.2 = (f32[3,128,896]{2,1,0:T(8,128)S(1)}, f32[128,1]{1,0:T(8,128)S(1)}) custom-call(s32[3]{0:T(128)S(1)} %copy-done.6, bf16[128,896]{1,0:T(8,128)(2,1)} %collective-permute-done.10.mine, bf16[128,896]{1,0:T(8,128)(2,1)S(1)} %collective-permute-done.11.theirs, bf16[1,3584]{1,0:T(2,128)(2,1)S(1)} %copy-done.3, bf16[1,3,1792,896]{3,2,1,0:T(8,128)(2,1)S(1)} %stage.1.weight), custom_call_target="tpu_custom_call" | custom-call | flops 1150000 | bytes 1000 | tf_op jit(solution)/shard_map/early/pallas_call | solution.py:241
  54.0 2.9 %collective-permute-done.8.received = bf16[400,896]{1,0:T(8,128)(2,1)} collective-permute-done((bf16[400,896]{1,0:T(8,128)(2,1)}, bf16[400,896]{1,0:T(8,128)(2,1)}, u32[]{:S(2)}, u32[]{:S(2)}) %collective-permute-start.8) | collective-permute-done | bytes 716832 | tf_op jit(solution)/shard_map/ppermute | solution.py:36
  56.9 2.2 %attend.3.refs_1_ = bf16[128,896]{1,0:T(8,128)(2,1)S(1)} custom-call(f32[3,128,896]{2,1,0:T(8,128)S(1)} %get-tuple-element.56.kept, bf16[400,896]{1,0:T(8,128)(2,1)} %collective-permute-done.8.received, f32[128,1]{1,0:T(8,128)S(1)} %get-tuple-element.58.kept_mean, bf16[128,896]{1,0:T(8,128)(2,1)S(1)} %get-tuple-element.64.block, ...), custom_call_target="tpu_custom_call" | custom-call | flops 287500009472 | bytes 1000 | tf_op jit(solution)/shard_map/attend/pallas_call | solution.py:435
  59.2 8.7 %collective-permute-start.12 = (bf16[128,896]{1,0:T(8,128)(2,1)S(1)}, bf16[128,896]{1,0:T(8,128)(2,1)S(1)}, u32[]{:S(2)}, u32[]{:S(2)}) collective-permute-start(bf16[128,896]{1,0:T(8,128)(2,1)S(1)} %attend.3.refs_1_), channel_id=1, source_target_pairs={{0,8},{1,9},{2,12},{3,13},{4,10},{5,11},{6,14},{7,15},{8,16},{9,17... | collective-permute-start | bytes 688136 | tf_op jit(solution)/shard_map/ppermute | solution.py:36
  67.9 2.9 %late.2 = (bf16[400,896]{1,0:T(8,128)(2,1)S(1)}, f32[3,128,896]{2,1,0:T(8,128)S(1)}, f32[128,1]{1,0:T(8,128)S(1)}) custom-call(s32[3]{0:T(128)S(1)} %copy-done.7, bf16[128,896]{1,0:T(8,128)(2,1)} %collective-permute-done.13.mine, bf16[128,896]{1,0:T(8,128)(2,1)S(1)} %collective-permute-done.14.theirs, bf16[1,3584]{1,0:T(2,128)(2,1)S(1)} %copy-done.4, ...), custom_call_target="tpu_custom_call" | custom-call | flops 3449999872 | bytes 1000 | tf_op jit(solution)/shard_map/late/pallas_call | solution.py:285
  70.9 2.1 %collective-permute-done.12.mine = bf16[128,896]{1,0:T(8,128)(2,1)S(1)} collective-permute-done((bf16[128,896]{1,0:T(8,128)(2,1)S(1)}, bf16[128,896]{1,0:T(8,128)(2,1)S(1)}, u32[]{:S(2)}, u32[]{:S(2)}) %collective-permute-start.12) | collective-permute-done | bytes 229408 | tf_op jit(solution)/shard_map/ppermute | solution.py:36
  74.2 4.6 %collective-permute-start.20 = (bf16[128,896]{1,0:T(8,128)(2,1)S(1)}, bf16[128,896]{1,0:T(8,128)(2,1)S(1)}, u32[]{:S(2)}, u32[]{:S(2)}) collective-permute-start(bf16[128,896]{1,0:T(8,128)(2,1)S(1)} %copy-done.9), channel_id=1, source_target_pairs={{0,8},{1,9},{2,10},{3,11},{4,12},{5,13},{6,14},{7,15},{8,16},{9,17... | collective-permute-start | bytes 688136 | tf_op jit(solution)/shard_map/ppermute | solution.py:36
  80.1 2.4 %early.3 = (f32[3,128,896]{2,1,0:T(8,128)S(1)}, f32[128,1]{1,0:T(8,128)S(1)}, bf16[128,896]{1,0:T(8,128)(2,1)}, bf16[128,896]{1,0:T(8,128)(2,1)}) custom-call(s32[3]{0:T(128)S(1)} %copy-done.7, bf16[128,896]{1,0:T(8,128)(2,1)S(1)} %collective-permute-done.12.mine, bf16[128,896]{1,0:T(8,128)(2,1)S(1)} %collective-permute-done.17.theirs, ...), custom_call_target="tpu_custom_call" | custom-call | flops 3449999872 | bytes 1000 | tf_op jit(solution)/shard_map/early/pallas_call | solution.py:241
  82.5 3.2 %late.3 = (bf16[400,640]{1,0:T(8,128)(2,1)}, bf16[384,256]{1,0:T(8,128)(2,1)}, f32[3,128,896]{2,1,0:T(8,128)S(1)}, f32[128,1]{1,0:T(8,128)S(1)}) custom-call(s32[3]{0:T(128)S(1)} %copy-done.7, bf16[128,896]{1,0:T(8,128)(2,1)S(1)} %collective-permute-done.15.mine, bf16[128,896]{1,0:T(8,128)(2,1)S(1)} %collective-permute-done.16.theirs, ...), custom_call_target="tpu_custom_call" | custom-call | flops 1150000000 | bytes 1000 | tf_op jit(solution)/shard_map/late/pallas_call | solution.py:285
  88.9 4.6 %collective-permute-start.22 = (bf16[128,896]{1,0:T(8,128)(2,1)}, bf16[128,896]{1,0:T(8,128)(2,1)}, u32[]{:S(2)}, u32[]{:S(2)}) collective-permute-start(bf16[128,896]{1,0:T(8,128)(2,1)} %get-tuple-element.86.own_last), channel_id=1, source_target_pairs={{0,8},{1,9},{2,10},{3,11},{4,12},{5,13},{6,14},{7,15},{8,16},{9,17... | collective-permute-start | bytes 688136 | tf_op jit(solution)/shard_map/ppermute | solution.py:36
  94.4 6.1 %collective-permute-done.19.received = bf16[400,640]{1,0:T(8,128)(2,1)} collective-permute-done((bf16[400,640]{1,0:T(8,128)(2,1)}, bf16[400,640]{1,0:T(8,128)(2,1)}, u32[]{:S(2)}, u32[]{:S(2)}) %collective-permute-start.19) | collective-permute-done | bytes 512032 | tf_op jit(solution)/shard_map/ppermute | solution.py:36
  104.5 2.1 %final.1 = bf16[256,896]{1,0:T(8,128)(2,1)} custom-call(s32[1]{0:T(128)S(6)} %copy.7.flag, f32[3,128,896]{2,1,0:T(8,128)S(1)} %get-tuple-element.72.kept, bf16[384,256]{1,0:T(8,128)(2,1)} %collective-permute-done.18.received, f32[128,1]{1,0:T(8,128)S(1)} %get-tuple-element.80.scale_kept, ...), custom_call_target="tpu_custom_call", output_to_operand_aliasing={{}: (8, {})} | custom-call | flops 287500009472 | bytes 1000 | tf_op jit(solution)/shard_map/final/pallas_call | solution.py:579
  (70 shorter events, 16.9 us)
Async XLA Ops:
  1.1 12.8 %collective-permute-start.1 = (bf16[128,896]{1,0:T(8,128)(2,1)S(1)}, bf16[128,896]{1,0:T(8,128)(2,1)S(1)}, u32[]{:S(2)}, u32[]{:S(2)}) collective-permute-start(bf16[128,896]{1,0:T(8,128)(2,1)S(1)} %get-tuple-element.61.block), channel_id=1, source_target_pairs={{0,2},{1,3},{2,6},{3,7},{4,0},{5,1},{6,4},{7,5},{8,10},{9,11},{10,... | collective-permute-start | bytes 688136 | tf_op jit(solution)/shard_map/ppermute | solution.py:36
  4.1 9.8 %collective-permute-start.2 = (bf16[128,896]{1,0:T(8,128)(2,1)S(1)}, bf16[128,896]{1,0:T(8,128)(2,1)S(1)}, u32[]{:S(2)}, u32[]{:S(2)}) collective-permute-start(bf16[128,896]{1,0:T(8,128)(2,1)S(1)} %get-tuple-element.61.block), channel_id=1, source_target_pairs={{0,0},{1,1},{2,4},{3,5},{4,2},{5,3},{6,6},{7,7},{8,8},{9,9},{10,12... | collective-permute-start | bytes 688136 | tf_op jit(solution)/shard_map/ppermute | solution.py:36
  9.2 42.0 %copy-start = (bf16[1,3,1792,896]{3,2,1,0:T(8,128)(2,1)}, bf16[1,3,1792,896]{3,2,1,0:T(8,128)(2,1)S(1)}, u32[]{:S(2)}) copy-start(bf16[1,3,1792,896]{3,2,1,0:T(8,128)(2,1)S(1)} %stage.1.weight) | copy-start | bytes 28901380
  13.9 3.0 %collective-permute-start.3 = (bf16[128,896]{1,0:T(8,128)(2,1)S(1)}, bf16[128,896]{1,0:T(8,128)(2,1)S(1)}, u32[]{:S(2)}, u32[]{:S(2)}) collective-permute-start(bf16[128,896]{1,0:T(8,128)(2,1)S(1)} %collective-permute-done.2.crossed), channel_id=1, source_target_pairs={{0,1},{1,0},{2,3},{3,2},{4,5},{5,4},{6,7},{7,6},{8,9},{9,8},{10,11... | collective-permute-start | bytes 688136 | tf_op jit(solution)/shard_map/ppermute | solution.py:36
  13.9 3.0 %collective-permute-start.4 = (bf16[128,896]{1,0:T(8,128)(2,1)S(1)}, bf16[128,896]{1,0:T(8,128)(2,1)S(1)}, u32[]{:S(2)}, u32[]{:S(2)}) collective-permute-start(bf16[128,896]{1,0:T(8,128)(2,1)S(1)} %collective-permute-done.1.ringed), channel_id=1, source_target_pairs={{0,1},{1,0},{2,3},{3,2},{4,5},{5,4},{6,7},{7,6},{8,9},{9,8},{10,11... | collective-permute-start | bytes 688136 | tf_op jit(solution)/shard_map/ppermute | solution.py:36
  14.4 9.1 %collective-permute-start = (bf16[128,896]{1,0:T(8,128)(2,1)S(1)}, bf16[128,896]{1,0:T(8,128)(2,1)S(1)}, u32[]{:S(2)}, u32[]{:S(2)}) collective-permute-start(bf16[128,896]{1,0:T(8,128)(2,1)S(1)} %get-tuple-element.64.block), channel_id=1, source_target_pairs={{0,2},{1,3},{2,6},{3,7},{4,0},{5,1},{6,4},{7,5},{8,10},{9,11},{10,... | collective-permute-start | bytes 688136 | tf_op jit(solution)/shard_map/ppermute | solution.py:36
  20.9 19.3 %collective-permute-start.9 = (bf16[400,896]{1,0:T(8,128)(2,1)S(1)}, bf16[400,896]{1,0:T(8,128)(2,1)S(1)}, u32[]{:S(2)}, u32[]{:S(2)}) collective-permute-start(bf16[400,896]{1,0:T(8,128)(2,1)S(1)} %get-tuple-element.60), channel_id=1, source_target_pairs={{0,4},{1,5},{2,6},{3,7},{4,0},{5,1},{6,2},{7,3},{8,12},{9,13},{10,... | collective-permute-start | bytes 2150408 | tf_op jit(solution)/shard_map/ppermute | solution.py:36
  23.6 6.9 %collective-permute-start.5 = (bf16[128,896]{1,0:T(8,128)(2,1)S(1)}, bf16[128,896]{1,0:T(8,128)(2,1)S(1)}, u32[]{:S(2)}, u32[]{:S(2)}) collective-permute-start(bf16[128,896]{1,0:T(8,128)(2,1)S(1)} %collective-permute-done.ringed), channel_id=1, source_target_pairs={{0,2},{1,3},{6,4},{7,5},{8,10},{9,11},{14,12},{15,13},{16,18},{17,... | collective-permute-start | bytes 688136 | tf_op jit(solution)/shard_map/ppermute | solution.py:36
  26.3 4.3 %collective-permute-start.7 = (bf16[128,896]{1,0:T(8,128)(2,1)S(1)}, bf16[128,896]{1,0:T(8,128)(2,1)S(1)}, u32[]{:S(2)}, u32[]{:S(2)}) collective-permute-start(bf16[128,896]{1,0:T(8,128)(2,1)S(1)} %collective-permute-done.ringed), channel_id=1, source_target_pairs={{0,1},{1,0},{2,3},{3,2},{4,5},{5,4},{6,7},{7,6},{8,9},{9,8},{10,11... | collective-permute-start | bytes 688136 | tf_op jit(solution)/shard_map/ppermute | solution.py:36
  30.5 1.6 %collective-permute-start.6 = (bf16[128,896]{1,0:T(8,128)(2,1)S(1)}, bf16[128,896]{1,0:T(8,128)(2,1)S(1)}, u32[]{:S(2)}, u32[]{:S(2)}) collective-permute-start(bf16[128,896]{1,0:T(8,128)(2,1)S(1)} %broadcast_select_fusion.crossed), channel_id=1, source_target_pairs={{0,1},{1,0},{2,3},{3,2},{4,5},{5,4},{6,7},{7,6},{8,9},{9,8},{10,11... | collective-permute-start | bytes 688136 | tf_op jit(solution)/shard_map/ppermute | solution.py:36
  36.7 20.1 %collective-permute-start.8 = (bf16[400,896]{1,0:T(8,128)(2,1)}, bf16[400,896]{1,0:T(8,128)(2,1)}, u32[]{:S(2)}, u32[]{:S(2)}) collective-permute-start(bf16[400,896]{1,0:T(8,128)(2,1)} %get-tuple-element.57), channel_id=1, source_target_pairs={{0,4},{1,5},{2,6},{3,7},{4,0},{5,1},{6,2},{7,3},{8,12},{9,13},{10,... | collective-permute-start | bytes 2150408 | tf_op jit(solution)/shard_map/ppermute | solution.py:36
  41.1 8.4 %collective-permute-start.10 = (bf16[128,896]{1,0:T(8,128)(2,1)S(1)}, bf16[128,896]{1,0:T(8,128)(2,1)}, u32[]{:S(2)}, u32[]{:S(2)}) collective-permute-start(bf16[128,896]{1,0:T(8,128)(2,1)S(1)} %get-tuple-element.62.refs_0_), channel_id=1, source_target_pairs={{0,8},{1,9},{2,12},{3,13},{4,10},{5,11},{6,14},{7,15},{8,16},{9,17... | collective-permute-start | bytes 688136 | tf_op jit(solution)/shard_map/ppermute | solution.py:36
  49.5 1.7 %collective-permute-start.11 = (bf16[128,896]{1,0:T(8,128)(2,1)}, bf16[128,896]{1,0:T(8,128)(2,1)S(1)}, u32[]{:S(2)}, u32[]{:S(2)}) collective-permute-start(bf16[128,896]{1,0:T(8,128)(2,1)} %collective-permute-done.10.mine), channel_id=1, source_target_pairs={{0,1},{1,0},{2,3},{3,2},{4,5},{5,4},{6,7},{7,6},{8,9},{9,8},{10,11... | collective-permute-start | bytes 688136 | tf_op jit(solution)/shard_map/ppermute | solution.py:36
  49.5 9.6 %collective-permute-start.13 = (bf16[128,896]{1,0:T(8,128)(2,1)}, bf16[128,896]{1,0:T(8,128)(2,1)}, u32[]{:S(2)}, u32[]{:S(2)}) collective-permute-start(bf16[128,896]{1,0:T(8,128)(2,1)} %collective-permute-done.10.mine), channel_id=1, source_target_pairs={{0,2},{1,3},{2,0},{3,1},{4,6},{5,7},{6,4},{7,5},{8,10},{9,11},{10,... | collective-permute-start | bytes 688136 | tf_op jit(solution)/shard_map/ppermute | solution.py:36
  59.1 8.8 %collective-permute-start.14 = (bf16[128,896]{1,0:T(8,128)(2,1)}, bf16[128,896]{1,0:T(8,128)(2,1)S(1)}, u32[]{:S(2)}, u32[]{:S(2)}) collective-permute-start(bf16[128,896]{1,0:T(8,128)(2,1)} %collective-permute-done.13.mine), channel_id=1, source_target_pairs={{0,1},{1,0},{2,3},{3,2},{4,5},{5,4},{6,7},{7,6},{8,9},{9,8},{10,11... | collective-permute-start | bytes 688136 | tf_op jit(solution)/shard_map/ppermute | solution.py:36
  59.2 13.9 %collective-permute-start.12 = (bf16[128,896]{1,0:T(8,128)(2,1)S(1)}, bf16[128,896]{1,0:T(8,128)(2,1)S(1)}, u32[]{:S(2)}, u32[]{:S(2)}) collective-permute-start(bf16[128,896]{1,0:T(8,128)(2,1)S(1)} %attend.3.refs_1_), channel_id=1, source_target_pairs={{0,8},{1,9},{2,12},{3,13},{4,10},{5,11},{6,14},{7,15},{8,16},{9,17... | collective-permute-start | bytes 688136 | tf_op jit(solution)/shard_map/ppermute | solution.py:36
  70.8 18.1 %collective-permute-start.21 = (bf16[400,896]{1,0:T(8,128)(2,1)S(1)}, bf16[400,896]{1,0:T(8,128)(2,1)S(1)}, u32[]{:S(2)}, u32[]{:S(2)}) collective-permute-start(bf16[400,896]{1,0:T(8,128)(2,1)S(1)} %get-tuple-element.77), channel_id=1, source_target_pairs={{0,4},{1,5},{2,6},{3,7},{4,0},{5,1},{6,2},{7,3},{8,12},{9,13},{10,... | collective-permute-start | bytes 2150408 | tf_op jit(solution)/shard_map/ppermute | solution.py:36
  73.0 7.1 %collective-permute-start.15 = (bf16[128,896]{1,0:T(8,128)(2,1)S(1)}, bf16[128,896]{1,0:T(8,128)(2,1)S(1)}, u32[]{:S(2)}, u32[]{:S(2)}) collective-permute-start(bf16[128,896]{1,0:T(8,128)(2,1)S(1)} %collective-permute-done.12.mine), channel_id=1, source_target_pairs={{0,2},{1,3},{2,0},{3,1},{4,6},{5,7},{6,4},{7,5},{8,10},{9,11},{10,... | collective-permute-start | bytes 688136 | tf_op jit(solution)/shard_map/ppermute | solution.py:36
  73.5 6.6 %collective-permute-start.17 = (bf16[128,896]{1,0:T(8,128)(2,1)S(1)}, bf16[128,896]{1,0:T(8,128)(2,1)S(1)}, u32[]{:S(2)}, u32[]{:S(2)}) collective-permute-start(bf16[128,896]{1,0:T(8,128)(2,1)S(1)} %collective-permute-done.12.mine), channel_id=1, source_target_pairs={{0,1},{1,0},{2,3},{3,2},{4,5},{5,4},{6,7},{7,6},{8,9},{9,8},{10,11... | collective-permute-start | bytes 688136 | tf_op jit(solution)/shard_map/ppermute | solution.py:36
  74.2 13.6 %collective-permute-start.20 = (bf16[128,896]{1,0:T(8,128)(2,1)S(1)}, bf16[128,896]{1,0:T(8,128)(2,1)S(1)}, u32[]{:S(2)}, u32[]{:S(2)}) collective-permute-start(bf16[128,896]{1,0:T(8,128)(2,1)S(1)} %copy-done.9), channel_id=1, source_target_pairs={{0,8},{1,9},{2,10},{3,11},{4,12},{5,13},{6,14},{7,15},{8,16},{9,17... | collective-permute-start | bytes 688136 | tf_op jit(solution)/shard_map/ppermute | solution.py:36
  80.1 2.4 %collective-permute-start.16 = (bf16[128,896]{1,0:T(8,128)(2,1)S(1)}, bf16[128,896]{1,0:T(8,128)(2,1)S(1)}, u32[]{:S(2)}, u32[]{:S(2)}) collective-permute-start(bf16[128,896]{1,0:T(8,128)(2,1)S(1)} %collective-permute-done.15.mine), channel_id=1, source_target_pairs={{0,1},{1,0},{2,3},{3,2},{4,5},{5,4},{6,7},{7,6},{8,9},{9,8},{10,11... | collective-permute-start | bytes 688136 | tf_op jit(solution)/shard_map/ppermute | solution.py:36
  85.7 14.8 %collective-permute-start.19 = (bf16[400,640]{1,0:T(8,128)(2,1)}, bf16[400,640]{1,0:T(8,128)(2,1)}, u32[]{:S(2)}, u32[]{:S(2)}) collective-permute-start(bf16[400,640]{1,0:T(8,128)(2,1)} %get-tuple-element.74), channel_id=1, source_target_pairs={{0,4},{1,5},{2,6},{3,7},{4,0},{5,1},{6,2},{7,3},{8,12},{9,13},{10,... | collective-permute-start | bytes 1536008 | tf_op jit(solution)/shard_map/ppermute | solution.py:36
  85.9 18.6 %collective-permute-start.18 = (bf16[384,256]{1,0:T(8,128)(2,1)}, bf16[384,256]{1,0:T(8,128)(2,1)}, u32[]{:S(2)}, u32[]{:S(2)}) collective-permute-start(bf16[384,256]{1,0:T(8,128)(2,1)} %get-tuple-element.73), channel_id=1, source_target_pairs={{0,4},{1,5},{2,6},{3,7},{4,0},{5,1},{6,2},{7,3},{8,12},{9,13},{10,... | collective-permute-start | bytes 589832 | tf_op jit(solution)/shard_map/ppermute | solution.py:36
  88.9 13.5 %collective-permute-start.22 = (bf16[128,896]{1,0:T(8,128)(2,1)}, bf16[128,896]{1,0:T(8,128)(2,1)}, u32[]{:S(2)}, u32[]{:S(2)}) collective-permute-start(bf16[128,896]{1,0:T(8,128)(2,1)} %get-tuple-element.86.own_last), channel_id=1, source_target_pairs={{0,8},{1,9},{2,10},{3,11},{4,12},{5,13},{6,14},{7,15},{8,16},{9,17... | collective-permute-start | bytes 688136 | tf_op jit(solution)/shard_map/ppermute | solution.py:36
  (15 other events, 143.8 us)

commit v15 on v14

--- a/solution.py
+++ b/solution.py
@@ -224,6 +224,51 @@
     )(place, *four, gain, weight)
 
 
+def half_kernel(
+    own, place, crossed, ringed, sib_crossed, sib_ringed, gain, weight, out, mean, normed
+):
+    rows = normed.shape[0]
+
+    def from_pair(mine, theirs):
+        mean[...] = normalize(mine, theirs, place, gain, normed, slice(None))
+
+    crossed_is_ours = place[2] == int(own)
+
+    @pl.when(crossed_is_ours)
+    def _():
+        from_pair(crossed, sib_crossed)
+
+    @pl.when(jnp.logical_not(crossed_is_ours))
+    def _():
+        from_pair(ringed, sib_ringed)
+
+    if not own:
+        put_statistics(out, statistics(mean[...]))
+    for k in range(3):
+        product = jnp.dot(normed[...], weight[0, k], preferred_element_type=F32)
+        if own:
+            out[k] = product
+        else:
+            out[STAT_ROWS + k * rows : STAT_ROWS + (k + 1) * rows] = product.astype(BF16)
+
+
+def half(own, place, four, gain, weight, estimate):
+    rows, width = four[0].shape
+    sent = pltpu.VMEM((3 * rows + STAT_ROWS, width), BF16)
+    return pl.pallas_call(
+        functools.partial(half_kernel, own),
+        in_specs=[smem_spec()] + [vmem_spec()] * 6,
+        out_shape=[
+            pltpu.VMEM((3, rows, width), F32) if own else sent,
+            pltpu.VMEM((rows, 1), F32),
+        ],
+        scratch_shapes=[pltpu.VMEM((rows, 2 * width), BF16)],
+        compiler_params=pltpu.CompilerParams(vmem_limit_bytes=VMEM_BYTES),
+        cost_estimate=cost(estimate),
+        name="half",
+    )(place, *four, gain, weight)
+
+
 def early_kernel(count, place, mine, theirs, gain, weight, *refs):
     owns, (product, mean), kept = refs[:count], refs[count : count + 2], refs[count + 2 : -2]
     normed, semaphores = refs[-2:]
@@ -385,19 +430,12 @@
     mix(kept, received, scales_of(received, kept_mean), (earlier,), None, put)
 
 
-def settle_kernel(flag, held, part, before, before_last, own, own_last, out, rest, rest_own):
-    rows, done = held.shape[0], part.shape[1]
-    shadow = flag[0] == 1
-
-    def settle(mixture, before, own):
-        result = jnp.where(shadow, before.astype(F32) + mixture, own.astype(F32))
-        return result.astype(BF16)
-
-    out[:rows] = settle(held[...], before[...], own[...])
-    out[rows:, :done] = settle(part[...], before_last[:, :done], own_last[:, :done])
-    out[rows:, done:] = own_last[:, done:]
-    rest[...] = before_last[:, done:]
-    rest_own[...] = own_last[:, done:]
+def settle_kernel(flag, held, before, own, out, piece, semaphore):
+    result = before[...].astype(F32) + held[...]
+    piece[...] = jnp.where(flag[0] == 1, result, own[...].astype(F32)).astype(BF16)
+    copy = pltpu.make_async_copy(piece, out.at[pl.ds(0, piece.shape[0])], semaphore)
+    copy.start()
+    copy.wait()
 
 
 def final_kernel(
@@ -407,26 +445,24 @@
     scale_kept,
     scale_peer,
     earlier,
-    rest,
-    rest_own,
+    part,
+    before,
+    own,
     settled,
     out,
     piece,
     semaphore,
 ):
-    rows, width = kept.shape[1:]
-    done = width - rest.shape[1]
-    shadow = flag[0] == 1
+    done = part.shape[1]
 
     def put(at, mixture):
-        here = slice(at.start - done, at.stop - done)
-        result = rest[:, here].astype(F32) + mixture
-        piece[:, here] = jnp.where(shadow, result, rest_own[:, here].astype(F32)).astype(BF16)
-
+        result = before[:, at].astype(F32) + mixture
+        piece[:, at] = jnp.where(flag[0] == 1, result, own[:, at].astype(F32)).astype(BF16)
+
+    put(slice(0, done), part[...])
     mix(kept, received, (scale_kept[...], scale_peer[...]), (earlier,), None, put, done, 0)
-    copy = pltpu.make_async_copy(
-        piece, out.at[pl.ds(out.shape[0] - rows, rows), pl.ds(done, width - done)], semaphore
-    )
+    rows = piece.shape[0]
+    copy = pltpu.make_async_copy(piece, out.at[pl.ds(out.shape[0] - rows, rows)], semaphore)
     copy.start()
     copy.wait()
 
@@ -473,15 +509,18 @@
         weight = pltpu.with_memory_space_constraint(weight, pltpu.VMEM)
         width = block.shape[1]
         heads = width // HD
-        sent, *sums = project(
-            place, spread(crossed, ringed[0]), norm_gain, weight, [(0, width)], False, 3
-        )
+        four = spread(crossed, ringed[0])
+        sent, mean = half(False, place, four, norm_gain, weight, 3)
         (received,) = send([sent])
-        behind, _ = lax.optimization_barrier((ringed[1], sums[1]))
+        *four, _ = lax.optimization_barrier((*four, mean))
+        sums = half(True, place, four, norm_gain, weight, 0.001)
+        behind, _ = lax.optimization_barrier((ringed[1], mean))
         forwarded = permute(behind, sections, forward)
+        forwarded, _ = lax.optimization_barrier((forwarded, sums[1]))
         crossed = jnp.where(diagonal, parts[1], forwarded)
+        four = spread(crossed, behind)
         sent, *behind_sums = project(
-            place, spread(crossed, behind), norm_gain, weight, [(0, width)], True, 0.001
+            place, four, norm_gain, weight, [(0, width)], True, 0.001
         )
         (received_behind,) = send([sent])
 
@@ -566,30 +605,25 @@
         )
         own_last, _ = lax.optimization_barrier((own_last, arrived))
         before_last = permute(own_last, sections, onward(direct))
-        part, *scales = start_part(kept, received[0], kept_mean, pairs, cut)
-        rest_of = pltpu.VMEM((below, width - cut), BF16)
-        out, *rest = call_attend(
-            settle_kernel,
-            "settle",
-            [preempted],
-            [mixture, part, before, before_last, own, own_last],
-            [jax.ShapeDtypeStruct(block.shape, BF16), rest_of, rest_of],
-        )
-        last = [kept, received[1], *scales, pairs, *rest]
-        out = pl.pallas_call(
-            final_kernel,
-            in_specs=[smem_spec()] + [vmem_spec() for _ in last] + [any_spec()],
-            out_specs=any_spec(),
-            out_shape=jax.ShapeDtypeStruct(block.shape, BF16),
-            input_output_aliases={1 + len(last): 0},
-            scratch_shapes=[
-                pltpu.VMEM((below, width - cut), BF16),
-                pltpu.SemaphoreType.DMA(()),
-            ],
-            compiler_params=pltpu.CompilerParams(vmem_limit_bytes=VMEM_BYTES),
-            cost_estimate=cost(250),
-            name="final",
-        )(preempted, *last, out)
+        def finish(kernel, name, arrays, rows, into):
+            whole = [] if into is None else [into]
+            return pl.pallas_call(
+                kernel,
+                in_specs=[smem_spec()] + [vmem_spec() for _ in arrays] + [any_spec() for _ in whole],
+                out_specs=any_spec(),
+                out_shape=jax.ShapeDtypeStruct(block.shape, BF16),
+                input_output_aliases={1 + len(arrays): 0} if whole else {},
+                scratch_shapes=[pltpu.VMEM((rows, width), BF16), pltpu.SemaphoreType.DMA(())],
+                compiler_params=pltpu.CompilerParams(vmem_limit_bytes=VMEM_BYTES),
+                cost_estimate=cost(250),
+                name=name,
+            )(preempted, *arrays, *whole)
+
+        out = finish(settle_kernel, "settle", [mixture, before, own], above, None)
+        first_piece, _ = lax.optimization_barrier((received[0], out))
+        part, *scales = start_part(kept, first_piece, kept_mean, pairs, cut)
+        last = [kept, received[1], *scales, pairs, part, before_last, own_last]
+        out = finish(final_kernel, "final", last, below, out)
         return out[None, None]
 
     placed = (

time: 107 us -> 107 us (level)
  waiting for transfers between devices: 28 us -> 30.3 us
  starting transfers between devices: 41.6 us -> 40.2 us
    pallas_call x1 -> x4, Pallas kernels: 2.14 us -> 8.12 us  [the longest x2 4.9 us: half(): pl.pallas_call(functools.partial(half_kernel, own), in_specs=[smem_spec()...]
    pallas_call x2 -> x1, Pallas kernels: 8.71 us -> 4.73 us  [project(): pl.pallas_call(functools.partial(project_kernel, cuts, apart), in_specs=[...]
    ppermute x23, waiting for transfers between devices: 28 us -> 30.3 us  [permute(): return lax.ppermute(array, AXES, pairs)]
    pallas_call x5 -> x4, Pallas kernels: 7.77 us -> 5.7 us  [call_attend(): pl.pallas_call(kernel, in_specs=[smem_spec() for _ in scalars] + [vmem_sp...]
    ppermute x23, starting transfers between devices: 41.6 us -> 40.2 us  [permute(): return lax.ppermute(array, AXES, pairs)]
  transfers between devices with their start and end apart: 23 -> 23, of which waited for: 11 -> 12; matrix products, arithmetic and copies ran while one was open for 0% -> 0% of each run, Pallas kernels for 30% -> 30%
where the time goes in v15:
time: 107 us
  starting transfers between devices  40.2 us (38%)
  Pallas kernels  34.1 us (32%)
  waiting for transfers between devices  30.3 us (28%)
  local copies, waits for them, and re-layouts  1.22 us (1%)
  between operations  1.12 us (1%)
    ppermute x23, starting transfers between devices, permute(): return lax.ppermute(array, AXES, pairs)  40.2 us
    ppermute x23, waiting for transfers between devices, permute(): return lax.ppermute(array, AXES, pairs)  30.3 us
    pallas_call x2, Pallas kernels, late(): pl.pallas_call(functools.partial(late_kernel, cuts, apart), in_specs=[sme...  6.03 us
    pallas_call x4, Pallas kernels, call_attend(): pl.pallas_call(kernel, in_specs=[smem_spec() for _ in scalars] + [vmem_sp...  5.7 us
    pallas_call x2, Pallas kernels, early(): pl.pallas_call(functools.partial(early_kernel, len(owns)), in_specs=[smem...  5.23 us
    pallas_call x2, Pallas kernels, half(): pl.pallas_call(functools.partial(half_kernel, own), in_specs=[smem_spec()...  4.9 us
    pallas_call x1, Pallas kernels, project(): pl.pallas_call(functools.partial(project_kernel, cuts, apart), in_specs=[...  4.73 us
    pallas_call x1, Pallas kernels, stage(): pl.pallas_call(stage_kernel, in_specs=[smem_spec(), any_spec()], out_spec...  4.29 us
  transfers between devices with their start and end apart: 23, of which 12 were waited for; matrix products, arithmetic and copies ran while one was open for 0% of the time, Pallas kernels for 30%

profile of v15, /device:TPU:0, one launch (start us, length us, event | category | flops | bytes accessed | tf_op | source)
XLA Modules:
  0.0 107.0 jit_solution(4457797579320455251)
XLA Ops:
  1.1 3.0 %collective-permute-start.1 = (bf16[128,896]{1,0:T(8,128)(2,1)S(1)}, bf16[128,896]{1,0:T(8,128)(2,1)S(1)}, u32[]{:S(2)}, u32[]{:S(2)}) collective-permute-start(bf16[128,896]{1,0:T(8,128)(2,1)S(1)} %get-tuple-element.71.block), channel_id=1, source_target_pairs={{0,2},{1,3},{2,6},{3,7},{4,0},{5,1},{6,4},{7,5},{8,10},{9,11},{10,... | collective-permute-start | bytes 688136 | tf_op jit(solution)/shard_map/ppermute | solution.py:36
  4.9 4.3 %stage.1.weight = bf16[1,3,1792,896]{3,2,1,0:T(8,128)(2,1)S(1)} custom-call(s32[3]{0:T(128)S(1)} %pad_add_fusion.place, bf16[1,3,1792,896]{3,2,1,0:T(8,128)(2,1)} %weight), custom_call_target="tpu_custom_call" | custom-call | flops 4600000000 | bytes 1000 | tf_op jit(solution)/shard_map/stage/pallas_call | solution.py:98
  9.2 4.7 %collective-permute-done.1.ringed = bf16[128,896]{1,0:T(8,128)(2,1)S(1)} collective-permute-done((bf16[128,896]{1,0:T(8,128)(2,1)S(1)}, bf16[128,896]{1,0:T(8,128)(2,1)S(1)}, u32[]{:S(2)}, u32[]{:S(2)}) %collective-permute-start.1) | collective-permute-done | bytes 229408 | tf_op jit(solution)/shard_map/ppermute | solution.py:36
  14.4 2.4 %collective-permute-start = (bf16[128,896]{1,0:T(8,128)(2,1)S(1)}, bf16[128,896]{1,0:T(8,128)(2,1)S(1)}, u32[]{:S(2)}, u32[]{:S(2)}) collective-permute-start(bf16[128,896]{1,0:T(8,128)(2,1)S(1)} %get-tuple-element.74.block), channel_id=1, source_target_pairs={{0,2},{1,3},{2,6},{3,7},{4,0},{5,1},{6,4},{7,5},{8,10},{9,11},{10,... | collective-permute-start | bytes 688136 | tf_op jit(solution)/shard_map/ppermute | solution.py:36
  16.9 2.5 %half.2 = (bf16[400,896]{1,0:T(8,128)(2,1)S(1)}, f32[128,1]{1,0:T(8,128)}) custom-call(s32[3]{0:T(128)S(1)} %pad_add_fusion.place, bf16[128,896]{1,0:T(8,128)(2,1)S(1)} %collective-permute-done.2.crossed, bf16[128,896]{1,0:T(8,128)(2,1)S(1)} %collective-permute-done.1.ringed, bf16[128,896]{1,0:T(8,128)(2,1)S(1)} %collective-permute-done.3.sib_crossed, ...), custom_call_target="tpu_custom_call" | custom-call | flops 3449999872 | bytes 1000 | tf_op jit(solution)/shard_map/half/pallas_call | solution.py:258
  19.4 2.3 %collective-permute-start.9 = (bf16[400,896]{1,0:T(8,128)(2,1)S(1)}, bf16[400,896]{1,0:T(8,128)(2,1)S(1)}, u32[]{:S(2)}, u32[]{:S(2)}) collective-permute-start(bf16[400,896]{1,0:T(8,128)(2,1)S(1)} %get-tuple-element.70), channel_id=1, source_target_pairs={{0,4},{1,5},{2,6},{3,7},{4,0},{5,1},{6,2},{7,3},{8,12},{9,13},{10,... | collective-permute-start | bytes 2150408 | tf_op jit(solution)/shard_map/ppermute | solution.py:36
  21.6 2.6 %collective-permute-done.ringed = bf16[128,896]{1,0:T(8,128)(2,1)S(1)} collective-permute-done((bf16[128,896]{1,0:T(8,128)(2,1)S(1)}, bf16[128,896]{1,0:T(8,128)(2,1)S(1)}, u32[]{:S(2)}, u32[]{:S(2)}) %collective-permute-start) | collective-permute-done | bytes 229408 | tf_op jit(solution)/shard_map/ppermute | solution.py:36
  26.4 2.4 %half.3 = (f32[3,128,896]{2,1,0:T(8,128)S(1)}, f32[128,1]{1,0:T(8,128)S(1)}) custom-call(s32[3]{0:T(128)S(1)} %pad_add_fusion.place, bf16[128,896]{1,0:T(8,128)(2,1)S(1)} %collective-permute-done.2.crossed, bf16[128,896]{1,0:T(8,128)(2,1)S(1)} %collective-permute-done.1.ringed, bf16[128,896]{1,0:T(8,128)(2,1)S(1)} %collective-permute-done.3.sib_crossed, ...), custom_call_target="tpu_custom_call" | custom-call | flops 1150000 | bytes 1000 | tf_op jit(solution)/shard_map/half/pallas_call | solution.py:258
  32.0 4.7 %project.1 = (bf16[400,896]{1,0:T(8,128)(2,1)}, f32[3,128,896]{2,1,0:T(8,128)S(1)}, f32[128,1]{1,0:T(8,128)S(1)}) custom-call(s32[3]{0:T(128)S(1)} %pad_add_fusion.place, bf16[128,896]{1,0:T(8,128)(2,1)S(1)} %broadcast_select_fusion.crossed, bf16[128,896]{1,0:T(8,128)(2,1)S(1)} %collective-permute-done.ringed, ...), custom_call_target="tpu_custom_call" | custom-call | flops 1150000 | bytes 1000 | tf_op jit(solution)/shard_map/project/pallas_call | solution.py:212
  36.8 3.5 %collective-permute-start.8 = (bf16[400,896]{1,0:T(8,128)(2,1)}, bf16[400,896]{1,0:T(8,128)(2,1)}, u32[]{:S(2)}, u32[]{:S(2)}) collective-permute-start(bf16[400,896]{1,0:T(8,128)(2,1)} %get-tuple-element.67), channel_id=1, source_target_pairs={{0,4},{1,5},{2,6},{3,7},{4,0},{5,1},{6,2},{7,3},{8,12},{9,13},{10,... | collective-permute-start | bytes 2150408 | tf_op jit(solution)/shard_map/ppermute | solution.py:36
  41.1 4.2 %collective-permute-start.10 = (bf16[128,896]{1,0:T(8,128)(2,1)S(1)}, bf16[128,896]{1,0:T(8,128)(2,1)}, u32[]{:S(2)}, u32[]{:S(2)}) collective-permute-start(bf16[128,896]{1,0:T(8,128)(2,1)S(1)} %get-tuple-element.72.refs_0_), channel_id=1, source_target_pairs={{0,8},{1,9},{2,12},{3,13},{4,10},{5,11},{6,14},{7,15},{8,16},{9,17... | collective-permute-start | bytes 688136 | tf_op jit(solution)/shard_map/ppermute | solution.py:36
  45.3 4.2 %collective-permute-done.10.mine = bf16[128,896]{1,0:T(8,128)(2,1)} collective-permute-done((bf16[128,896]{1,0:T(8,128)(2,1)S(1)}, bf16[128,896]{1,0:T(8,128)(2,1)}, u32[]{:S(2)}, u32[]{:S(2)}) %collective-permute-start.10) | collective-permute-done | bytes 229408 | tf_op jit(solution)/shard_map/ppermute | solution.py:36
  51.2 2.8 %early.2 = (f32[3,128,896]{2,1,0:T(8,128)S(1)}, f32[128,1]{1,0:T(8,128)S(1)}) custom-call(s32[3]{0:T(128)S(1)} %copy-done.6, bf16[128,896]{1,0:T(8,128)(2,1)} %collective-permute-done.10.mine, bf16[128,896]{1,0:T(8,128)(2,1)S(1)} %collective-permute-done.11.theirs, bf16[1,3584]{1,0:T(2,128)(2,1)S(1)} %copy-done.3, bf16[1,3,1792,896]{3,2,1,0:T(8,128)(2,1)S(1)} %stage.1.weight), custom_call_target="tpu_custom_call" | custom-call | flops 1150000 | bytes 1000 | tf_op jit(solution)/shard_map/early/pallas_call | solution.py:286
  54.0 2.9 %collective-permute-done.8.received = bf16[400,896]{1,0:T(8,128)(2,1)} collective-permute-done((bf16[400,896]{1,0:T(8,128)(2,1)}, bf16[400,896]{1,0:T(8,128)(2,1)}, u32[]{:S(2)}, u32[]{:S(2)}) %collective-permute-start.8) | collective-permute-done | bytes 716832 | tf_op jit(solution)/shard_map/ppermute | solution.py:36
  56.9 2.2 %attend.3.refs_1_ = bf16[128,896]{1,0:T(8,128)(2,1)S(1)} custom-call(f32[3,128,896]{2,1,0:T(8,128)S(1)} %get-tuple-element.66.kept, bf16[400,896]{1,0:T(8,128)(2,1)} %collective-permute-done.8.received, f32[128,1]{1,0:T(8,128)S(1)} %get-tuple-element.68.kept_mean, bf16[128,896]{1,0:T(8,128)(2,1)S(1)} %get-tuple-element.74.block, ...), custom_call_target="tpu_custom_call" | custom-call | flops 287500009472 | bytes 1000 | tf_op jit(solution)/shard_map/attend/pallas_call | solution.py:471
  59.2 8.7 %collective-permute-start.12 = (bf16[128,896]{1,0:T(8,128)(2,1)S(1)}, bf16[128,896]{1,0:T(8,128)(2,1)S(1)}, u32[]{:S(2)}, u32[]{:S(2)}) collective-permute-start(bf16[128,896]{1,0:T(8,128)(2,1)S(1)} %attend.3.refs_1_), channel_id=1, source_target_pairs={{0,8},{1,9},{2,12},{3,13},{4,10},{5,11},{6,14},{7,15},{8,16},{9,17... | collective-permute-start | bytes 688136 | tf_op jit(solution)/shard_map/ppermute | solution.py:36
  68.0 2.9 %late.2 = (bf16[400,896]{1,0:T(8,128)(2,1)S(1)}, f32[3,128,896]{2,1,0:T(8,128)S(1)}, f32[128,1]{1,0:T(8,128)S(1)}) custom-call(s32[3]{0:T(128)S(1)} %copy-done.7, bf16[128,896]{1,0:T(8,128)(2,1)} %collective-permute-done.13.mine, bf16[128,896]{1,0:T(8,128)(2,1)S(1)} %collective-permute-done.14.theirs, bf16[1,3584]{1,0:T(2,128)(2,1)S(1)} %copy-done.4, ...), custom_call_target="tpu_custom_call" | custom-call | flops 3449999872 | bytes 1000 | tf_op jit(solution)/shard_map/late/pallas_call | solution.py:330
  70.9 2.1 %collective-permute-done.12.mine = bf16[128,896]{1,0:T(8,128)(2,1)S(1)} collective-permute-done((bf16[128,896]{1,0:T(8,128)(2,1)S(1)}, bf16[128,896]{1,0:T(8,128)(2,1)S(1)}, u32[]{:S(2)}, u32[]{:S(2)}) %collective-permute-start.12) | collective-permute-done | bytes 229408 | tf_op jit(solution)/shard_map/ppermute | solution.py:36
  74.2 4.6 %collective-permute-start.20 = (bf16[128,896]{1,0:T(8,128)(2,1)S(1)}, bf16[128,896]{1,0:T(8,128)(2,1)S(1)}, u32[]{:S(2)}, u32[]{:S(2)}) collective-permute-start(bf16[128,896]{1,0:T(8,128)(2,1)S(1)} %copy-done.9), channel_id=1, source_target_pairs={{0,8},{1,9},{2,10},{3,11},{4,12},{5,13},{6,14},{7,15},{8,16},{9,17... | collective-permute-start | bytes 688136 | tf_op jit(solution)/shard_map/ppermute | solution.py:36
  80.2 2.4 %early.3 = (f32[3,128,896]{2,1,0:T(8,128)S(1)}, f32[128,1]{1,0:T(8,128)S(1)}, bf16[128,896]{1,0:T(8,128)(2,1)}, bf16[128,896]{1,0:T(8,128)(2,1)}) custom-call(s32[3]{0:T(128)S(1)} %copy-done.7, bf16[128,896]{1,0:T(8,128)(2,1)S(1)} %collective-permute-done.12.mine, bf16[128,896]{1,0:T(8,128)(2,1)S(1)} %collective-permute-done.17.theirs, ...), custom_call_target="tpu_custom_call" | custom-call | flops 3449999872 | bytes 1000 | tf_op jit(solution)/shard_map/early/pallas_call | solution.py:286
  82.6 3.1 %late.3 = (bf16[400,640]{1,0:T(8,128)(2,1)}, bf16[384,256]{1,0:T(8,128)(2,1)}, f32[3,128,896]{2,1,0:T(8,128)S(1)}, f32[128,1]{1,0:T(8,128)S(1)}) custom-call(s32[3]{0:T(128)S(1)} %copy-done.7, bf16[128,896]{1,0:T(8,128)(2,1)S(1)} %collective-permute-done.15.mine, bf16[128,896]{1,0:T(8,128)(2,1)S(1)} %collective-permute-done.16.theirs, ...), custom_call_target="tpu_custom_call" | custom-call | flops 1150000000 | bytes 1000 | tf_op jit(solution)/shard_map/late/pallas_call | solution.py:330
  89.0 4.2 %collective-permute-start.22 = (bf16[128,896]{1,0:T(8,128)(2,1)}, bf16[128,896]{1,0:T(8,128)(2,1)}, u32[]{:S(2)}, u32[]{:S(2)}) collective-permute-start(bf16[128,896]{1,0:T(8,128)(2,1)} %get-tuple-element.98.own), channel_id=1, source_target_pairs={{0,8},{1,9},{2,10},{3,11},{4,12},{5,13},{6,14},{7,15},{8,16},{9,17... | collective-permute-start | bytes 688136 | tf_op jit(solution)/shard_map/ppermute | solution.py:36
  94.9 5.7 %collective-permute-done.19.received = bf16[400,640]{1,0:T(8,128)(2,1)} collective-permute-done((bf16[400,640]{1,0:T(8,128)(2,1)}, bf16[400,640]{1,0:T(8,128)(2,1)}, u32[]{:S(2)}, u32[]{:S(2)}) %collective-permute-start.19) | collective-permute-done | bytes 512032 | tf_op jit(solution)/shard_map/ppermute | solution.py:36
  104.4 2.5 %final.1 = bf16[256,896]{1,0:T(8,128)(2,1)} custom-call(s32[1]{0:T(128)S(6)} %copy.7.flag, f32[3,128,896]{2,1,0:T(8,128)S(1)} %get-tuple-element.82.kept, bf16[384,256]{1,0:T(8,128)(2,1)} %collective-permute-done.18.received, f32[128,1]{1,0:T(8,128)S(1)} %get-tuple-element.94.scale_kept, ...), custom_call_target="tpu_custom_call", output_to_operand_aliasing={{}: (9, {})} | custom-call | flops 287500009472 | bytes 1000 | tf_op jit(solution)/shard_map/final/pallas_call | solution.py:610
  (63 shorter events, 21.0 us)
Async XLA Ops:
  1.1 12.8 %collective-permute-start.1 = (bf16[128,896]{1,0:T(8,128)(2,1)S(1)}, bf16[128,896]{1,0:T(8,128)(2,1)S(1)}, u32[]{:S(2)}, u32[]{:S(2)}) collective-permute-start(bf16[128,896]{1,0:T(8,128)(2,1)S(1)} %get-tuple-element.71.block), channel_id=1, source_target_pairs={{0,2},{1,3},{2,6},{3,7},{4,0},{5,1},{6,4},{7,5},{8,10},{9,11},{10,... | collective-permute-start | bytes 688136 | tf_op jit(solution)/shard_map/ppermute | solution.py:36
  4.1 9.8 %collective-permute-start.2 = (bf16[128,896]{1,0:T(8,128)(2,1)S(1)}, bf16[128,896]{1,0:T(8,128)(2,1)S(1)}, u32[]{:S(2)}, u32[]{:S(2)}) collective-permute-start(bf16[128,896]{1,0:T(8,128)(2,1)S(1)} %get-tuple-element.71.block), channel_id=1, source_target_pairs={{0,0},{1,1},{2,4},{3,5},{4,2},{5,3},{6,6},{7,7},{8,8},{9,9},{10,12... | collective-permute-start | bytes 688136 | tf_op jit(solution)/shard_map/ppermute | solution.py:36
  9.2 42.0 %copy-start = (bf16[1,3,1792,896]{3,2,1,0:T(8,128)(2,1)}, bf16[1,3,1792,896]{3,2,1,0:T(8,128)(2,1)S(1)}, u32[]{:S(2)}) copy-start(bf16[1,3,1792,896]{3,2,1,0:T(8,128)(2,1)S(1)} %stage.1.weight) | copy-start | bytes 28901380
  13.9 3.0 %collective-permute-start.3 = (bf16[128,896]{1,0:T(8,128)(2,1)S(1)}, bf16[128,896]{1,0:T(8,128)(2,1)S(1)}, u32[]{:S(2)}, u32[]{:S(2)}) collective-permute-start(bf16[128,896]{1,0:T(8,128)(2,1)S(1)} %collective-permute-done.2.crossed), channel_id=1, source_target_pairs={{0,1},{1,0},{2,3},{3,2},{4,5},{5,4},{6,7},{7,6},{8,9},{9,8},{10,11... | collective-permute-start | bytes 688136 | tf_op jit(solution)/shard_map/ppermute | solution.py:36
  13.9 3.0 %collective-permute-start.4 = (bf16[128,896]{1,0:T(8,128)(2,1)S(1)}, bf16[128,896]{1,0:T(8,128)(2,1)S(1)}, u32[]{:S(2)}, u32[]{:S(2)}) collective-permute-start(bf16[128,896]{1,0:T(8,128)(2,1)S(1)} %collective-permute-done.1.ringed), channel_id=1, source_target_pairs={{0,1},{1,0},{2,3},{3,2},{4,5},{5,4},{6,7},{7,6},{8,9},{9,8},{10,11... | collective-permute-start | bytes 688136 | tf_op jit(solution)/shard_map/ppermute | solution.py:36
  14.4 9.8 %collective-permute-start = (bf16[128,896]{1,0:T(8,128)(2,1)S(1)}, bf16[128,896]{1,0:T(8,128)(2,1)S(1)}, u32[]{:S(2)}, u32[]{:S(2)}) collective-permute-start(bf16[128,896]{1,0:T(8,128)(2,1)S(1)} %get-tuple-element.74.block), channel_id=1, source_target_pairs={{0,2},{1,3},{2,6},{3,7},{4,0},{5,1},{6,4},{7,5},{8,10},{9,11},{10,... | collective-permute-start | bytes 688136 | tf_op jit(solution)/shard_map/ppermute | solution.py:36
  19.4 20.9 %collective-permute-start.9 = (bf16[400,896]{1,0:T(8,128)(2,1)S(1)}, bf16[400,896]{1,0:T(8,128)(2,1)S(1)}, u32[]{:S(2)}, u32[]{:S(2)}) collective-permute-start(bf16[400,896]{1,0:T(8,128)(2,1)S(1)} %get-tuple-element.70), channel_id=1, source_target_pairs={{0,4},{1,5},{2,6},{3,7},{4,0},{5,1},{6,2},{7,3},{8,12},{9,13},{10,... | collective-permute-start | bytes 2150408 | tf_op jit(solution)/shard_map/ppermute | solution.py:36
  24.2 6.2 %collective-permute-start.5 = (bf16[128,896]{1,0:T(8,128)(2,1)S(1)}, bf16[128,896]{1,0:T(8,128)(2,1)S(1)}, u32[]{:S(2)}, u32[]{:S(2)}) collective-permute-start(bf16[128,896]{1,0:T(8,128)(2,1)S(1)} %collective-permute-done.ringed), channel_id=1, source_target_pairs={{0,2},{1,3},{6,4},{7,5},{8,10},{9,11},{14,12},{15,13},{16,18},{17,... | collective-permute-start | bytes 688136 | tf_op jit(solution)/shard_map/ppermute | solution.py:36
  26.3 4.3 %collective-permute-start.7 = (bf16[128,896]{1,0:T(8,128)(2,1)S(1)}, bf16[128,896]{1,0:T(8,128)(2,1)S(1)}, u32[]{:S(2)}, u32[]{:S(2)}) collective-permute-start(bf16[128,896]{1,0:T(8,128)(2,1)S(1)} %collective-permute-done.ringed), channel_id=1, source_target_pairs={{0,1},{1,0},{2,3},{3,2},{4,5},{5,4},{6,7},{7,6},{8,9},{9,8},{10,11... | collective-permute-start | bytes 688136 | tf_op jit(solution)/shard_map/ppermute | solution.py:36
  30.5 1.6 %collective-permute-start.6 = (bf16[128,896]{1,0:T(8,128)(2,1)S(1)}, bf16[128,896]{1,0:T(8,128)(2,1)S(1)}, u32[]{:S(2)}, u32[]{:S(2)}) collective-permute-start(bf16[128,896]{1,0:T(8,128)(2,1)S(1)} %broadcast_select_fusion.crossed), channel_id=1, source_target_pairs={{0,1},{1,0},{2,3},{3,2},{4,5},{5,4},{6,7},{7,6},{8,9},{9,8},{10,11... | collective-permute-start | bytes 688136 | tf_op jit(solution)/shard_map/ppermute | solution.py:36
  36.8 20.1 %collective-permute-start.8 = (bf16[400,896]{1,0:T(8,128)(2,1)}, bf16[400,896]{1,0:T(8,128)(2,1)}, u32[]{:S(2)}, u32[]{:S(2)}) collective-permute-start(bf16[400,896]{1,0:T(8,128)(2,1)} %get-tuple-element.67), channel_id=1, source_target_pairs={{0,4},{1,5},{2,6},{3,7},{4,0},{5,1},{6,2},{7,3},{8,12},{9,13},{10,... | collective-permute-start | bytes 2150408 | tf_op jit(solution)/shard_map/ppermute | solution.py:36
  41.1 8.4 %collective-permute-start.10 = (bf16[128,896]{1,0:T(8,128)(2,1)S(1)}, bf16[128,896]{1,0:T(8,128)(2,1)}, u32[]{:S(2)}, u32[]{:S(2)}) collective-permute-start(bf16[128,896]{1,0:T(8,128)(2,1)S(1)} %get-tuple-element.72.refs_0_), channel_id=1, source_target_pairs={{0,8},{1,9},{2,12},{3,13},{4,10},{5,11},{6,14},{7,15},{8,16},{9,17... | collective-permute-start | bytes 688136 | tf_op jit(solution)/shard_map/ppermute | solution.py:36
  49.5 1.7 %collective-permute-start.11 = (bf16[128,896]{1,0:T(8,128)(2,1)}, bf16[128,896]{1,0:T(8,128)(2,1)S(1)}, u32[]{:S(2)}, u32[]{:S(2)}) collective-permute-start(bf16[128,896]{1,0:T(8,128)(2,1)} %collective-permute-done.10.mine), channel_id=1, source_target_pairs={{0,1},{1,0},{2,3},{3,2},{4,5},{5,4},{6,7},{7,6},{8,9},{9,8},{10,11... | collective-permute-start | bytes 688136 | tf_op jit(solution)/shard_map/ppermute | solution.py:36
  49.5 9.6 %collective-permute-start.13 = (bf16[128,896]{1,0:T(8,128)(2,1)}, bf16[128,896]{1,0:T(8,128)(2,1)}, u32[]{:S(2)}, u32[]{:S(2)}) collective-permute-start(bf16[128,896]{1,0:T(8,128)(2,1)} %collective-permute-done.10.mine), channel_id=1, source_target_pairs={{0,2},{1,3},{2,0},{3,1},{4,6},{5,7},{6,4},{7,5},{8,10},{9,11},{10,... | collective-permute-start | bytes 688136 | tf_op jit(solution)/shard_map/ppermute | solution.py:36
  59.1 8.8 %collective-permute-start.14 = (bf16[128,896]{1,0:T(8,128)(2,1)}, bf16[128,896]{1,0:T(8,128)(2,1)S(1)}, u32[]{:S(2)}, u32[]{:S(2)}) collective-permute-start(bf16[128,896]{1,0:T(8,128)(2,1)} %collective-permute-done.13.mine), channel_id=1, source_target_pairs={{0,1},{1,0},{2,3},{3,2},{4,5},{5,4},{6,7},{7,6},{8,9},{9,8},{10,11... | collective-permute-start | bytes 688136 | tf_op jit(solution)/shard_map/ppermute | solution.py:36
  59.2 13.9 %collective-permute-start.12 = (bf16[128,896]{1,0:T(8,128)(2,1)S(1)}, bf16[128,896]{1,0:T(8,128)(2,1)S(1)}, u32[]{:S(2)}, u32[]{:S(2)}) collective-permute-start(bf16[128,896]{1,0:T(8,128)(2,1)S(1)} %attend.3.refs_1_), channel_id=1, source_target_pairs={{0,8},{1,9},{2,12},{3,13},{4,10},{5,11},{6,14},{7,15},{8,16},{9,17... | collective-permute-start | bytes 688136 | tf_op jit(solution)/shard_map/ppermute | solution.py:36
  70.9 18.1 %collective-permute-start.21 = (bf16[400,896]{1,0:T(8,128)(2,1)S(1)}, bf16[400,896]{1,0:T(8,128)(2,1)S(1)}, u32[]{:S(2)}, u32[]{:S(2)}) collective-permute-start(bf16[400,896]{1,0:T(8,128)(2,1)S(1)} %get-tuple-element.86), channel_id=1, source_target_pairs={{0,4},{1,5},{2,6},{3,7},{4,0},{5,1},{6,2},{7,3},{8,12},{9,13},{10,... | collective-permute-start | bytes 2150408 | tf_op jit(solution)/shard_map/ppermute | solution.py:36
  73.1 7.1 %collective-permute-start.15 = (bf16[128,896]{1,0:T(8,128)(2,1)S(1)}, bf16[128,896]{1,0:T(8,128)(2,1)S(1)}, u32[]{:S(2)}, u32[]{:S(2)}) collective-permute-start(bf16[128,896]{1,0:T(8,128)(2,1)S(1)} %collective-permute-done.12.mine), channel_id=1, source_target_pairs={{0,2},{1,3},{2,0},{3,1},{4,6},{5,7},{6,4},{7,5},{8,10},{9,11},{10,... | collective-permute-start | bytes 688136 | tf_op jit(solution)/shard_map/ppermute | solution.py:36
  73.5 6.6 %collective-permute-start.17 = (bf16[128,896]{1,0:T(8,128)(2,1)S(1)}, bf16[128,896]{1,0:T(8,128)(2,1)S(1)}, u32[]{:S(2)}, u32[]{:S(2)}) collective-permute-start(bf16[128,896]{1,0:T(8,128)(2,1)S(1)} %collective-permute-done.12.mine), channel_id=1, source_target_pairs={{0,1},{1,0},{2,3},{3,2},{4,5},{5,4},{6,7},{7,6},{8,9},{9,8},{10,11... | collective-permute-start | bytes 688136 | tf_op jit(solution)/shard_map/ppermute | solution.py:36
  74.2 13.6 %collective-permute-start.20 = (bf16[128,896]{1,0:T(8,128)(2,1)S(1)}, bf16[128,896]{1,0:T(8,128)(2,1)S(1)}, u32[]{:S(2)}, u32[]{:S(2)}) collective-permute-start(bf16[128,896]{1,0:T(8,128)(2,1)S(1)} %copy-done.9), channel_id=1, source_target_pairs={{0,8},{1,9},{2,10},{3,11},{4,12},{5,13},{6,14},{7,15},{8,16},{9,17... | collective-permute-start | bytes 688136 | tf_op jit(solution)/shard_map/ppermute | solution.py:36
  80.1 2.4 %collective-permute-start.16 = (bf16[128,896]{1,0:T(8,128)(2,1)S(1)}, bf16[128,896]{1,0:T(8,128)(2,1)S(1)}, u32[]{:S(2)}, u32[]{:S(2)}) collective-permute-start(bf16[128,896]{1,0:T(8,128)(2,1)S(1)} %collective-permute-done.15.mine), channel_id=1, source_target_pairs={{0,1},{1,0},{2,3},{3,2},{4,5},{5,4},{6,7},{7,6},{8,9},{9,8},{10,11... | collective-permute-start | bytes 688136 | tf_op jit(solution)/shard_map/ppermute | solution.py:36
  85.7 14.8 %collective-permute-start.19 = (bf16[400,640]{1,0:T(8,128)(2,1)}, bf16[400,640]{1,0:T(8,128)(2,1)}, u32[]{:S(2)}, u32[]{:S(2)}) collective-permute-start(bf16[400,640]{1,0:T(8,128)(2,1)} %get-tuple-element.84), channel_id=1, source_target_pairs={{0,4},{1,5},{2,6},{3,7},{4,0},{5,1},{6,2},{7,3},{8,12},{9,13},{10,... | collective-permute-start | bytes 1536008 | tf_op jit(solution)/shard_map/ppermute | solution.py:36
  85.9 18.5 %collective-permute-start.18 = (bf16[384,256]{1,0:T(8,128)(2,1)}, bf16[384,256]{1,0:T(8,128)(2,1)}, u32[]{:S(2)}, u32[]{:S(2)}) collective-permute-start(bf16[384,256]{1,0:T(8,128)(2,1)} %get-tuple-element.83), channel_id=1, source_target_pairs={{0,4},{1,5},{2,6},{3,7},{4,0},{5,1},{6,2},{7,3},{8,12},{9,13},{10,... | collective-permute-start | bytes 589832 | tf_op jit(solution)/shard_map/ppermute | solution.py:36
  89.0 15.4 %collective-permute-start.22 = (bf16[128,896]{1,0:T(8,128)(2,1)}, bf16[128,896]{1,0:T(8,128)(2,1)}, u32[]{:S(2)}, u32[]{:S(2)}) collective-permute-start(bf16[128,896]{1,0:T(8,128)(2,1)} %get-tuple-element.98.own), channel_id=1, source_target_pairs={{0,8},{1,9},{2,10},{3,11},{4,12},{5,13},{6,14},{7,15},{8,16},{9,17... | collective-permute-start | bytes 688136 | tf_op jit(solution)/shard_map/ppermute | solution.py:36
  (11 other events, 116.5 us)

commit v16 on v15

--- a/solution.py
+++ b/solution.py
@@ -175,53 +175,6 @@
 
 def tops_of(cuts):
     return [STAT_ROWS] + [0] * (len(cuts) - 1)
-
-
-def project_kernel(
-    cuts, apart, place, crossed, ringed, sib_crossed, sib_ringed, gain, weight, *refs
-):
-    count = len(cuts)
-    sents, (kept, kept_mean, normed) = refs[:count], refs[count : count + 3]
-    outs, semaphores = refs[count + 3 : -1] if apart else sents, refs[-1]
-    rows = normed.shape[0] // 2
-    diagonal = place[2]
-    copies = Copies(semaphores)
-    means = []
-    for mine, theirs, offset in (
-        (crossed, sib_crossed, diagonal),
-        (ringed, sib_ringed, 1 - diagonal),
-    ):
-        at = pl.ds(pl.multiple_of(offset * rows, rows), rows)
-        means.append(normalize(mine, theirs, place, gain, normed, at))
-    kept_mean[...] = jnp.where(diagonal == 1, means[0], means[1])
-    put_statistics(outs[0], statistics(jnp.where(diagonal == 1, means[1], means[0])))
-    for (begin, end), out, sent, top in zip(cuts, outs, sents, tops_of(cuts)):
-        for k in range(3):
-            product = jnp.dot(normed[...], weight[0, k, :, begin:end], preferred_element_type=F32)
-            out[top + k * rows : top + (k + 1) * rows] = product[:rows].astype(BF16)
-            kept[k, :, begin:end] = product[rows:]
-            if apart:
-                at = piece_of(k, rows, top)
-                copies.start(out.at[at], sent.at[at])
-    copies.wait()
-
-
-def project(place, four, gain, weight, cuts, apart, estimate):
-    rows, width = four[0].shape
-    shapes = [(top + 3 * rows, end - begin) for (begin, end), top in zip(cuts, tops_of(cuts))]
-    return pl.pallas_call(
-        functools.partial(project_kernel, cuts, apart),
-        in_specs=[smem_spec()] + [vmem_spec()] * 6,
-        out_specs=[any_spec() if apart else vmem_spec() for _ in cuts] + [vmem_spec()] * 2,
-        out_shape=[(pltpu.HBM if apart else pltpu.VMEM)(shape, BF16) for shape in shapes]
-        + [pltpu.VMEM((3, rows, width), F32), pltpu.VMEM((rows, 1), F32)],
-        scratch_shapes=[pltpu.VMEM((2 * rows, 2 * width), BF16)]
-        + [pltpu.VMEM(shape, BF16) for shape in shapes] * apart
-        + [pltpu.SemaphoreType.DMA((3 * len(cuts),))],
-        compiler_params=pltpu.CompilerParams(vmem_limit_bytes=VMEM_BYTES),
-        cost_estimate=cost(estimate),
-        name="project",
-    )(place, *four, gain, weight)
 
 
 def half_kernel(
@@ -519,9 +472,7 @@
         forwarded, _ = lax.optimization_barrier((forwarded, sums[1]))
         crossed = jnp.where(diagonal, parts[1], forwarded)
         four = spread(crossed, behind)
-        sent, *behind_sums = project(
-            place, four, norm_gain, weight, [(0, width)], True, 0.001
-        )
+        sent, mean = half(False, place, four, norm_gain, weight, 0.001)
         (received_behind,) = send([sent])
 
         def carry(own):
@@ -538,7 +489,7 @@
             )
 
         pairs_of = pltpu.VMEM((2, above, width), BF16)
-        part, _ = lax.optimization_barrier((parts[0], behind_sums[1]))
+        part, _ = lax.optimization_barrier((parts[0], mean))
         first, pairs = call_attend(
             attend_kernel,
             "attend",
@@ -546,7 +497,9 @@
             [sums[0], received, sums[1], part],
             [pltpu.VMEM(part.shape, BF16), pairs_of],
         )
-        crossed = carry(first)
+        *four, _ = lax.optimization_barrier((*four, first))
+        behind_sums = half(True, place, four, norm_gain, weight, 0.001)
+        crossed, _ = lax.optimization_barrier((carry(first), behind_sums[1]))
         swapped = permute(crossed, sections, swap)
         beside = permute(crossed, sections, sibling)
         product, mean = early(place, crossed, beside, norm_gain, weight, [], 0.001)

time: 107 us -> 106 us (level)
  waiting for transfers between devices: 30.3 us -> 27 us
  Pallas kernels: 34.1 us -> 35.3 us
    pallas_call x2 -> x4, Pallas kernels: 4.9 us -> 10.8 us  [half(): pl.pallas_call(functools.partial(half_kernel, own), in_specs=[smem_spec()...]
    pallas_call x1 -> x0, Pallas kernels: 4.73 us -> none  [project(): pl.pallas_call(functools.partial(project_kernel, cuts, apart), in_specs=[...]
    ppermute x23, waiting for transfers between devices: 30.3 us -> 27 us  [permute(): return lax.ppermute(array, AXES, pairs)]
  transfers between devices with their start and end apart: 23 -> 23, of which waited for: 12 -> 13; matrix products, arithmetic and copies ran while one was open for 0% -> 0% of each run, Pallas kernels for 30% -> 31%
where the time goes in v16:
time: 106 us
  starting transfers between devices  40.1 us (38%)
  Pallas kernels  35.3 us (33%)
  waiting for transfers between devices  27 us (25%)
  local copies, waits for them, and re-layouts  1.88 us (2%)
  between operations  1.18 us (1%)
    ppermute x23, starting transfers between devices, permute(): return lax.ppermute(array, AXES, pairs)  40.1 us
    ppermute x23, waiting for transfers between devices, permute(): return lax.ppermute(array, AXES, pairs)  27 us
    pallas_call x4, Pallas kernels, half(): pl.pallas_call(functools.partial(half_kernel, own), in_specs=[smem_spec()...  10.8 us
    pallas_call x2, Pallas kernels, late(): pl.pallas_call(functools.partial(late_kernel, cuts, apart), in_specs=[sme...  6.07 us
    pallas_call x4, Pallas kernels, call_attend(): pl.pallas_call(kernel, in_specs=[smem_spec() for _ in scalars] + [vmem_sp...  5.69 us
    pallas_call x2, Pallas kernels, early(): pl.pallas_call(functools.partial(early_kernel, len(owns)), in_specs=[smem...  5.23 us
    pallas_call x1, Pallas kernels, stage(): pl.pallas_call(stage_kernel, in_specs=[smem_spec(), any_spec()], out_spec...  4.29 us
    pallas_call x2, Pallas kernels, finish(): pl.pallas_call(kernel, in_specs=[smem_spec()] + [vmem_spec() for _ in arr...  3.23 us
  transfers between devices with their start and end apart: 23, of which 13 were waited for; matrix products, arithmetic and copies ran while one was open for 0% of the time, Pallas kernels for 31%

profile of v16, /device:TPU:0, one launch (start us, length us, event | category | flops | bytes accessed | tf_op | source)
XLA Modules:
  0.0 105.6 jit_solution(11531827200295533644)
XLA Ops:
  1.1 3.0 %collective-permute-start.1 = (bf16[128,896]{1,0:T(8,128)(2,1)S(1)}, bf16[128,896]{1,0:T(8,128)(2,1)S(1)}, u32[]{:S(2)}, u32[]{:S(2)}) collective-permute-start(bf16[128,896]{1,0:T(8,128)(2,1)S(1)} %get-tuple-element.107.block), channel_id=1, source_target_pairs={{0,2},{1,3},{2,6},{3,7},{4,0},{5,1},{6,4},{7,5},{8,10},{9,11},{10,... | collective-permute-start | bytes 688136 | tf_op jit(solution)/shard_map/ppermute | solution.py:36
  4.9 4.3 %stage.1.weight = bf16[1,3,1792,896]{3,2,1,0:T(8,128)(2,1)S(1)} custom-call(s32[3]{0:T(128)S(1)} %pad_add_fusion.place, bf16[1,3,1792,896]{3,2,1,0:T(8,128)(2,1)} %weight), custom_call_target="tpu_custom_call" | custom-call | flops 4600000000 | bytes 1000 | tf_op jit(solution)/shard_map/stage/pallas_call | solution.py:98
  9.2 4.7 %collective-permute-done.1.ringed = bf16[128,896]{1,0:T(8,128)(2,1)S(1)} collective-permute-done((bf16[128,896]{1,0:T(8,128)(2,1)S(1)}, bf16[128,896]{1,0:T(8,128)(2,1)S(1)}, u32[]{:S(2)}, u32[]{:S(2)}) %collective-permute-start.1) | collective-permute-done | bytes 229408 | tf_op jit(solution)/shard_map/ppermute | solution.py:36
  14.4 2.4 %collective-permute-start = (bf16[128,896]{1,0:T(8,128)(2,1)S(1)}, bf16[128,896]{1,0:T(8,128)(2,1)S(1)}, u32[]{:S(2)}, u32[]{:S(2)}) collective-permute-start(bf16[128,896]{1,0:T(8,128)(2,1)S(1)} %get-tuple-element.82.block), channel_id=1, source_target_pairs={{0,2},{1,3},{2,6},{3,7},{4,0},{5,1},{6,4},{7,5},{8,10},{9,11},{10,... | collective-permute-start | bytes 688136 | tf_op jit(solution)/shard_map/ppermute | solution.py:36
  16.9 2.5 %half.4 = (bf16[400,896]{1,0:T(8,128)(2,1)S(1)}, f32[128,1]{1,0:T(8,128)}) custom-call(s32[3]{0:T(128)S(1)} %pad_add_fusion.place, bf16[128,896]{1,0:T(8,128)(2,1)S(1)} %collective-permute-done.2.crossed, bf16[128,896]{1,0:T(8,128)(2,1)S(1)} %collective-permute-done.1.ringed, bf16[128,896]{1,0:T(8,128)(2,1)S(1)} %collective-permute-done.3.sib_crossed, ...), custom_call_target="tpu_custom_call" | custom-call | flops 3449999872 | bytes 1000 | tf_op jit(solution)/shard_map/half/pallas_call | solution.py:211
  19.4 2.3 %collective-permute-start.8 = (bf16[400,896]{1,0:T(8,128)(2,1)S(1)}, bf16[400,896]{1,0:T(8,128)(2,1)S(1)}, u32[]{:S(2)}, u32[]{:S(2)}) collective-permute-start(bf16[400,896]{1,0:T(8,128)(2,1)S(1)} %get-tuple-element.71), channel_id=1, source_target_pairs={{0,4},{1,5},{2,6},{3,7},{4,0},{5,1},{6,2},{7,3},{8,12},{9,13},{10,... | collective-permute-start | bytes 2150408 | tf_op jit(solution)/shard_map/ppermute | solution.py:36
  21.6 2.6 %collective-permute-done.ringed = bf16[128,896]{1,0:T(8,128)(2,1)S(1)} collective-permute-done((bf16[128,896]{1,0:T(8,128)(2,1)S(1)}, bf16[128,896]{1,0:T(8,128)(2,1)S(1)}, u32[]{:S(2)}, u32[]{:S(2)}) %collective-permute-start) | collective-permute-done | bytes 229408 | tf_op jit(solution)/shard_map/ppermute | solution.py:36
  26.4 2.4 %half.5 = (f32[3,128,896]{2,1,0:T(8,128)S(1)}, f32[128,1]{1,0:T(8,128)S(1)}) custom-call(s32[3]{0:T(128)S(1)} %pad_add_fusion.place, bf16[128,896]{1,0:T(8,128)(2,1)S(1)} %collective-permute-done.2.crossed, bf16[128,896]{1,0:T(8,128)(2,1)S(1)} %collective-permute-done.1.ringed, bf16[128,896]{1,0:T(8,128)(2,1)S(1)} %collective-permute-done.3.sib_crossed, ...), custom_call_target="tpu_custom_call" | custom-call | flops 1150000 | bytes 1000 | tf_op jit(solution)/shard_map/half/pallas_call | solution.py:211
  32.1 3.3 %half.7 = (bf16[400,896]{1,0:T(8,128)(2,1)}, f32[128,1]{1,0:T(8,128)}) custom-call(s32[3]{0:T(128)S(1)} %pad_add_fusion.place, bf16[128,896]{1,0:T(8,128)(2,1)S(1)} %broadcast_select_fusion.crossed, bf16[128,896]{1,0:T(8,128)(2,1)S(1)} %collective-permute-done.ringed, bf16[128,896]{1,0:T(8,128)(2,1)S(1)} %collective-permute-done.6.sib_crossed, ...), custom_call_target="tpu_custom_call" | custom-call | flops 1150000 | bytes 1000 | tf_op jit(solution)/shard_map/half/pallas_call | solution.py:211
  35.4 3.5 %collective-permute-start.9 = (bf16[400,896]{1,0:T(8,128)(2,1)}, bf16[400,896]{1,0:T(8,128)(2,1)}, u32[]{:S(2)}, u32[]{:S(2)}) collective-permute-start(bf16[400,896]{1,0:T(8,128)(2,1)} %get-tuple-element.78), channel_id=1, source_target_pairs={{0,4},{1,5},{2,6},{3,7},{4,0},{5,1},{6,2},{7,3},{8,12},{9,13},{10,... | collective-permute-start | bytes 2150408 | tf_op jit(solution)/shard_map/ppermute | solution.py:36
  39.8 4.2 %collective-permute-start.10 = (bf16[128,896]{1,0:T(8,128)(2,1)S(1)}, bf16[128,896]{1,0:T(8,128)(2,1)}, u32[]{:S(2)}, u32[]{:S(2)}) collective-permute-start(bf16[128,896]{1,0:T(8,128)(2,1)S(1)} %get-tuple-element.72.refs_0_), channel_id=1, source_target_pairs={{0,8},{1,9},{2,12},{3,13},{4,10},{5,11},{6,14},{7,15},{8,16},{9,17... | collective-permute-start | bytes 688136 | tf_op jit(solution)/shard_map/ppermute | solution.py:36
  44.0 2.6 %half.6 = (f32[3,128,896]{2,1,0:T(8,128)S(1)}, f32[128,1]{1,0:T(8,128)S(1)}) custom-call(s32[3]{0:T(128)S(1)} %pad_add_fusion.place, bf16[128,896]{1,0:T(8,128)(2,1)S(1)} %copy-done.3, bf16[128,896]{1,0:T(8,128)(2,1)S(1)} %copy-done.5, bf16[128,896]{1,0:T(8,128)(2,1)S(1)} %copy-done.9, bf16[128,896]{1,0:T(8,128)(2,1)S(1)} %copy-done.7, ...), custom_call_target="tpu_custom_call" | custom-call | flops 1150000 | bytes 1000 | tf_op jit(solution)/shard_map/half/pallas_call | solution.py:211
  50.5 2.8 %early.2 = (f32[3,128,896]{2,1,0:T(8,128)S(1)}, f32[128,1]{1,0:T(8,128)S(1)}) custom-call(s32[3]{0:T(128)S(1)} %copy-done.13, bf16[128,896]{1,0:T(8,128)(2,1)} %collective-permute-done.10.mine, bf16[128,896]{1,0:T(8,128)(2,1)S(1)} %collective-permute-done.11.theirs, bf16[1,3584]{1,0:T(2,128)(2,1)S(1)} %copy-done.11, bf16[1,3,1792,896]{3,2,1,0:T(8,128)(2,1)S(1)} %stage.1.weight), custom_call_target="tpu_custom_call" | custom-call | flops 1150000 | bytes 1000 | tf_op jit(solution)/shard_map/early/pallas_call | solution.py:239
  53.3 2.2 %collective-permute-done.9.received = bf16[400,896]{1,0:T(8,128)(2,1)} collective-permute-done((bf16[400,896]{1,0:T(8,128)(2,1)}, bf16[400,896]{1,0:T(8,128)(2,1)}, u32[]{:S(2)}, u32[]{:S(2)}) %collective-permute-start.9) | collective-permute-done | bytes 716832 | tf_op jit(solution)/shard_map/ppermute | solution.py:36
  55.5 2.2 %attend.3.refs_1_ = bf16[128,896]{1,0:T(8,128)(2,1)S(1)} custom-call(f32[3,128,896]{2,1,0:T(8,128)S(1)} %get-tuple-element.77.kept, bf16[400,896]{1,0:T(8,128)(2,1)} %collective-permute-done.9.received, f32[128,1]{1,0:T(8,128)S(1)} %get-tuple-element.79.kept_mean, bf16[128,896]{1,0:T(8,128)(2,1)S(1)} %get-tuple-element.82.block, ...), custom_call_target="tpu_custom_call" | custom-call | flops 287500009472 | bytes 1000 | tf_op jit(solution)/shard_map/attend/pallas_call | solution.py:424
  57.8 8.5 %collective-permute-start.12 = (bf16[128,896]{1,0:T(8,128)(2,1)S(1)}, bf16[128,896]{1,0:T(8,128)(2,1)S(1)}, u32[]{:S(2)}, u32[]{:S(2)}) collective-permute-start(bf16[128,896]{1,0:T(8,128)(2,1)S(1)} %attend.3.refs_1_), channel_id=1, source_target_pairs={{0,8},{1,9},{2,12},{3,13},{4,10},{5,11},{6,14},{7,15},{8,16},{9,17... | collective-permute-start | bytes 688136 | tf_op jit(solution)/shard_map/ppermute | solution.py:36
  66.4 2.9 %late.2 = (bf16[400,896]{1,0:T(8,128)(2,1)S(1)}, f32[3,128,896]{2,1,0:T(8,128)S(1)}, f32[128,1]{1,0:T(8,128)S(1)}) custom-call(s32[3]{0:T(128)S(1)} %copy-done.14, bf16[128,896]{1,0:T(8,128)(2,1)} %collective-permute-done.13.mine, bf16[128,896]{1,0:T(8,128)(2,1)S(1)} %collective-permute-done.14.theirs, bf16[1,3584]{1,0:T(2,128)(2,1)S(1)} %copy-done.11, ...), custom_call_target="tpu_custom_call" | custom-call | flops 3449999872 | bytes 1000 | tf_op jit(solution)/shard_map/late/pallas_call | solution.py:283
  69.4 2.3 %collective-permute-done.12.mine = bf16[128,896]{1,0:T(8,128)(2,1)S(1)} collective-permute-done((bf16[128,896]{1,0:T(8,128)(2,1)S(1)}, bf16[128,896]{1,0:T(8,128)(2,1)S(1)}, u32[]{:S(2)}, u32[]{:S(2)}) %collective-permute-start.12) | collective-permute-done | bytes 229408 | tf_op jit(solution)/shard_map/ppermute | solution.py:36
  72.8 4.6 %collective-permute-start.20 = (bf16[128,896]{1,0:T(8,128)(2,1)S(1)}, bf16[128,896]{1,0:T(8,128)(2,1)S(1)}, u32[]{:S(2)}, u32[]{:S(2)}) collective-permute-start(bf16[128,896]{1,0:T(8,128)(2,1)S(1)} %copy-done.16), channel_id=1, source_target_pairs={{0,8},{1,9},{2,10},{3,11},{4,12},{5,13},{6,14},{7,15},{8,16},{9,17... | collective-permute-start | bytes 688136 | tf_op jit(solution)/shard_map/ppermute | solution.py:36
  78.7 2.4 %early.3 = (f32[3,128,896]{2,1,0:T(8,128)S(1)}, f32[128,1]{1,0:T(8,128)S(1)}, bf16[128,896]{1,0:T(8,128)(2,1)}, bf16[128,896]{1,0:T(8,128)(2,1)}) custom-call(s32[3]{0:T(128)S(1)} %copy-done.14, bf16[128,896]{1,0:T(8,128)(2,1)S(1)} %collective-permute-done.12.mine, bf16[128,896]{1,0:T(8,128)(2,1)S(1)} %collective-permute-done.17.theirs, ...), custom_call_target="tpu_custom_call" | custom-call | flops 3449999872 | bytes 1000 | tf_op jit(solution)/shard_map/early/pallas_call | solution.py:239
  81.2 3.1 %late.3 = (bf16[400,640]{1,0:T(8,128)(2,1)}, bf16[384,256]{1,0:T(8,128)(2,1)}, f32[3,128,896]{2,1,0:T(8,128)S(1)}, f32[128,1]{1,0:T(8,128)S(1)}) custom-call(s32[3]{0:T(128)S(1)} %copy-done.14, bf16[128,896]{1,0:T(8,128)(2,1)S(1)} %collective-permute-done.15.mine, bf16[128,896]{1,0:T(8,128)(2,1)S(1)} %collective-permute-done.16.theirs, ...), custom_call_target="tpu_custom_call" | custom-call | flops 1150000000 | bytes 1000 | tf_op jit(solution)/shard_map/late/pallas_call | solution.py:283
  87.4 4.2 %collective-permute-start.22 = (bf16[128,896]{1,0:T(8,128)(2,1)}, bf16[128,896]{1,0:T(8,128)(2,1)}, u32[]{:S(2)}, u32[]{:S(2)}) collective-permute-start(bf16[128,896]{1,0:T(8,128)(2,1)} %get-tuple-element.106.own), channel_id=1, source_target_pairs={{0,8},{1,9},{2,10},{3,11},{4,12},{5,13},{6,14},{7,15},{8,16},{9,17... | collective-permute-start | bytes 688136 | tf_op jit(solution)/shard_map/ppermute | solution.py:36
  93.3 5.8 %collective-permute-done.19.received = bf16[400,640]{1,0:T(8,128)(2,1)} collective-permute-done((bf16[400,640]{1,0:T(8,128)(2,1)}, bf16[400,640]{1,0:T(8,128)(2,1)}, u32[]{:S(2)}, u32[]{:S(2)}) %collective-permute-start.19) | collective-permute-done | bytes 512032 | tf_op jit(solution)/shard_map/ppermute | solution.py:36
  103.0 2.4 %final.1 = bf16[256,896]{1,0:T(8,128)(2,1)} custom-call(s32[1]{0:T(128)S(6)} %copy.7.flag, f32[3,128,896]{2,1,0:T(8,128)S(1)} %get-tuple-element.90.kept, bf16[384,256]{1,0:T(8,128)(2,1)} %collective-permute-done.18.received, f32[128,1]{1,0:T(8,128)S(1)} %get-tuple-element.102.scale_kept, ...), custom_call_target="tpu_custom_call", output_to_operand_aliasing={{}: (9, {})} | custom-call | flops 287500009472 | bytes 1000 | tf_op jit(solution)/shard_map/final/pallas_call | solution.py:563
  (78 shorter events, 23.1 us)
Async XLA Ops:
  1.1 12.8 %collective-permute-start.1 = (bf16[128,896]{1,0:T(8,128)(2,1)S(1)}, bf16[128,896]{1,0:T(8,128)(2,1)S(1)}, u32[]{:S(2)}, u32[]{:S(2)}) collective-permute-start(bf16[128,896]{1,0:T(8,128)(2,1)S(1)} %get-tuple-element.107.block), channel_id=1, source_target_pairs={{0,2},{1,3},{2,6},{3,7},{4,0},{5,1},{6,4},{7,5},{8,10},{9,11},{10,... | collective-permute-start | bytes 688136 | tf_op jit(solution)/shard_map/ppermute | solution.py:36
  4.1 9.8 %collective-permute-start.2 = (bf16[128,896]{1,0:T(8,128)(2,1)S(1)}, bf16[128,896]{1,0:T(8,128)(2,1)S(1)}, u32[]{:S(2)}, u32[]{:S(2)}) collective-permute-start(bf16[128,896]{1,0:T(8,128)(2,1)S(1)} %get-tuple-element.107.block), channel_id=1, source_target_pairs={{0,0},{1,1},{2,4},{3,5},{4,2},{5,3},{6,6},{7,7},{8,8},{9,9},{10,12... | collective-permute-start | bytes 688136 | tf_op jit(solution)/shard_map/ppermute | solution.py:36
  9.2 40.6 %copy-start = (bf16[1,3,1792,896]{3,2,1,0:T(8,128)(2,1)}, bf16[1,3,1792,896]{3,2,1,0:T(8,128)(2,1)S(1)}, u32[]{:S(2)}) copy-start(bf16[1,3,1792,896]{3,2,1,0:T(8,128)(2,1)S(1)} %stage.1.weight) | copy-start | bytes 28901380
  13.9 3.0 %collective-permute-start.3 = (bf16[128,896]{1,0:T(8,128)(2,1)S(1)}, bf16[128,896]{1,0:T(8,128)(2,1)S(1)}, u32[]{:S(2)}, u32[]{:S(2)}) collective-permute-start(bf16[128,896]{1,0:T(8,128)(2,1)S(1)} %collective-permute-done.2.crossed), channel_id=1, source_target_pairs={{0,1},{1,0},{2,3},{3,2},{4,5},{5,4},{6,7},{7,6},{8,9},{9,8},{10,11... | collective-permute-start | bytes 688136 | tf_op jit(solution)/shard_map/ppermute | solution.py:36
  13.9 3.0 %collective-permute-start.4 = (bf16[128,896]{1,0:T(8,128)(2,1)S(1)}, bf16[128,896]{1,0:T(8,128)(2,1)S(1)}, u32[]{:S(2)}, u32[]{:S(2)}) collective-permute-start(bf16[128,896]{1,0:T(8,128)(2,1)S(1)} %collective-permute-done.1.ringed), channel_id=1, source_target_pairs={{0,1},{1,0},{2,3},{3,2},{4,5},{5,4},{6,7},{7,6},{8,9},{9,8},{10,11... | collective-permute-start | bytes 688136 | tf_op jit(solution)/shard_map/ppermute | solution.py:36
  14.4 9.8 %collective-permute-start = (bf16[128,896]{1,0:T(8,128)(2,1)S(1)}, bf16[128,896]{1,0:T(8,128)(2,1)S(1)}, u32[]{:S(2)}, u32[]{:S(2)}) collective-permute-start(bf16[128,896]{1,0:T(8,128)(2,1)S(1)} %get-tuple-element.82.block), channel_id=1, source_target_pairs={{0,2},{1,3},{2,6},{3,7},{4,0},{5,1},{6,4},{7,5},{8,10},{9,11},{10,... | collective-permute-start | bytes 688136 | tf_op jit(solution)/shard_map/ppermute | solution.py:36
  19.4 19.6 %collective-permute-start.8 = (bf16[400,896]{1,0:T(8,128)(2,1)S(1)}, bf16[400,896]{1,0:T(8,128)(2,1)S(1)}, u32[]{:S(2)}, u32[]{:S(2)}) collective-permute-start(bf16[400,896]{1,0:T(8,128)(2,1)S(1)} %get-tuple-element.71), channel_id=1, source_target_pairs={{0,4},{1,5},{2,6},{3,7},{4,0},{5,1},{6,2},{7,3},{8,12},{9,13},{10,... | collective-permute-start | bytes 2150408 | tf_op jit(solution)/shard_map/ppermute | solution.py:36
  24.2 6.2 %collective-permute-start.5 = (bf16[128,896]{1,0:T(8,128)(2,1)S(1)}, bf16[128,896]{1,0:T(8,128)(2,1)S(1)}, u32[]{:S(2)}, u32[]{:S(2)}) collective-permute-start(bf16[128,896]{1,0:T(8,128)(2,1)S(1)} %collective-permute-done.ringed), channel_id=1, source_target_pairs={{0,2},{1,3},{6,4},{7,5},{8,10},{9,11},{14,12},{15,13},{16,18},{17,... | collective-permute-start | bytes 688136 | tf_op jit(solution)/shard_map/ppermute | solution.py:36
  26.3 4.3 %collective-permute-start.7 = (bf16[128,896]{1,0:T(8,128)(2,1)S(1)}, bf16[128,896]{1,0:T(8,128)(2,1)S(1)}, u32[]{:S(2)}, u32[]{:S(2)}) collective-permute-start(bf16[128,896]{1,0:T(8,128)(2,1)S(1)} %collective-permute-done.ringed), channel_id=1, source_target_pairs={{0,1},{1,0},{2,3},{3,2},{4,5},{5,4},{6,7},{7,6},{8,9},{9,8},{10,11... | collective-permute-start | bytes 688136 | tf_op jit(solution)/shard_map/ppermute | solution.py:36
  30.5 1.6 %collective-permute-start.6 = (bf16[128,896]{1,0:T(8,128)(2,1)S(1)}, bf16[128,896]{1,0:T(8,128)(2,1)S(1)}, u32[]{:S(2)}, u32[]{:S(2)}) collective-permute-start(bf16[128,896]{1,0:T(8,128)(2,1)S(1)} %broadcast_select_fusion.crossed), channel_id=1, source_target_pairs={{0,1},{1,0},{2,3},{3,2},{4,5},{5,4},{6,7},{7,6},{8,9},{9,8},{10,11... | collective-permute-start | bytes 688136 | tf_op jit(solution)/shard_map/ppermute | solution.py:36
  35.4 20.1 %collective-permute-start.9 = (bf16[400,896]{1,0:T(8,128)(2,1)}, bf16[400,896]{1,0:T(8,128)(2,1)}, u32[]{:S(2)}, u32[]{:S(2)}) collective-permute-start(bf16[400,896]{1,0:T(8,128)(2,1)} %get-tuple-element.78), channel_id=1, source_target_pairs={{0,4},{1,5},{2,6},{3,7},{4,0},{5,1},{6,2},{7,3},{8,12},{9,13},{10,... | collective-permute-start | bytes 2150408 | tf_op jit(solution)/shard_map/ppermute | solution.py:36
  39.8 8.3 %collective-permute-start.10 = (bf16[128,896]{1,0:T(8,128)(2,1)S(1)}, bf16[128,896]{1,0:T(8,128)(2,1)}, u32[]{:S(2)}, u32[]{:S(2)}) collective-permute-start(bf16[128,896]{1,0:T(8,128)(2,1)S(1)} %get-tuple-element.72.refs_0_), channel_id=1, source_target_pairs={{0,8},{1,9},{2,12},{3,13},{4,10},{5,11},{6,14},{7,15},{8,16},{9,17... | collective-permute-start | bytes 688136 | tf_op jit(solution)/shard_map/ppermute | solution.py:36
  48.1 1.7 %collective-permute-start.11 = (bf16[128,896]{1,0:T(8,128)(2,1)}, bf16[128,896]{1,0:T(8,128)(2,1)S(1)}, u32[]{:S(2)}, u32[]{:S(2)}) collective-permute-start(bf16[128,896]{1,0:T(8,128)(2,1)} %collective-permute-done.10.mine), channel_id=1, source_target_pairs={{0,1},{1,0},{2,3},{3,2},{4,5},{5,4},{6,7},{7,6},{8,9},{9,8},{10,11... | collective-permute-start | bytes 688136 | tf_op jit(solution)/shard_map/ppermute | solution.py:36
  48.1 9.6 %collective-permute-start.13 = (bf16[128,896]{1,0:T(8,128)(2,1)}, bf16[128,896]{1,0:T(8,128)(2,1)}, u32[]{:S(2)}, u32[]{:S(2)}) collective-permute-start(bf16[128,896]{1,0:T(8,128)(2,1)} %collective-permute-done.10.mine), channel_id=1, source_target_pairs={{0,2},{1,3},{2,0},{3,1},{4,6},{5,7},{6,4},{7,5},{8,10},{9,11},{10,... | collective-permute-start | bytes 688136 | tf_op jit(solution)/shard_map/ppermute | solution.py:36
  57.7 8.6 %collective-permute-start.14 = (bf16[128,896]{1,0:T(8,128)(2,1)}, bf16[128,896]{1,0:T(8,128)(2,1)S(1)}, u32[]{:S(2)}, u32[]{:S(2)}) collective-permute-start(bf16[128,896]{1,0:T(8,128)(2,1)} %collective-permute-done.13.mine), channel_id=1, source_target_pairs={{0,1},{1,0},{2,3},{3,2},{4,5},{5,4},{6,7},{7,6},{8,9},{9,8},{10,11... | collective-permute-start | bytes 688136 | tf_op jit(solution)/shard_map/ppermute | solution.py:36
  57.8 13.9 %collective-permute-start.12 = (bf16[128,896]{1,0:T(8,128)(2,1)S(1)}, bf16[128,896]{1,0:T(8,128)(2,1)S(1)}, u32[]{:S(2)}, u32[]{:S(2)}) collective-permute-start(bf16[128,896]{1,0:T(8,128)(2,1)S(1)} %attend.3.refs_1_), channel_id=1, source_target_pairs={{0,8},{1,9},{2,12},{3,13},{4,10},{5,11},{6,14},{7,15},{8,16},{9,17... | collective-permute-start | bytes 688136 | tf_op jit(solution)/shard_map/ppermute | solution.py:36
  69.3 18.1 %collective-permute-start.21 = (bf16[400,896]{1,0:T(8,128)(2,1)S(1)}, bf16[400,896]{1,0:T(8,128)(2,1)S(1)}, u32[]{:S(2)}, u32[]{:S(2)}) collective-permute-start(bf16[400,896]{1,0:T(8,128)(2,1)S(1)} %get-tuple-element.94), channel_id=1, source_target_pairs={{0,4},{1,5},{2,6},{3,7},{4,0},{5,1},{6,2},{7,3},{8,12},{9,13},{10,... | collective-permute-start | bytes 2150408 | tf_op jit(solution)/shard_map/ppermute | solution.py:36
  71.7 7.1 %collective-permute-start.15 = (bf16[128,896]{1,0:T(8,128)(2,1)S(1)}, bf16[128,896]{1,0:T(8,128)(2,1)S(1)}, u32[]{:S(2)}, u32[]{:S(2)}) collective-permute-start(bf16[128,896]{1,0:T(8,128)(2,1)S(1)} %collective-permute-done.12.mine), channel_id=1, source_target_pairs={{0,2},{1,3},{2,0},{3,1},{4,6},{5,7},{6,4},{7,5},{8,10},{9,11},{10,... | collective-permute-start | bytes 688136 | tf_op jit(solution)/shard_map/ppermute | solution.py:36
  72.1 6.6 %collective-permute-start.17 = (bf16[128,896]{1,0:T(8,128)(2,1)S(1)}, bf16[128,896]{1,0:T(8,128)(2,1)S(1)}, u32[]{:S(2)}, u32[]{:S(2)}) collective-permute-start(bf16[128,896]{1,0:T(8,128)(2,1)S(1)} %collective-permute-done.12.mine), channel_id=1, source_target_pairs={{0,1},{1,0},{2,3},{3,2},{4,5},{5,4},{6,7},{7,6},{8,9},{9,8},{10,11... | collective-permute-start | bytes 688136 | tf_op jit(solution)/shard_map/ppermute | solution.py:36
  72.8 13.6 %collective-permute-start.20 = (bf16[128,896]{1,0:T(8,128)(2,1)S(1)}, bf16[128,896]{1,0:T(8,128)(2,1)S(1)}, u32[]{:S(2)}, u32[]{:S(2)}) collective-permute-start(bf16[128,896]{1,0:T(8,128)(2,1)S(1)} %copy-done.16), channel_id=1, source_target_pairs={{0,8},{1,9},{2,10},{3,11},{4,12},{5,13},{6,14},{7,15},{8,16},{9,17... | collective-permute-start | bytes 688136 | tf_op jit(solution)/shard_map/ppermute | solution.py:36
  78.7 2.4 %collective-permute-start.16 = (bf16[128,896]{1,0:T(8,128)(2,1)S(1)}, bf16[128,896]{1,0:T(8,128)(2,1)S(1)}, u32[]{:S(2)}, u32[]{:S(2)}) collective-permute-start(bf16[128,896]{1,0:T(8,128)(2,1)S(1)} %collective-permute-done.15.mine), channel_id=1, source_target_pairs={{0,1},{1,0},{2,3},{3,2},{4,5},{5,4},{6,7},{7,6},{8,9},{9,8},{10,11... | collective-permute-start | bytes 688136 | tf_op jit(solution)/shard_map/ppermute | solution.py:36
  84.3 14.8 %collective-permute-start.19 = (bf16[400,640]{1,0:T(8,128)(2,1)}, bf16[400,640]{1,0:T(8,128)(2,1)}, u32[]{:S(2)}, u32[]{:S(2)}) collective-permute-start(bf16[400,640]{1,0:T(8,128)(2,1)} %get-tuple-element.92), channel_id=1, source_target_pairs={{0,4},{1,5},{2,6},{3,7},{4,0},{5,1},{6,2},{7,3},{8,12},{9,13},{10,... | collective-permute-start | bytes 1536008 | tf_op jit(solution)/shard_map/ppermute | solution.py:36
  84.4 18.6 %collective-permute-start.18 = (bf16[384,256]{1,0:T(8,128)(2,1)}, bf16[384,256]{1,0:T(8,128)(2,1)}, u32[]{:S(2)}, u32[]{:S(2)}) collective-permute-start(bf16[384,256]{1,0:T(8,128)(2,1)} %get-tuple-element.91), channel_id=1, source_target_pairs={{0,4},{1,5},{2,6},{3,7},{4,0},{5,1},{6,2},{7,3},{8,12},{9,13},{10,... | collective-permute-start | bytes 589832 | tf_op jit(solution)/shard_map/ppermute | solution.py:36
  87.4 15.6 %collective-permute-start.22 = (bf16[128,896]{1,0:T(8,128)(2,1)}, bf16[128,896]{1,0:T(8,128)(2,1)}, u32[]{:S(2)}, u32[]{:S(2)}) collective-permute-start(bf16[128,896]{1,0:T(8,128)(2,1)} %get-tuple-element.106.own), channel_id=1, source_target_pairs={{0,8},{1,9},{2,10},{3,11},{4,12},{5,13},{6,14},{7,15},{8,16},{9,17... | collective-permute-start | bytes 688136 | tf_op jit(solution)/shard_map/ppermute | solution.py:36
  (18 other events, 145.0 us)

commit v17 on v16

--- a/solution.py
+++ b/solution.py
@@ -178,9 +178,10 @@
 
 
 def half_kernel(
-    own, place, crossed, ringed, sib_crossed, sib_ringed, gain, weight, out, mean, normed
+    own, apart, place, crossed, ringed, sib_crossed, sib_ringed, gain, weight, to, mean, normed, *more
 ):
     rows = normed.shape[0]
+    out, copies = (more[0], Copies(more[1])) if apart else (to, Copies(None))
 
     def from_pair(mine, theirs):
         mean[...] = normalize(mine, theirs, place, gain, normed, slice(None))
@@ -203,19 +204,26 @@
             out[k] = product
         else:
             out[STAT_ROWS + k * rows : STAT_ROWS + (k + 1) * rows] = product.astype(BF16)
-
-
-def half(own, place, four, gain, weight, estimate):
+        if apart:
+            at = piece_of(k, rows, STAT_ROWS)
+            copies.start(out.at[at], to.at[at])
+    copies.wait()
+
+
+def half(own, apart, place, four, gain, weight, estimate):
     rows, width = four[0].shape
-    sent = pltpu.VMEM((3 * rows + STAT_ROWS, width), BF16)
+    shape = (3 * rows + STAT_ROWS, width)
+    sent = (pltpu.HBM if apart else pltpu.VMEM)(shape, BF16)
     return pl.pallas_call(
-        functools.partial(half_kernel, own),
+        functools.partial(half_kernel, own, apart),
         in_specs=[smem_spec()] + [vmem_spec()] * 6,
+        out_specs=[any_spec() if apart else vmem_spec(), vmem_spec()],
         out_shape=[
             pltpu.VMEM((3, rows, width), F32) if own else sent,
             pltpu.VMEM((rows, 1), F32),
         ],
-        scratch_shapes=[pltpu.VMEM((rows, 2 * width), BF16)],
+        scratch_shapes=[pltpu.VMEM((rows, 2 * width), BF16)]
+        + [pltpu.VMEM(shape, BF16), pltpu.SemaphoreType.DMA((3,))] * apart,
         compiler_params=pltpu.CompilerParams(vmem_limit_bytes=VMEM_BYTES),
         cost_estimate=cost(estimate),
         name="half",
@@ -463,16 +471,16 @@
         width = block.shape[1]
         heads = width // HD
         four = spread(crossed, ringed[0])
-        sent, mean = half(False, place, four, norm_gain, weight, 3)
+        sent, mean = half(False, False, place, four, norm_gain, weight, 3)
         (received,) = send([sent])
         *four, _ = lax.optimization_barrier((*four, mean))
-        sums = half(True, place, four, norm_gain, weight, 0.001)
+        sums = half(True, False, place, four, norm_gain, weight, 0.001)
         behind, _ = lax.optimization_barrier((ringed[1], mean))
         forwarded = permute(behind, sections, forward)
         forwarded, _ = lax.optimization_barrier((forwarded, sums[1]))
         crossed = jnp.where(diagonal, parts[1], forwarded)
         four = spread(crossed, behind)
-        sent, mean = half(False, place, four, norm_gain, weight, 0.001)
+        sent, mean = half(False, True, place, four, norm_gain, weight, 0.001)
         (received_behind,) = send([sent])
 
         def carry(own):
@@ -498,7 +506,7 @@
             [pltpu.VMEM(part.shape, BF16), pairs_of],
         )
         *four, _ = lax.optimization_barrier((*four, first))
-        behind_sums = half(True, place, four, norm_gain, weight, 0.001)
+        behind_sums = half(True, False, place, four, norm_gain, weight, 0.001)
         crossed, _ = lax.optimization_barrier((carry(first), behind_sums[1]))
         swapped = permute(crossed, sections, swap)
         beside = permute(crossed, sections, sibling)

time: 106 us -> 107 us (level)
  transfers between devices with their start and end apart: 23 -> 23, of which waited for: 13 -> 12; matrix products, arithmetic and copies ran while one was open for 0% -> 0% of each run, Pallas kernels for 31% -> 31%
where the time goes in v17:
time: 107 us; the launch traced here: 106 us
  starting transfers between devices  40 us (37%)
  Pallas kernels  35.8 us (33%)
  waiting for transfers between devices  27.1 us (25%)
  local copies, waits for them, and re-layouts  1.88 us (2%)
  between operations  1.21 us (1%)
    ppermute x23, starting transfers between devices, permute(): return lax.ppermute(array, AXES, pairs)  40 us
    ppermute x23, waiting for transfers between devices, permute(): return lax.ppermute(array, AXES, pairs)  27.1 us
    pallas_call x4, Pallas kernels, half(): pl.pallas_call(functools.partial(half_kernel, own, apart), in_specs=[smem...  11.3 us
    pallas_call x2, Pallas kernels, late(): pl.pallas_call(functools.partial(late_kernel, cuts, apart), in_specs=[sme...  6.07 us
    pallas_call x4, Pallas kernels, call_attend(): pl.pallas_call(kernel, in_specs=[smem_spec() for _ in scalars] + [vmem_sp...  5.68 us
    pallas_call x2, Pallas kernels, early(): pl.pallas_call(functools.partial(early_kernel, len(owns)), in_specs=[smem...  5.22 us
    pallas_call x1, Pallas kernels, stage(): pl.pallas_call(stage_kernel, in_specs=[smem_spec(), any_spec()], out_spec...  4.29 us
    pallas_call x2, Pallas kernels, finish(): pl.pallas_call(kernel, in_specs=[smem_spec()] + [vmem_spec() for _ in arr...  3.23 us
  transfers between devices with their start and end apart: 23, of which 12 were waited for; matrix products, arithmetic and copies ran while one was open for 0% of the time, Pallas kernels for 31%

profile of v17, /device:TPU:0, one launch (start us, length us, event | category | flops | bytes accessed | tf_op | source)
XLA Modules:
  0.0 106.1 jit_solution(15024806070798117701)
XLA Ops:
  1.1 3.0 %collective-permute-start.1 = (bf16[128,896]{1,0:T(8,128)(2,1)S(1)}, bf16[128,896]{1,0:T(8,128)(2,1)S(1)}, u32[]{:S(2)}, u32[]{:S(2)}) collective-permute-start(bf16[128,896]{1,0:T(8,128)(2,1)S(1)} %get-tuple-element.107.block), channel_id=1, source_target_pairs={{0,2},{1,3},{2,6},{3,7},{4,0},{5,1},{6,4},{7,5},{8,10},{9,11},{10,... | collective-permute-start | bytes 688136 | tf_op jit(solution)/shard_map/ppermute | solution.py:36
  4.9 4.3 %stage.1.weight = bf16[1,3,1792,896]{3,2,1,0:T(8,128)(2,1)S(1)} custom-call(s32[3]{0:T(128)S(1)} %pad_add_fusion.place, bf16[1,3,1792,896]{3,2,1,0:T(8,128)(2,1)} %weight), custom_call_target="tpu_custom_call" | custom-call | flops 4600000000 | bytes 1000 | tf_op jit(solution)/shard_map/stage/pallas_call | solution.py:98
  9.2 4.7 %collective-permute-done.1.ringed = bf16[128,896]{1,0:T(8,128)(2,1)S(1)} collective-permute-done((bf16[128,896]{1,0:T(8,128)(2,1)S(1)}, bf16[128,896]{1,0:T(8,128)(2,1)S(1)}, u32[]{:S(2)}, u32[]{:S(2)}) %collective-permute-start.1) | collective-permute-done | bytes 229408 | tf_op jit(solution)/shard_map/ppermute | solution.py:36
  14.4 2.4 %collective-permute-start = (bf16[128,896]{1,0:T(8,128)(2,1)S(1)}, bf16[128,896]{1,0:T(8,128)(2,1)S(1)}, u32[]{:S(2)}, u32[]{:S(2)}) collective-permute-start(bf16[128,896]{1,0:T(8,128)(2,1)S(1)} %get-tuple-element.82.block), channel_id=1, source_target_pairs={{0,2},{1,3},{2,6},{3,7},{4,0},{5,1},{6,4},{7,5},{8,10},{9,11},{10,... | collective-permute-start | bytes 688136 | tf_op jit(solution)/shard_map/ppermute | solution.py:36
  16.9 2.5 %half.4 = (bf16[400,896]{1,0:T(8,128)(2,1)S(1)}, f32[128,1]{1,0:T(8,128)}) custom-call(s32[3]{0:T(128)S(1)} %pad_add_fusion.place, bf16[128,896]{1,0:T(8,128)(2,1)S(1)} %collective-permute-done.2.crossed, bf16[128,896]{1,0:T(8,128)(2,1)S(1)} %collective-permute-done.1.ringed, bf16[128,896]{1,0:T(8,128)(2,1)S(1)} %collective-permute-done.3.sib_crossed, ...), custom_call_target="tpu_custom_call" | custom-call | flops 3449999872 | bytes 1000 | tf_op jit(solution)/shard_map/half/pallas_call | solution.py:217
  19.4 2.3 %collective-permute-start.8 = (bf16[400,896]{1,0:T(8,128)(2,1)S(1)}, bf16[400,896]{1,0:T(8,128)(2,1)S(1)}, u32[]{:S(2)}, u32[]{:S(2)}) collective-permute-start(bf16[400,896]{1,0:T(8,128)(2,1)S(1)} %get-tuple-element.71), channel_id=1, source_target_pairs={{0,4},{1,5},{2,6},{3,7},{4,0},{5,1},{6,2},{7,3},{8,12},{9,13},{10,... | collective-permute-start | bytes 2150408 | tf_op jit(solution)/shard_map/ppermute | solution.py:36
  21.6 2.6 %collective-permute-done.ringed = bf16[128,896]{1,0:T(8,128)(2,1)S(1)} collective-permute-done((bf16[128,896]{1,0:T(8,128)(2,1)S(1)}, bf16[128,896]{1,0:T(8,128)(2,1)S(1)}, u32[]{:S(2)}, u32[]{:S(2)}) %collective-permute-start) | collective-permute-done | bytes 229408 | tf_op jit(solution)/shard_map/ppermute | solution.py:36
  26.4 2.4 %half.5 = (f32[3,128,896]{2,1,0:T(8,128)S(1)}, f32[128,1]{1,0:T(8,128)S(1)}) custom-call(s32[3]{0:T(128)S(1)} %pad_add_fusion.place, bf16[128,896]{1,0:T(8,128)(2,1)S(1)} %collective-permute-done.2.crossed, bf16[128,896]{1,0:T(8,128)(2,1)S(1)} %collective-permute-done.1.ringed, bf16[128,896]{1,0:T(8,128)(2,1)S(1)} %collective-permute-done.3.sib_crossed, ...), custom_call_target="tpu_custom_call" | custom-call | flops 1150000 | bytes 1000 | tf_op jit(solution)/shard_map/half/pallas_call | solution.py:217
  32.1 3.8 %half.7 = (bf16[400,896]{1,0:T(8,128)(2,1)}, f32[128,1]{1,0:T(8,128)}) custom-call(s32[3]{0:T(128)S(1)} %pad_add_fusion.place, bf16[128,896]{1,0:T(8,128)(2,1)S(1)} %broadcast_select_fusion.crossed, bf16[128,896]{1,0:T(8,128)(2,1)S(1)} %collective-permute-done.ringed, bf16[128,896]{1,0:T(8,128)(2,1)S(1)} %collective-permute-done.6.sib_crossed, ...), custom_call_target="tpu_custom_call" | custom-call | flops 1150000 | bytes 1000 | tf_op jit(solution)/shard_map/half/pallas_call | solution.py:217
  35.9 3.5 %collective-permute-start.9 = (bf16[400,896]{1,0:T(8,128)(2,1)}, bf16[400,896]{1,0:T(8,128)(2,1)}, u32[]{:S(2)}, u32[]{:S(2)}) collective-permute-start(bf16[400,896]{1,0:T(8,128)(2,1)} %get-tuple-element.78), channel_id=1, source_target_pairs={{0,4},{1,5},{2,6},{3,7},{4,0},{5,1},{6,2},{7,3},{8,12},{9,13},{10,... | collective-permute-start | bytes 2150408 | tf_op jit(solution)/shard_map/ppermute | solution.py:36
  40.3 4.2 %collective-permute-start.10 = (bf16[128,896]{1,0:T(8,128)(2,1)S(1)}, bf16[128,896]{1,0:T(8,128)(2,1)}, u32[]{:S(2)}, u32[]{:S(2)}) collective-permute-start(bf16[128,896]{1,0:T(8,128)(2,1)S(1)} %get-tuple-element.72.refs_0_), channel_id=1, source_target_pairs={{0,8},{1,9},{2,12},{3,13},{4,10},{5,11},{6,14},{7,15},{8,16},{9,17... | collective-permute-start | bytes 688136 | tf_op jit(solution)/shard_map/ppermute | solution.py:36
  44.5 2.6 %half.6 = (f32[3,128,896]{2,1,0:T(8,128)S(1)}, f32[128,1]{1,0:T(8,128)S(1)}) custom-call(s32[3]{0:T(128)S(1)} %pad_add_fusion.place, bf16[128,896]{1,0:T(8,128)(2,1)S(1)} %copy-done.3, bf16[128,896]{1,0:T(8,128)(2,1)S(1)} %copy-done.5, bf16[128,896]{1,0:T(8,128)(2,1)S(1)} %copy-done.9, bf16[128,896]{1,0:T(8,128)(2,1)S(1)} %copy-done.7, ...), custom_call_target="tpu_custom_call" | custom-call | flops 1150000 | bytes 1000 | tf_op jit(solution)/shard_map/half/pallas_call | solution.py:217
  51.0 2.8 %early.2 = (f32[3,128,896]{2,1,0:T(8,128)S(1)}, f32[128,1]{1,0:T(8,128)S(1)}) custom-call(s32[3]{0:T(128)S(1)} %copy-done.13, bf16[128,896]{1,0:T(8,128)(2,1)} %collective-permute-done.10.mine, bf16[128,896]{1,0:T(8,128)(2,1)S(1)} %collective-permute-done.11.theirs, bf16[1,3584]{1,0:T(2,128)(2,1)S(1)} %copy-done.11, bf16[1,3,1792,896]{3,2,1,0:T(8,128)(2,1)S(1)} %stage.1.weight), custom_call_target="tpu_custom_call" | custom-call | flops 1150000 | bytes 1000 | tf_op jit(solution)/shard_map/early/pallas_call | solution.py:247
  53.8 2.2 %collective-permute-done.9.received = bf16[400,896]{1,0:T(8,128)(2,1)} collective-permute-done((bf16[400,896]{1,0:T(8,128)(2,1)}, bf16[400,896]{1,0:T(8,128)(2,1)}, u32[]{:S(2)}, u32[]{:S(2)}) %collective-permute-start.9) | collective-permute-done | bytes 716832 | tf_op jit(solution)/shard_map/ppermute | solution.py:36
  56.0 2.1 %attend.3.refs_1_ = bf16[128,896]{1,0:T(8,128)(2,1)S(1)} custom-call(f32[3,128,896]{2,1,0:T(8,128)S(1)} %get-tuple-element.77.kept, bf16[400,896]{1,0:T(8,128)(2,1)} %collective-permute-done.9.received, f32[128,1]{1,0:T(8,128)S(1)} %get-tuple-element.79.kept_mean, bf16[128,896]{1,0:T(8,128)(2,1)S(1)} %get-tuple-element.82.block, ...), custom_call_target="tpu_custom_call" | custom-call | flops 287500009472 | bytes 1000 | tf_op jit(solution)/shard_map/attend/pallas_call | solution.py:432
  58.3 8.5 %collective-permute-start.12 = (bf16[128,896]{1,0:T(8,128)(2,1)S(1)}, bf16[128,896]{1,0:T(8,128)(2,1)S(1)}, u32[]{:S(2)}, u32[]{:S(2)}) collective-permute-start(bf16[128,896]{1,0:T(8,128)(2,1)S(1)} %attend.3.refs_1_), channel_id=1, source_target_pairs={{0,8},{1,9},{2,12},{3,13},{4,10},{5,11},{6,14},{7,15},{8,16},{9,17... | collective-permute-start | bytes 688136 | tf_op jit(solution)/shard_map/ppermute | solution.py:36
  66.9 2.9 %late.2 = (bf16[400,896]{1,0:T(8,128)(2,1)S(1)}, f32[3,128,896]{2,1,0:T(8,128)S(1)}, f32[128,1]{1,0:T(8,128)S(1)}) custom-call(s32[3]{0:T(128)S(1)} %copy-done.14, bf16[128,896]{1,0:T(8,128)(2,1)} %collective-permute-done.13.mine, bf16[128,896]{1,0:T(8,128)(2,1)S(1)} %collective-permute-done.14.theirs, bf16[1,3584]{1,0:T(2,128)(2,1)S(1)} %copy-done.11, ...), custom_call_target="tpu_custom_call" | custom-call | flops 3449999872 | bytes 1000 | tf_op jit(solution)/shard_map/late/pallas_call | solution.py:291
  69.9 2.3 %collective-permute-done.12.mine = bf16[128,896]{1,0:T(8,128)(2,1)S(1)} collective-permute-done((bf16[128,896]{1,0:T(8,128)(2,1)S(1)}, bf16[128,896]{1,0:T(8,128)(2,1)S(1)}, u32[]{:S(2)}, u32[]{:S(2)}) %collective-permute-start.12) | collective-permute-done | bytes 229408 | tf_op jit(solution)/shard_map/ppermute | solution.py:36
  73.3 4.6 %collective-permute-start.20 = (bf16[128,896]{1,0:T(8,128)(2,1)S(1)}, bf16[128,896]{1,0:T(8,128)(2,1)S(1)}, u32[]{:S(2)}, u32[]{:S(2)}) collective-permute-start(bf16[128,896]{1,0:T(8,128)(2,1)S(1)} %copy-done.16), channel_id=1, source_target_pairs={{0,8},{1,9},{2,10},{3,11},{4,12},{5,13},{6,14},{7,15},{8,16},{9,17... | collective-permute-start | bytes 688136 | tf_op jit(solution)/shard_map/ppermute | solution.py:36
  79.2 2.4 %early.3 = (f32[3,128,896]{2,1,0:T(8,128)S(1)}, f32[128,1]{1,0:T(8,128)S(1)}, bf16[128,896]{1,0:T(8,128)(2,1)}, bf16[128,896]{1,0:T(8,128)(2,1)}) custom-call(s32[3]{0:T(128)S(1)} %copy-done.14, bf16[128,896]{1,0:T(8,128)(2,1)S(1)} %collective-permute-done.12.mine, bf16[128,896]{1,0:T(8,128)(2,1)S(1)} %collective-permute-done.17.theirs, ...), custom_call_target="tpu_custom_call" | custom-call | flops 3449999872 | bytes 1000 | tf_op jit(solution)/shard_map/early/pallas_call | solution.py:247
  81.6 3.1 %late.3 = (bf16[400,640]{1,0:T(8,128)(2,1)}, bf16[384,256]{1,0:T(8,128)(2,1)}, f32[3,128,896]{2,1,0:T(8,128)S(1)}, f32[128,1]{1,0:T(8,128)S(1)}) custom-call(s32[3]{0:T(128)S(1)} %copy-done.14, bf16[128,896]{1,0:T(8,128)(2,1)S(1)} %collective-permute-done.15.mine, bf16[128,896]{1,0:T(8,128)(2,1)S(1)} %collective-permute-done.16.theirs, ...), custom_call_target="tpu_custom_call" | custom-call | flops 1150000000 | bytes 1000 | tf_op jit(solution)/shard_map/late/pallas_call | solution.py:291
  87.9 4.2 %collective-permute-start.22 = (bf16[128,896]{1,0:T(8,128)(2,1)}, bf16[128,896]{1,0:T(8,128)(2,1)}, u32[]{:S(2)}, u32[]{:S(2)}) collective-permute-start(bf16[128,896]{1,0:T(8,128)(2,1)} %get-tuple-element.106.own), channel_id=1, source_target_pairs={{0,8},{1,9},{2,10},{3,11},{4,12},{5,13},{6,14},{7,15},{8,16},{9,17... | collective-permute-start | bytes 688136 | tf_op jit(solution)/shard_map/ppermute | solution.py:36
  93.8 5.8 %collective-permute-done.19.received = bf16[400,640]{1,0:T(8,128)(2,1)} collective-permute-done((bf16[400,640]{1,0:T(8,128)(2,1)}, bf16[400,640]{1,0:T(8,128)(2,1)}, u32[]{:S(2)}, u32[]{:S(2)}) %collective-permute-start.19) | collective-permute-done | bytes 512032 | tf_op jit(solution)/shard_map/ppermute | solution.py:36
  103.5 2.5 %final.1 = bf16[256,896]{1,0:T(8,128)(2,1)} custom-call(s32[1]{0:T(128)S(6)} %copy.7.flag, f32[3,128,896]{2,1,0:T(8,128)S(1)} %get-tuple-element.90.kept, bf16[384,256]{1,0:T(8,128)(2,1)} %collective-permute-done.18.received, f32[128,1]{1,0:T(8,128)S(1)} %get-tuple-element.102.scale_kept, ...), custom_call_target="tpu_custom_call", output_to_operand_aliasing={{}: (9, {})} | custom-call | flops 287500009472 | bytes 1000 | tf_op jit(solution)/shard_map/final/pallas_call | solution.py:571
  (78 shorter events, 23.1 us)
Async XLA Ops:
  1.1 12.8 %collective-permute-start.1 = (bf16[128,896]{1,0:T(8,128)(2,1)S(1)}, bf16[128,896]{1,0:T(8,128)(2,1)S(1)}, u32[]{:S(2)}, u32[]{:S(2)}) collective-permute-start(bf16[128,896]{1,0:T(8,128)(2,1)S(1)} %get-tuple-element.107.block), channel_id=1, source_target_pairs={{0,2},{1,3},{2,6},{3,7},{4,0},{5,1},{6,4},{7,5},{8,10},{9,11},{10,... | collective-permute-start | bytes 688136 | tf_op jit(solution)/shard_map/ppermute | solution.py:36
  4.1 9.8 %collective-permute-start.2 = (bf16[128,896]{1,0:T(8,128)(2,1)S(1)}, bf16[128,896]{1,0:T(8,128)(2,1)S(1)}, u32[]{:S(2)}, u32[]{:S(2)}) collective-permute-start(bf16[128,896]{1,0:T(8,128)(2,1)S(1)} %get-tuple-element.107.block), channel_id=1, source_target_pairs={{0,0},{1,1},{2,4},{3,5},{4,2},{5,3},{6,6},{7,7},{8,8},{9,9},{10,12... | collective-permute-start | bytes 688136 | tf_op jit(solution)/shard_map/ppermute | solution.py:36
  9.2 41.2 %copy-start = (bf16[1,3,1792,896]{3,2,1,0:T(8,128)(2,1)}, bf16[1,3,1792,896]{3,2,1,0:T(8,128)(2,1)S(1)}, u32[]{:S(2)}) copy-start(bf16[1,3,1792,896]{3,2,1,0:T(8,128)(2,1)S(1)} %stage.1.weight) | copy-start | bytes 28901380
  13.9 3.0 %collective-permute-start.3 = (bf16[128,896]{1,0:T(8,128)(2,1)S(1)}, bf16[128,896]{1,0:T(8,128)(2,1)S(1)}, u32[]{:S(2)}, u32[]{:S(2)}) collective-permute-start(bf16[128,896]{1,0:T(8,128)(2,1)S(1)} %collective-permute-done.2.crossed), channel_id=1, source_target_pairs={{0,1},{1,0},{2,3},{3,2},{4,5},{5,4},{6,7},{7,6},{8,9},{9,8},{10,11... | collective-permute-start | bytes 688136 | tf_op jit(solution)/shard_map/ppermute | solution.py:36
  13.9 3.0 %collective-permute-start.4 = (bf16[128,896]{1,0:T(8,128)(2,1)S(1)}, bf16[128,896]{1,0:T(8,128)(2,1)S(1)}, u32[]{:S(2)}, u32[]{:S(2)}) collective-permute-start(bf16[128,896]{1,0:T(8,128)(2,1)S(1)} %collective-permute-done.1.ringed), channel_id=1, source_target_pairs={{0,1},{1,0},{2,3},{3,2},{4,5},{5,4},{6,7},{7,6},{8,9},{9,8},{10,11... | collective-permute-start | bytes 688136 | tf_op jit(solution)/shard_map/ppermute | solution.py:36
  14.4 9.8 %collective-permute-start = (bf16[128,896]{1,0:T(8,128)(2,1)S(1)}, bf16[128,896]{1,0:T(8,128)(2,1)S(1)}, u32[]{:S(2)}, u32[]{:S(2)}) collective-permute-start(bf16[128,896]{1,0:T(8,128)(2,1)S(1)} %get-tuple-element.82.block), channel_id=1, source_target_pairs={{0,2},{1,3},{2,6},{3,7},{4,0},{5,1},{6,4},{7,5},{8,10},{9,11},{10,... | collective-permute-start | bytes 688136 | tf_op jit(solution)/shard_map/ppermute | solution.py:36
  19.4 20.0 %collective-permute-start.8 = (bf16[400,896]{1,0:T(8,128)(2,1)S(1)}, bf16[400,896]{1,0:T(8,128)(2,1)S(1)}, u32[]{:S(2)}, u32[]{:S(2)}) collective-permute-start(bf16[400,896]{1,0:T(8,128)(2,1)S(1)} %get-tuple-element.71), channel_id=1, source_target_pairs={{0,4},{1,5},{2,6},{3,7},{4,0},{5,1},{6,2},{7,3},{8,12},{9,13},{10,... | collective-permute-start | bytes 2150408 | tf_op jit(solution)/shard_map/ppermute | solution.py:36
  24.2 6.2 %collective-permute-start.5 = (bf16[128,896]{1,0:T(8,128)(2,1)S(1)}, bf16[128,896]{1,0:T(8,128)(2,1)S(1)}, u32[]{:S(2)}, u32[]{:S(2)}) collective-permute-start(bf16[128,896]{1,0:T(8,128)(2,1)S(1)} %collective-permute-done.ringed), channel_id=1, source_target_pairs={{0,2},{1,3},{6,4},{7,5},{8,10},{9,11},{14,12},{15,13},{16,18},{17,... | collective-permute-start | bytes 688136 | tf_op jit(solution)/shard_map/ppermute | solution.py:36
  26.3 4.3 %collective-permute-start.7 = (bf16[128,896]{1,0:T(8,128)(2,1)S(1)}, bf16[128,896]{1,0:T(8,128)(2,1)S(1)}, u32[]{:S(2)}, u32[]{:S(2)}) collective-permute-start(bf16[128,896]{1,0:T(8,128)(2,1)S(1)} %collective-permute-done.ringed), channel_id=1, source_target_pairs={{0,1},{1,0},{2,3},{3,2},{4,5},{5,4},{6,7},{7,6},{8,9},{9,8},{10,11... | collective-permute-start | bytes 688136 | tf_op jit(solution)/shard_map/ppermute | solution.py:36
  30.5 1.6 %collective-permute-start.6 = (bf16[128,896]{1,0:T(8,128)(2,1)S(1)}, bf16[128,896]{1,0:T(8,128)(2,1)S(1)}, u32[]{:S(2)}, u32[]{:S(2)}) collective-permute-start(bf16[128,896]{1,0:T(8,128)(2,1)S(1)} %broadcast_select_fusion.crossed), channel_id=1, source_target_pairs={{0,1},{1,0},{2,3},{3,2},{4,5},{5,4},{6,7},{7,6},{8,9},{9,8},{10,11... | collective-permute-start | bytes 688136 | tf_op jit(solution)/shard_map/ppermute | solution.py:36
  35.9 20.1 %collective-permute-start.9 = (bf16[400,896]{1,0:T(8,128)(2,1)}, bf16[400,896]{1,0:T(8,128)(2,1)}, u32[]{:S(2)}, u32[]{:S(2)}) collective-permute-start(bf16[400,896]{1,0:T(8,128)(2,1)} %get-tuple-element.78), channel_id=1, source_target_pairs={{0,4},{1,5},{2,6},{3,7},{4,0},{5,1},{6,2},{7,3},{8,12},{9,13},{10,... | collective-permute-start | bytes 2150408 | tf_op jit(solution)/shard_map/ppermute | solution.py:36
  40.3 8.4 %collective-permute-start.10 = (bf16[128,896]{1,0:T(8,128)(2,1)S(1)}, bf16[128,896]{1,0:T(8,128)(2,1)}, u32[]{:S(2)}, u32[]{:S(2)}) collective-permute-start(bf16[128,896]{1,0:T(8,128)(2,1)S(1)} %get-tuple-element.72.refs_0_), channel_id=1, source_target_pairs={{0,8},{1,9},{2,12},{3,13},{4,10},{5,11},{6,14},{7,15},{8,16},{9,17... | collective-permute-start | bytes 688136 | tf_op jit(solution)/shard_map/ppermute | solution.py:36
  48.6 1.7 %collective-permute-start.11 = (bf16[128,896]{1,0:T(8,128)(2,1)}, bf16[128,896]{1,0:T(8,128)(2,1)S(1)}, u32[]{:S(2)}, u32[]{:S(2)}) collective-permute-start(bf16[128,896]{1,0:T(8,128)(2,1)} %collective-permute-done.10.mine), channel_id=1, source_target_pairs={{0,1},{1,0},{2,3},{3,2},{4,5},{5,4},{6,7},{7,6},{8,9},{9,8},{10,11... | collective-permute-start | bytes 688136 | tf_op jit(solution)/shard_map/ppermute | solution.py:36
  48.6 9.5 %collective-permute-start.13 = (bf16[128,896]{1,0:T(8,128)(2,1)}, bf16[128,896]{1,0:T(8,128)(2,1)}, u32[]{:S(2)}, u32[]{:S(2)}) collective-permute-start(bf16[128,896]{1,0:T(8,128)(2,1)} %collective-permute-done.10.mine), channel_id=1, source_target_pairs={{0,2},{1,3},{2,0},{3,1},{4,6},{5,7},{6,4},{7,5},{8,10},{9,11},{10,... | collective-permute-start | bytes 688136 | tf_op jit(solution)/shard_map/ppermute | solution.py:36
  58.2 8.6 %collective-permute-start.14 = (bf16[128,896]{1,0:T(8,128)(2,1)}, bf16[128,896]{1,0:T(8,128)(2,1)S(1)}, u32[]{:S(2)}, u32[]{:S(2)}) collective-permute-start(bf16[128,896]{1,0:T(8,128)(2,1)} %collective-permute-done.13.mine), channel_id=1, source_target_pairs={{0,1},{1,0},{2,3},{3,2},{4,5},{5,4},{6,7},{7,6},{8,9},{9,8},{10,11... | collective-permute-start | bytes 688136 | tf_op jit(solution)/shard_map/ppermute | solution.py:36
  58.3 13.9 %collective-permute-start.12 = (bf16[128,896]{1,0:T(8,128)(2,1)S(1)}, bf16[128,896]{1,0:T(8,128)(2,1)S(1)}, u32[]{:S(2)}, u32[]{:S(2)}) collective-permute-start(bf16[128,896]{1,0:T(8,128)(2,1)S(1)} %attend.3.refs_1_), channel_id=1, source_target_pairs={{0,8},{1,9},{2,12},{3,13},{4,10},{5,11},{6,14},{7,15},{8,16},{9,17... | collective-permute-start | bytes 688136 | tf_op jit(solution)/shard_map/ppermute | solution.py:36
  69.8 18.1 %collective-permute-start.21 = (bf16[400,896]{1,0:T(8,128)(2,1)S(1)}, bf16[400,896]{1,0:T(8,128)(2,1)S(1)}, u32[]{:S(2)}, u32[]{:S(2)}) collective-permute-start(bf16[400,896]{1,0:T(8,128)(2,1)S(1)} %get-tuple-element.94), channel_id=1, source_target_pairs={{0,4},{1,5},{2,6},{3,7},{4,0},{5,1},{6,2},{7,3},{8,12},{9,13},{10,... | collective-permute-start | bytes 2150408 | tf_op jit(solution)/shard_map/ppermute | solution.py:36
  72.2 7.1 %collective-permute-start.15 = (bf16[128,896]{1,0:T(8,128)(2,1)S(1)}, bf16[128,896]{1,0:T(8,128)(2,1)S(1)}, u32[]{:S(2)}, u32[]{:S(2)}) collective-permute-start(bf16[128,896]{1,0:T(8,128)(2,1)S(1)} %collective-permute-done.12.mine), channel_id=1, source_target_pairs={{0,2},{1,3},{2,0},{3,1},{4,6},{5,7},{6,4},{7,5},{8,10},{9,11},{10,... | collective-permute-start | bytes 688136 | tf_op jit(solution)/shard_map/ppermute | solution.py:36
  72.6 6.6 %collective-permute-start.17 = (bf16[128,896]{1,0:T(8,128)(2,1)S(1)}, bf16[128,896]{1,0:T(8,128)(2,1)S(1)}, u32[]{:S(2)}, u32[]{:S(2)}) collective-permute-start(bf16[128,896]{1,0:T(8,128)(2,1)S(1)} %collective-permute-done.12.mine), channel_id=1, source_target_pairs={{0,1},{1,0},{2,3},{3,2},{4,5},{5,4},{6,7},{7,6},{8,9},{9,8},{10,11... | collective-permute-start | bytes 688136 | tf_op jit(solution)/shard_map/ppermute | solution.py:36
  73.3 13.6 %collective-permute-start.20 = (bf16[128,896]{1,0:T(8,128)(2,1)S(1)}, bf16[128,896]{1,0:T(8,128)(2,1)S(1)}, u32[]{:S(2)}, u32[]{:S(2)}) collective-permute-start(bf16[128,896]{1,0:T(8,128)(2,1)S(1)} %copy-done.16), channel_id=1, source_target_pairs={{0,8},{1,9},{2,10},{3,11},{4,12},{5,13},{6,14},{7,15},{8,16},{9,17... | collective-permute-start | bytes 688136 | tf_op jit(solution)/shard_map/ppermute | solution.py:36
  79.2 2.4 %collective-permute-start.16 = (bf16[128,896]{1,0:T(8,128)(2,1)S(1)}, bf16[128,896]{1,0:T(8,128)(2,1)S(1)}, u32[]{:S(2)}, u32[]{:S(2)}) collective-permute-start(bf16[128,896]{1,0:T(8,128)(2,1)S(1)} %collective-permute-done.15.mine), channel_id=1, source_target_pairs={{0,1},{1,0},{2,3},{3,2},{4,5},{5,4},{6,7},{7,6},{8,9},{9,8},{10,11... | collective-permute-start | bytes 688136 | tf_op jit(solution)/shard_map/ppermute | solution.py:36
  84.8 14.8 %collective-permute-start.19 = (bf16[400,640]{1,0:T(8,128)(2,1)}, bf16[400,640]{1,0:T(8,128)(2,1)}, u32[]{:S(2)}, u32[]{:S(2)}) collective-permute-start(bf16[400,640]{1,0:T(8,128)(2,1)} %get-tuple-element.92), channel_id=1, source_target_pairs={{0,4},{1,5},{2,6},{3,7},{4,0},{5,1},{6,2},{7,3},{8,12},{9,13},{10,... | collective-permute-start | bytes 1536008 | tf_op jit(solution)/shard_map/ppermute | solution.py:36
  84.9 18.6 %collective-permute-start.18 = (bf16[384,256]{1,0:T(8,128)(2,1)}, bf16[384,256]{1,0:T(8,128)(2,1)}, u32[]{:S(2)}, u32[]{:S(2)}) collective-permute-start(bf16[384,256]{1,0:T(8,128)(2,1)} %get-tuple-element.91), channel_id=1, source_target_pairs={{0,4},{1,5},{2,6},{3,7},{4,0},{5,1},{6,2},{7,3},{8,12},{9,13},{10,... | collective-permute-start | bytes 589832 | tf_op jit(solution)/shard_map/ppermute | solution.py:36
  87.9 15.6 %collective-permute-start.22 = (bf16[128,896]{1,0:T(8,128)(2,1)}, bf16[128,896]{1,0:T(8,128)(2,1)}, u32[]{:S(2)}, u32[]{:S(2)}) collective-permute-start(bf16[128,896]{1,0:T(8,128)(2,1)} %get-tuple-element.106.own), channel_id=1, source_target_pairs={{0,8},{1,9},{2,10},{3,11},{4,12},{5,13},{6,14},{7,15},{8,16},{9,17... | collective-permute-start | bytes 688136 | tf_op jit(solution)/shard_map/ppermute | solution.py:36
  (18 other events, 147.0 us)

commit v18 on v16

--- a/solution.py
+++ b/solution.py
@@ -547,8 +547,7 @@
             1,
         )
         received = send(sents)
-        before = permute(first, sections, onward(direct))
-        before, arrived, _ = lax.optimization_barrier((before, arrived, kept_mean))
+        arrived, _ = lax.optimization_barrier((arrived, kept_mean))
         mixture, pairs = call_attend(
             hold_kernel,
             "hold",
@@ -556,7 +555,8 @@
             [upper[0], arrived, upper[1]],
             [pltpu.VMEM((above, width), F32), pairs_of],
         )
-        own_last, _ = lax.optimization_barrier((own_last, arrived))
+        own, own_last, _ = lax.optimization_barrier((own, own_last, arrived))
+        before = permute(own, sections, onward(direct))
         before_last = permute(own_last, sections, onward(direct))
         def finish(kernel, name, arrays, rows, into):
             whole = [] if into is None else [into]

time: 106 us -> 106 us (level)
  Pallas kernels: 35.3 us -> 36.4 us
  starting transfers between devices: 40.1 us -> 39 us
    ppermute x23, starting transfers between devices: 40.1 us -> 39 us  [permute(): return lax.ppermute(array, AXES, pairs)]
  transfers between devices with their start and end apart: 23 -> 23, of which waited for: 13 -> 14; matrix products, arithmetic and copies ran while one was open for 0% -> 0% of each run, Pallas kernels for 31% -> 32%
where the time goes in v18:
time: 106 us
  starting transfers between devices  39 us (37%)
  Pallas kernels  36.4 us (34%)
  waiting for transfers between devices  27.1 us (26%)
  local copies, waits for them, and re-layouts  1.82 us (2%)
  between operations  1.17 us (1%)
    ppermute x23, starting transfers between devices, permute(): return lax.ppermute(array, AXES, pairs)  39 us
    ppermute x23, waiting for transfers between devices, permute(): return lax.ppermute(array, AXES, pairs)  27.1 us
    pallas_call x4, Pallas kernels, half(): pl.pallas_call(functools.partial(half_kernel, own), in_specs=[smem_spec()...  10.8 us
    pallas_call x2, Pallas kernels, late(): pl.pallas_call(functools.partial(late_kernel, cuts, apart), in_specs=[sme...  6.06 us
    pallas_call x4, Pallas kernels, call_attend(): pl.pallas_call(kernel, in_specs=[smem_spec() for _ in scalars] + [vmem_sp...  5.69 us
    pallas_call x2, Pallas kernels, early(): pl.pallas_call(functools.partial(early_kernel, len(owns)), in_specs=[smem...  5.23 us
    pallas_call x1, Pallas kernels, stage(): pl.pallas_call(stage_kernel, in_specs=[smem_spec(), any_spec()], out_spec...  4.29 us
    pallas_call x2, Pallas kernels, finish(): pl.pallas_call(kernel, in_specs=[smem_spec()] + [vmem_spec() for _ in arr...  4.26 us
  transfers between devices with their start and end apart: 23, of which 14 were waited for; matrix products, arithmetic and copies ran while one was open for 0% of the time, Pallas kernels for 32%

profile of v18, /device:TPU:0, one launch (start us, length us, event | category | flops | bytes accessed | tf_op | source)
XLA Modules:
  0.0 105.6 jit_solution(15080403560063655219)
XLA Ops:
  1.1 3.0 %collective-permute-start.1 = (bf16[128,896]{1,0:T(8,128)(2,1)S(1)}, bf16[128,896]{1,0:T(8,128)(2,1)S(1)}, u32[]{:S(2)}, u32[]{:S(2)}) collective-permute-start(bf16[128,896]{1,0:T(8,128)(2,1)S(1)} %get-tuple-element.107.block), channel_id=1, source_target_pairs={{0,2},{1,3},{2,6},{3,7},{4,0},{5,1},{6,4},{7,5},{8,10},{9,11},{10,... | collective-permute-start | bytes 688136 | tf_op jit(solution)/shard_map/ppermute | solution.py:36
  4.9 4.3 %stage.1.weight = bf16[1,3,1792,896]{3,2,1,0:T(8,128)(2,1)S(1)} custom-call(s32[3]{0:T(128)S(1)} %pad_add_fusion.place, bf16[1,3,1792,896]{3,2,1,0:T(8,128)(2,1)} %weight), custom_call_target="tpu_custom_call" | custom-call | flops 4600000000 | bytes 1000 | tf_op jit(solution)/shard_map/stage/pallas_call | solution.py:98
  9.2 4.7 %collective-permute-done.1.ringed = bf16[128,896]{1,0:T(8,128)(2,1)S(1)} collective-permute-done((bf16[128,896]{1,0:T(8,128)(2,1)S(1)}, bf16[128,896]{1,0:T(8,128)(2,1)S(1)}, u32[]{:S(2)}, u32[]{:S(2)}) %collective-permute-start.1) | collective-permute-done | bytes 229408 | tf_op jit(solution)/shard_map/ppermute | solution.py:36
  14.4 2.4 %collective-permute-start = (bf16[128,896]{1,0:T(8,128)(2,1)S(1)}, bf16[128,896]{1,0:T(8,128)(2,1)S(1)}, u32[]{:S(2)}, u32[]{:S(2)}) collective-permute-start(bf16[128,896]{1,0:T(8,128)(2,1)S(1)} %get-tuple-element.82.block), channel_id=1, source_target_pairs={{0,2},{1,3},{2,6},{3,7},{4,0},{5,1},{6,4},{7,5},{8,10},{9,11},{10,... | collective-permute-start | bytes 688136 | tf_op jit(solution)/shard_map/ppermute | solution.py:36
  16.9 2.5 %half.4 = (bf16[400,896]{1,0:T(8,128)(2,1)S(1)}, f32[128,1]{1,0:T(8,128)}) custom-call(s32[3]{0:T(128)S(1)} %pad_add_fusion.place, bf16[128,896]{1,0:T(8,128)(2,1)S(1)} %collective-permute-done.2.crossed, bf16[128,896]{1,0:T(8,128)(2,1)S(1)} %collective-permute-done.1.ringed, bf16[128,896]{1,0:T(8,128)(2,1)S(1)} %collective-permute-done.3.sib_crossed, ...), custom_call_target="tpu_custom_call" | custom-call | flops 3449999872 | bytes 1000 | tf_op jit(solution)/shard_map/half/pallas_call | solution.py:211
  19.4 2.3 %collective-permute-start.8 = (bf16[400,896]{1,0:T(8,128)(2,1)S(1)}, bf16[400,896]{1,0:T(8,128)(2,1)S(1)}, u32[]{:S(2)}, u32[]{:S(2)}) collective-permute-start(bf16[400,896]{1,0:T(8,128)(2,1)S(1)} %get-tuple-element.71), channel_id=1, source_target_pairs={{0,4},{1,5},{2,6},{3,7},{4,0},{5,1},{6,2},{7,3},{8,12},{9,13},{10,... | collective-permute-start | bytes 2150408 | tf_op jit(solution)/shard_map/ppermute | solution.py:36
  21.6 2.6 %collective-permute-done.ringed = bf16[128,896]{1,0:T(8,128)(2,1)S(1)} collective-permute-done((bf16[128,896]{1,0:T(8,128)(2,1)S(1)}, bf16[128,896]{1,0:T(8,128)(2,1)S(1)}, u32[]{:S(2)}, u32[]{:S(2)}) %collective-permute-start) | collective-permute-done | bytes 229408 | tf_op jit(solution)/shard_map/ppermute | solution.py:36
  26.4 2.4 %half.5 = (f32[3,128,896]{2,1,0:T(8,128)S(1)}, f32[128,1]{1,0:T(8,128)S(1)}) custom-call(s32[3]{0:T(128)S(1)} %pad_add_fusion.place, bf16[128,896]{1,0:T(8,128)(2,1)S(1)} %collective-permute-done.2.crossed, bf16[128,896]{1,0:T(8,128)(2,1)S(1)} %collective-permute-done.1.ringed, bf16[128,896]{1,0:T(8,128)(2,1)S(1)} %collective-permute-done.3.sib_crossed, ...), custom_call_target="tpu_custom_call" | custom-call | flops 1150000 | bytes 1000 | tf_op jit(solution)/shard_map/half/pallas_call | solution.py:211
  32.1 3.3 %half.7 = (bf16[400,896]{1,0:T(8,128)(2,1)}, f32[128,1]{1,0:T(8,128)}) custom-call(s32[3]{0:T(128)S(1)} %pad_add_fusion.place, bf16[128,896]{1,0:T(8,128)(2,1)S(1)} %broadcast_select_fusion.crossed, bf16[128,896]{1,0:T(8,128)(2,1)S(1)} %collective-permute-done.ringed, bf16[128,896]{1,0:T(8,128)(2,1)S(1)} %collective-permute-done.6.sib_crossed, ...), custom_call_target="tpu_custom_call" | custom-call | flops 1150000 | bytes 1000 | tf_op jit(solution)/shard_map/half/pallas_call | solution.py:211
  35.4 3.5 %collective-permute-start.9 = (bf16[400,896]{1,0:T(8,128)(2,1)}, bf16[400,896]{1,0:T(8,128)(2,1)}, u32[]{:S(2)}, u32[]{:S(2)}) collective-permute-start(bf16[400,896]{1,0:T(8,128)(2,1)} %get-tuple-element.78), channel_id=1, source_target_pairs={{0,4},{1,5},{2,6},{3,7},{4,0},{5,1},{6,2},{7,3},{8,12},{9,13},{10,... | collective-permute-start | bytes 2150408 | tf_op jit(solution)/shard_map/ppermute | solution.py:36
  39.8 4.2 %collective-permute-start.10 = (bf16[128,896]{1,0:T(8,128)(2,1)S(1)}, bf16[128,896]{1,0:T(8,128)(2,1)}, u32[]{:S(2)}, u32[]{:S(2)}) collective-permute-start(bf16[128,896]{1,0:T(8,128)(2,1)S(1)} %get-tuple-element.72.refs_0_), channel_id=1, source_target_pairs={{0,8},{1,9},{2,12},{3,13},{4,10},{5,11},{6,14},{7,15},{8,16},{9,17... | collective-permute-start | bytes 688136 | tf_op jit(solution)/shard_map/ppermute | solution.py:36
  44.1 2.6 %half.6 = (f32[3,128,896]{2,1,0:T(8,128)S(1)}, f32[128,1]{1,0:T(8,128)S(1)}) custom-call(s32[3]{0:T(128)S(1)} %pad_add_fusion.place, bf16[128,896]{1,0:T(8,128)(2,1)S(1)} %copy-done.3, bf16[128,896]{1,0:T(8,128)(2,1)S(1)} %copy-done.5, bf16[128,896]{1,0:T(8,128)(2,1)S(1)} %copy-done.9, bf16[128,896]{1,0:T(8,128)(2,1)S(1)} %copy-done.7, ...), custom_call_target="tpu_custom_call" | custom-call | flops 1150000 | bytes 1000 | tf_op jit(solution)/shard_map/half/pallas_call | solution.py:211
  50.5 2.8 %early.2 = (f32[3,128,896]{2,1,0:T(8,128)S(1)}, f32[128,1]{1,0:T(8,128)S(1)}) custom-call(s32[3]{0:T(128)S(1)} %copy-done.13, bf16[128,896]{1,0:T(8,128)(2,1)} %collective-permute-done.10.mine, bf16[128,896]{1,0:T(8,128)(2,1)S(1)} %collective-permute-done.11.theirs, bf16[1,3584]{1,0:T(2,128)(2,1)S(1)} %copy-done.11, bf16[1,3,1792,896]{3,2,1,0:T(8,128)(2,1)S(1)} %stage.1.weight), custom_call_target="tpu_custom_call" | custom-call | flops 1150000 | bytes 1000 | tf_op jit(solution)/shard_map/early/pallas_call | solution.py:239
  53.3 2.2 %collective-permute-done.9.received = bf16[400,896]{1,0:T(8,128)(2,1)} collective-permute-done((bf16[400,896]{1,0:T(8,128)(2,1)}, bf16[400,896]{1,0:T(8,128)(2,1)}, u32[]{:S(2)}, u32[]{:S(2)}) %collective-permute-start.9) | collective-permute-done | bytes 716832 | tf_op jit(solution)/shard_map/ppermute | solution.py:36
  55.5 2.2 %attend.3.refs_1_ = bf16[128,896]{1,0:T(8,128)(2,1)S(1)} custom-call(f32[3,128,896]{2,1,0:T(8,128)S(1)} %get-tuple-element.77.kept, bf16[400,896]{1,0:T(8,128)(2,1)} %collective-permute-done.9.received, f32[128,1]{1,0:T(8,128)S(1)} %get-tuple-element.79.kept_mean, bf16[128,896]{1,0:T(8,128)(2,1)S(1)} %get-tuple-element.82.block, ...), custom_call_target="tpu_custom_call" | custom-call | flops 287500009472 | bytes 1000 | tf_op jit(solution)/shard_map/attend/pallas_call | solution.py:424
  57.8 8.5 %collective-permute-start.12 = (bf16[128,896]{1,0:T(8,128)(2,1)S(1)}, bf16[128,896]{1,0:T(8,128)(2,1)S(1)}, u32[]{:S(2)}, u32[]{:S(2)}) collective-permute-start(bf16[128,896]{1,0:T(8,128)(2,1)S(1)} %attend.3.refs_1_), channel_id=1, source_target_pairs={{0,8},{1,9},{2,12},{3,13},{4,10},{5,11},{6,14},{7,15},{8,16},{9,17... | collective-permute-start | bytes 688136 | tf_op jit(solution)/shard_map/ppermute | solution.py:36
  66.4 2.9 %late.2 = (bf16[400,896]{1,0:T(8,128)(2,1)S(1)}, f32[3,128,896]{2,1,0:T(8,128)S(1)}, f32[128,1]{1,0:T(8,128)S(1)}) custom-call(s32[3]{0:T(128)S(1)} %copy-done.14, bf16[128,896]{1,0:T(8,128)(2,1)} %collective-permute-done.13.mine, bf16[128,896]{1,0:T(8,128)(2,1)S(1)} %collective-permute-done.14.theirs, bf16[1,3584]{1,0:T(2,128)(2,1)S(1)} %copy-done.11, ...), custom_call_target="tpu_custom_call" | custom-call | flops 3449999872 | bytes 1000 | tf_op jit(solution)/shard_map/late/pallas_call | solution.py:283
  69.4 2.3 %collective-permute-done.12.mine = bf16[128,896]{1,0:T(8,128)(2,1)S(1)} collective-permute-done((bf16[128,896]{1,0:T(8,128)(2,1)S(1)}, bf16[128,896]{1,0:T(8,128)(2,1)S(1)}, u32[]{:S(2)}, u32[]{:S(2)}) %collective-permute-start.12) | collective-permute-done | bytes 229408 | tf_op jit(solution)/shard_map/ppermute | solution.py:36
  72.8 6.0 %collective-permute-done.15.mine = bf16[128,896]{1,0:T(8,128)(2,1)S(1)} collective-permute-done((bf16[128,896]{1,0:T(8,128)(2,1)S(1)}, bf16[128,896]{1,0:T(8,128)(2,1)S(1)}, u32[]{:S(2)}, u32[]{:S(2)}) %collective-permute-start.15) | collective-permute-done | bytes 229408 | tf_op jit(solution)/shard_map/ppermute | solution.py:36
  78.7 2.4 %early.3 = (f32[3,128,896]{2,1,0:T(8,128)S(1)}, f32[128,1]{1,0:T(8,128)S(1)}, bf16[128,896]{1,0:T(8,128)(2,1)}, bf16[128,896]{1,0:T(8,128)(2,1)}) custom-call(s32[3]{0:T(128)S(1)} %copy-done.14, bf16[128,896]{1,0:T(8,128)(2,1)S(1)} %collective-permute-done.12.mine, bf16[128,896]{1,0:T(8,128)(2,1)S(1)} %collective-permute-done.17.theirs, ...), custom_call_target="tpu_custom_call" | custom-call | flops 3449999872 | bytes 1000 | tf_op jit(solution)/shard_map/early/pallas_call | solution.py:239
  81.2 3.1 %late.3 = (bf16[400,640]{1,0:T(8,128)(2,1)}, bf16[384,256]{1,0:T(8,128)(2,1)}, f32[3,128,896]{2,1,0:T(8,128)S(1)}, f32[128,1]{1,0:T(8,128)S(1)}) custom-call(s32[3]{0:T(128)S(1)} %copy-done.14, bf16[128,896]{1,0:T(8,128)(2,1)S(1)} %collective-permute-done.15.mine, bf16[128,896]{1,0:T(8,128)(2,1)S(1)} %collective-permute-done.16.theirs, ...), custom_call_target="tpu_custom_call" | custom-call | flops 1150000000 | bytes 1000 | tf_op jit(solution)/shard_map/late/pallas_call | solution.py:283
  87.4 4.2 %collective-permute-start.21 = (bf16[128,896]{1,0:T(8,128)(2,1)}, bf16[128,896]{1,0:T(8,128)(2,1)}, u32[]{:S(2)}, u32[]{:S(2)}) collective-permute-start(bf16[128,896]{1,0:T(8,128)(2,1)} %get-tuple-element.100.own), channel_id=1, source_target_pairs={{0,8},{1,9},{2,10},{3,11},{4,12},{5,13},{6,14},{7,15},{8,16},{9,17... | collective-permute-start | bytes 688136 | tf_op jit(solution)/shard_map/ppermute | solution.py:36
  92.4 3.5 %collective-permute-start.22 = (bf16[128,896]{1,0:T(8,128)(2,1)}, bf16[128,896]{1,0:T(8,128)(2,1)}, u32[]{:S(2)}, u32[]{:S(2)}) collective-permute-start(bf16[128,896]{1,0:T(8,128)(2,1)} %get-tuple-element.106.own), channel_id=1, source_target_pairs={{0,8},{1,9},{2,10},{3,11},{4,12},{5,13},{6,14},{7,15},{8,16},{9,17... | collective-permute-start | bytes 688136 | tf_op jit(solution)/shard_map/ppermute | solution.py:36
  103.0 2.5 %final.1 = bf16[256,896]{1,0:T(8,128)(2,1)} custom-call(s32[1]{0:T(128)S(6)} %copy.7.flag, f32[3,128,896]{2,1,0:T(8,128)S(1)} %get-tuple-element.90.kept, bf16[384,256]{1,0:T(8,128)(2,1)} %collective-permute-done.18.received, f32[128,1]{1,0:T(8,128)S(1)} %get-tuple-element.103.scale_kept, ...), custom_call_target="tpu_custom_call", output_to_operand_aliasing={{}: (9, {})} | custom-call | flops 287500009472 | bytes 1000 | tf_op jit(solution)/shard_map/final/pallas_call | solution.py:563
  (76 shorter events, 24.0 us)
Async XLA Ops:
  1.1 12.8 %collective-permute-start.1 = (bf16[128,896]{1,0:T(8,128)(2,1)S(1)}, bf16[128,896]{1,0:T(8,128)(2,1)S(1)}, u32[]{:S(2)}, u32[]{:S(2)}) collective-permute-start(bf16[128,896]{1,0:T(8,128)(2,1)S(1)} %get-tuple-element.107.block), channel_id=1, source_target_pairs={{0,2},{1,3},{2,6},{3,7},{4,0},{5,1},{6,4},{7,5},{8,10},{9,11},{10,... | collective-permute-start | bytes 688136 | tf_op jit(solution)/shard_map/ppermute | solution.py:36
  4.1 9.8 %collective-permute-start.2 = (bf16[128,896]{1,0:T(8,128)(2,1)S(1)}, bf16[128,896]{1,0:T(8,128)(2,1)S(1)}, u32[]{:S(2)}, u32[]{:S(2)}) collective-permute-start(bf16[128,896]{1,0:T(8,128)(2,1)S(1)} %get-tuple-element.107.block), channel_id=1, source_target_pairs={{0,0},{1,1},{2,4},{3,5},{4,2},{5,3},{6,6},{7,7},{8,8},{9,9},{10,12... | collective-permute-start | bytes 688136 | tf_op jit(solution)/shard_map/ppermute | solution.py:36
  9.2 40.6 %copy-start = (bf16[1,3,1792,896]{3,2,1,0:T(8,128)(2,1)}, bf16[1,3,1792,896]{3,2,1,0:T(8,128)(2,1)S(1)}, u32[]{:S(2)}) copy-start(bf16[1,3,1792,896]{3,2,1,0:T(8,128)(2,1)S(1)} %stage.1.weight) | copy-start | bytes 28901380
  13.9 3.0 %collective-permute-start.3 = (bf16[128,896]{1,0:T(8,128)(2,1)S(1)}, bf16[128,896]{1,0:T(8,128)(2,1)S(1)}, u32[]{:S(2)}, u32[]{:S(2)}) collective-permute-start(bf16[128,896]{1,0:T(8,128)(2,1)S(1)} %collective-permute-done.2.crossed), channel_id=1, source_target_pairs={{0,1},{1,0},{2,3},{3,2},{4,5},{5,4},{6,7},{7,6},{8,9},{9,8},{10,11... | collective-permute-start | bytes 688136 | tf_op jit(solution)/shard_map/ppermute | solution.py:36
  13.9 3.0 %collective-permute-start.4 = (bf16[128,896]{1,0:T(8,128)(2,1)S(1)}, bf16[128,896]{1,0:T(8,128)(2,1)S(1)}, u32[]{:S(2)}, u32[]{:S(2)}) collective-permute-start(bf16[128,896]{1,0:T(8,128)(2,1)S(1)} %collective-permute-done.1.ringed), channel_id=1, source_target_pairs={{0,1},{1,0},{2,3},{3,2},{4,5},{5,4},{6,7},{7,6},{8,9},{9,8},{10,11... | collective-permute-start | bytes 688136 | tf_op jit(solution)/shard_map/ppermute | solution.py:36
  14.4 9.8 %collective-permute-start = (bf16[128,896]{1,0:T(8,128)(2,1)S(1)}, bf16[128,896]{1,0:T(8,128)(2,1)S(1)}, u32[]{:S(2)}, u32[]{:S(2)}) collective-permute-start(bf16[128,896]{1,0:T(8,128)(2,1)S(1)} %get-tuple-element.82.block), channel_id=1, source_target_pairs={{0,2},{1,3},{2,6},{3,7},{4,0},{5,1},{6,4},{7,5},{8,10},{9,11},{10,... | collective-permute-start | bytes 688136 | tf_op jit(solution)/shard_map/ppermute | solution.py:36
  19.4 19.6 %collective-permute-start.8 = (bf16[400,896]{1,0:T(8,128)(2,1)S(1)}, bf16[400,896]{1,0:T(8,128)(2,1)S(1)}, u32[]{:S(2)}, u32[]{:S(2)}) collective-permute-start(bf16[400,896]{1,0:T(8,128)(2,1)S(1)} %get-tuple-element.71), channel_id=1, source_target_pairs={{0,4},{1,5},{2,6},{3,7},{4,0},{5,1},{6,2},{7,3},{8,12},{9,13},{10,... | collective-permute-start | bytes 2150408 | tf_op jit(solution)/shard_map/ppermute | solution.py:36
  24.2 6.2 %collective-permute-start.5 = (bf16[128,896]{1,0:T(8,128)(2,1)S(1)}, bf16[128,896]{1,0:T(8,128)(2,1)S(1)}, u32[]{:S(2)}, u32[]{:S(2)}) collective-permute-start(bf16[128,896]{1,0:T(8,128)(2,1)S(1)} %collective-permute-done.ringed), channel_id=1, source_target_pairs={{0,2},{1,3},{6,4},{7,5},{8,10},{9,11},{14,12},{15,13},{16,18},{17,... | collective-permute-start | bytes 688136 | tf_op jit(solution)/shard_map/ppermute | solution.py:36
  26.3 4.3 %collective-permute-start.7 = (bf16[128,896]{1,0:T(8,128)(2,1)S(1)}, bf16[128,896]{1,0:T(8,128)(2,1)S(1)}, u32[]{:S(2)}, u32[]{:S(2)}) collective-permute-start(bf16[128,896]{1,0:T(8,128)(2,1)S(1)} %collective-permute-done.ringed), channel_id=1, source_target_pairs={{0,1},{1,0},{2,3},{3,2},{4,5},{5,4},{6,7},{7,6},{8,9},{9,8},{10,11... | collective-permute-start | bytes 688136 | tf_op jit(solution)/shard_map/ppermute | solution.py:36
  30.5 1.6 %collective-permute-start.6 = (bf16[128,896]{1,0:T(8,128)(2,1)S(1)}, bf16[128,896]{1,0:T(8,128)(2,1)S(1)}, u32[]{:S(2)}, u32[]{:S(2)}) collective-permute-start(bf16[128,896]{1,0:T(8,128)(2,1)S(1)} %broadcast_select_fusion.crossed), channel_id=1, source_target_pairs={{0,1},{1,0},{2,3},{3,2},{4,5},{5,4},{6,7},{7,6},{8,9},{9,8},{10,11... | collective-permute-start | bytes 688136 | tf_op jit(solution)/shard_map/ppermute | solution.py:36
  35.4 20.1 %collective-permute-start.9 = (bf16[400,896]{1,0:T(8,128)(2,1)}, bf16[400,896]{1,0:T(8,128)(2,1)}, u32[]{:S(2)}, u32[]{:S(2)}) collective-permute-start(bf16[400,896]{1,0:T(8,128)(2,1)} %get-tuple-element.78), channel_id=1, source_target_pairs={{0,4},{1,5},{2,6},{3,7},{4,0},{5,1},{6,2},{7,3},{8,12},{9,13},{10,... | collective-permute-start | bytes 2150408 | tf_op jit(solution)/shard_map/ppermute | solution.py:36
  39.8 8.3 %collective-permute-start.10 = (bf16[128,896]{1,0:T(8,128)(2,1)S(1)}, bf16[128,896]{1,0:T(8,128)(2,1)}, u32[]{:S(2)}, u32[]{:S(2)}) collective-permute-start(bf16[128,896]{1,0:T(8,128)(2,1)S(1)} %get-tuple-element.72.refs_0_), channel_id=1, source_target_pairs={{0,8},{1,9},{2,12},{3,13},{4,10},{5,11},{6,14},{7,15},{8,16},{9,17... | collective-permute-start | bytes 688136 | tf_op jit(solution)/shard_map/ppermute | solution.py:36
  48.1 1.7 %collective-permute-start.11 = (bf16[128,896]{1,0:T(8,128)(2,1)}, bf16[128,896]{1,0:T(8,128)(2,1)S(1)}, u32[]{:S(2)}, u32[]{:S(2)}) collective-permute-start(bf16[128,896]{1,0:T(8,128)(2,1)} %collective-permute-done.10.mine), channel_id=1, source_target_pairs={{0,1},{1,0},{2,3},{3,2},{4,5},{5,4},{6,7},{7,6},{8,9},{9,8},{10,11... | collective-permute-start | bytes 688136 | tf_op jit(solution)/shard_map/ppermute | solution.py:36
  48.1 9.6 %collective-permute-start.13 = (bf16[128,896]{1,0:T(8,128)(2,1)}, bf16[128,896]{1,0:T(8,128)(2,1)}, u32[]{:S(2)}, u32[]{:S(2)}) collective-permute-start(bf16[128,896]{1,0:T(8,128)(2,1)} %collective-permute-done.10.mine), channel_id=1, source_target_pairs={{0,2},{1,3},{2,0},{3,1},{4,6},{5,7},{6,4},{7,5},{8,10},{9,11},{10,... | collective-permute-start | bytes 688136 | tf_op jit(solution)/shard_map/ppermute | solution.py:36
  57.7 8.6 %collective-permute-start.14 = (bf16[128,896]{1,0:T(8,128)(2,1)}, bf16[128,896]{1,0:T(8,128)(2,1)S(1)}, u32[]{:S(2)}, u32[]{:S(2)}) collective-permute-start(bf16[128,896]{1,0:T(8,128)(2,1)} %collective-permute-done.13.mine), channel_id=1, source_target_pairs={{0,1},{1,0},{2,3},{3,2},{4,5},{5,4},{6,7},{7,6},{8,9},{9,8},{10,11... | collective-permute-start | bytes 688136 | tf_op jit(solution)/shard_map/ppermute | solution.py:36
  57.8 13.9 %collective-permute-start.12 = (bf16[128,896]{1,0:T(8,128)(2,1)S(1)}, bf16[128,896]{1,0:T(8,128)(2,1)S(1)}, u32[]{:S(2)}, u32[]{:S(2)}) collective-permute-start(bf16[128,896]{1,0:T(8,128)(2,1)S(1)} %attend.3.refs_1_), channel_id=1, source_target_pairs={{0,8},{1,9},{2,12},{3,13},{4,10},{5,11},{6,14},{7,15},{8,16},{9,17... | collective-permute-start | bytes 688136 | tf_op jit(solution)/shard_map/ppermute | solution.py:36
  69.3 18.1 %collective-permute-start.20 = (bf16[400,896]{1,0:T(8,128)(2,1)S(1)}, bf16[400,896]{1,0:T(8,128)(2,1)S(1)}, u32[]{:S(2)}, u32[]{:S(2)}) collective-permute-start(bf16[400,896]{1,0:T(8,128)(2,1)S(1)} %get-tuple-element.94), channel_id=1, source_target_pairs={{0,4},{1,5},{2,6},{3,7},{4,0},{5,1},{6,2},{7,3},{8,12},{9,13},{10,... | collective-permute-start | bytes 2150408 | tf_op jit(solution)/shard_map/ppermute | solution.py:36
  71.7 7.1 %collective-permute-start.15 = (bf16[128,896]{1,0:T(8,128)(2,1)S(1)}, bf16[128,896]{1,0:T(8,128)(2,1)S(1)}, u32[]{:S(2)}, u32[]{:S(2)}) collective-permute-start(bf16[128,896]{1,0:T(8,128)(2,1)S(1)} %collective-permute-done.12.mine), channel_id=1, source_target_pairs={{0,2},{1,3},{2,0},{3,1},{4,6},{5,7},{6,4},{7,5},{8,10},{9,11},{10,... | collective-permute-start | bytes 688136 | tf_op jit(solution)/shard_map/ppermute | solution.py:36
  72.1 6.6 %collective-permute-start.17 = (bf16[128,896]{1,0:T(8,128)(2,1)S(1)}, bf16[128,896]{1,0:T(8,128)(2,1)S(1)}, u32[]{:S(2)}, u32[]{:S(2)}) collective-permute-start(bf16[128,896]{1,0:T(8,128)(2,1)S(1)} %collective-permute-done.12.mine), channel_id=1, source_target_pairs={{0,1},{1,0},{2,3},{3,2},{4,5},{5,4},{6,7},{7,6},{8,9},{9,8},{10,11... | collective-permute-start | bytes 688136 | tf_op jit(solution)/shard_map/ppermute | solution.py:36
  78.7 2.4 %collective-permute-start.16 = (bf16[128,896]{1,0:T(8,128)(2,1)S(1)}, bf16[128,896]{1,0:T(8,128)(2,1)S(1)}, u32[]{:S(2)}, u32[]{:S(2)}) collective-permute-start(bf16[128,896]{1,0:T(8,128)(2,1)S(1)} %collective-permute-done.15.mine), channel_id=1, source_target_pairs={{0,1},{1,0},{2,3},{3,2},{4,5},{5,4},{6,7},{7,6},{8,9},{9,8},{10,11... | collective-permute-start | bytes 688136 | tf_op jit(solution)/shard_map/ppermute | solution.py:36
  84.3 14.8 %collective-permute-start.19 = (bf16[400,640]{1,0:T(8,128)(2,1)}, bf16[400,640]{1,0:T(8,128)(2,1)}, u32[]{:S(2)}, u32[]{:S(2)}) collective-permute-start(bf16[400,640]{1,0:T(8,128)(2,1)} %get-tuple-element.92), channel_id=1, source_target_pairs={{0,4},{1,5},{2,6},{3,7},{4,0},{5,1},{6,2},{7,3},{8,12},{9,13},{10,... | collective-permute-start | bytes 1536008 | tf_op jit(solution)/shard_map/ppermute | solution.py:36
  84.4 18.6 %collective-permute-start.18 = (bf16[384,256]{1,0:T(8,128)(2,1)}, bf16[384,256]{1,0:T(8,128)(2,1)}, u32[]{:S(2)}, u32[]{:S(2)}) collective-permute-start(bf16[384,256]{1,0:T(8,128)(2,1)} %get-tuple-element.91), channel_id=1, source_target_pairs={{0,4},{1,5},{2,6},{3,7},{4,0},{5,1},{6,2},{7,3},{8,12},{9,13},{10,... | collective-permute-start | bytes 589832 | tf_op jit(solution)/shard_map/ppermute | solution.py:36
  87.4 9.4 %collective-permute-start.21 = (bf16[128,896]{1,0:T(8,128)(2,1)}, bf16[128,896]{1,0:T(8,128)(2,1)}, u32[]{:S(2)}, u32[]{:S(2)}) collective-permute-start(bf16[128,896]{1,0:T(8,128)(2,1)} %get-tuple-element.100.own), channel_id=1, source_target_pairs={{0,8},{1,9},{2,10},{3,11},{4,12},{5,13},{6,14},{7,15},{8,16},{9,17... | collective-permute-start | bytes 688136 | tf_op jit(solution)/shard_map/ppermute | solution.py:36
  92.4 10.6 %collective-permute-start.22 = (bf16[128,896]{1,0:T(8,128)(2,1)}, bf16[128,896]{1,0:T(8,128)(2,1)}, u32[]{:S(2)}, u32[]{:S(2)}) collective-permute-start(bf16[128,896]{1,0:T(8,128)(2,1)} %get-tuple-element.106.own), channel_id=1, source_target_pairs={{0,8},{1,9},{2,10},{3,11},{4,12},{5,13},{6,14},{7,15},{8,16},{9,17... | collective-permute-start | bytes 688136 | tf_op jit(solution)/shard_map/ppermute | solution.py:36
  (17 other events, 150.1 us)
